TPU v7x, 32 devices: a whole 2x2x4 slice. The times are simulated.
32 devices in a mesh: group: 2 (over y), expert: 16 (over z, x, core), dp: 1.
Axes of the slice: x: 2, y: 2, z: 4, core: 2. Of those that a mesh axis runs over, the one named last changes fastest.
Arguments:
- tokens: bfloat16 [1536, 3584], P(('group', 'expert', 'dp')), parts along dimension 0, may hold values from -6 to 6
- expert_ids: int32 [1536, 8], P(('group', 'expert', 'dp')), parts along dimension 0, may hold values from 0 to 15, all different within a row; in each aligned block of 48 rows (0 to 47, 48 to 95, ...) at most 36 rows name the same one
- route_probs: float32 [1536, 8], P(('group', 'expert', 'dp')), parts along dimension 0, may hold values from 0.1 to 1
- cotangents: bfloat16 [1536, 8, 2560], P(('group', 'expert', 'dp')), parts along dimension 0, may hold values from -6 to 6
- sketch: float32 [2560, 32], replicated, may hold values from -6 to 6
Outputs:
- basis: float32 [32, 32, 3584], P(('group', 'expert'), None, 'dp'), parts along dimension 0
- coeffs: float32 [32, 32, 2560], P(('group', 'expert'), None, 'dp'), parts along dimension 0
There are 2 independent parts, one for each index of `group`. A program takes and returns all parts, laid end to end along the dimension named above; an argument that names none is the same for every part. Nothing has to cross between parts.
Inputs may be any that keep to these rules, and one draw needn't show every extreme that they name: `expert_ids`: each row names 8 different experts. In the rows of one device no expert is named more than 36 times, and exactly 36 times for some expert in some devices.
All inputs are finite; a program needn't handle non-finite values.
Results may differ from a plain program's by a relative error of at most 0.019.
Values may be sent and summed in bfloat16 or wider, within the bound.
No kernel may reach another device: no remote copies, remote signals or barrier semaphores. Data moves between devices by JAX's collectives and lax.ppermute only.
A program may use at most 128 MiB of HBM per device.

v0:
```python
import math

import jax
import jax.numpy as jnp
from jax import lax
from jax.sharding import PartitionSpec as P

EXP_DEV = 1


def triangular(lower, right):
    return jax.vmap(
        lambda left_m, right_m: jax.scipy.linalg.solve_triangular(left_m, right_m, lower=True)
    )(lower, right)


def shards(tokens, expert_ids, route_probs, cotangents, sketch):
    high = lax.Precision.HIGHEST
    n_owner = lax.axis_size("expert")
    tok = tokens.shape[0]
    width = tokens.shape[1]
    top = expert_ids.shape[1]
    hidden = cotangents.shape[2]
    experts_all = EXP_DEV * n_owner
    cap = min(tok, max(2, 3 * tok * top // (2 * experts_all)))
    rows_local = tok * top
    flat_ids = expert_ids.reshape(-1)
    table = (flat_ids[:, None] == jnp.arange(experts_all, dtype=jnp.int32)[None, :]).astype(
        jnp.int32
    )
    ranks = jnp.sum((jnp.cumsum(table, axis=0) - 1) * table, axis=1)
    target = flat_ids * cap + ranks
    weighted = (
        (route_probs[..., None] * cotangents.astype(jnp.float32))
        .astype(jnp.bfloat16)
        .reshape(rows_local, hidden)
    )
    repeated = jnp.repeat(tokens, top, axis=0)
    send_rows = jnp.zeros((experts_all * cap, width), jnp.bfloat16).at[target].set(repeated)
    send_grads = jnp.zeros((experts_all * cap, hidden), jnp.bfloat16).at[target].set(weighted)
    send_rows = send_rows.reshape(n_owner, EXP_DEV * cap, width)
    send_grads = send_grads.reshape(n_owner, EXP_DEV * cap, hidden)
    recv_rows, recv_grads = (
        lax.all_to_all(send_rows, "expert", split_axis=0, concat_axis=0, tiled=True),
        lax.all_to_all(send_grads, "expert", split_axis=0, concat_axis=0, tiled=True),
    )
    recv_rows = recv_rows.reshape(n_owner, EXP_DEV, cap, width)
    recv_grads = recv_grads.reshape(n_owner, EXP_DEV, cap, hidden)
    scale = 1.0 / math.sqrt(tok * top)
    local_grad = (
        jnp.einsum("sjcd,sjcf->jdf", recv_rows, recv_grads, preferred_element_type=jnp.float32)
        * scale
    ).astype(jnp.bfloat16)
    shares = lax.psum_scatter(local_grad, "dp", scatter_dimension=1, tiled=True).astype(jnp.float32)
    range_rows = jnp.einsum("jdf,fk->jdk", shares, sketch, precision=high)
    gram = lax.psum(jnp.einsum("jdk,jdl->jkl", range_rows, range_rows, precision=high), "dp")
    ortho = triangular(jnp.linalg.cholesky(gram), jnp.swapaxes(range_rows, 1, 2))
    projected = jnp.einsum("jkd,jdf->jkf", ortho, shares, precision=high)
    coeffs = lax.psum_scatter(
        projected.astype(jnp.bfloat16), "dp", scatter_dimension=2, tiled=True
    ).astype(jnp.float32)
    basis = math.sqrt(width) * ortho
    return (basis, coeffs)


def solution(mesh):
    in_specs = (
        P(("group", "expert", "dp"), None),
        P(("group", "expert", "dp"), None),
        P(("group", "expert", "dp"), None),
        P(("group", "expert", "dp"), None, None),
        P(),
    )
    out_specs = (P(("group", "expert"), None, "dp"), P(("group", "expert"), None, "dp"))
    return jax.shard_map(shards, mesh=mesh, in_specs=in_specs, out_specs=out_specs, check_vma=False)
```

profile of v0, /device:TPU:0, one launch (start us, length us, event | category | flops | bytes accessed | tf_op | source)
XLA Modules:
  0.0 259.3 jit_solution(12055491965343399323)
XLA Ops:
  0.6 0.7 broadcast_multiply_fusion
  1.4 0.8 copy.11
  2.4 0.1 mul.45
  2.5 0.9 reduce-window.6
  3.4 0.2 slice_reduce_fusion
  3.6 0.8 copy.14
  4.4 0.1 fusion.15
  4.5 5.4 %scatter_custom_fusion.1 = bf16[576,2560]{1,0:T(8,128)(2,1)S(1)} fusion(s32[384]{0:T(512)S(1)} %fusion.20, bf16[48,8,2560]{2,1,0:T(8,128)(2,1)} %param.8, f32[48,8]{1,0:T(8,128)S(1)} %copy.14, bf16[]{:T(256)} %constant.56.clone.1), kind=kCustom, calls=%fused_computation.12 | custom fusion | flops 2949120 | bytes 4939778 | tf_op jit(solution)/shard_map/scatter | solution.py:40
  9.9 2.5 reshape.149
  12.4 7.4 %all-to-all-start.1 = ((bf16[16,36,2560]{2,1,0:T(8,128)(2,1)}), bf16[16,36,2560]{2,1,0:T(8,128)(2,1)}, u32[]{:S(2)}, u32[]{:S(2)}) async-start(bf16[16,36,2560]{2,1,0:T(8,128)(2,1)} %reshape.149), calls=%async_computation.1 | async-start | bytes 6553600 | tf_op jit(solution)/shard_map/all_to_all | solution.py:45
  19.8 6.8 %scatter_custom_fusion = bf16[576,3584]{1,0:T(8,128)(2,1)} fusion(s32[384]{0:T(512)S(1)} %fusion.20, bf16[]{:T(256)} %constant.56.clone.1, bf16[48,3584]{1,0:T(8,128)(2,1)S(1)} %copy-done), kind=kCustom, calls=%fused_computation.8 | custom fusion | bytes 4472834 | tf_op jit(solution)/shard_map/scatter | solution.py:39
  26.6 6.9 %reshape.147 = bf16[16,36,3584]{2,1,0:T(8,128)(2,1)} reshape(bf16[576,3584]{1,0:T(8,128)(2,1)} %scatter_custom_fusion) | data formatting | bytes 8257536 | tf_op jit(solution)/shard_map/reshape | solution.py:41
  33.5 48.0 %all-to-all-done.1 = bf16[16,36,2560]{2,1,0:T(8,128)(2,1)} async-done(((bf16[16,36,2560]{2,1,0:T(8,128)(2,1)}), bf16[16,36,2560]{2,1,0:T(8,128)(2,1)}, u32[]{:S(2)}, u32[]{:S(2)}) %all-to-all-start.1) | async-done | bytes 2949152 | tf_op jit(solution)/shard_map/all_to_all | solution.py:45
  81.5 117.2 %all_to_all.10 = bf16[16,36,3584]{2,1,0:T(8,128)(2,1)S(1)} all-to-all(bf16[16,36,3584]{2,1,0:T(8,128)(2,1)} %reshape.147), channel_id=1, replica_groups=mesh['group'=2,'expert'=16,'dp'=1] {'expert'}, dimensions={0} | all-to-all | bytes 8257536 | tf_op jit(solution)/shard_map/all_to_all | solution.py:44
  198.6 19.2 %fusion = bf16[3584,2560]{1,0:T(8,128)(2,1)} fusion(bf16[16,36,3584]{2,1,0:T(8,128)(2,1)S(1)} %all_to_all.10, bf16[16,36,2560]{2,1,0:T(8,128)(2,1)} %all-to-all-done.1), kind=kOutput, calls=%fused_computation.3 | convolution fusion | flops 10587996160 | bytes 25427968 | tf_op jit(solution)/shard_map/sjcd,sjcf->jdf/dot_general | solution.py:51
  217.9 19.3 %fusion.21 = f32[3584,32]{0,1:T(8,128)S(1)} fusion(bf16[3584,2560]{1,0:T(8,128)(2,1)} %fusion, f32[2560,32]{0,1:T(8,128)S(1)} %copy-done.1), kind=kOutput, calls=%fused_computation.39 | convolution fusion | flops 3523215360 | bytes 19136512 | tf_op jit(solution)/shard_map/jdf,fk->jdk/dot_general | solution.py:55
  237.2 0.5 fusion.22
  237.8 2.9 %custom-call.8 = f32[1,32,32]{2,1,0:T(8,128)S(1)} custom-call(f32[1,32,32]{2,1,0:T(8,128)S(1)} %fusion.18), custom_call_target="Cholesky" | custom-call | tf_op jit(solution)/shard_map/jit(cholesky)/cholesky | solution.py:57
  240.7 0.6 compare_reduce_fusion
  241.4 0.7 fusion.17
  242.0 2.4 custom-call.9
  244.4 0.6 fusion.12
  245.1 13.4 %fusion.2 = f32[1,32,2560]{2,1,0:T(8,128)} fusion(f32[32,3584]{1,0:T(8,128)S(1)} %fusion.12, bf16[3584,2560]{1,0:T(8,128)(2,1)} %fusion), kind=kOutput, calls=%fused_computation.7 | convolution fusion | flops 3523379200 | bytes 19136512 | tf_op jit(solution)/shard_map/jkd,jdf->jkf/dot_general | solution.py:58
  258.5 0.8 multiply_bitcast_fusion
  (13 shorter events, 0.5 us)
Async XLA Ops:
  0.6 19.1 %copy-start = (bf16[48,3584]{1,0:T(8,128)(2,1)S(1)}, bf16[48,3584]{1,0:T(8,128)(2,1)}, u32[]{:S(2)}) copy-start(bf16[48,3584]{1,0:T(8,128)(2,1)} %param.5) | copy-start | bytes 1032196
  12.4 69.1 %all-to-all-start.1 = ((bf16[16,36,2560]{2,1,0:T(8,128)(2,1)}), bf16[16,36,2560]{2,1,0:T(8,128)(2,1)}, u32[]{:S(2)}, u32[]{:S(2)}) async-start(bf16[16,36,2560]{2,1,0:T(8,128)(2,1)} %reshape.149), calls=%async_computation.1 | async-start | bytes 6553600 | tf_op jit(solution)/shard_map/all_to_all | solution.py:45
  198.6 19.2 %copy-start.1 = (f32[2560,32]{0,1:T(8,128)S(1)}, f32[2560,32]{0,1:T(8,128)}, u32[]{:S(2)}) copy-start(f32[2560,32]{0,1:T(8,128)} %param.9) | copy-start | bytes 983044
where the time goes:
time: 260 us; the launch traced here: 259 us
  blocking collectives  117 us (45%)
  matrix products  53 us (20%)
  waiting for transfers between devices  48 us (18%)
  local copies, waits for them, and re-layouts  18.4 us (7%)
  other arithmetic  14.6 us (6%)
  starting transfers between devices  7.4 us (3%)
    all_to_all x1, blocking collectives, shards(): lax.all_to_all(send_rows, 'expert', split_axis=0, concat_axis=0, tiled=True)  117 us
    all_to_all x1, waiting for transfers between devices, shards(): lax.all_to_all(send_grads, 'expert', split_axis=0, concat_axis=0, tiled=T...  48 us
    dot_general x1, matrix products, shards(): range_rows = jnp.einsum('jdf,fk->jdk', shares, sketch, precision=high)  19.3 us
    dot_general x1, matrix products, shards(): jnp.einsum('sjcd,sjcf->jdf', recv_rows, recv_grads, preferred_element_typ...  19.2 us
    dot_general x1, matrix products, shards(): projected = jnp.einsum('jkd,jdf->jkf', ortho, shares, precision=high)  13.4 us
    all_to_all x1, starting transfers between devices, shards(): lax.all_to_all(send_grads, 'expert', split_axis=0, concat_axis=0, tiled=T...  7.4 us
    reshape x1, local copies, waits for them, and re-layouts, shards(): send_rows = send_rows.reshape(n_owner, EXP_DEV * cap, width)  6.88 us
    scatter x1, local copies, waits for them, and re-layouts, shards(): jnp.zeros((experts_all * cap, width), jnp.bfloat16).at[target].set(repeated)  6.85 us
  transfers between devices with their start and end apart: 1, of which 1 were waited for; matrix products, arithmetic and copies ran while one was open for 5% of the time, Pallas kernels for 0%

commit v1 on v0

v1 whole, which is shorter than its diff:
```python
import math

import jax
import jax.numpy as jnp
from jax import lax
from jax.sharding import PartitionSpec as P

AXES = ("expert", "dp")
HIGH = lax.Precision.HIGHEST


def dot(left, right, dims):
    return lax.dot_general(left, right, (dims, ((), ())), preferred_element_type=jnp.float32)


def shards(tokens, expert_ids, route_probs, cotangents, sketch):
    n_expert = lax.axis_size("expert")
    n_dp = lax.axis_size("dp")
    tok, width = tokens.shape
    top = expert_ids.shape[1]
    hidden, rank = sketch.shape
    rows = tok * top
    scale = 1.0 / math.sqrt(rows)
    cot = cotangents.reshape(rows, hidden)

    x_all = lax.all_gather(tokens, AXES, axis=0, tiled=True)

    high = sketch.astype(jnp.bfloat16)
    low = (sketch - high.astype(jnp.float32)).astype(jnp.bfloat16)
    both = dot(cot, jnp.concatenate([high, low], axis=1), ((1,), (0,)))
    pair = (both[:, :rank] + both[:, rank:]).reshape(tok, top, rank) * route_probs[..., None]
    chosen = expert_ids[..., None] == jnp.arange(n_expert, dtype=jnp.int32)
    y = jnp.sum(jnp.where(chosen[..., None], pair[:, :, None, :], 0.0), axis=1)
    y = y.reshape(tok, n_expert * rank).astype(jnp.bfloat16)
    y_all = lax.all_gather(y, AXES, axis=0, tiled=True)

    near = dot(tokens, x_all, ((1,), (1,))).astype(jnp.bfloat16)
    z = dot(near, y_all, ((1,), (0,)))
    weights = jnp.where(chosen, route_probs[..., None], 0.0)
    spread = z.reshape(tok, 1, n_expert, rank) * weights[..., None]
    spread = spread.reshape(rows, n_expert * rank).astype(jnp.bfloat16)
    part = dot(spread, cot, ((0,), (0,))).astype(jnp.bfloat16)
    if n_dp > 1:
        part = part.reshape(n_expert, rank, n_dp, hidden // n_dp).swapaxes(1, 2)
        part = part.reshape(n_expert * n_dp * rank, hidden // n_dp)
    total = lax.psum_scatter(part, AXES, scatter_dimension=0, tiled=True).astype(jnp.float32)

    own = lax.axis_index("expert")
    y_own = lax.dynamic_slice_in_dim(y_all, own * rank, rank, axis=1)
    range_rows = dot(y_own, x_all, ((0,), (0,)))
    gram = lax.dot_general(range_rows, range_rows, (((1,), (1,)), ((), ())), precision=HIGH)
    lower = jnp.linalg.cholesky(gram)
    inverse = jax.scipy.linalg.solve_triangular(
        lower, jnp.eye(rank, dtype=jnp.float32), lower=True
    )
    share = width // n_dp
    kept = lax.dynamic_slice_in_dim(range_rows, lax.axis_index("dp") * share, share, axis=1)
    basis = jnp.dot(inverse * math.sqrt(width), kept, precision=HIGH)
    coeffs = jnp.dot(inverse * scale, total, precision=HIGH)
    return basis[None], coeffs[None]


def solution(mesh):
    in_specs = (
        P(("group", "expert", "dp"), None),
        P(("group", "expert", "dp"), None),
        P(("group", "expert", "dp"), None),
        P(("group", "expert", "dp"), None, None),
        P(),
    )
    out_specs = (P(("group", "expert"), None, "dp"), P(("group", "expert"), None, "dp"))
    return jax.shard_map(shards, mesh=mesh, in_specs=in_specs, out_specs=out_specs, check_vma=False)
```

time: 260 us -> 158 us (0.61)
  blocking collectives: 117 us -> 27.9 us
  matrix products: 53 us -> 17.1 us
  waiting for transfers between devices: 48 us -> 83.6 us
  local copies, waits for them, and re-layouts: 18.4 us -> 3.86 us
  between operations: 0.72 us -> 14.2 us
  starting transfers between devices: 7.4 us -> 0.08 us
  other arithmetic: 14.6 us -> 11.2 us
    all_to_all x1 -> x0, blocking collectives: 117 us -> none  [shards(): lax.all_to_all(send_rows, 'expert', split_axis=0, concat_axis=0, tiled=True)]
    reduce_scatter x0 -> x1, waiting for transfers between devices: none -> 50.2 us  [shards(): lax.psum_scatter(part, AXES, scatter_dimension=0, tiled=True)]
    all_to_all x1 -> x0, waiting for transfers between devices: 48 us -> none  [shards(): lax.all_to_all(send_grads, 'expert', split_axis=0, concat_axis=0, tiled=T...]
    dot_general x4 -> x7, matrix products: 52.4 us -> 16.9 us  [the longest x4 13.2 us: dot(): lax.dot_general(left, right, (dims, ((), ())), preferred_element_type=jnp...]
    all_gather x0 -> x1, waiting for transfers between devices: none -> 32.8 us  [shards(): x_all = lax.all_gather(tokens, AXES, axis=0, tiled=True)]
    all_gather x0 -> x1, blocking collectives: none -> 27.9 us  [shards(): y_all = lax.all_gather(y, AXES, axis=0, tiled=True)]
    reshape x2 -> x0, local copies, waits for them, and re-layouts: 9.33 us -> none  [the longest x1 6.88 us: shards(): send_rows = send_rows.reshape(n_owner, EXP_DEV * cap, width)]
    all_to_all x1 -> x0, starting transfers between devices: 7.4 us -> none  [shards(): lax.all_to_all(send_grads, 'expert', split_axis=0, concat_axis=0, tiled=T...]
  transfers between devices with their start and end apart: 1 -> 2, of which waited for: 1 -> 2; matrix products, arithmetic and copies ran while one was open for 5% -> 10% of each run, Pallas kernels for 0% -> 0%
where the time goes in v1:
time: 158 us
  waiting for transfers between devices  83.6 us (53%)
  blocking collectives  27.9 us (18%)
  matrix products  17.1 us (11%)
  between operations  14.2 us (9%)
  other arithmetic  11.2 us (7%)
  local copies, waits for them, and re-layouts  3.86 us (2%)
    reduce_scatter x1, waiting for transfers between devices, shards(): lax.psum_scatter(part, AXES, scatter_dimension=0, tiled=True)  50.2 us
    all_gather x1, waiting for transfers between devices, shards(): x_all = lax.all_gather(tokens, AXES, axis=0, tiled=True)  32.8 us
    all_gather x1, blocking collectives, shards(): y_all = lax.all_gather(y, AXES, axis=0, tiled=True)  27.9 us
    dot_general x4, matrix products, dot(): lax.dot_general(left, right, (dims, ((), ())), preferred_element_type=jnp...  13.2 us
    another operation x3, other arithmetic, shards(): lower = jnp.linalg.cholesky(gram)  3.6 us
  transfers between devices with their start and end apart: 2, of which 2 were waited for; matrix products, arithmetic and copies ran while one was open for 10% of the time, Pallas kernels for 0%

profile of v1, /device:TPU:0, one launch (start us, length us, event | category | flops | bytes accessed | tf_op | source)
XLA Modules:
  0.0 158.0 jit_solution(14285243410442403251)
XLA Ops:
  7.2 0.7 all-gather.2.cloned.1.call-update
  8.0 1.1 subtract_convert_fusion
  9.1 0.7 fusion.3
  10.4 0.1 iota_compare_fusion
  10.6 0.1 copy.18
  10.7 0.4 select_reduce_fusion
  11.2 0.8 broadcast_select_fusion
  12.0 27.9 %all_gather.6 = bf16[768,512]{1,0:T(8,128)(2,1)S(1)} all-gather(bf16[48,512]{1,0:T(8,128)(2,1)S(1)} %copy.25), channel_id=1, replica_groups=mesh['group'=2,'expert'=16,'dp'=1] {'expert','dp'}, dimensions={0}, use_global_device_ids=true | all-gather | bytes 835584 | tf_op jit(solution)/shard_map/all_gather | solution.py:35
  39.9 32.8 %all-gather.2.cloned.1.call-done = bf16[768,3584]{1,0:T(8,128)(2,1)} async-done(((bf16[48,3584]{1,0:T(8,128)(2,1)}), bf16[768,3584]{1,0:T(8,128)(2,1)}) %all-gather.2.cloned.1.call-update) | async-done | bytes 5505040 | tf_op jit(solution)/shard_map/all_gather | solution.py:26
  72.7 4.6 %fusion.6 = f32[48,512]{1,0:T(8,128)S(1)} fusion(bf16[768,512]{1,0:T(8,128)(2,1)S(1)} %all_gather.6, bf16[48,3584]{1,0:T(8,128)(2,1)S(1)} %copy-done.2, bf16[768,3584]{1,0:T(8,128)(2,1)} %all-gather.2.cloned.1.call-done), kind=kOutput, calls=%fused_computation.10 | convolution fusion | flops 302026752 | bytes 6733824 | tf_op jit(solution)/shard_map/dot_general | solution.py:13
  77.3 0.9 mul.58
  78.2 2.0 %multiply_convert_fusion = bf16[48,8,16,32]{3,2,1,0:T(8,128)(2,1)S(1)} fusion(f32[48,8,16]{2,1,0:T(8,128)} %broadcast_select_fusion, f32[48,16,32]{2,1,0:T(8,128)} %mul.58), kind=kLoop, calls=%fused_computation.3 | loop fusion | flops 393216 | bytes 516096 | tf_op jit(solution)/shard_map/convert_element_type | solution.py:41
  80.1 2.3 %convert_element_type.42 = bf16[384,512]{1,0:T(8,128)(2,1)} reshape(bf16[48,8,16,32]{3,2,1,0:T(8,128)(2,1)S(1)} %multiply_convert_fusion) | data formatting | bytes 786432 | tf_op jit(solution)/shard_map/convert_element_type | solution.py:41
  82.4 4.0 %convolution_convert_fusion = bf16[512,2560]{1,0:T(8,128)(2,1)} fusion(bf16[384,512]{1,0:T(8,128)(2,1)} %convert_element_type.42, bf16[48,8,2560]{2,1,0:T(8,128)(2,1)S(1)} %copy-done), kind=kOutput, calls=%fused_computation.1 | convolution fusion | flops 1007943680 | bytes 4980736 | tf_op jit(solution)/shard_map/dot_general | solution.py:13
  86.4 3.8 %fusion.10 = f32[32,3584]{1,0:T(8,128)S(1)} fusion(bf16[768,3584]{1,0:T(8,128)(2,1)} %all-gather.2.cloned.1.call-done, bf16[768,512]{1,0:T(8,128)(2,1)} %copy-done.1, s32[]{:T(128)S(6)} %select_n.21), kind=kOutput, calls=%fused_computation.16 | convolution fusion | flops 176160768 | bytes 6160388 | tf_op jit(solution)/shard_map/dot_general | solution.py:13
  90.3 0.5 fusion.24
  90.9 2.9 %cholesky.17 = f32[32,32]{1,0:T(8,128)S(1)} custom-call(f32[32,32]{1,0:T(8,128)S(1)} %fusion.15), custom_call_target="Cholesky" | custom-call | tf_op jit(solution)/shard_map/jit(cholesky)/cholesky | solution.py:52
  93.8 0.6 compare_reduce_fusion
  94.5 0.7 fusion.12
  95.1 2.4 %custom-call.7 = f32[1,32,32]{1,2,0:T(8,128)S(1)} custom-call(f32[1,32,32]{2,1,0:T(8,128)S(1)} %fusion.12), custom_call_target="InvertDiagBlocksLowerTriangular" | custom-call | tf_op jit(solution)/shard_map/jit(_solve_triangular)/triangular_solve | solution.py:53
  97.6 0.2 fusion.13
  97.8 1.3 convolution_bitcast_fusion
  99.1 50.2 %reduce-scatter.2.cloned.1.call-done = bf16[32,2560]{1,0:T(8,128)(2,1)} async-done(((bf16[512,2560]{1,0:T(8,128)(2,1)}), bf16[32,2560]{1,0:T(8,128)(2,1)}) %reduce-scatter.2.cloned.1.call-update) | async-done | bytes 163856 | tf_op jit(solution)/shard_map/reduce_scatter | solution.py:46
  149.2 1.9 %convolution_bitcast_fusion.1 = f32[1,32,2560]{2,1,0:T(8,128)} fusion(bf16[32,2560]{1,0:T(8,128)(2,1)} %reduce-scatter.2.cloned.1.call-done, f32[32,32]{1,0:T(8,128)S(1)} %fusion.13), kind=kOutput, calls=%fused_computation.2 | convolution fusion | flops 31458304 | bytes 495616 | tf_op jit(solution)/shard_map/dot_general | solution.py:59
  (23 shorter events, 0.8 us)
Async XLA Ops:
  7.2 1.9 %copy-start = (bf16[48,8,2560]{2,1,0:T(8,128)(2,1)S(1)}, bf16[48,8,2560]{2,1,0:T(8,128)(2,1)}, u32[]{:S(2)}) copy-start(bf16[48,8,2560]{2,1,0:T(8,128)(2,1)} %param.8) | copy-start | bytes 5898244
  7.2 2.8 %copy-start.3 = (f32[48,8]{0,1:T(8,128)S(1)}, f32[48,8]{0,1:T(8,128)}, u32[]{:S(2)}) copy-start(f32[48,8]{0,1:T(8,128)} %param.7) | copy-start | bytes 4612
  7.2 3.2 %copy-start.4 = (s32[48,8]{0,1:T(8,128)S(1)}, s32[48,8]{0,1:T(8,128)}, u32[]{:S(2)}) copy-start(s32[48,8]{0,1:T(8,128)} %param.6) | copy-start | bytes 4612
  7.2 65.5 %all-gather.2.cloned.1.call-start = ((), (), s32[]{:S(2)}) async-start(), calls=%async_computation.1 | async-start | bytes 5849088 | tf_op jit(solution)/shard_map/all_gather | solution.py:26
  7.9 141.3 %reduce-scatter.2.cloned.1.call-start = ((), (), s32[]{:S(2)}) async-start(), calls=%async_computation.2 | async-start | bytes 2785280 | tf_op jit(solution)/shard_map/reduce_scatter | solution.py:46
  9.1 63.6 %copy-start.2 = (bf16[48,3584]{1,0:T(8,128)(2,1)S(1)}, bf16[48,3584]{1,0:T(8,128)(2,1)}, u32[]{:S(2)}) copy-start(bf16[48,3584]{1,0:T(8,128)(2,1)} %param.5) | copy-start | bytes 1032196
  39.9 37.4 %copy-start.1 = (bf16[768,512]{1,0:T(8,128)(2,1)}, bf16[768,512]{1,0:T(8,128)(2,1)S(1)}, u32[]{:S(2)}) copy-start(bf16[768,512]{1,0:T(8,128)(2,1)S(1)} %all_gather.6) | copy-start | bytes 2359300
Sparse Core Ops, SparseCore 0:
  10.3 62.3 all-gather.1
  86.6 62.6 reduce-scatter.1

commit v2 on v1

v2 whole, which is shorter than its diff:
```python
import math

import jax
import jax.numpy as jnp
from jax import lax
from jax.sharding import PartitionSpec as P

AXES = ("expert", "dp")
HIGH = lax.Precision.HIGHEST
CHUNKS = 2


def dot(left, right, dims):
    return lax.dot_general(left, right, (dims, ((), ())), preferred_element_type=jnp.float32)


def exchange(block, step, count):
    return lax.ppermute(block, AXES, [(i, i ^ step) for i in range(count)])


def scatter_sum(blocks, count):
    step = 1
    while blocks.shape[0] > 4:
        pairs = blocks.reshape(-1, 2, *blocks.shape[1:])
        other = exchange(pairs[:, 1], step, count)
        blocks = (pairs[:, 0].astype(jnp.float32) + other.astype(jnp.float32)).astype(jnp.bfloat16)
        step *= 2
    total = blocks[0].astype(jnp.float32)
    others = [exchange(blocks[j], j * step, count) for j in range(1, blocks.shape[0])]
    for other in others:
        total = total + other.astype(jnp.float32)
    return total


def shards(tokens, expert_ids, route_probs, cotangents, sketch):
    n_expert = lax.axis_size("expert")
    n_dp = lax.axis_size("dp")
    count = n_expert * n_dp
    tok, width = tokens.shape
    top = expert_ids.shape[1]
    hidden, rank = sketch.shape
    rows = tok * top
    share = width // count
    lanes = -(-(share + top) // 128) * 128
    scale = 1.0 / math.sqrt(rows)
    cot = cotangents.reshape(rows, hidden)
    own = lax.axis_index("expert")
    half = lax.axis_index("dp")

    cut = tokens.reshape(tok, count, share).swapaxes(0, 1)
    names = jnp.broadcast_to(expert_ids.astype(jnp.bfloat16)[None], (count, tok, top))
    cut = jnp.concatenate(
        [cut, names, jnp.zeros((count, tok, lanes - share - top), jnp.bfloat16)], axis=2
    )
    cut = lax.all_to_all(cut, AXES, split_axis=0, concat_axis=0, tiled=True)
    cut = cut.reshape(count * tok, lanes)
    names_all = cut[:, share : share + top]
    x = jnp.where(jnp.arange(lanes) < share, cut, jnp.zeros((), jnp.bfloat16))

    block = jnp.arange(n_expert * rank, dtype=jnp.int32) // rank
    ids = expert_ids.reshape(rows, 1)
    probs = route_probs.reshape(rows, 1)
    wide = jnp.tile(sketch.astype(jnp.bfloat16), (1, n_expert))
    y = jnp.where(ids == block, dot(cot, wide, ((1,), (0,))) * probs, 0.0)
    y = jnp.sum(y.reshape(tok, top, n_expert * rank), axis=1).astype(jnp.bfloat16)
    y_all = lax.all_gather(y, AXES, axis=0, tiled=True)

    columns = dot(y_all, x, ((0,), (0,))).astype(jnp.bfloat16)
    z = dot(x, columns, ((1,), (1,)))
    fold = (jnp.arange(n_expert * rank)[:, None] % rank == jnp.arange(rank)).astype(jnp.bfloat16)
    taken = [
        dot(
            jnp.where(names_all[:, s : s + 1] == block.astype(jnp.bfloat16), z, 0.0).astype(
                jnp.bfloat16
            ),
            fold,
            ((1,), (0,)),
        ).astype(jnp.bfloat16)
        for s in range(top)
    ]
    z = jnp.concatenate(taken, axis=1).reshape(count, tok, top * rank)
    z = lax.all_to_all(z, AXES, split_axis=0, concat_axis=0, tiled=True)
    columns = jnp.repeat(columns.reshape(n_expert, rank, lanes), n_dp, axis=0)
    columns = lax.all_to_all(columns, AXES, split_axis=0, concat_axis=0, tiled=True)

    z = jnp.repeat(jnp.sum(z.astype(jnp.float32), axis=0), top, axis=0) * probs
    slot = jnp.arange(top * rank) // rank
    z = jnp.where(jnp.arange(rows)[:, None] % top == slot, z, 0.0).astype(jnp.bfloat16)
    spread = jnp.arange(top * rank)[:, None] % rank == jnp.arange(n_expert * rank) % rank
    spread = dot(z, spread.astype(jnp.bfloat16), ((1,), (0,)))
    spread = jnp.where((ids ^ own) == block, spread, 0.0).astype(jnp.bfloat16)
    piece = hidden // n_dp // CHUNKS
    totals = []
    for chunk in range(CHUNKS):
        terms = []
        for h in range(n_dp):
            start = (half ^ h) * (hidden // n_dp) + chunk * piece
            columns_cot = (
                lax.dynamic_slice_in_dim(cot, start, piece, axis=1)
                if n_dp > 1
                else cot[:, chunk * piece : (chunk + 1) * piece]
            )
            part = dot(spread, columns_cot, ((0,), (0,))).astype(jnp.bfloat16)
            terms.append(part.reshape(n_expert, rank, piece))
        totals.append(scatter_sum(jnp.stack(terms, axis=1).reshape(count, rank, piece), count))
    total = jnp.concatenate(totals, axis=1)

    range_rows = columns[:, :, :share].swapaxes(0, 1).reshape(rank, width).astype(jnp.float32)
    gram = lax.dot_general(range_rows, range_rows, (((1,), (1,)), ((), ())), precision=HIGH)
    lower = jnp.linalg.cholesky(gram)
    inverse = jax.scipy.linalg.solve_triangular(
        lower, jnp.eye(rank, dtype=jnp.float32), lower=True
    )
    kept = lax.dynamic_slice_in_dim(range_rows, half * (width // n_dp), width // n_dp, axis=1)
    basis = jnp.dot(inverse * math.sqrt(width), kept, precision=HIGH)
    coeffs = jnp.dot(inverse * scale, total, precision=HIGH)
    return basis[None], coeffs[None]


def solution(mesh):
    in_specs = (
        P(("group", "expert", "dp"), None),
        P(("group", "expert", "dp"), None),
        P(("group", "expert", "dp"), None),
        P(("group", "expert", "dp"), None, None),
        P(),
    )
    out_specs = (P(("group", "expert"), None, "dp"), P(("group", "expert"), None, "dp"))
    return jax.shard_map(shards, mesh=mesh, in_specs=in_specs, out_specs=out_specs, check_vma=False)
```

time: 158 us -> 104 us (0.66)
  waiting for transfers between devices: 83.6 us -> 24.1 us
  starting transfers between devices: 0.08 us -> 26 us
  between operations: 14.2 us -> 0.99 us
  matrix products: 17.1 us -> 13 us
  blocking collectives: 27.9 us -> 24 us
  local copies, waits for them, and re-layouts: 3.86 us -> 7.19 us
  other arithmetic: 11.2 us -> 8.25 us
    reduce_scatter x1 -> x0, waiting for transfers between devices: 50.2 us -> none  [shards(): lax.psum_scatter(part, AXES, scatter_dimension=0, tiled=True)]
    all_gather x1 -> x0, waiting for transfers between devices: 32.8 us -> none  [shards(): x_all = lax.all_gather(tokens, AXES, axis=0, tiled=True)]
    ppermute x0 -> x10, waiting for transfers between devices: none -> 16.3 us  [exchange(): return lax.ppermute(block, AXES, [(i, i ^ step) for i in range(count)])]
    all_to_all x0 -> x3, starting transfers between devices: none -> 14.6 us  [the longest x1 7.36 us: shards(): cut = lax.all_to_all(cut, AXES, split_axis=0, concat_axis=0, tiled=True)]
    ppermute x0 -> x10, starting transfers between devices: none -> 11.4 us  [exchange(): return lax.ppermute(block, AXES, [(i, i ^ step) for i in range(count)])]
    all_to_all x0 -> x3, waiting for transfers between devices: none -> 7.8 us  [the longest x1 4.68 us: shards(): lax.all_to_all(columns, AXES, split_axis=0, concat_axis=0, tiled=True)]
    all_gather x1, blocking collectives: 27.9 us -> 24 us  [shards(): y_all = lax.all_gather(y, AXES, axis=0, tiled=True)]
    dot_general x4 -> x14, matrix products: 13.2 us -> 10.3 us  [dot(): lax.dot_general(left, right, (dims, ((), ())), preferred_element_type=jnp...]
  transfers between devices with their start and end apart: 2 -> 13, of which waited for: 2 -> 8; matrix products, arithmetic and copies ran while one was open for 10% -> 17% of each run, Pallas kernels for 0% -> 0%
where the time goes in v2:
time: 104 us
  starting transfers between devices  26 us (25%)
  waiting for transfers between devices  24.1 us (23%)
  blocking collectives  24 us (23%)
  matrix products  13 us (12%)
  other arithmetic  8.25 us (8%)
  local copies, waits for them, and re-layouts  7.19 us (7%)
    all_gather x1, blocking collectives, shards(): y_all = lax.all_gather(y, AXES, axis=0, tiled=True)  24 us
    ppermute x10, waiting for transfers between devices, exchange(): return lax.ppermute(block, AXES, [(i, i ^ step) for i in range(count)])  16.3 us
    ppermute x10, starting transfers between devices, exchange(): return lax.ppermute(block, AXES, [(i, i ^ step) for i in range(count)])  11.4 us
    dot_general x14, matrix products, dot(): lax.dot_general(left, right, (dims, ((), ())), preferred_element_type=jnp...  10.3 us
    all_to_all x1, starting transfers between devices, shards(): cut = lax.all_to_all(cut, AXES, split_axis=0, concat_axis=0, tiled=True)  7.36 us
    all_to_all x1, waiting for transfers between devices, shards(): lax.all_to_all(columns, AXES, split_axis=0, concat_axis=0, tiled=True)  4.68 us
    all_to_all x1, starting transfers between devices, shards(): z = lax.all_to_all(z, AXES, split_axis=0, concat_axis=0, tiled=True)  3.73 us
    another operation x3, other arithmetic, shards(): lower = jnp.linalg.cholesky(gram)  3.6 us
  transfers between devices with their start and end apart: 13, of which 8 were waited for; matrix products, arithmetic and copies ran while one was open for 17% of the time, Pallas kernels for 0%

profile of v2, /device:TPU:0, one launch (start us, length us, event | category | flops | bytes accessed | tf_op | source)
XLA Modules:
  0.0 103.6 jit_solution(13399565777431411782)
XLA Ops:
  0.6 1.5 %reshape.154 = bf16[48,16,224]{2,1,0:T(8,128)(2,1)S(1)} reshape(bf16[48,3584]{1,0:T(8,128)(2,1)} %param.5) | data formatting | bytes 688128 | tf_op jit(solution)/shard_map/reshape | solution.py:50
  4.2 7.4 %all-to-all-start = ((bf16[16,48,256]{2,1,0:T(8,128)(2,1)}), bf16[16,48,256]{2,1,0:T(8,128)(2,1)S(1)}, u32[]{:S(2)}, u32[]{:S(2)}) async-start(bf16[16,48,256]{2,1,0:T(8,128)(2,1)} %copy.41), calls=%async_computation | async-start | bytes 786432 | tf_op jit(solution)/shard_map/all_to_all | solution.py:55
  12.3 1.2 %copy-done.3 = bf16[48,8,2560]{2,1,0:T(8,128)(2,1)S(1)} copy-done((bf16[48,8,2560]{2,1,0:T(8,128)(2,1)S(1)}, bf16[48,8,2560]{2,1,0:T(8,128)(2,1)}, u32[]{:S(2)}) %copy-start.3) | copy-done | bytes 1966104
  13.5 1.4 %fusion.5 = bf16[48,512]{1,0:T(8,128)(2,1)S(1)} fusion(bf16[2560,512]{0,1:T(8,128)(2,1)S(1)} %bitcast.110, f32[384]{0:T(512)S(1)} %mul.31, s32[512]{0:T(512)S(1)} %add_select_fusion.1, s32[384]{0:T(512)S(1)} %eq.238, bf16[48,8,2560]{2,1,0:T(8,128)(2,1)S(1)} %copy-done.3), kind=kOutput, calls=%fused_computation.21 | convolution fusion | flops 1007394816 | bytes 4641792 | tf_op jit(solution)/shard_map/dot_general | solution.py:14
  14.9 24.0 %all_gather.3 = bf16[768,512]{1,0:T(8,128)(2,1)S(1)} all-gather(bf16[48,512]{1,0:T(8,128)(2,1)S(1)} %fusion.5), channel_id=1, replica_groups=mesh['group'=2,'expert'=16,'dp'=1] {'expert','dp'}, dimensions={0}, use_global_device_ids=true | all-gather | bytes 835584 | tf_op jit(solution)/shard_map/all_gather | solution.py:66
  38.9 1.0 slice_reduce_fusion
  39.9 1.1 %convolution_convert_fusion.2 = bf16[512,256]{1,0:T(8,128)(2,1)} fusion(bf16[768,512]{1,0:T(8,128)(2,1)S(1)} %all_gather.3, bf16[768,256]{1,0:T(8,128)(2,1)S(1)} %bitcast.108, pred[256]{0:T(512)(128)(4,1)S(1)} %iota_compare_fusion.12), kind=kOutput, calls=%fused_computation.22 | convolution fusion | flops 201654272 | bytes 1442048 | tf_op jit(solution)/shard_map/dot_general | solution.py:14
  41.0 1.3 %fusion.45 = bf16[768,512]{1,0:T(8,128)(2,1)S(1)} fusion(bf16[512,256]{1,0:T(8,128)(2,1)} %convolution_convert_fusion.2, bf16[768,256]{1,0:T(8,128)(2,1)S(1)} %bitcast.109, pred[256]{0:T(512)(128)(4,1)S(1)} %iota_compare_fusion.12), kind=kOutput, calls=%fused_computation.81 | convolution fusion | flops 201523200 | bytes 1442048 | tf_op jit(solution)/shard_map/dot_general | solution.py:14
  42.4 3.5 %all-to-all-start.1 = ((bf16[16,32,256]{2,1,0:T(8,128)(2,1)}), bf16[16,32,256]{2,1,0:T(8,128)(2,1)S(1)}, u32[]{:S(2)}, u32[]{:S(2)}) async-start(bf16[16,32,256]{2,1,0:T(8,128)(2,1)} %bitcast.5), calls=%async_computation.1 | async-start | bytes 524288 | tf_op jit(solution)/shard_map/all_to_all | solution.py:84
  51.3 4.7 %all-to-all-done.1 = bf16[16,32,256]{2,1,0:T(8,128)(2,1)S(1)} async-done(((bf16[16,32,256]{2,1,0:T(8,128)(2,1)}), bf16[16,32,256]{2,1,0:T(8,128)(2,1)S(1)}, u32[]{:S(2)}, u32[]{:S(2)}) %all-to-all-start.1) | async-done | bytes 262176 | tf_op jit(solution)/shard_map/all_to_all | solution.py:84
  55.9 3.7 %all-to-all-start.2 = ((bf16[16,48,256]{2,1,0:T(8,128)(2,1)}), bf16[16,48,256]{2,1,0:T(8,128)(2,1)S(1)}, u32[]{:S(2)}, u32[]{:S(2)}) async-start(bf16[16,48,256]{2,1,0:T(8,128)(2,1)} %bitcast.12), calls=%async_computation.2 | async-start | bytes 786432 | tf_op jit(solution)/shard_map/all_to_all | solution.py:82
  60.0 2.9 %cholesky.17 = f32[32,32]{1,0:T(8,128)S(1)} custom-call(f32[32,32]{1,0:T(8,128)S(1)} %fusion.74), custom_call_target="Cholesky" | custom-call | tf_op jit(solution)/shard_map/jit(cholesky)/cholesky | solution.py:110
  64.2 2.4 %custom-call.7 = f32[1,32,32]{1,2,0:T(8,128)S(1)} custom-call(f32[1,32,32]{2,1,0:T(8,128)S(1)} %fusion.71), custom_call_target="InvertDiagBlocksLowerTriangular" | custom-call | tf_op jit(solution)/shard_map/jit(_solve_triangular)/triangular_solve | solution.py:111
  67.4 1.1 %convolution_bitcast_fusion = f32[1,32,3584]{2,1,0:T(8,128)} fusion(bf16[32,3584]{1,0:T(8,128)(2,1)S(1)} %reshape.156, f32[32,32]{1,0:T(8,128)S(1)} %fusion.72), kind=kOutput, calls=%fused_computation | convolution fusion | flops 44041216 | bytes 692224 | tf_op jit(solution)/shard_map/dot_general | solution.py:115
  68.5 3.1 %all-to-all-done.2 = bf16[16,48,256]{2,1,0:T(8,128)(2,1)S(1)} async-done(((bf16[16,48,256]{2,1,0:T(8,128)(2,1)}), bf16[16,48,256]{2,1,0:T(8,128)(2,1)S(1)}, u32[]{:S(2)}, u32[]{:S(2)}) %all-to-all-start.2) | async-done | bytes 393248 | tf_op jit(solution)/shard_map/all_to_all | solution.py:82
  76.5 1.2 %collective-permute-start.6 = (bf16[4,32,1280]{2,1,0:T(8,128)(2,1)S(1)}, bf16[4,32,1280]{2,1,0:T(8,128)(2,1)S(1)}, u32[]{:S(2)}, u32[]{:S(2)}) collective-permute-start(bf16[4,32,1280]{2,1,0:T(8,128)(2,1)S(1)} %slice_bitcast_fusion.4), channel_id=1, source_target_pairs={{0,2},{1,3},{2,0},{3,1},{4,6},{5,7},{6,4},{7,5},{8,10},{9,11},{10,... | collective-permute-start | bytes 983048 | tf_op jit(solution)/shard_map/ppermute | solution.py:18
  77.8 8.3 %collective-permute-done.1 = bf16[4,32,1280]{2,1,0:T(8,128)(2,1)S(1)} collective-permute-done((bf16[4,32,1280]{2,1,0:T(8,128)(2,1)S(1)}, bf16[4,32,1280]{2,1,0:T(8,128)(2,1)S(1)}, u32[]{:S(2)}, u32[]{:S(2)}) %collective-permute-start.1) | collective-permute-done | bytes 327712 | tf_op jit(solution)/shard_map/ppermute | solution.py:18
  87.1 1.0 collective-permute-start.3
  88.0 2.5 %collective-permute-start.4 = (bf16[32,1280]{1,0:T(8,128)(2,1)S(1)}, bf16[32,1280]{1,0:T(8,128)(2,1)S(1)}, u32[]{:S(2)}, u32[]{:S(2)}) collective-permute-start(bf16[32,1280]{1,0:T(8,128)(2,1)S(1)} %get-tuple-element.11), channel_id=1, source_target_pairs={{0,12},{1,13},{2,14},{3,15},{4,8},{5,9},{6,10},{7,11},{8,4},{9,5},... | collective-permute-start | bytes 245768 | tf_op jit(solution)/shard_map/ppermute | solution.py:18
  90.6 1.7 %collective-permute-done.6 = bf16[4,32,1280]{2,1,0:T(8,128)(2,1)S(1)} collective-permute-done((bf16[4,32,1280]{2,1,0:T(8,128)(2,1)S(1)}, bf16[4,32,1280]{2,1,0:T(8,128)(2,1)S(1)}, u32[]{:S(2)}, u32[]{:S(2)}) %collective-permute-start.6) | collective-permute-done | bytes 327712 | tf_op jit(solution)/shard_map/ppermute | solution.py:18
  92.3 1.2 %collective-permute-start.7 = (bf16[32,1280]{1,0:T(8,128)(2,1)S(1)}, bf16[32,1280]{1,0:T(8,128)(2,1)S(1)}, u32[]{:S(2)}, u32[]{:S(2)}) collective-permute-start(bf16[32,1280]{1,0:T(8,128)(2,1)S(1)} %get-tuple-element.13), channel_id=1, source_target_pairs={{0,4},{1,5},{2,6},{3,7},{4,0},{5,1},{6,2},{7,3},{8,12},{9,13},{10,... | collective-permute-start | bytes 245768 | tf_op jit(solution)/shard_map/ppermute | solution.py:18
  94.5 2.3 %collective-permute-start.9 = (bf16[32,1280]{1,0:T(8,128)(2,1)S(1)}, bf16[32,1280]{1,0:T(8,128)(2,1)S(1)}, u32[]{:S(2)}, u32[]{:S(2)}) collective-permute-start(bf16[32,1280]{1,0:T(8,128)(2,1)S(1)} %get-tuple-element.14), channel_id=1, source_target_pairs={{0,12},{1,13},{2,14},{3,15},{4,8},{5,9},{6,10},{7,11},{8,4},{9,5},... | collective-permute-start | bytes 245768 | tf_op jit(solution)/shard_map/ppermute | solution.py:18
  97.0 5.3 %collective-permute-done.8 = bf16[32,1280]{1,0:T(8,128)(2,1)S(1)} collective-permute-done((bf16[32,1280]{1,0:T(8,128)(2,1)S(1)}, bf16[32,1280]{1,0:T(8,128)(2,1)S(1)}, u32[]{:S(2)}, u32[]{:S(2)}) %collective-permute-start.8) | collective-permute-done | bytes 81952 | tf_op jit(solution)/shard_map/ppermute | solution.py:18
  102.4 1.1 %convolution_bitcast_fusion.1 = f32[1,32,2560]{2,1,0:T(8,128)} fusion(f32[32,1280]{1,0:T(8,128)S(1)} %fusion.60, f32[32,1280]{1,0:T(8,128)S(1)} %fusion.62, f32[32,32]{1,0:T(8,128)S(1)} %fusion.72), kind=kOutput, calls=%fused_computation.1 | convolution fusion | flops 31540224 | bytes 659456 | tf_op jit(solution)/shard_map/dot_general | solution.py:116
  (74 shorter events, 17.4 us)
Async XLA Ops:
  2.2 9.4 %copy-start.1 = (s32[48,8]{0,1:T(8,128)S(1)}, s32[48,8]{0,1:T(8,128)}, u32[]{:S(2)}) copy-start(s32[48,8]{0,1:T(8,128)} %param.6) | copy-start | bytes 4612
  2.2 9.6 %copy-start.2 = (f32[48,8]{0,1:T(8,128)S(1)}, f32[48,8]{0,1:T(8,128)}, u32[]{:S(2)}) copy-start(f32[48,8]{0,1:T(8,128)} %param.7) | copy-start | bytes 4612
  2.2 9.8 %copy-start = (f32[2560,32]{0,1:T(8,128)S(1)}, f32[2560,32]{0,1:T(8,128)}, u32[]{:S(2)}) copy-start(f32[2560,32]{0,1:T(8,128)} %param.9) | copy-start | bytes 983044
  4.2 34.7 %all-to-all-start = ((bf16[16,48,256]{2,1,0:T(8,128)(2,1)}), bf16[16,48,256]{2,1,0:T(8,128)(2,1)S(1)}, u32[]{:S(2)}, u32[]{:S(2)}) async-start(bf16[16,48,256]{2,1,0:T(8,128)(2,1)} %copy.41), calls=%async_computation | async-start | bytes 786432 | tf_op jit(solution)/shard_map/all_to_all | solution.py:55
  12.0 1.5 %copy-start.3 = (bf16[48,8,2560]{2,1,0:T(8,128)(2,1)S(1)}, bf16[48,8,2560]{2,1,0:T(8,128)(2,1)}, u32[]{:S(2)}) copy-start(bf16[48,8,2560]{2,1,0:T(8,128)(2,1)} %param.8) | copy-start | bytes 5898244
  42.4 13.6 %all-to-all-start.1 = ((bf16[16,32,256]{2,1,0:T(8,128)(2,1)}), bf16[16,32,256]{2,1,0:T(8,128)(2,1)S(1)}, u32[]{:S(2)}, u32[]{:S(2)}) async-start(bf16[16,32,256]{2,1,0:T(8,128)(2,1)} %bitcast.5), calls=%async_computation.1 | async-start | bytes 524288 | tf_op jit(solution)/shard_map/all_to_all | solution.py:84
  55.9 15.7 %all-to-all-start.2 = ((bf16[16,48,256]{2,1,0:T(8,128)(2,1)}), bf16[16,48,256]{2,1,0:T(8,128)(2,1)S(1)}, u32[]{:S(2)}, u32[]{:S(2)}) async-start(bf16[16,48,256]{2,1,0:T(8,128)(2,1)} %bitcast.12), calls=%async_computation.2 | async-start | bytes 786432 | tf_op jit(solution)/shard_map/all_to_all | solution.py:82
  73.0 2.2 %collective-permute-start = (bf16[8,32,1280]{2,1,0:T(8,128)(2,1)S(1)}, bf16[8,32,1280]{2,1,0:T(8,128)(2,1)S(1)}, u32[]{:S(2)}, u32[]{:S(2)}) collective-permute-start(bf16[8,32,1280]{2,1,0:T(8,128)(2,1)S(1)} %slice_bitcast_fusion.2), channel_id=1, source_target_pairs={{0,1},{1,0},{2,3},{3,2},{4,5},{5,4},{6,7},{7,6},{8,9},{9,8},{10,11... | collective-permute-start | bytes 1966088 | tf_op jit(solution)/shard_map/ppermute | solution.py:18
  74.2 2.2 %collective-permute-start.5 = (bf16[8,32,1280]{2,1,0:T(8,128)(2,1)S(1)}, bf16[8,32,1280]{2,1,0:T(8,128)(2,1)S(1)}, u32[]{:S(2)}, u32[]{:S(2)}) collective-permute-start(bf16[8,32,1280]{2,1,0:T(8,128)(2,1)S(1)} %slice_bitcast_fusion), channel_id=1, source_target_pairs={{0,1},{1,0},{2,3},{3,2},{4,5},{5,4},{6,7},{7,6},{8,9},{9,8},{10,11... | collective-permute-start | bytes 1966088 | tf_op jit(solution)/shard_map/ppermute | solution.py:18
  75.4 10.6 %collective-permute-start.1 = (bf16[4,32,1280]{2,1,0:T(8,128)(2,1)S(1)}, bf16[4,32,1280]{2,1,0:T(8,128)(2,1)S(1)}, u32[]{:S(2)}, u32[]{:S(2)}) collective-permute-start(bf16[4,32,1280]{2,1,0:T(8,128)(2,1)S(1)} %slice_bitcast_fusion.6), channel_id=1, source_target_pairs={{0,2},{1,3},{2,0},{3,1},{4,6},{5,7},{6,4},{7,5},{8,10},{9,11},{10,... | collective-permute-start | bytes 983048 | tf_op jit(solution)/shard_map/ppermute | solution.py:18
  76.5 15.7 %collective-permute-start.6 = (bf16[4,32,1280]{2,1,0:T(8,128)(2,1)S(1)}, bf16[4,32,1280]{2,1,0:T(8,128)(2,1)S(1)}, u32[]{:S(2)}, u32[]{:S(2)}) collective-permute-start(bf16[4,32,1280]{2,1,0:T(8,128)(2,1)S(1)} %slice_bitcast_fusion.4), channel_id=1, source_target_pairs={{0,2},{1,3},{2,0},{3,1},{4,6},{5,7},{6,4},{7,5},{8,10},{9,11},{10,... | collective-permute-start | bytes 983048 | tf_op jit(solution)/shard_map/ppermute | solution.py:18
  86.1 8.4 %collective-permute-start.2 = (bf16[32,1280]{1,0:T(8,128)(2,1)S(1)}, bf16[32,1280]{1,0:T(8,128)(2,1)S(1)}, u32[]{:S(2)}, u32[]{:S(2)}) collective-permute-start(bf16[32,1280]{1,0:T(8,128)(2,1)S(1)} %get-tuple-element.10), channel_id=1, source_target_pairs={{0,4},{1,5},{2,6},{3,7},{4,0},{5,1},{6,2},{7,3},{8,12},{9,13},{10,... | collective-permute-start | bytes 245768 | tf_op jit(solution)/shard_map/ppermute | solution.py:18
  87.1 9.7 %collective-permute-start.3 = (bf16[32,1280]{1,0:T(8,128)(2,1)S(1)}, bf16[32,1280]{1,0:T(8,128)(2,1)S(1)}, u32[]{:S(2)}, u32[]{:S(2)}) collective-permute-start(bf16[32,1280]{1,0:T(8,128)(2,1)S(1)} %get-tuple-element.12), channel_id=1, source_target_pairs={{0,8},{1,9},{2,10},{3,11},{4,12},{5,13},{6,14},{7,15},{8,0},{9,1},... | collective-permute-start | bytes 245768 | tf_op jit(solution)/shard_map/ppermute | solution.py:18
  88.0 8.8 %collective-permute-start.4 = (bf16[32,1280]{1,0:T(8,128)(2,1)S(1)}, bf16[32,1280]{1,0:T(8,128)(2,1)S(1)}, u32[]{:S(2)}, u32[]{:S(2)}) collective-permute-start(bf16[32,1280]{1,0:T(8,128)(2,1)S(1)} %get-tuple-element.11), channel_id=1, source_target_pairs={{0,12},{1,13},{2,14},{3,15},{4,8},{5,9},{6,10},{7,11},{8,4},{9,5},... | collective-permute-start | bytes 245768 | tf_op jit(solution)/shard_map/ppermute | solution.py:18
  92.3 4.7 %collective-permute-start.7 = (bf16[32,1280]{1,0:T(8,128)(2,1)S(1)}, bf16[32,1280]{1,0:T(8,128)(2,1)S(1)}, u32[]{:S(2)}, u32[]{:S(2)}) collective-permute-start(bf16[32,1280]{1,0:T(8,128)(2,1)S(1)} %get-tuple-element.13), channel_id=1, source_target_pairs={{0,4},{1,5},{2,6},{3,7},{4,0},{5,1},{6,2},{7,3},{8,12},{9,13},{10,... | collective-permute-start | bytes 245768 | tf_op jit(solution)/shard_map/ppermute | solution.py:18
  93.5 8.9 %collective-permute-start.8 = (bf16[32,1280]{1,0:T(8,128)(2,1)S(1)}, bf16[32,1280]{1,0:T(8,128)(2,1)S(1)}, u32[]{:S(2)}, u32[]{:S(2)}) collective-permute-start(bf16[32,1280]{1,0:T(8,128)(2,1)S(1)} %get-tuple-element.15), channel_id=1, source_target_pairs={{0,8},{1,9},{2,10},{3,11},{4,12},{5,13},{6,14},{7,15},{8,0},{9,1},... | collective-permute-start | bytes 245768 | tf_op jit(solution)/shard_map/ppermute | solution.py:18
  94.5 7.9 %collective-permute-start.9 = (bf16[32,1280]{1,0:T(8,128)(2,1)S(1)}, bf16[32,1280]{1,0:T(8,128)(2,1)S(1)}, u32[]{:S(2)}, u32[]{:S(2)}) collective-permute-start(bf16[32,1280]{1,0:T(8,128)(2,1)S(1)} %get-tuple-element.14), channel_id=1, source_target_pairs={{0,12},{1,13},{2,14},{3,15},{4,8},{5,9},{6,10},{7,11},{8,4},{9,5},... | collective-permute-start | bytes 245768 | tf_op jit(solution)/shard_map/ppermute | solution.py:18

commit v3 on v2

v3 whole, which is shorter than its diff:
```python
import math

import jax
import jax.numpy as jnp
from jax import lax
from jax.sharding import PartitionSpec as P

AXES = ("expert", "dp")
HIGH = lax.Precision.HIGHEST
CHUNKS = 2
SLICES = 4


def dot(left, right, dims):
    return lax.dot_general(left, right, (dims, ((), ())), preferred_element_type=jnp.float32)


def exchange(block, step, count):
    return lax.ppermute(block, AXES, [(i, i ^ step) for i in range(count)])


def scatter_sum(blocks, count):
    step = 1
    while blocks.shape[0] > SLICES:
        pairs = blocks.reshape(-1, 2, *blocks.shape[1:])
        other = exchange(pairs[:, 1], step, count)
        blocks = (pairs[:, 0].astype(jnp.float32) + other.astype(jnp.float32)).astype(jnp.bfloat16)
        step *= 2
    return line_sum([blocks[j] for j in range(blocks.shape[0])], count)


def line_sum(blocks, count):
    line = count // SLICES
    others = [exchange(blocks[j], j * line, count) for j in range(1, SLICES)]
    total = blocks[0].astype(jnp.float32)
    for other in others:
        total = total + other.astype(jnp.float32)
    return total


def spread_rows(rows, count):
    step = count // SLICES // 2
    while step:
        rows = jnp.concatenate([rows, exchange(rows, step, count)], axis=0)
        step //= 2
    return rows


def shards(tokens, expert_ids, route_probs, cotangents, sketch):
    n_expert = lax.axis_size("expert")
    n_dp = lax.axis_size("dp")
    count = n_expert * n_dp
    line = count // SLICES
    tok, width = tokens.shape
    top = expert_ids.shape[1]
    hidden, rank = sketch.shape
    rows = tok * top
    share = width // SLICES
    scale = 1.0 / math.sqrt(rows)
    cot = cotangents.reshape(rows, hidden)
    own = lax.axis_index("expert")
    half = lax.axis_index("dp")
    place = lax.axis_index(AXES) // line

    cuts = [
        lax.dynamic_slice_in_dim(tokens, (place ^ j) * share, share, axis=1) for j in range(SLICES)
    ]
    x_line = jnp.concatenate(
        [cuts[0]] + [exchange(cuts[j], j * line, count) for j in range(1, SLICES)], axis=0
    )
    x = spread_rows(x_line, count)

    block = jnp.arange(n_expert * rank, dtype=jnp.int32) // rank
    ids = expert_ids.reshape(rows, 1)
    probs = route_probs.reshape(rows, 1)
    wide = jnp.tile(sketch.astype(jnp.bfloat16), (1, n_expert))
    y = jnp.where(ids == block, dot(cot, wide, ((1,), (0,))) * probs, 0.0)
    y = jnp.sum(y.reshape(tok, top, n_expert * rank), axis=1).astype(jnp.bfloat16)
    y = jnp.concatenate([y] + [exchange(y, j * line, count) for j in range(1, SLICES)], axis=0)
    y = spread_rows(y, count)

    columns = dot(y, x, ((0,), (0,))).astype(jnp.bfloat16)
    z = dot(x_line, columns, ((1,), (1,))).astype(jnp.bfloat16)
    z = line_sum([z[j * tok : (j + 1) * tok] for j in range(SLICES)], count)

    lane = jnp.arange(n_expert * rank, dtype=jnp.int32)
    turn = lane[:, None] == (((lane // rank) ^ own) * rank + lane % rank)
    z = dot(z.astype(jnp.bfloat16), turn.astype(jnp.bfloat16), ((1,), (0,)))
    spread = jnp.where((ids ^ own) == block, jnp.repeat(z, top, axis=0) * probs, 0.0)
    spread = spread.astype(jnp.bfloat16)
    piece = hidden // n_dp // CHUNKS
    totals = []
    for chunk in range(CHUNKS):
        terms = []
        for h in range(n_dp):
            start = (half ^ h) * (hidden // n_dp) + chunk * piece
            part_cot = (
                lax.dynamic_slice_in_dim(cot, start, piece, axis=1)
                if n_dp > 1
                else cot[:, chunk * piece : (chunk + 1) * piece]
            )
            part = dot(spread, part_cot, ((0,), (0,))).astype(jnp.bfloat16)
            terms.append(part.reshape(n_expert, rank, piece))
        totals.append(scatter_sum(jnp.stack(terms, axis=1).reshape(count, rank, piece), count))
    total = jnp.concatenate(totals, axis=1)

    parts = []
    for j in range(SLICES):
        expert = own ^ (j * n_expert // SLICES)
        part = lax.dynamic_slice_in_dim(columns, expert * rank, rank, axis=0)
        parts.append(exchange(part, j * line, count) if j else part)
    parts = jnp.stack(parts)
    parts = [lax.dynamic_index_in_dim(parts, place ^ j, 0, False) for j in range(SLICES)]
    range_rows = jnp.concatenate(parts, axis=1).astype(jnp.float32)
    gram = lax.dot_general(range_rows, range_rows, (((1,), (1,)), ((), ())), precision=HIGH)
    lower = jnp.linalg.cholesky(gram)
    inverse = jax.scipy.linalg.solve_triangular(
        lower, jnp.eye(rank, dtype=jnp.float32), lower=True
    )
    kept = lax.dynamic_slice_in_dim(range_rows, half * (width // n_dp), width // n_dp, axis=1)
    basis = jnp.dot(inverse * math.sqrt(width), kept, precision=HIGH)
    coeffs = jnp.dot(inverse * scale, total, precision=HIGH)
    return basis[None], coeffs[None]


def solution(mesh):
    in_specs = (
        P(("group", "expert", "dp"), None),
        P(("group", "expert", "dp"), None),
        P(("group", "expert", "dp"), None),
        P(("group", "expert", "dp"), None, None),
        P(),
    )
    out_specs = (P(("group", "expert"), None, "dp"), P(("group", "expert"), None, "dp"))
    return jax.shard_map(shards, mesh=mesh, in_specs=in_specs, out_specs=out_specs, check_vma=False)
```

time: 104 us -> 92.7 us (0.89)
  blocking collectives: 24 us -> 0 us
  starting transfers between devices: 26 us -> 36.7 us
  matrix products: 13 us -> 9.16 us
  other arithmetic: 8.25 us -> 10.5 us
  waiting for transfers between devices: 24.1 us -> 26.2 us
  local copies, waits for them, and re-layouts: 7.19 us -> 8.88 us
    ppermute x10 -> x26, starting transfers between devices: 11.4 us -> 36.7 us  [exchange(): return lax.ppermute(block, AXES, [(i, i ^ step) for i in range(count)])]
    all_gather x1 -> x0, blocking collectives: 24 us -> none  [shards(): y_all = lax.all_gather(y, AXES, axis=0, tiled=True)]
    all_to_all x3 -> x0, starting transfers between devices: 14.6 us -> none  [the longest x1 7.36 us: shards(): cut = lax.all_to_all(cut, AXES, split_axis=0, concat_axis=0, tiled=True)]
    ppermute x10 -> x26, waiting for transfers between devices: 16.3 us -> 26.2 us  [exchange(): return lax.ppermute(block, AXES, [(i, i ^ step) for i in range(count)])]
    all_to_all x3 -> x0, waiting for transfers between devices: 7.8 us -> none  [the longest x1 4.68 us: shards(): lax.all_to_all(columns, AXES, split_axis=0, concat_axis=0, tiled=True)]
    unnamed x10 -> x16, local copies, waits for them, and re-layouts: 1.42 us -> 5.45 us
    dot_general x14 -> x6, matrix products: 10.3 us -> 6.51 us  [dot(): lax.dot_general(left, right, (dims, ((), ())), preferred_element_type=jnp...]
    convert_element_type x4, other arithmetic: 0.47 us -> 2.65 us  [scatter_sum(): (pairs[:, 0].astype(jnp.float32) + other.astype(jnp.float32)).astype(jnp....]
  transfers between devices with their start and end apart: 13 -> 26, of which waited for: 8 -> 11; matrix products, arithmetic and copies ran while one was open for 17% -> 19% of each run, Pallas kernels for 0% -> 0%
where the time goes in v3:
time: 92.7 us; the launch traced here: 92.3 us
  starting transfers between devices  36.7 us (40%)
  waiting for transfers between devices  26.2 us (28%)
  other arithmetic  10.5 us (11%)
  matrix products  9.16 us (10%)
  local copies, waits for them, and re-layouts  8.88 us (10%)
    ppermute x26, starting transfers between devices, exchange(): return lax.ppermute(block, AXES, [(i, i ^ step) for i in range(count)])  36.7 us
    ppermute x26, waiting for transfers between devices, exchange(): return lax.ppermute(block, AXES, [(i, i ^ step) for i in range(count)])  26.2 us
    dot_general x6, matrix products, dot(): lax.dot_general(left, right, (dims, ((), ())), preferred_element_type=jnp...  6.51 us
    unnamed x16, local copies, waits for them, and re-layouts  5.45 us
    another operation x3, other arithmetic, shards(): lower = jnp.linalg.cholesky(gram)  3.6 us
    another operation x2, other arithmetic, shards(): jax.scipy.linalg.solve_triangular(lower, jnp.eye(rank, dtype=jnp.float32)...  3.09 us
    convert_element_type x4, other arithmetic, scatter_sum(): (pairs[:, 0].astype(jnp.float32) + other.astype(jnp.float32)).astype(jnp....  2.65 us
  transfers between devices with their start and end apart: 26, of which 11 were waited for; matrix products, arithmetic and copies ran while one was open for 19% of the time, Pallas kernels for 0%

profile of v3, /device:TPU:0, one launch (start us, length us, event | category | flops | bytes accessed | tf_op | source)
XLA Modules:
  0.0 92.3 jit_solution(12635236685201740386)
XLA Ops:
  4.9 1.4 %fusion.4 = bf16[48,512]{1,0:T(8,128)(2,1)S(1)} fusion(bf16[2560,512]{0,1:T(8,128)(2,1)S(1)} %bitcast.110, f32[384]{0:T(512)S(1)} %mul.61, s32[512]{0:T(512)S(1)} %add_select_fusion, s32[384]{0:T(512)S(1)} %eq.22, bf16[48,8,2560]{2,1,0:T(8,128)(2,1)S(1)} %copy-done.1), kind=kOutput, calls=%fused_computation.12 | convolution fusion | flops 1007394816 | bytes 4641792 | tf_op jit(solution)/shard_map/dot_general | solution.py:15
  6.3 3.1 %collective-permute-start = (bf16[48,512]{1,0:T(8,128)(2,1)S(1)}, bf16[48,512]{1,0:T(8,128)(2,1)S(1)}, u32[]{:S(2)}, u32[]{:S(2)}) collective-permute-start(bf16[48,512]{1,0:T(8,128)(2,1)S(1)} %fusion.4), channel_id=1, source_target_pairs={{0,4},{1,5},{2,6},{3,7},{4,0},{5,1},{6,2},{7,3},{8,12},{9,13},{10,... | collective-permute-start | bytes 147464 | tf_op jit(solution)/shard_map/ppermute | solution.py:19
  9.4 2.6 %collective-permute-start.1 = (bf16[48,512]{1,0:T(8,128)(2,1)S(1)}, bf16[48,512]{1,0:T(8,128)(2,1)S(1)}, u32[]{:S(2)}, u32[]{:S(2)}) collective-permute-start(bf16[48,512]{1,0:T(8,128)(2,1)S(1)} %fusion.4), channel_id=1, source_target_pairs={{0,8},{1,9},{2,10},{3,11},{4,12},{5,13},{6,14},{7,15},{8,0},{9,1},... | collective-permute-start | bytes 147464 | tf_op jit(solution)/shard_map/ppermute | solution.py:19
  13.0 3.5 %collective-permute-start.6 = (bf16[48,896]{1,0:T(8,128)(2,1)S(1)}, bf16[48,896]{1,0:T(8,128)(2,1)S(1)}, u32[]{:S(2)}, u32[]{:S(2)}) collective-permute-start(bf16[48,896]{1,0:T(8,128)(2,1)S(1)} %get-tuple-element.14), channel_id=1, source_target_pairs={{0,8},{1,9},{2,10},{3,11},{4,12},{5,13},{6,14},{7,15},{8,0},{9,1},... | collective-permute-start | bytes 258056 | tf_op jit(solution)/shard_map/ppermute | solution.py:19
  17.1 1.4 %collective-permute-done.2 = bf16[48,512]{1,0:T(8,128)(2,1)S(1)} collective-permute-done((bf16[48,512]{1,0:T(8,128)(2,1)S(1)}, bf16[48,512]{1,0:T(8,128)(2,1)S(1)}, u32[]{:S(2)}, u32[]{:S(2)}) %collective-permute-start.2) | collective-permute-done | bytes 49184 | tf_op jit(solution)/shard_map/ppermute | solution.py:19
  18.6 1.6 %collective-permute-start.3 = (bf16[192,512]{1,0:T(8,128)(2,1)S(1)}, bf16[192,512]{1,0:T(8,128)(2,1)S(1)}, u32[]{:S(2)}, u32[]{:S(2)}) collective-permute-start(bf16[192,512]{1,0:T(8,128)(2,1)S(1)} %pad_maximum_fusion.3), channel_id=1, source_target_pairs={{0,2},{1,3},{2,0},{3,1},{4,6},{5,7},{6,4},{7,5},{8,10},{9,11},{10,... | collective-permute-start | bytes 589832 | tf_op jit(solution)/shard_map/ppermute | solution.py:19
  20.2 2.2 %collective-permute-done.6 = bf16[48,896]{1,0:T(8,128)(2,1)S(1)} collective-permute-done((bf16[48,896]{1,0:T(8,128)(2,1)S(1)}, bf16[48,896]{1,0:T(8,128)(2,1)S(1)}, u32[]{:S(2)}, u32[]{:S(2)}) %collective-permute-start.6) | collective-permute-done | bytes 86048 | tf_op jit(solution)/shard_map/ppermute | solution.py:19
  23.5 1.6 %collective-permute-start.8 = (bf16[192,896]{1,0:T(8,128)(2,1)S(1)}, bf16[192,896]{1,0:T(8,128)(2,1)S(1)}, u32[]{:S(2)}, u32[]{:S(2)}) collective-permute-start(bf16[192,896]{1,0:T(8,128)(2,1)S(1)} %pad_maximum_fusion), channel_id=1, source_target_pairs={{0,2},{1,3},{2,0},{3,1},{4,6},{5,7},{6,4},{7,5},{8,10},{9,11},{10,... | collective-permute-start | bytes 1032200 | tf_op jit(solution)/shard_map/ppermute | solution.py:19
  27.0 4.6 %collective-permute-done.8 = bf16[192,896]{1,0:T(8,128)(2,1)S(1)} collective-permute-done((bf16[192,896]{1,0:T(8,128)(2,1)S(1)}, bf16[192,896]{1,0:T(8,128)(2,1)S(1)}, u32[]{:S(2)}, u32[]{:S(2)}) %collective-permute-start.8) | collective-permute-done | bytes 344096 | tf_op jit(solution)/shard_map/ppermute | solution.py:19
  33.1 2.1 %collective-permute-done.4 = bf16[384,512]{1,0:T(8,128)(2,1)S(1)} collective-permute-done((bf16[384,512]{1,0:T(8,128)(2,1)S(1)}, bf16[384,512]{1,0:T(8,128)(2,1)S(1)}, u32[]{:S(2)}, u32[]{:S(2)}) %collective-permute-start.4) | collective-permute-done | bytes 393248 | tf_op jit(solution)/shard_map/ppermute | solution.py:19
  36.2 2.4 %convolution_convert_fusion.2 = bf16[512,896]{1,0:T(8,128)(2,1)S(1)} fusion(bf16[768,512]{1,0:T(8,128)(2,1)S(1)} %constant_dynamic-update-slice_fusion.5, bf16[768,896]{1,0:T(8,128)(2,1)} %constant_dynamic-update-slice_fusion.16), kind=kOutput, calls=%fused_computation.4 | convolution fusion | flops 705101824 | bytes 3080192 | tf_op jit(solution)/shard_map/dot_general | solution.py:15
  39.0 2.7 %collective-permute-start.13 = (bf16[48,512]{1,0:T(8,128)(2,1)S(1)}, bf16[48,512]{1,0:T(8,128)(2,1)S(1)}, u32[]{:S(2)}, u32[]{:S(2)}) collective-permute-start(bf16[48,512]{1,0:T(8,128)(2,1)S(1)} %get-tuple-element.25), channel_id=1, source_target_pairs={{0,4},{1,5},{2,6},{3,7},{4,0},{5,1},{6,2},{7,3},{8,12},{9,13},{10,... | collective-permute-start | bytes 147464 | tf_op jit(solution)/shard_map/ppermute | solution.py:19
  42.4 1.8 %collective-permute-start.15 = (bf16[48,512]{1,0:T(8,128)(2,1)S(1)}, bf16[48,512]{1,0:T(8,128)(2,1)S(1)}, u32[]{:S(2)}, u32[]{:S(2)}) collective-permute-start(bf16[48,512]{1,0:T(8,128)(2,1)S(1)} %get-tuple-element.26), channel_id=1, source_target_pairs={{0,12},{1,13},{2,14},{3,15},{4,8},{5,9},{6,10},{7,11},{8,4},{9,5},... | collective-permute-start | bytes 147464 | tf_op jit(solution)/shard_map/ppermute | solution.py:19
  45.3 1.5 %collective-permute-start.11 = (bf16[32,896]{1,0:T(8,128)(2,1)S(1)}, bf16[32,896]{1,0:T(8,128)(2,1)S(1)}, u32[]{:S(2)}, u32[]{:S(2)}) collective-permute-start(bf16[32,896]{1,0:T(8,128)(2,1)S(1)} %get-tuple-element.6), channel_id=1, source_target_pairs={{0,8},{1,9},{2,10},{3,11},{4,12},{5,13},{6,14},{7,15},{8,0},{9,1},... | collective-permute-start | bytes 172040 | tf_op jit(solution)/shard_map/ppermute | solution.py:19
  46.9 1.8 %collective-permute-start.12 = (bf16[32,896]{1,0:T(8,128)(2,1)S(1)}, bf16[32,896]{1,0:T(8,128)(2,1)S(1)}, u32[]{:S(2)}, u32[]{:S(2)}) collective-permute-start(bf16[32,896]{1,0:T(8,128)(2,1)S(1)} %get-tuple-element.5), channel_id=1, source_target_pairs={{0,12},{1,13},{2,14},{3,15},{4,8},{5,9},{6,10},{7,11},{8,4},{9,5},... | collective-permute-start | bytes 172040 | tf_op jit(solution)/shard_map/ppermute | solution.py:19
  53.8 2.9 %cholesky.17 = f32[32,32]{1,0:T(8,128)S(1)} custom-call(f32[32,32]{1,0:T(8,128)S(1)} %fusion.37), custom_call_target="Cholesky" | custom-call | tf_op jit(solution)/shard_map/jit(cholesky)/cholesky | solution.py:116
  58.1 2.4 %custom-call.7 = f32[1,32,32]{1,2,0:T(8,128)S(1)} custom-call(f32[1,32,32]{2,1,0:T(8,128)S(1)} %fusion.34), custom_call_target="InvertDiagBlocksLowerTriangular" | custom-call | tf_op jit(solution)/shard_map/jit(_solve_triangular)/triangular_solve | solution.py:117
  63.1 1.6 %collective-permute-start.17 = (bf16[4,32,1280]{2,1,0:T(8,128)(2,1)S(1)}, bf16[4,32,1280]{2,1,0:T(8,128)(2,1)S(1)}, u32[]{:S(2)}, u32[]{:S(2)}) collective-permute-start(bf16[4,32,1280]{2,1,0:T(8,128)(2,1)S(1)} %slice_bitcast_fusion.6), channel_id=1, source_target_pairs={{0,2},{1,3},{2,0},{3,1},{4,6},{5,7},{6,4},{7,5},{8,10},{9,11},{10,... | collective-permute-start | bytes 983048 | tf_op jit(solution)/shard_map/ppermute | solution.py:19
  66.6 7.3 %collective-permute-done.17 = bf16[4,32,1280]{2,1,0:T(8,128)(2,1)S(1)} collective-permute-done((bf16[4,32,1280]{2,1,0:T(8,128)(2,1)S(1)}, bf16[4,32,1280]{2,1,0:T(8,128)(2,1)S(1)}, u32[]{:S(2)}, u32[]{:S(2)}) %collective-permute-start.17) | collective-permute-done | bytes 327712 | tf_op jit(solution)/shard_map/ppermute | solution.py:19
  73.9 2.6 %collective-permute-start.18 = (bf16[32,1280]{1,0:T(8,128)(2,1)S(1)}, bf16[32,1280]{1,0:T(8,128)(2,1)S(1)}, u32[]{:S(2)}, u32[]{:S(2)}) collective-permute-start(bf16[32,1280]{1,0:T(8,128)(2,1)S(1)} %get-tuple-element.15), channel_id=1, source_target_pairs={{0,4},{1,5},{2,6},{3,7},{4,0},{5,1},{6,2},{7,3},{8,12},{9,13},{10,... | collective-permute-start | bytes 245768 | tf_op jit(solution)/shard_map/ppermute | solution.py:19
  77.0 1.9 %collective-permute-start.20 = (bf16[32,1280]{1,0:T(8,128)(2,1)S(1)}, bf16[32,1280]{1,0:T(8,128)(2,1)S(1)}, u32[]{:S(2)}, u32[]{:S(2)}) collective-permute-start(bf16[32,1280]{1,0:T(8,128)(2,1)S(1)} %get-tuple-element.16), channel_id=1, source_target_pairs={{0,12},{1,13},{2,14},{3,15},{4,8},{5,9},{6,10},{7,11},{8,4},{9,5},... | collective-permute-start | bytes 245768 | tf_op jit(solution)/shard_map/ppermute | solution.py:19
  79.6 3.0 %collective-permute-start.23 = (bf16[32,1280]{1,0:T(8,128)(2,1)S(1)}, bf16[32,1280]{1,0:T(8,128)(2,1)S(1)}, u32[]{:S(2)}, u32[]{:S(2)}) collective-permute-start(bf16[32,1280]{1,0:T(8,128)(2,1)S(1)} %get-tuple-element.18), channel_id=1, source_target_pairs={{0,4},{1,5},{2,6},{3,7},{4,0},{5,1},{6,2},{7,3},{8,12},{9,13},{10,... | collective-permute-start | bytes 245768 | tf_op jit(solution)/shard_map/ppermute | solution.py:19
  83.2 1.9 %collective-permute-start.25 = (bf16[32,1280]{1,0:T(8,128)(2,1)S(1)}, bf16[32,1280]{1,0:T(8,128)(2,1)S(1)}, u32[]{:S(2)}, u32[]{:S(2)}) collective-permute-start(bf16[32,1280]{1,0:T(8,128)(2,1)S(1)} %get-tuple-element.19), channel_id=1, source_target_pairs={{0,12},{1,13},{2,14},{3,15},{4,8},{5,9},{6,10},{7,11},{8,4},{9,5},... | collective-permute-start | bytes 245768 | tf_op jit(solution)/shard_map/ppermute | solution.py:19
  85.9 5.2 %collective-permute-done.24 = bf16[32,1280]{1,0:T(8,128)(2,1)S(1)} collective-permute-done((bf16[32,1280]{1,0:T(8,128)(2,1)S(1)}, bf16[32,1280]{1,0:T(8,128)(2,1)S(1)}, u32[]{:S(2)}, u32[]{:S(2)}) %collective-permute-start.24) | collective-permute-done | bytes 81952 | tf_op jit(solution)/shard_map/ppermute | solution.py:19
  (91 shorter events, 28.3 us)
Async XLA Ops:
  6.3 10.8 %collective-permute-start = (bf16[48,512]{1,0:T(8,128)(2,1)S(1)}, bf16[48,512]{1,0:T(8,128)(2,1)S(1)}, u32[]{:S(2)}, u32[]{:S(2)}) collective-permute-start(bf16[48,512]{1,0:T(8,128)(2,1)S(1)} %fusion.4), channel_id=1, source_target_pairs={{0,4},{1,5},{2,6},{3,7},{4,0},{5,1},{6,2},{7,3},{8,12},{9,13},{10,... | collective-permute-start | bytes 147464 | tf_op jit(solution)/shard_map/ppermute | solution.py:19
  9.4 7.7 %collective-permute-start.1 = (bf16[48,512]{1,0:T(8,128)(2,1)S(1)}, bf16[48,512]{1,0:T(8,128)(2,1)S(1)}, u32[]{:S(2)}, u32[]{:S(2)}) collective-permute-start(bf16[48,512]{1,0:T(8,128)(2,1)S(1)} %fusion.4), channel_id=1, source_target_pairs={{0,8},{1,9},{2,10},{3,11},{4,12},{5,13},{6,14},{7,15},{8,0},{9,1},... | collective-permute-start | bytes 147464 | tf_op jit(solution)/shard_map/ppermute | solution.py:19
  12.0 6.6 %collective-permute-start.2 = (bf16[48,512]{1,0:T(8,128)(2,1)S(1)}, bf16[48,512]{1,0:T(8,128)(2,1)S(1)}, u32[]{:S(2)}, u32[]{:S(2)}) collective-permute-start(bf16[48,512]{1,0:T(8,128)(2,1)S(1)} %fusion.4), channel_id=1, source_target_pairs={{0,12},{1,13},{2,14},{3,15},{4,8},{5,9},{6,10},{7,11},{8,4},{9,5},... | collective-permute-start | bytes 147464 | tf_op jit(solution)/shard_map/ppermute | solution.py:19
  12.0 8.1 %collective-permute-start.5 = (bf16[48,896]{1,0:T(8,128)(2,1)S(1)}, bf16[48,896]{1,0:T(8,128)(2,1)S(1)}, u32[]{:S(2)}, u32[]{:S(2)}) collective-permute-start(bf16[48,896]{1,0:T(8,128)(2,1)S(1)} %get-tuple-element.11), channel_id=1, source_target_pairs={{0,4},{1,5},{2,6},{3,7},{4,0},{5,1},{6,2},{7,3},{8,12},{9,13},{10,... | collective-permute-start | bytes 258056 | tf_op jit(solution)/shard_map/ppermute | solution.py:19
  13.0 9.4 %collective-permute-start.6 = (bf16[48,896]{1,0:T(8,128)(2,1)S(1)}, bf16[48,896]{1,0:T(8,128)(2,1)S(1)}, u32[]{:S(2)}, u32[]{:S(2)}) collective-permute-start(bf16[48,896]{1,0:T(8,128)(2,1)S(1)} %get-tuple-element.14), channel_id=1, source_target_pairs={{0,8},{1,9},{2,10},{3,11},{4,12},{5,13},{6,14},{7,15},{8,0},{9,1},... | collective-permute-start | bytes 258056 | tf_op jit(solution)/shard_map/ppermute | solution.py:19
  17.1 6.4 %collective-permute-start.7 = (bf16[48,896]{1,0:T(8,128)(2,1)S(1)}, bf16[48,896]{1,0:T(8,128)(2,1)S(1)}, u32[]{:S(2)}, u32[]{:S(2)}) collective-permute-start(bf16[48,896]{1,0:T(8,128)(2,1)S(1)} %get-tuple-element.10), channel_id=1, source_target_pairs={{0,12},{1,13},{2,14},{3,15},{4,8},{5,9},{6,10},{7,11},{8,4},{9,5},... | collective-permute-start | bytes 258056 | tf_op jit(solution)/shard_map/ppermute | solution.py:19
  18.6 13.9 %collective-permute-start.3 = (bf16[192,512]{1,0:T(8,128)(2,1)S(1)}, bf16[192,512]{1,0:T(8,128)(2,1)S(1)}, u32[]{:S(2)}, u32[]{:S(2)}) collective-permute-start(bf16[192,512]{1,0:T(8,128)(2,1)S(1)} %pad_maximum_fusion.3), channel_id=1, source_target_pairs={{0,2},{1,3},{2,0},{3,1},{4,6},{5,7},{6,4},{7,5},{8,10},{9,11},{10,... | collective-permute-start | bytes 589832 | tf_op jit(solution)/shard_map/ppermute | solution.py:19
  23.5 8.1 %collective-permute-start.8 = (bf16[192,896]{1,0:T(8,128)(2,1)S(1)}, bf16[192,896]{1,0:T(8,128)(2,1)S(1)}, u32[]{:S(2)}, u32[]{:S(2)}) collective-permute-start(bf16[192,896]{1,0:T(8,128)(2,1)S(1)} %pad_maximum_fusion), channel_id=1, source_target_pairs={{0,2},{1,3},{2,0},{3,1},{4,6},{5,7},{6,4},{7,5},{8,10},{9,11},{10,... | collective-permute-start | bytes 1032200 | tf_op jit(solution)/shard_map/ppermute | solution.py:19
  39.0 7.8 %collective-permute-start.13 = (bf16[48,512]{1,0:T(8,128)(2,1)S(1)}, bf16[48,512]{1,0:T(8,128)(2,1)S(1)}, u32[]{:S(2)}, u32[]{:S(2)}) collective-permute-start(bf16[48,512]{1,0:T(8,128)(2,1)S(1)} %get-tuple-element.25), channel_id=1, source_target_pairs={{0,4},{1,5},{2,6},{3,7},{4,0},{5,1},{6,2},{7,3},{8,12},{9,13},{10,... | collective-permute-start | bytes 147464 | tf_op jit(solution)/shard_map/ppermute | solution.py:19
  41.8 7.4 %collective-permute-start.14 = (bf16[48,512]{1,0:T(8,128)(2,1)S(1)}, bf16[48,512]{1,0:T(8,128)(2,1)S(1)}, u32[]{:S(2)}, u32[]{:S(2)}) collective-permute-start(bf16[48,512]{1,0:T(8,128)(2,1)S(1)} %get-tuple-element.27), channel_id=1, source_target_pairs={{0,8},{1,9},{2,10},{3,11},{4,12},{5,13},{6,14},{7,15},{8,0},{9,1},... | collective-permute-start | bytes 147464 | tf_op jit(solution)/shard_map/ppermute | solution.py:19
  42.4 6.8 %collective-permute-start.15 = (bf16[48,512]{1,0:T(8,128)(2,1)S(1)}, bf16[48,512]{1,0:T(8,128)(2,1)S(1)}, u32[]{:S(2)}, u32[]{:S(2)}) collective-permute-start(bf16[48,512]{1,0:T(8,128)(2,1)S(1)} %get-tuple-element.26), channel_id=1, source_target_pairs={{0,12},{1,13},{2,14},{3,15},{4,8},{5,9},{6,10},{7,11},{8,4},{9,5},... | collective-permute-start | bytes 147464 | tf_op jit(solution)/shard_map/ppermute | solution.py:19
  44.2 8.8 %collective-permute-start.10 = (bf16[32,896]{1,0:T(8,128)(2,1)S(1)}, bf16[32,896]{1,0:T(8,128)(2,1)S(1)}, u32[]{:S(2)}, u32[]{:S(2)}) collective-permute-start(bf16[32,896]{1,0:T(8,128)(2,1)S(1)} %get-tuple-element.7), channel_id=1, source_target_pairs={{0,4},{1,5},{2,6},{3,7},{4,0},{5,1},{6,2},{7,3},{8,12},{9,13},{10,... | collective-permute-start | bytes 172040 | tf_op jit(solution)/shard_map/ppermute | solution.py:19
  45.3 8.1 %collective-permute-start.11 = (bf16[32,896]{1,0:T(8,128)(2,1)S(1)}, bf16[32,896]{1,0:T(8,128)(2,1)S(1)}, u32[]{:S(2)}, u32[]{:S(2)}) collective-permute-start(bf16[32,896]{1,0:T(8,128)(2,1)S(1)} %get-tuple-element.6), channel_id=1, source_target_pairs={{0,8},{1,9},{2,10},{3,11},{4,12},{5,13},{6,14},{7,15},{8,0},{9,1},... | collective-permute-start | bytes 172040 | tf_op jit(solution)/shard_map/ppermute | solution.py:19
  46.9 6.6 %collective-permute-start.12 = (bf16[32,896]{1,0:T(8,128)(2,1)S(1)}, bf16[32,896]{1,0:T(8,128)(2,1)S(1)}, u32[]{:S(2)}, u32[]{:S(2)}) collective-permute-start(bf16[32,896]{1,0:T(8,128)(2,1)S(1)} %get-tuple-element.5), channel_id=1, source_target_pairs={{0,12},{1,13},{2,14},{3,15},{4,8},{5,9},{6,10},{7,11},{8,4},{9,5},... | collective-permute-start | bytes 172040 | tf_op jit(solution)/shard_map/ppermute | solution.py:19
  52.4 9.4 %collective-permute-start.16 = (bf16[8,32,1280]{2,1,0:T(8,128)(2,1)}, bf16[8,32,1280]{2,1,0:T(8,128)(2,1)}, u32[]{:S(2)}, u32[]{:S(2)}) collective-permute-start(bf16[8,32,1280]{2,1,0:T(8,128)(2,1)} %slice_bitcast_fusion.2), channel_id=1, source_target_pairs={{0,1},{1,0},{2,3},{3,2},{4,5},{5,4},{6,7},{7,6},{8,9},{9,8},{10,11... | collective-permute-start | bytes 1966088 | tf_op jit(solution)/shard_map/ppermute | solution.py:19
  52.5 12.2 %collective-permute-start.21 = (bf16[8,32,1280]{2,1,0:T(8,128)(2,1)S(1)}, bf16[8,32,1280]{2,1,0:T(8,128)(2,1)}, u32[]{:S(2)}, u32[]{:S(2)}) collective-permute-start(bf16[8,32,1280]{2,1,0:T(8,128)(2,1)S(1)} %slice_bitcast_fusion), channel_id=1, source_target_pairs={{0,1},{1,0},{2,3},{3,2},{4,5},{5,4},{6,7},{7,6},{8,9},{9,8},{10,11... | collective-permute-start | bytes 1966088 | tf_op jit(solution)/shard_map/ppermute | solution.py:19
  63.1 10.7 %collective-permute-start.17 = (bf16[4,32,1280]{2,1,0:T(8,128)(2,1)S(1)}, bf16[4,32,1280]{2,1,0:T(8,128)(2,1)S(1)}, u32[]{:S(2)}, u32[]{:S(2)}) collective-permute-start(bf16[4,32,1280]{2,1,0:T(8,128)(2,1)S(1)} %slice_bitcast_fusion.6), channel_id=1, source_target_pairs={{0,2},{1,3},{2,0},{3,1},{4,6},{5,7},{6,4},{7,5},{8,10},{9,11},{10,... | collective-permute-start | bytes 983048 | tf_op jit(solution)/shard_map/ppermute | solution.py:19
  66.0 13.5 %collective-permute-start.22 = (bf16[4,32,1280]{2,1,0:T(8,128)(2,1)S(1)}, bf16[4,32,1280]{2,1,0:T(8,128)(2,1)S(1)}, u32[]{:S(2)}, u32[]{:S(2)}) collective-permute-start(bf16[4,32,1280]{2,1,0:T(8,128)(2,1)S(1)} %slice_bitcast_fusion.4), channel_id=1, source_target_pairs={{0,2},{1,3},{2,0},{3,1},{4,6},{5,7},{6,4},{7,5},{8,10},{9,11},{10,... | collective-permute-start | bytes 983048 | tf_op jit(solution)/shard_map/ppermute | solution.py:19
  73.9 9.3 %collective-permute-start.18 = (bf16[32,1280]{1,0:T(8,128)(2,1)S(1)}, bf16[32,1280]{1,0:T(8,128)(2,1)S(1)}, u32[]{:S(2)}, u32[]{:S(2)}) collective-permute-start(bf16[32,1280]{1,0:T(8,128)(2,1)S(1)} %get-tuple-element.15), channel_id=1, source_target_pairs={{0,4},{1,5},{2,6},{3,7},{4,0},{5,1},{6,2},{7,3},{8,12},{9,13},{10,... | collective-permute-start | bytes 245768 | tf_op jit(solution)/shard_map/ppermute | solution.py:19
  76.5 8.6 %collective-permute-start.19 = (bf16[32,1280]{1,0:T(8,128)(2,1)S(1)}, bf16[32,1280]{1,0:T(8,128)(2,1)S(1)}, u32[]{:S(2)}, u32[]{:S(2)}) collective-permute-start(bf16[32,1280]{1,0:T(8,128)(2,1)S(1)} %get-tuple-element.17), channel_id=1, source_target_pairs={{0,8},{1,9},{2,10},{3,11},{4,12},{5,13},{6,14},{7,15},{8,0},{9,1},... | collective-permute-start | bytes 245768 | tf_op jit(solution)/shard_map/ppermute | solution.py:19
  77.0 8.0 %collective-permute-start.20 = (bf16[32,1280]{1,0:T(8,128)(2,1)S(1)}, bf16[32,1280]{1,0:T(8,128)(2,1)S(1)}, u32[]{:S(2)}, u32[]{:S(2)}) collective-permute-start(bf16[32,1280]{1,0:T(8,128)(2,1)S(1)} %get-tuple-element.16), channel_id=1, source_target_pairs={{0,12},{1,13},{2,14},{3,15},{4,8},{5,9},{6,10},{7,11},{8,4},{9,5},... | collective-permute-start | bytes 245768 | tf_op jit(solution)/shard_map/ppermute | solution.py:19
  79.6 6.4 %collective-permute-start.23 = (bf16[32,1280]{1,0:T(8,128)(2,1)S(1)}, bf16[32,1280]{1,0:T(8,128)(2,1)S(1)}, u32[]{:S(2)}, u32[]{:S(2)}) collective-permute-start(bf16[32,1280]{1,0:T(8,128)(2,1)S(1)} %get-tuple-element.18), channel_id=1, source_target_pairs={{0,4},{1,5},{2,6},{3,7},{4,0},{5,1},{6,2},{7,3},{8,12},{9,13},{10,... | collective-permute-start | bytes 245768 | tf_op jit(solution)/shard_map/ppermute | solution.py:19
  82.6 8.5 %collective-permute-start.24 = (bf16[32,1280]{1,0:T(8,128)(2,1)S(1)}, bf16[32,1280]{1,0:T(8,128)(2,1)S(1)}, u32[]{:S(2)}, u32[]{:S(2)}) collective-permute-start(bf16[32,1280]{1,0:T(8,128)(2,1)S(1)} %get-tuple-element.20), channel_id=1, source_target_pairs={{0,8},{1,9},{2,10},{3,11},{4,12},{5,13},{6,14},{7,15},{8,0},{9,1},... | collective-permute-start | bytes 245768 | tf_op jit(solution)/shard_map/ppermute | solution.py:19
  83.2 8.0 %collective-permute-start.25 = (bf16[32,1280]{1,0:T(8,128)(2,1)S(1)}, bf16[32,1280]{1,0:T(8,128)(2,1)S(1)}, u32[]{:S(2)}, u32[]{:S(2)}) collective-permute-start(bf16[32,1280]{1,0:T(8,128)(2,1)S(1)} %get-tuple-element.19), channel_id=1, source_target_pairs={{0,12},{1,13},{2,14},{3,15},{4,8},{5,9},{6,10},{7,11},{8,4},{9,5},... | collective-permute-start | bytes 245768 | tf_op jit(solution)/shard_map/ppermute | solution.py:19
  (5 other events, 24.9 us)

commit v4 on v1

v4 whole, which is shorter than its diff:
```python
import functools
import math

import jax
import jax.numpy as jnp
from jax import lax
from jax.experimental import pallas as pl
from jax.experimental.pallas import tpu as pltpu
from jax.sharding import PartitionSpec as P

AXES = ("expert", "dp")
HIGH = lax.Precision.HIGHEST
CHUNKS = 2
SLICES = 4
VMEM = pl.BlockSpec(memory_space=pltpu.VMEM)
SMEM = pl.BlockSpec(memory_space=pltpu.SMEM)
BF16 = jnp.bfloat16
F32 = jnp.float32


def dot(left, right, left_dim, right_dim):
    dims = (((left_dim,), (right_dim,)), ((), ()))
    return lax.dot_general(left, right, dims, preferred_element_type=F32)


def iota(shape, dim):
    return lax.broadcasted_iota(jnp.int32, shape, dim)


def call(body, shapes, flops, size, *args, spaces=None):
    return pl.pallas_call(
        body,
        out_shape=shapes,
        in_specs=spaces or [VMEM] * len(args),
        out_specs=jax.tree.map(lambda _: VMEM, shapes),
        compiler_params=pltpu.CompilerParams(vmem_limit_bytes=48 * 1024 * 1024),
        cost_estimate=pl.CostEstimate(flops=flops, bytes_accessed=size, transcendentals=0),
    )(*args)


def pair_columns(ids, probs):
    tok, top = ids.shape
    rows = tok * top
    pick = (iota((rows, tok), 0) // top == iota((rows, tok), 1)).astype(BF16)
    here = iota((rows, top), 0) % top == iota((rows, top), 1)
    names = dot(pick, ids.astype(BF16), 1, 0)
    weights, rest = jnp.zeros((rows, top), F32), probs
    for _ in range(3):
        piece = rest.astype(BF16)
        weights = weights + dot(pick, piece, 1, 0)
        rest = rest - piece.astype(F32)
    names = jnp.sum(jnp.where(here, names, 0.0), axis=1, keepdims=True)
    weights = jnp.sum(jnp.where(here, weights, 0.0), axis=1, keepdims=True)
    return names, weights


def lane_names(n_expert, rank, groups):
    block = iota((1, n_expert * rank), 1) // rank
    per = n_expert // groups
    return ((block % per) * groups + block // per).astype(F32)


def y_kernel(groups, cot, sketch, ids, probs, *outs):
    rows, _ = cot.shape
    tok, top = ids.shape
    rank = sketch.shape[1]
    lanes = outs[0].shape[1] * len(outs)
    high = sketch[...].astype(BF16)
    low = (sketch[...] - high.astype(F32)).astype(BF16)
    pair = dot(cot[...], high, 1, 0) + dot(cot[...], low, 1, 0)
    names, weights = pair_columns(ids[...], probs[...])
    pair = (pair * weights).astype(BF16)
    tile = (iota((rank, lanes), 0) == iota((rank, lanes), 1) % rank).astype(BF16)
    y = jnp.where(names == lane_names(lanes // rank, rank, groups), dot(pair, tile, 1, 0), 0.0)
    y = jnp.sum(y.reshape(tok, top, lanes), axis=1).astype(BF16)
    each = lanes // len(outs)
    for i, out in enumerate(outs):
        out[...] = y[:, i * each : (i + 1) * each]


def z_kernel(n, *refs):
    xs, ys, (columns, z) = refs[: 2 * n], refs[2 * n : 3 * n], refs[3 * n :]
    total = 0.0
    for b in range(n):
        for core in range(2):
            y = jnp.concatenate([ys[b][i, core] for i in range(SLICES)], axis=0)
            x = jnp.concatenate([xs[2 * b + core][i] for i in range(SLICES)], axis=0)
            total = total + dot(y, x, 0, 0)
    total = total.astype(BF16)
    columns[...] = total
    for core in range(2):
        tok = xs[core].shape[1]
        x = jnp.concatenate([xs[core][i] for i in range(SLICES)], axis=0)
        part = dot(x, total, 1, 1).astype(BF16)
        for i in range(SLICES):
            z[i, core] = part[i * tok : (i + 1) * tok]


def shards(tokens, expert_ids, route_probs, cotangents, sketch):
    n_expert = lax.axis_size("expert")
    n_dp = lax.axis_size("dp")
    count = n_expert * n_dp
    line = count // SLICES
    low = line // 2
    groups = 2 // n_dp
    tok, width = tokens.shape
    top = expert_ids.shape[1]
    hidden, rank = sketch.shape
    rows = tok * top
    share = width // SLICES
    lanes = count // 2 * rank
    part = hidden // n_dp
    scale = 1.0 / math.sqrt(rows)
    own = lax.axis_index("expert")
    half = lax.axis_index("dp")
    me = lax.axis_index(AXES)
    core = me % 2
    place = me // line

    def exchange(block, step):
        return lax.ppermute(block, AXES, [(i, i ^ step) for i in range(count)])

    def along(blocks):
        lists = [[i + j * line for j in range(SLICES)] for i in range(line)]
        return lax.all_to_all(
            blocks, AXES, split_axis=0, concat_axis=0, axis_index_groups=lists, tiled=True
        )

    xs = [along(tokens.reshape(tok, SLICES, share).swapaxes(0, 1))]

    cot = cotangents.reshape(rows, hidden)
    if n_dp > 1:
        mine = lax.dynamic_slice_in_dim(cot, half * part, part, axis=1)
        other = exchange(lax.dynamic_slice_in_dim(cot, (1 - half) * part, part, axis=1), 1)
    else:
        mine, other = cot, exchange(cot, 1)
    names = expert_ids ^ core if groups == 2 else expert_ids
    pairs = jnp.concatenate([expert_ids.astype(F32), route_probs], axis=1)
    pairs = jnp.stack([pairs, exchange(pairs, 1)])

    y = call(
        functools.partial(y_kernel, groups),
        [jax.ShapeDtypeStruct((tok, lanes), BF16)] * groups,
        4 * rows * hidden * rank,
        2 * rows * hidden,
        cot,
        sketch,
        names,
        route_probs,
    )
    y = jnp.stack([y[0], exchange(y[-1], 1)])
    ys = [along(jnp.broadcast_to(y[None], (SLICES, 2, tok, lanes)))]
    step = 2
    while step < line:
        ys = ys + [exchange(b, step) for b in ys]
        xs = xs + [exchange(b, step) for b in xs]
        step *= 2
    xs = [b for x in xs for b in (x, exchange(x, 1))]

    small = n_dp == 1
    if small:
        columns, z = call(
            functools.partial(z_kernel, len(ys)),
            [
                jax.ShapeDtypeStruct((lanes, share), BF16),
                jax.ShapeDtypeStruct((SLICES, 2, tok, lanes), BF16),
            ],
            2 * count * tok * lanes * share * 3 // 2,
            2 * count * tok * (lanes + share),
            *xs,
            *ys,
        )
    else:
        left = jnp.concatenate(ys, axis=0).reshape(-1, lanes)
        right = [jnp.stack(xs[i : i + 2], axis=1) for i in range(0, len(xs), 2)]
        right = jnp.concatenate(right, axis=0).reshape(-1, share)
        columns = dot(left, right, 0, 0)
        columns = columns.astype(BF16)
        z = jnp.stack(
            [dot(x.reshape(SLICES * tok, share), columns, 1, 1).astype(BF16) for x in xs[:2]]
        )
        z = z.reshape(2, SLICES, tok, lanes).swapaxes(0, 1)
    z = along(z)
    columns, z = lax.optimization_barrier((columns, z))

    z = jnp.sum(z.astype(F32), axis=0).reshape(2 * tok, lanes)
    pairs = pairs.reshape(2 * tok, 2 * top)
    ids = pairs[:, :top].reshape(2 * rows, 1).astype(jnp.int32)
    probs = pairs[:, top:].reshape(2 * rows, 1)
    block = jnp.arange(lanes, dtype=jnp.int32) // rank * groups + (core if groups == 2 else 0)
    spread = jnp.where(ids == block, jnp.repeat(z, top, axis=0) * probs, 0.0).astype(BF16).T
    spread = spread.reshape(SLICES, low, rank, 2 * rows)
    lower = me // 2 % low
    spread = [
        lax.dynamic_index_in_dim(spread, r ^ lower, 1, False).reshape(SLICES * rank, 2 * rows)
        for r in range(low)
    ]
    piece = part // CHUNKS
    sums = []
    for chunk in range(CHUNKS):
        cut = slice(chunk * piece, (chunk + 1) * piece)
        terms = [
            (dot(s[:, :rows], mine[:, cut], 1, 0) + dot(s[:, rows:], other[:, cut], 1, 0))
            .astype(BF16)
            .reshape(SLICES, rank, piece)
            for s in spread
        ]
        step = 2
        while len(terms) > 1:
            terms = [
                (keep.astype(F32) + exchange(send, step).astype(F32)).astype(BF16)
                for keep, send in zip(terms[::2], terms[1::2])
            ]
            step *= 2
        sums.append(terms[0])
    totals = [jnp.sum(along(s).astype(F32), axis=0) for s in sums]

    columns, _ = lax.optimization_barrier((columns, sums[0]))
    parts = columns.reshape(SLICES, n_expert // SLICES // groups, rank, share)
    parts = lax.dynamic_index_in_dim(parts, own % (n_expert // SLICES) // groups, 1, False)
    range_rows = along(parts).swapaxes(0, 1).reshape(rank, width).astype(F32)
    gram = lax.dot_general(range_rows, range_rows, (((1,), (1,)), ((), ())), precision=HIGH)
    lower = jnp.linalg.cholesky(gram)
    inverse = jax.scipy.linalg.solve_triangular(lower, jnp.eye(rank, dtype=F32), lower=True)
    kept = lax.dynamic_slice_in_dim(range_rows, half * (width // n_dp), width // n_dp, axis=1)
    basis = jnp.dot(inverse * math.sqrt(width), kept, precision=HIGH)
    coeffs = [jnp.dot(inverse * scale, total, precision=HIGH) for total in totals]
    return basis[None], jnp.concatenate(coeffs, axis=1)[None]


def solution(mesh):
    in_specs = (
        P(("group", "expert", "dp"), None),
        P(("group", "expert", "dp"), None),
        P(("group", "expert", "dp"), None),
        P(("group", "expert", "dp"), None, None),
        P(),
    )
    out_specs = (P(("group", "expert"), None, "dp"), P(("group", "expert"), None, "dp"))
    return jax.shard_map(shards, mesh=mesh, in_specs=in_specs, out_specs=out_specs, check_vma=False)
```

time: 158 us -> 111 us (0.70)
  waiting for transfers between devices: 83.6 us -> 50 us
  starting transfers between devices: 0.08 us -> 29.1 us
  blocking collectives: 27.9 us -> 0 us
  between operations: 14.2 us -> 0.96 us
  matrix products: 17.1 us -> 9.44 us
  Pallas kernels: 0 us -> 4.52 us
  local copies, waits for them, and re-layouts: 3.86 us -> 6.27 us
  other arithmetic: 11.2 us -> 9.48 us
    reduce_scatter x1 -> x0, waiting for transfers between devices: 50.2 us -> none  [shards(): lax.psum_scatter(part, AXES, scatter_dimension=0, tiled=True)]
    all_to_all x0 -> x6, waiting for transfers between devices: none -> 40.6 us  [along(): lax.all_to_all(blocks, AXES, split_axis=0, concat_axis=0, axis_index_grou...]
    all_gather x1 -> x0, waiting for transfers between devices: 32.8 us -> none  [shards(): x_all = lax.all_gather(tokens, AXES, axis=0, tiled=True)]
    all_gather x1 -> x0, blocking collectives: 27.9 us -> none  [shards(): y_all = lax.all_gather(y, AXES, axis=0, tiled=True)]
    all_to_all x0 -> x6, starting transfers between devices: none -> 24.2 us  [along(): lax.all_to_all(blocks, AXES, split_axis=0, concat_axis=0, axis_index_grou...]
    ppermute x0 -> x9, waiting for transfers between devices: none -> 9.39 us  [exchange(): return lax.ppermute(block, AXES, [(i, i ^ step) for i in range(count)])]
    dot_general x5 -> x10, matrix products: 15.1 us -> 7.98 us  [the longest x8 7.44 us: dot(): return lax.dot_general(left, right, dims, preferred_element_type=F32)]
    ppermute x0 -> x9, starting transfers between devices: none -> 5 us  [exchange(): return lax.ppermute(block, AXES, [(i, i ^ step) for i in range(count)])]
  transfers between devices with their start and end apart: 2 -> 15, of which waited for: 2 -> 9; matrix products, arithmetic and copies ran while one was open for 10% -> 19% of each run, Pallas kernels for 0% -> 4%
where the time goes in v4:
time: 111 us; the launch traced here: 110 us
  waiting for transfers between devices  50 us (45%)
  starting transfers between devices  29.1 us (26%)
  other arithmetic  9.48 us (9%)
  matrix products  9.44 us (9%)
  local copies, waits for them, and re-layouts  6.27 us (6%)
  Pallas kernels  4.52 us (4%)
    all_to_all x6, waiting for transfers between devices, along(): lax.all_to_all(blocks, AXES, split_axis=0, concat_axis=0, axis_index_grou...  40.6 us
    all_to_all x6, starting transfers between devices, along(): lax.all_to_all(blocks, AXES, split_axis=0, concat_axis=0, axis_index_grou...  24.2 us
    ppermute x9, waiting for transfers between devices, exchange(): return lax.ppermute(block, AXES, [(i, i ^ step) for i in range(count)])  9.39 us
    dot_general x8, matrix products, dot(): return lax.dot_general(left, right, dims, preferred_element_type=F32)  7.44 us
    ppermute x9, starting transfers between devices, exchange(): return lax.ppermute(block, AXES, [(i, i ^ step) for i in range(count)])  5 us
    pallas_call x2, Pallas kernels, call(): pl.pallas_call(body, out_shape=shapes, in_specs=spaces or [VMEM] * len(ar...  4.52 us
    another operation x3, other arithmetic, shards(): lower = jnp.linalg.cholesky(gram)  3.63 us
    another operation x2, other arithmetic, shards(): jax.scipy.linalg.solve_triangular(lower, jnp.eye(rank, dtype=F32), lower=...  3.07 us
  transfers between devices with their start and end apart: 15, of which 9 were waited for; matrix products, arithmetic and copies ran while one was open for 19% of the time, Pallas kernels for 4%

profile of v4, /device:TPU:0, one launch (start us, length us, event | category | flops | bytes accessed | tf_op | source)
XLA Modules:
  0.0 109.8 jit_solution(4805983548623428654)
XLA Ops:
  0.6 1.9 %copy.44 = bf16[6,4,8,896]{3,2,0,1:T(8,128)(2,1)} copy(bf16[6,4,8,896]{3,2,1,0:T(8,128)(2,1)} %bitcast.83) | data formatting | bytes 688128 | tf_op jit(solution)/shard_map/reshape | solution.py:129
  2.5 6.3 %all-to-all-start = ((bf16[4,48,896]{2,1,0:T(8,128)(2,1)}), bf16[4,48,896]{2,1,0:T(8,128)(2,1)}, u32[]{:S(2)}, u32[]{:S(2)}) async-start(bf16[4,48,896]{2,1,0:T(8,128)(2,1)} %bitcast.60), calls=%async_computation | async-start | bytes 688128 | tf_op jit(solution)/shard_map/all_to_all | solution.py:125
  9.6 10.0 %all-to-all-done.refs_0_ = bf16[4,48,896]{2,1,0:T(8,128)(2,1)} async-done(((bf16[4,48,896]{2,1,0:T(8,128)(2,1)}), bf16[4,48,896]{2,1,0:T(8,128)(2,1)}, u32[]{:S(2)}, u32[]{:S(2)}) %all-to-all-start) | async-done | bytes 344096 | tf_op jit(solution)/shard_map/all_to_all | solution.py:125
  22.6 1.7 %shard_map.68 = (bf16[48,256]{1,0:T(8,128)(2,1)S(1)}, bf16[48,256]{1,0:T(8,128)(2,1)S(1)}) custom-call(bf16[384,2560]{1,0:T(8,128)(2,1)S(1)} %bitcast.61, f32[2560,32]{1,0:T(8,128)S(1)} %copy.33.sketch, s32[48,8]{1,0:T(8,128)S(1)} %broadcast_xor_fusion.ids, f32[48,8]{1,0:T(8,128)S(1)} %copy.34.probs), custom_call_target="tpu_custom_call" | custom-call | flops 125829120 | bytes 1966080 | tf_op jit(solution)/shard_map/pallas_call | solution.py:31
  26.2 3.4 %all-to-all-start.1 = ((bf16[4,2,48,256]{3,2,1,0:T(8,128)(2,1)}), bf16[4,2,48,256]{3,2,1,0:T(8,128)(2,1)S(1)}, u32[]{:S(2)}, u32[]{:S(2)}) async-start(bf16[4,2,48,256]{3,2,1,0:T(8,128)(2,1)} %broadcast_in_dim.22), calls=%async_computation.1 | async-start | bytes 393216 | tf_op jit(solution)/shard_map/all_to_all | solution.py:125
  30.4 7.3 %all-to-all-done.1.refs_4_ = bf16[4,2,48,256]{3,2,1,0:T(8,128)(2,1)S(1)} async-done(((bf16[4,2,48,256]{3,2,1,0:T(8,128)(2,1)}), bf16[4,2,48,256]{3,2,1,0:T(8,128)(2,1)S(1)}, u32[]{:S(2)}, u32[]{:S(2)}) %all-to-all-start.1) | async-done | bytes 196640 | tf_op jit(solution)/shard_map/all_to_all | solution.py:125
  38.3 5.0 %collective-permute-done.4.refs_5_ = bf16[4,2,48,256]{3,2,1,0:T(8,128)(2,1)S(1)} collective-permute-done((bf16[4,2,48,256]{3,2,1,0:T(8,128)(2,1)S(1)}, bf16[4,2,48,256]{3,2,1,0:T(8,128)(2,1)S(1)}, u32[]{:S(2)}, u32[]{:S(2)}) %collective-permute-start.4) | collective-permute-done | bytes 196640 | tf_op jit(solution)/shard_map/ppermute | solution.py:121
  43.3 2.8 %shard_map.69 = (bf16[256,896]{1,0:T(8,128)(2,1)S(1)}, bf16[4,2,48,256]{3,2,1,0:T(8,128)(2,1)}) custom-call(bf16[4,48,896]{2,1,0:T(8,128)(2,1)} %all-to-all-done.refs_0_, bf16[4,48,896]{2,1,0:T(8,128)(2,1)S(1)} %collective-permute-done.refs_1_, bf16[4,48,896]{2,1,0:T(8,128)(2,1)} %collective-permute-done.1.refs_2_, ...), custom_call_target="tpu_custom_call" | custom-call | flops 528482304 | bytes 1769472 | tf_op jit(solution)/shard_map/pallas_call | solution.py:31
  46.1 3.4 %all-to-all-start.2 = ((bf16[4,2,48,256]{3,2,1,0:T(8,128)(2,1)}), bf16[4,2,48,256]{3,2,1,0:T(8,128)(2,1)S(1)}, u32[]{:S(2)}, u32[]{:S(2)}) async-start(bf16[4,2,48,256]{3,2,1,0:T(8,128)(2,1)} %get-tuple-element.12), calls=%async_computation.2 | async-start | bytes 393216 | tf_op jit(solution)/shard_map/all_to_all | solution.py:125
  50.0 5.7 %all-to-all-done.2 = bf16[4,2,48,256]{3,2,1,0:T(8,128)(2,1)S(1)} async-done(((bf16[4,2,48,256]{3,2,1,0:T(8,128)(2,1)}), bf16[4,2,48,256]{3,2,1,0:T(8,128)(2,1)S(1)}, u32[]{:S(2)}, u32[]{:S(2)}) %all-to-all-start.2) | async-done | bytes 196640 | tf_op jit(solution)/shard_map/all_to_all | solution.py:125
  57.6 1.5 %fusion.1 = bf16[128,1280]{1,0:T(8,128)(2,1)S(1)} fusion(f32[128,1280]{1,0:T(8,128)S(1)} %fusion.12, bf16[384,2560]{1,0:T(8,128)(2,1)} %collective-permute-done.6, bf16[128,768]{1,0:T(8,128)(2,1)S(1)} %bitcast.75), kind=kOutput, calls=%fused_computation.6 | convolution fusion | flops 126156800 | bytes 2064384 | tf_op jit(solution)/shard_map/dot_general | solution.py:23
  59.7 1.5 %fusion.3 = bf16[128,1280]{1,0:T(8,128)(2,1)S(1)} fusion(f32[128,1280]{1,0:T(8,128)S(1)} %fusion.6, bf16[384,2560]{1,0:T(8,128)(2,1)} %collective-permute-done.6, bf16[128,768]{1,0:T(8,128)(2,1)S(1)} %bitcast.76), kind=kOutput, calls=%fused_computation.8 | convolution fusion | flops 126156800 | bytes 2064384 | tf_op jit(solution)/shard_map/dot_general | solution.py:23
  61.3 1.6 %collective-permute-start.8 = (bf16[4,32,1280]{2,1,0:T(8,128)(2,1)S(1)}, bf16[4,32,1280]{2,1,0:T(8,128)(2,1)S(1)}, u32[]{:S(2)}, u32[]{:S(2)}) collective-permute-start(bf16[4,32,1280]{2,1,0:T(8,128)(2,1)S(1)} %bitcast.84), channel_id=1, source_target_pairs={{0,2},{1,3},{2,0},{3,1},{4,6},{5,7},{6,4},{7,5},{8,10},{9,11},{10,... | collective-permute-start | bytes 983048 | tf_op jit(solution)/shard_map/ppermute | solution.py:121
  62.8 1.5 %fusion = bf16[128,1280]{1,0:T(8,128)(2,1)S(1)} fusion(f32[128,1280]{1,0:T(8,128)S(1)} %fusion.14, bf16[384,2560]{1,0:T(8,128)(2,1)} %collective-permute-done.6, bf16[128,768]{1,0:T(8,128)(2,1)S(1)} %bitcast.71), kind=kOutput, calls=%fused_computation.5 | convolution fusion | flops 126156800 | bytes 2064384 | tf_op jit(solution)/shard_map/dot_general | solution.py:23
  64.4 1.5 %fusion.2 = bf16[128,1280]{1,0:T(8,128)(2,1)S(1)} fusion(f32[128,1280]{1,0:T(8,128)S(1)} %fusion.8, bf16[384,2560]{1,0:T(8,128)(2,1)} %collective-permute-done.6, bf16[128,768]{1,0:T(8,128)(2,1)S(1)} %bitcast.72), kind=kOutput, calls=%fused_computation.7 | convolution fusion | flops 126156800 | bytes 2064384 | tf_op jit(solution)/shard_map/dot_general | solution.py:23
  65.9 3.1 %collective-permute-done.7 = bf16[4,32,1280]{2,1,0:T(8,128)(2,1)S(1)} collective-permute-done((bf16[4,32,1280]{2,1,0:T(8,128)(2,1)S(1)}, bf16[4,32,1280]{2,1,0:T(8,128)(2,1)S(1)}, u32[]{:S(2)}, u32[]{:S(2)}) %collective-permute-start.7) | collective-permute-done | bytes 327712 | tf_op jit(solution)/shard_map/ppermute | solution.py:121
  70.6 3.4 %all-to-all-start.3 = ((bf16[4,32,896]{2,1,0:T(8,128)(2,1)}), bf16[4,32,896]{2,1,0:T(8,128)(2,1)S(1)}, u32[]{:S(2)}, u32[]{:S(2)}) async-start(bf16[4,32,896]{2,1,0:T(8,128)(2,1)} %dynamic-slice_bitcast_fusion), calls=%async_computation.3 | async-start | bytes 458752 | tf_op jit(solution)/shard_map/all_to_all | solution.py:125
  74.8 7.5 %all-to-all-done.3 = bf16[4,32,896]{2,1,0:T(8,128)(2,1)S(1)} async-done(((bf16[4,32,896]{2,1,0:T(8,128)(2,1)}), bf16[4,32,896]{2,1,0:T(8,128)(2,1)S(1)}, u32[]{:S(2)}, u32[]{:S(2)}) %all-to-all-start.3) | async-done | bytes 229408 | tf_op jit(solution)/shard_map/all_to_all | solution.py:125
  82.3 4.3 %all-to-all-start.4 = ((bf16[4,32,1280]{2,1,0:T(8,128)(2,1)}), bf16[4,32,1280]{2,1,0:T(8,128)(2,1)S(1)}, u32[]{:S(2)}, u32[]{:S(2)}) async-start(bf16[4,32,1280]{2,1,0:T(8,128)(2,1)} %fusion.19), calls=%async_computation.4 | async-start | bytes 655360 | tf_op jit(solution)/shard_map/all_to_all | solution.py:125
  86.8 2.9 %cholesky.17 = f32[32,32]{1,0:T(8,128)S(1)} custom-call(f32[32,32]{1,0:T(8,128)S(1)} %fusion.33), custom_call_target="Cholesky" | custom-call | tf_op jit(solution)/shard_map/jit(cholesky)/cholesky | solution.py:223
  91.1 2.4 %custom-call.7 = f32[1,32,32]{1,2,0:T(8,128)S(1)} custom-call(f32[1,32,32]{2,1,0:T(8,128)S(1)} %fusion.30), custom_call_target="InvertDiagBlocksLowerTriangular" | custom-call | tf_op jit(solution)/shard_map/jit(_solve_triangular)/triangular_solve | solution.py:224
  93.6 4.4 %all-to-all-done.4 = bf16[4,32,1280]{2,1,0:T(8,128)(2,1)S(1)} async-done(((bf16[4,32,1280]{2,1,0:T(8,128)(2,1)}), bf16[4,32,1280]{2,1,0:T(8,128)(2,1)S(1)}, u32[]{:S(2)}, u32[]{:S(2)}) %all-to-all-start.4) | async-done | bytes 327712 | tf_op jit(solution)/shard_map/all_to_all | solution.py:125
  98.0 3.5 %all-to-all-start.5 = ((bf16[4,32,1280]{2,1,0:T(8,128)(2,1)}), bf16[4,32,1280]{2,1,0:T(8,128)(2,1)S(1)}, u32[]{:S(2)}, u32[]{:S(2)}) async-start(bf16[4,32,1280]{2,1,0:T(8,128)(2,1)} %fusion.18), calls=%async_computation.5 | async-start | bytes 655360 | tf_op jit(solution)/shard_map/all_to_all | solution.py:125
  103.1 5.6 %all-to-all-done.5 = bf16[4,32,1280]{2,1,0:T(8,128)(2,1)S(1)} async-done(((bf16[4,32,1280]{2,1,0:T(8,128)(2,1)}), bf16[4,32,1280]{2,1,0:T(8,128)(2,1)S(1)}, u32[]{:S(2)}, u32[]{:S(2)}) %all-to-all-start.5) | async-done | bytes 327712 | tf_op jit(solution)/shard_map/all_to_all | solution.py:125
  (63 shorter events, 16.4 us)
Async XLA Ops:
  0.6 21.8 %copy-start.2 = (f32[48,8]{0,1:T(8,128)S(1)}, f32[48,8]{0,1:T(8,128)}, u32[]{:S(2)}) copy-start(f32[48,8]{0,1:T(8,128)} %param.7) | copy-start | bytes 4612
  0.6 21.9 %copy-start = (bf16[48,8,2560]{2,1,0:T(8,128)(2,1)S(1)}, bf16[48,8,2560]{2,1,0:T(8,128)(2,1)}, u32[]{:S(2)}) copy-start(bf16[48,8,2560]{2,1,0:T(8,128)(2,1)} %param.8) | copy-start | bytes 5898244
  2.5 17.1 %all-to-all-start = ((bf16[4,48,896]{2,1,0:T(8,128)(2,1)}), bf16[4,48,896]{2,1,0:T(8,128)(2,1)}, u32[]{:S(2)}, u32[]{:S(2)}) async-start(bf16[4,48,896]{2,1,0:T(8,128)(2,1)} %bitcast.60), calls=%async_computation | async-start | bytes 688128 | tf_op jit(solution)/shard_map/all_to_all | solution.py:125
  19.6 10.2 %collective-permute-start.1 = (bf16[4,48,896]{2,1,0:T(8,128)(2,1)}, bf16[4,48,896]{2,1,0:T(8,128)(2,1)}, u32[]{:S(2)}, u32[]{:S(2)}) collective-permute-start(bf16[4,48,896]{2,1,0:T(8,128)(2,1)} %all-to-all-done.refs_0_), channel_id=1, source_target_pairs={{0,2},{1,3},{2,0},{3,1},{4,6},{5,7},{6,4},{7,5},{8,10},{9,11},{10,... | collective-permute-start | bytes 1032200 | tf_op jit(solution)/shard_map/ppermute | solution.py:121
  22.6 7.8 %copy-start.1 = (s32[48,8]{0,1:T(8,128)S(1)}, s32[48,8]{0,1:T(8,128)}, u32[]{:S(2)}) copy-start(s32[48,8]{0,1:T(8,128)} %param.6) | copy-start | bytes 4612
  24.3 1.3 %collective-permute-start.3 = (bf16[48,256]{1,0:T(8,128)(2,1)S(1)}, bf16[48,256]{1,0:T(8,128)(2,1)S(1)}, u32[]{:S(2)}, u32[]{:S(2)}) collective-permute-start(bf16[48,256]{1,0:T(8,128)(2,1)S(1)} %get-tuple-element.10), channel_id=1, source_target_pairs={{0,1},{1,0},{2,3},{3,2},{4,5},{5,4},{6,7},{7,6},{8,9},{9,8},{10,11... | collective-permute-start | bytes 73736 | tf_op jit(solution)/shard_map/ppermute | solution.py:121
  26.2 11.4 %all-to-all-start.1 = ((bf16[4,2,48,256]{3,2,1,0:T(8,128)(2,1)}), bf16[4,2,48,256]{3,2,1,0:T(8,128)(2,1)S(1)}, u32[]{:S(2)}, u32[]{:S(2)}) async-start(bf16[4,2,48,256]{3,2,1,0:T(8,128)(2,1)} %broadcast_in_dim.22), calls=%async_computation.1 | async-start | bytes 393216 | tf_op jit(solution)/shard_map/all_to_all | solution.py:125
  29.6 13.7 %collective-permute-start = (bf16[4,48,896]{2,1,0:T(8,128)(2,1)}, bf16[4,48,896]{2,1,0:T(8,128)(2,1)S(1)}, u32[]{:S(2)}, u32[]{:S(2)}) collective-permute-start(bf16[4,48,896]{2,1,0:T(8,128)(2,1)} %all-to-all-done.refs_0_), channel_id=1, source_target_pairs={{0,1},{1,0},{2,3},{3,2},{4,5},{5,4},{6,7},{7,6},{8,9},{9,8},{10,11... | collective-permute-start | bytes 1032200 | tf_op jit(solution)/shard_map/ppermute | solution.py:121
  29.8 13.5 %collective-permute-start.2 = (bf16[4,48,896]{2,1,0:T(8,128)(2,1)}, bf16[4,48,896]{2,1,0:T(8,128)(2,1)S(1)}, u32[]{:S(2)}, u32[]{:S(2)}) collective-permute-start(bf16[4,48,896]{2,1,0:T(8,128)(2,1)} %collective-permute-done.1.refs_2_), channel_id=1, source_target_pairs={{0,1},{1,0},{2,3},{3,2},{4,5},{5,4},{6,7},{7,6},{8,9},{9,8},{10,11... | collective-permute-start | bytes 1032200 | tf_op jit(solution)/shard_map/ppermute | solution.py:121
  30.2 27.4 %collective-permute-start.6 = (bf16[384,2560]{1,0:T(8,128)(2,1)S(1)}, bf16[384,2560]{1,0:T(8,128)(2,1)}, u32[]{:S(2)}, u32[]{:S(2)}) collective-permute-start(bf16[384,2560]{1,0:T(8,128)(2,1)S(1)} %bitcast.62), channel_id=1, source_target_pairs={{0,1},{1,0},{2,3},{3,2},{4,5},{5,4},{6,7},{7,6},{8,9},{9,8},{10,11... | collective-permute-start | bytes 5898248 | tf_op jit(solution)/shard_map/ppermute | solution.py:121
  37.6 5.7 %collective-permute-start.4 = (bf16[4,2,48,256]{3,2,1,0:T(8,128)(2,1)S(1)}, bf16[4,2,48,256]{3,2,1,0:T(8,128)(2,1)S(1)}, u32[]{:S(2)}, u32[]{:S(2)}) collective-permute-start(bf16[4,2,48,256]{3,2,1,0:T(8,128)(2,1)S(1)} %all-to-all-done.1.refs_4_), channel_id=1, source_target_pairs={{0,2},{1,3},{2,0},{3,1},{4,6},{5,7},{6,4},{7,5},{8,10},{9,11},{10,... | collective-permute-start | bytes 589832 | tf_op jit(solution)/shard_map/ppermute | solution.py:121
  38.2 11.3 %collective-permute-start.5 = (f32[48,16]{0,1:T(8,128)S(1)}, f32[48,16]{0,1:T(8,128)S(1)}, u32[]{:S(2)}, u32[]{:S(2)}) collective-permute-start(f32[48,16]{0,1:T(8,128)S(1)} %get-tuple-element.21), channel_id=1, source_target_pairs={{0,1},{1,0},{2,3},{3,2},{4,5},{5,4},{6,7},{7,6},{8,9},{9,8},{10,11... | collective-permute-start | bytes 9224 | tf_op jit(solution)/shard_map/ppermute | solution.py:121
  46.1 9.6 %all-to-all-start.2 = ((bf16[4,2,48,256]{3,2,1,0:T(8,128)(2,1)}), bf16[4,2,48,256]{3,2,1,0:T(8,128)(2,1)S(1)}, u32[]{:S(2)}, u32[]{:S(2)}) async-start(bf16[4,2,48,256]{3,2,1,0:T(8,128)(2,1)} %get-tuple-element.12), calls=%async_computation.2 | async-start | bytes 393216 | tf_op jit(solution)/shard_map/all_to_all | solution.py:125
  59.1 9.9 %collective-permute-start.7 = (bf16[4,32,1280]{2,1,0:T(8,128)(2,1)S(1)}, bf16[4,32,1280]{2,1,0:T(8,128)(2,1)S(1)}, u32[]{:S(2)}, u32[]{:S(2)}) collective-permute-start(bf16[4,32,1280]{2,1,0:T(8,128)(2,1)S(1)} %bitcast.85), channel_id=1, source_target_pairs={{0,2},{1,3},{2,0},{3,1},{4,6},{5,7},{6,4},{7,5},{8,10},{9,11},{10,... | collective-permute-start | bytes 983048 | tf_op jit(solution)/shard_map/ppermute | solution.py:121
  61.3 12.7 %collective-permute-start.8 = (bf16[4,32,1280]{2,1,0:T(8,128)(2,1)S(1)}, bf16[4,32,1280]{2,1,0:T(8,128)(2,1)S(1)}, u32[]{:S(2)}, u32[]{:S(2)}) collective-permute-start(bf16[4,32,1280]{2,1,0:T(8,128)(2,1)S(1)} %bitcast.84), channel_id=1, source_target_pairs={{0,2},{1,3},{2,0},{3,1},{4,6},{5,7},{6,4},{7,5},{8,10},{9,11},{10,... | collective-permute-start | bytes 983048 | tf_op jit(solution)/shard_map/ppermute | solution.py:121
  70.6 11.7 %all-to-all-start.3 = ((bf16[4,32,896]{2,1,0:T(8,128)(2,1)}), bf16[4,32,896]{2,1,0:T(8,128)(2,1)S(1)}, u32[]{:S(2)}, u32[]{:S(2)}) async-start(bf16[4,32,896]{2,1,0:T(8,128)(2,1)} %dynamic-slice_bitcast_fusion), calls=%async_computation.3 | async-start | bytes 458752 | tf_op jit(solution)/shard_map/all_to_all | solution.py:125
  82.3 15.7 %all-to-all-start.4 = ((bf16[4,32,1280]{2,1,0:T(8,128)(2,1)}), bf16[4,32,1280]{2,1,0:T(8,128)(2,1)S(1)}, u32[]{:S(2)}, u32[]{:S(2)}) async-start(bf16[4,32,1280]{2,1,0:T(8,128)(2,1)} %fusion.19), calls=%async_computation.4 | async-start | bytes 655360 | tf_op jit(solution)/shard_map/all_to_all | solution.py:125
  98.0 10.7 %all-to-all-start.5 = ((bf16[4,32,1280]{2,1,0:T(8,128)(2,1)}), bf16[4,32,1280]{2,1,0:T(8,128)(2,1)S(1)}, u32[]{:S(2)}, u32[]{:S(2)}) async-start(bf16[4,32,1280]{2,1,0:T(8,128)(2,1)} %fusion.18), calls=%async_computation.5 | async-start | bytes 655360 | tf_op jit(solution)/shard_map/all_to_all | solution.py:125

commit v5 on v4

v5 whole, which is shorter than its diff:
```python
import functools
import math

import jax
import jax.numpy as jnp
from jax import lax
from jax.experimental import pallas as pl
from jax.experimental.pallas import tpu as pltpu
from jax.sharding import PartitionSpec as P

AXES = ("expert", "dp")
HIGH = lax.Precision.HIGHEST
CHUNKS = 2
SLICES = 4
LIMIT = 24 * 1024 * 1024
VMEM = pl.BlockSpec(memory_space=pltpu.VMEM)
SMEM = pl.BlockSpec(memory_space=pltpu.SMEM)
BF16 = jnp.bfloat16
F32 = jnp.float32


def dot(left, right, left_dim, right_dim):
    dims = (((left_dim,), (right_dim,)), ((), ()))
    return lax.dot_general(left, right, dims, preferred_element_type=F32)


def iota(shape, dim):
    return lax.broadcasted_iota(jnp.int32, shape, dim)


def call(body, shapes, flops, size, *args, spaces=None):
    return pl.pallas_call(
        body,
        out_shape=shapes,
        in_specs=spaces or [VMEM] * len(args),
        out_specs=jax.tree.map(lambda _: VMEM, shapes),
        compiler_params=pltpu.CompilerParams(vmem_limit_bytes=LIMIT),
        cost_estimate=pl.CostEstimate(flops=flops, bytes_accessed=size, transcendentals=0),
    )(*args)


def pair_columns(ids, probs):
    top, tok = ids.shape
    rows = tok * top
    pick = (iota((rows, tok), 0) // top == iota((rows, tok), 1)).astype(BF16)
    here = iota((rows, top), 0) % top == iota((rows, top), 1)
    names = dot(pick, ids.astype(BF16), 1, 1)
    weights, rest = jnp.zeros((rows, top), F32), probs
    for _ in range(3):
        piece = rest.astype(BF16)
        weights = weights + dot(pick, piece, 1, 1)
        rest = rest - piece.astype(F32)
    names = jnp.sum(jnp.where(here, names, 0.0), axis=1, keepdims=True)
    weights = jnp.sum(jnp.where(here, weights, 0.0), axis=1, keepdims=True)
    return names, weights


def y_kernel(groups, core, cot, sketch, pairs, *outs):
    rows = cot.shape[0]
    tok = pairs.shape[1]
    top = rows // tok
    rank = sketch.shape[0]
    lanes = outs[0].shape[1]
    high = sketch[...].astype(BF16)
    low = (sketch[...] - high.astype(F32)).astype(BF16)
    pair = dot(cot[...], high, 1, 1) + dot(cot[...], low, 1, 1)
    names, weights = pair_columns(pairs[:top], pairs[top:])
    pair = (pair * weights).astype(BF16)
    lane = iota((rank, lanes), 1)
    tiled = dot(pair, (iota((rank, lanes), 0) == lane % rank).astype(BF16), 1, 0)
    block = iota((1, lanes), 1) // rank * groups
    for i, out in enumerate(outs):
        name = block + (core[0] ^ i) if groups == 2 else block
        y = jnp.where(names == name.astype(F32), tiled, 0.0)
        out[...] = jnp.sum(y.reshape(tok, top, lanes), axis=1).astype(BF16)


def z_kernel(n, *refs):
    xs, ys, columns, zs = refs[: 2 * n], refs[2 * n : 3 * n], refs[3 * n], refs[3 * n + 1 :]
    total = 0.0
    for b in range(n):
        for core in range(2):
            y = ys[b][:, core].reshape(-1, columns.shape[0])
            total = total + dot(y, xs[2 * b + core][...], 0, 0)
    total = total.astype(BF16)
    columns[...] = total
    tok = zs[0].shape[1]
    each = xs[0].shape[0] // tok
    for core in range(2):
        for b in range(len(zs) // each):
            part = dot(xs[2 * b + core][...], total, 1, 1).astype(BF16)
            for i in range(each):
                zs[b * each + i][core] = part[i * tok : (i + 1) * tok]


def spread_kernel(groups, at, *refs):
    zs, pairs, outs = refs[:SLICES], refs[SLICES : SLICES + 2], refs[SLICES + 2 : -1]
    work = refs[-1]
    _, tok, lanes = zs[0].shape
    top = pairs[0].shape[0] // 2
    rows = tok * top
    rank = outs[0].shape[0] // SLICES
    block = iota((1, lanes), 1) // rank * groups + (at[0] if groups == 2 else 0)
    for core in range(2):
        z = zs[0][core].astype(F32)
        for other in zs[1:]:
            z = z + other[core].astype(F32)
        names, weights = pair_columns(pairs[core][:top], pairs[core][top:])
        z = jnp.broadcast_to(z[:, None], (tok, top, lanes)).reshape(rows, lanes)
        z = jnp.where(names == block.astype(F32), z * weights, 0.0).astype(BF16)
        work[:, core * rows : (core + 1) * rows] = z.T
    for r, out in enumerate(outs):
        for j in range(SLICES):
            start = pl.multiple_of((j * len(outs) + (at[1] ^ r)) * rank, rank)
            out[j * rank : (j + 1) * rank] = work[pl.ds(start, rank)]


def part_kernel(spread, mine, other, *outs):
    rows = mine.shape[0]
    start = 0
    for out in outs:
        size = out.shape[1]
        part = dot(spread[:, :rows], mine[:, start : start + size], 1, 0)
        part = part + dot(spread[:, rows:], other[:, start : start + size], 1, 0)
        out[...] = part.astype(BF16)
        start += size


def shards(tokens, expert_ids, route_probs, cotangents, sketch):
    n_expert = lax.axis_size("expert")
    n_dp = lax.axis_size("dp")
    count = n_expert * n_dp
    line = count // SLICES
    low = line // 2
    groups = 2 // n_dp
    tok, width = tokens.shape
    top = expert_ids.shape[1]
    hidden, rank = sketch.shape
    rows = tok * top
    share = width // SLICES
    lanes = count // 2 * rank
    part = hidden // n_dp
    scale = 1.0 / math.sqrt(rows)
    own = lax.axis_index("expert")
    half = lax.axis_index("dp")
    me = lax.axis_index(AXES)
    core = me % 2
    place = me // line
    lower = me // 2 % low
    shape = jax.ShapeDtypeStruct

    def exchange(block, step):
        return lax.ppermute(block, AXES, [(i, i ^ step) for i in range(count)])

    cuts = [
        lax.dynamic_slice_in_dim(tokens, (place ^ j) * share, share, axis=1) for j in range(SLICES)
    ]
    cuts = cuts[:1] + [exchange(cuts[j], j * line) for j in range(1, SLICES)]
    xs = [jnp.concatenate(cuts[i : i + 2], axis=0) for i in range(0, SLICES, 2)]

    cot = cotangents.reshape(rows, hidden)
    if n_dp > 1:
        mine = lax.dynamic_slice_in_dim(cot, half * part, part, axis=1)
        other = exchange(lax.dynamic_slice_in_dim(cot, (1 - half) * part, part, axis=1), 1)
    else:
        mine, other = cot, exchange(cot, 1)
    pairs = jnp.concatenate([expert_ids.T.astype(F32), route_probs.T], axis=0)
    pairs = [pairs, exchange(pairs, 1)]

    y = call(
        functools.partial(y_kernel, groups),
        [shape((tok, lanes), BF16)] * groups,
        4 * rows * hidden * rank,
        2 * rows * hidden,
        core.reshape(1),
        cot,
        sketch.T,
        pairs[0],
        spaces=[SMEM] + [VMEM] * 3,
    )
    y = jnp.stack([y[0], exchange(y[-1], 1)])
    ys = [y] + [exchange(y, j * line) for j in range(1, SLICES)]
    ys = [jnp.stack(ys[i : i + 2]) for i in range(0, SLICES, 2)]
    step = 2
    while step < line:
        ys = ys + [exchange(b, step) for b in ys]
        xs = xs + [exchange(b, step) for b in xs]
        step *= 2
    xs = [b for x in xs for b in (x, exchange(x, 1))]

    if n_dp == 1:
        columns, *zs = call(
            functools.partial(z_kernel, len(ys)),
            [shape((lanes, share), BF16)] + [shape((2, tok, lanes), BF16)] * SLICES,
            2 * count * tok * lanes * share * 3 // 2,
            2 * count * tok * (lanes + share),
            *xs,
            *ys,
        )
    else:
        left = jnp.concatenate(ys, axis=0).reshape(-1, lanes)
        right = [jnp.stack([xs[i], xs[i + 1]]) for i in range(0, len(xs), 2)]
        right = jnp.stack(right).reshape(-1, 2, 2, tok, share).swapaxes(1, 2)
        columns = dot(left, right.reshape(-1, share), 0, 0).astype(BF16)
        zs = [
            jnp.stack([dot(x[i : i + tok], columns, 1, 1).astype(BF16) for x in xs[b : b + 2]])
            for b in (0, 2)
            for i in (0, tok)
        ]
    zs = zs[:1] + [exchange(zs[j], j * line) for j in range(1, SLICES)]

    spread = pl.pallas_call(
        functools.partial(spread_kernel, groups),
        out_shape=[shape((SLICES * rank, 2 * rows), BF16)] * low,
        in_specs=[SMEM] + [VMEM] * (SLICES + 2),
        out_specs=[VMEM] * low,
        scratch_shapes=[pltpu.VMEM((lanes, 2 * rows), BF16)],
        compiler_params=pltpu.CompilerParams(vmem_limit_bytes=LIMIT),
        cost_estimate=pl.CostEstimate(
            flops=0, bytes_accessed=8 * rows * lanes, transcendentals=0
        ),
    )(jnp.stack([core, lower]), *zs, *pairs)
    piece = part // CHUNKS
    terms = [
        call(
            part_kernel,
            [shape((SLICES * rank, piece), BF16)] * CHUNKS,
            4 * rows * SLICES * rank * part,
            4 * rows * part,
            s,
            mine,
            other,
        )
        for s in spread[::-1]
    ][::-1]
    sums = []
    for chunk in range(CHUNKS):
        blocks = [term[chunk].reshape(SLICES, rank, piece) for term in terms]
        step = 2
        while len(blocks) > 1:
            blocks = [
                (keep.astype(F32) + exchange(send, step).astype(F32)).astype(BF16)
                for keep, send in zip(blocks[::2], blocks[1::2])
            ]
            step *= 2
        sums.append(blocks[0])
    totals = []
    for block in sums:
        gone = [
            exchange(lax.dynamic_index_in_dim(block, place ^ j, 0, False), j * line)
            for j in range(1, SLICES)
        ]
        total = lax.dynamic_index_in_dim(block, place, 0, False).astype(F32)
        for other in gone:
            total = total + other.astype(F32)
        totals.append(total)

    columns, _ = lax.optimization_barrier((columns, terms[0]))
    parts = columns.reshape(SLICES, n_expert // SLICES // groups, rank, share)
    parts = lax.dynamic_index_in_dim(parts, own % (n_expert // SLICES) // groups, 1, False)
    parts = [lax.dynamic_index_in_dim(parts, place ^ j, 0, False) for j in range(SLICES)]
    parts = jnp.stack(parts[:1] + [exchange(parts[j], j * line) for j in range(1, SLICES)])
    parts = [lax.dynamic_index_in_dim(parts, place ^ j, 0, False) for j in range(SLICES)]
    range_rows = jnp.concatenate(parts, axis=1).astype(F32)
    gram = lax.dot_general(range_rows, range_rows, (((1,), (1,)), ((), ())), precision=HIGH)
    lower = jnp.linalg.cholesky(gram)
    inverse = jax.scipy.linalg.solve_triangular(lower, jnp.eye(rank, dtype=F32), lower=True)
    kept = lax.dynamic_slice_in_dim(range_rows, half * (width // n_dp), width // n_dp, axis=1)
    basis = jnp.dot(inverse * math.sqrt(width), kept, precision=HIGH)
    coeffs = [jnp.dot(inverse * scale, total, precision=HIGH) for total in totals]
    return basis[None], jnp.concatenate(coeffs, axis=1)[None]


def solution(mesh):
    in_specs = (
        P(("group", "expert", "dp"), None),
        P(("group", "expert", "dp"), None),
        P(("group", "expert", "dp"), None),
        P(("group", "expert", "dp"), None, None),
        P(),
    )
    out_specs = (P(("group", "expert"), None, "dp"), P(("group", "expert"), None, "dp"))
    return jax.shard_map(shards, mesh=mesh, in_specs=in_specs, out_specs=out_specs, check_vma=False)
```

time: 111 us -> 94.2 us (0.85)
  waiting for transfers between devices: 50 us -> 27.7 us
  matrix products: 9.44 us -> 2.09 us
  Pallas kernels: 4.52 us -> 10.8 us
  starting transfers between devices: 29.1 us -> 34.1 us
  local copies, waits for them, and re-layouts: 6.27 us -> 9.08 us
    all_to_all x6 -> x0, waiting for transfers between devices: 40.6 us -> none  [along(): lax.all_to_all(blocks, AXES, split_axis=0, concat_axis=0, axis_index_grou...]
    ppermute x9 -> x31, starting transfers between devices: 5 us -> 34.1 us  [exchange(): return lax.ppermute(block, AXES, [(i, i ^ step) for i in range(count)])]
    all_to_all x6 -> x0, starting transfers between devices: 24.2 us -> none  [along(): lax.all_to_all(blocks, AXES, split_axis=0, concat_axis=0, axis_index_grou...]
    ppermute x9 -> x31, waiting for transfers between devices: 9.39 us -> 27.7 us  [exchange(): return lax.ppermute(block, AXES, [(i, i ^ step) for i in range(count)])]
    dot_general x8 -> x0, matrix products: 7.44 us -> none  [dot(): return lax.dot_general(left, right, dims, preferred_element_type=F32)]
    unnamed x9 -> x25, local copies, waits for them, and re-layouts: 2.22 us -> 8.84 us
    pallas_call x2 -> x4, Pallas kernels: 4.52 us -> 9.66 us  [call(): pl.pallas_call(body, out_shape=shapes, in_specs=spaces or [VMEM] * len(ar...]
    reshape x3 -> x0, local copies, waits for them, and re-layouts: 1.99 us -> none  [the longest x1 1.88 us: shards(): xs = [along(tokens.reshape(tok, SLICES, share).swapaxes(0, 1))]]
  transfers between devices with their start and end apart: 15 -> 31, of which waited for: 9 -> 13; matrix products, arithmetic and copies ran while one was open for 19% -> 11% of each run, Pallas kernels for 4% -> 9%
where the time goes in v5:
time: 94.2 us; the launch traced here: 93.7 us
  starting transfers between devices  34.1 us (36%)
  waiting for transfers between devices  27.7 us (29%)
  Pallas kernels  10.8 us (11%)
  other arithmetic  9.13 us (10%)
  local copies, waits for them, and re-layouts  9.08 us (10%)
  matrix products  2.09 us (2%)
    ppermute x31, starting transfers between devices, exchange(): return lax.ppermute(block, AXES, [(i, i ^ step) for i in range(count)])  34.1 us
    ppermute x31, waiting for transfers between devices, exchange(): return lax.ppermute(block, AXES, [(i, i ^ step) for i in range(count)])  27.7 us
    pallas_call x4, Pallas kernels, call(): pl.pallas_call(body, out_shape=shapes, in_specs=spaces or [VMEM] * len(ar...  9.66 us
    unnamed x25, local copies, waits for them, and re-layouts  8.84 us
    another operation x3, other arithmetic, shards(): lower = jnp.linalg.cholesky(gram)  3.6 us
    another operation x2, other arithmetic, shards(): jax.scipy.linalg.solve_triangular(lower, jnp.eye(rank, dtype=F32), lower=...  3.09 us
  transfers between devices with their start and end apart: 31, of which 13 were waited for; matrix products, arithmetic and copies ran while one was open for 11% of the time, Pallas kernels for 9%

profile of v5, /device:TPU:0, one launch (start us, length us, event | category | flops | bytes accessed | tf_op | source)
XLA Modules:
  0.0 93.7 jit_solution(16723414366921962184)
XLA Ops:
  2.5 1.5 %copy-done = bf16[48,8,2560]{2,1,0:T(8,128)(2,1)S(1)} copy-done((bf16[48,8,2560]{2,1,0:T(8,128)(2,1)S(1)}, bf16[48,8,2560]{2,1,0:T(8,128)(2,1)}, u32[]{:S(2)}) %copy-start) | copy-done | bytes 1966104
  5.0 1.6 %shard_map.68 = (bf16[48,256]{1,0:T(8,128)(2,1)S(1)}, bf16[48,256]{1,0:T(8,128)(2,1)S(1)}) custom-call(s32[1]{0:T(128)} %bitcast.core, bf16[384,2560]{1,0:T(8,128)(2,1)S(1)} %bitcast.78, f32[32,2560]{1,0:T(8,128)S(1)} %bitcast.81, f32[16,48]{1,0:T(8,128)S(1)} %pad_maximum_fusion.8.pairs.refs_4_), custom_call_target="tpu_custom_call" | custom-call | flops 125829120 | bytes 1966080 | tf_op jit(solution)/shard_map/pallas_call | solution.py:32
  8.0 4.8 %collective-permute-start.12 = (bf16[2,48,256]{2,1,0:T(8,128)(2,1)S(1)}, bf16[2,48,256]{2,1,0:T(8,128)(2,1)S(1)}, u32[]{:S(2)}, u32[]{:S(2)}) collective-permute-start(bf16[2,48,256]{2,1,0:T(8,128)(2,1)S(1)} %get-tuple-element.49), channel_id=1, source_target_pairs={{0,12},{1,13},{2,14},{3,15},{4,8},{5,9},{6,10},{7,11},{8,4},{9,5},... | collective-permute-start | bytes 147464 | tf_op jit(solution)/shard_map/ppermute | solution.py:153
  12.8 3.0 %collective-permute-start.2 = (bf16[48,896]{1,0:T(8,128)(2,1)S(1)}, bf16[48,896]{1,0:T(8,128)(2,1)S(1)}, u32[]{:S(2)}, u32[]{:S(2)}) collective-permute-start(bf16[48,896]{1,0:T(8,128)(2,1)S(1)} %get-tuple-element.37), channel_id=1, source_target_pairs={{0,8},{1,9},{2,10},{3,11},{4,12},{5,13},{6,14},{7,15},{8,0},{9,1},... | collective-permute-start | bytes 258056 | tf_op jit(solution)/shard_map/ppermute | solution.py:153
  16.5 3.3 %collective-permute-done.11 = bf16[2,48,256]{2,1,0:T(8,128)(2,1)S(1)} collective-permute-done((bf16[2,48,256]{2,1,0:T(8,128)(2,1)S(1)}, bf16[2,48,256]{2,1,0:T(8,128)(2,1)S(1)}, u32[]{:S(2)}, u32[]{:S(2)}) %collective-permute-start.11) | collective-permute-done | bytes 49184 | tf_op jit(solution)/shard_map/ppermute | solution.py:153
  19.8 3.7 %collective-permute-done.2 = bf16[48,896]{1,0:T(8,128)(2,1)S(1)} collective-permute-done((bf16[48,896]{1,0:T(8,128)(2,1)S(1)}, bf16[48,896]{1,0:T(8,128)(2,1)S(1)}, u32[]{:S(2)}, u32[]{:S(2)}) %collective-permute-start.2) | collective-permute-done | bytes 86048 | tf_op jit(solution)/shard_map/ppermute | solution.py:153
  23.5 1.5 %collective-permute-start.14 = (bf16[2,2,48,256]{3,2,1,0:T(8,128)(2,1)S(1)}, bf16[2,2,48,256]{3,2,1,0:T(8,128)(2,1)S(1)}, u32[]{:S(2)}, u32[]{:S(2)}) collective-permute-start(bf16[2,2,48,256]{3,2,1,0:T(8,128)(2,1)S(1)} %pad_maximum_fusion.4.refs_9_), channel_id=1, source_target_pairs={{0,2},{1,3},{2,0},{3,1},{4,6},{5,7},{6,4},{7,5},{8,10},{9,11},{10,... | collective-permute-start | bytes 294920 | tf_op jit(solution)/shard_map/ppermute | solution.py:153
  25.6 1.6 %collective-permute-start.5 = (bf16[96,896]{1,0:T(8,128)(2,1)S(1)}, bf16[96,896]{1,0:T(8,128)(2,1)S(1)}, u32[]{:S(2)}, u32[]{:S(2)}) collective-permute-start(bf16[96,896]{1,0:T(8,128)(2,1)S(1)} %pad_maximum_fusion.2.refs_0_), channel_id=1, source_target_pairs={{0,2},{1,3},{2,0},{3,1},{4,6},{5,7},{6,4},{7,5},{8,10},{9,11},{10,... | collective-permute-start | bytes 516104 | tf_op jit(solution)/shard_map/ppermute | solution.py:153
  29.0 8.7 %collective-permute-done.13.refs_10_ = bf16[2,2,48,256]{3,2,1,0:T(8,128)(2,1)S(1)} collective-permute-done((bf16[2,2,48,256]{3,2,1,0:T(8,128)(2,1)S(1)}, bf16[2,2,48,256]{3,2,1,0:T(8,128)(2,1)S(1)}, u32[]{:S(2)}, u32[]{:S(2)}) %collective-permute-start.13) | collective-permute-done | bytes 98336 | tf_op jit(solution)/shard_map/ppermute | solution.py:153
  45.1 3.2 %shard_map.69 = (bf16[256,896]{1,0:T(8,128)(2,1)S(1)}, bf16[2,48,256]{2,1,0:T(8,128)(2,1)S(1)}, bf16[2,48,256]{2,1,0:T(8,128)(2,1)}, bf16[2,48,256]{2,1,0:T(8,128)(2,1)}, bf16[2,48,256]{2,1,0:T(8,128)(2,1)S(1)}) custom-call(bf16[96,896]{1,0:T(8,128)(2,1)S(1)} %pad_maximum_fusion.2.refs_0_, bf16[96,896]{1,0:T(8,128)(2,1)S(1)} %copy-done.6, ...), custom_call_target="tpu_custom_call" | custom-call | flops 528482304 | bytes 1769472 | tf_op jit(solution)/shard_map/pallas_call | solution.py:32
  48.7 2.4 %collective-permute-start.16 = (bf16[2,48,256]{2,1,0:T(8,128)(2,1)}, bf16[2,48,256]{2,1,0:T(8,128)(2,1)S(1)}, u32[]{:S(2)}, u32[]{:S(2)}) collective-permute-start(bf16[2,48,256]{2,1,0:T(8,128)(2,1)} %get-tuple-element.21), channel_id=1, source_target_pairs={{0,8},{1,9},{2,10},{3,11},{4,12},{5,13},{6,14},{7,15},{8,0},{9,1},... | collective-permute-start | bytes 147464 | tf_op jit(solution)/shard_map/ppermute | solution.py:153
  51.0 1.6 %collective-permute-start.17 = (bf16[2,48,256]{2,1,0:T(8,128)(2,1)S(1)}, bf16[2,48,256]{2,1,0:T(8,128)(2,1)S(1)}, u32[]{:S(2)}, u32[]{:S(2)}) collective-permute-start(bf16[2,48,256]{2,1,0:T(8,128)(2,1)S(1)} %get-tuple-element.22), channel_id=1, source_target_pairs={{0,12},{1,13},{2,14},{3,15},{4,8},{5,9},{6,10},{7,11},{8,4},{9,5},... | collective-permute-start | bytes 147464 | tf_op jit(solution)/shard_map/ppermute | solution.py:153
  54.5 2.5 %collective-permute-done.17.refs_3_ = bf16[2,48,256]{2,1,0:T(8,128)(2,1)S(1)} collective-permute-done((bf16[2,48,256]{2,1,0:T(8,128)(2,1)S(1)}, bf16[2,48,256]{2,1,0:T(8,128)(2,1)S(1)}, u32[]{:S(2)}, u32[]{:S(2)}) %collective-permute-start.17) | collective-permute-done | bytes 49184 | tf_op jit(solution)/shard_map/ppermute | solution.py:153
  58.1 2.4 %shard_map.71 = (bf16[128,1280]{1,0:T(8,128)(2,1)S(1)}, bf16[128,1280]{1,0:T(8,128)(2,1)S(1)}) custom-call(bf16[128,768]{1,0:T(8,128)(2,1)S(1)} %get-tuple-element.23.spread, bf16[384,2560]{1,0:T(8,128)(2,1)S(1)} %bitcast.79, bf16[384,2560]{1,0:T(8,128)(2,1)} %collective-permute-done.19.other), custom_call_target="tpu_custom_call" | custom-call | flops 503316480 | bytes 3932160 | tf_op jit(solution)/shard_map/pallas_call | solution.py:32
  60.6 2.2 %collective-permute-start.21 = (bf16[32,896]{1,0:T(8,128)(2,1)S(1)}, bf16[32,896]{1,0:T(8,128)(2,1)S(1)}, u32[]{:S(2)}, u32[]{:S(2)}) collective-permute-start(bf16[32,896]{1,0:T(8,128)(2,1)S(1)} %get-tuple-element.32), channel_id=1, source_target_pairs={{0,8},{1,9},{2,10},{3,11},{4,12},{5,13},{6,14},{7,15},{8,0},{9,1},... | collective-permute-start | bytes 172040 | tf_op jit(solution)/shard_map/ppermute | solution.py:153
  62.8 2.2 %collective-permute-start.22 = (bf16[32,896]{1,0:T(8,128)(2,1)S(1)}, bf16[32,896]{1,0:T(8,128)(2,1)S(1)}, u32[]{:S(2)}, u32[]{:S(2)}) collective-permute-start(bf16[32,896]{1,0:T(8,128)(2,1)S(1)} %get-tuple-element.31), channel_id=1, source_target_pairs={{0,12},{1,13},{2,14},{3,15},{4,8},{5,9},{6,10},{7,11},{8,4},{9,5},... | collective-permute-start | bytes 172040 | tf_op jit(solution)/shard_map/ppermute | solution.py:153
  65.0 2.4 %shard_map.72 = (bf16[128,1280]{1,0:T(8,128)(2,1)S(1)}, bf16[128,1280]{1,0:T(8,128)(2,1)S(1)}) custom-call(bf16[128,768]{1,0:T(8,128)(2,1)S(1)} %get-tuple-element.27.spread, bf16[384,2560]{1,0:T(8,128)(2,1)S(1)} %bitcast.80, bf16[384,2560]{1,0:T(8,128)(2,1)} %collective-permute-done.19.other), custom_call_target="tpu_custom_call" | custom-call | flops 503316480 | bytes 3932160 | tf_op jit(solution)/shard_map/pallas_call | solution.py:32
  69.9 2.9 %cholesky.17 = f32[32,32]{1,0:T(8,128)S(1)} custom-call(f32[32,32]{1,0:T(8,128)S(1)} %fusion.24), custom_call_target="Cholesky" | custom-call | tf_op jit(solution)/shard_map/jit(cholesky)/cholesky | solution.py:266
  74.1 2.4 %custom-call.7 = f32[1,32,32]{1,2,0:T(8,128)S(1)} custom-call(f32[1,32,32]{2,1,0:T(8,128)S(1)} %fusion.21), custom_call_target="InvertDiagBlocksLowerTriangular" | custom-call | tf_op jit(solution)/shard_map/jit(_solve_triangular)/triangular_solve | solution.py:267
  78.3 2.2 %collective-permute-start.25 = (bf16[32,1280]{1,0:T(8,128)(2,1)S(1)}, bf16[32,1280]{1,0:T(8,128)(2,1)S(1)}, u32[]{:S(2)}, u32[]{:S(2)}) collective-permute-start(bf16[32,1280]{1,0:T(8,128)(2,1)S(1)} %get-tuple-element.40), channel_id=1, source_target_pairs={{0,8},{1,9},{2,10},{3,11},{4,12},{5,13},{6,14},{7,15},{8,0},{9,1},... | collective-permute-start | bytes 245768 | tf_op jit(solution)/shard_map/ppermute | solution.py:153
  80.5 2.2 %collective-permute-start.26 = (bf16[32,1280]{1,0:T(8,128)(2,1)S(1)}, bf16[32,1280]{1,0:T(8,128)(2,1)S(1)}, u32[]{:S(2)}, u32[]{:S(2)}) collective-permute-start(bf16[32,1280]{1,0:T(8,128)(2,1)S(1)} %get-tuple-element.39), channel_id=1, source_target_pairs={{0,12},{1,13},{2,14},{3,15},{4,8},{5,9},{6,10},{7,11},{8,4},{9,5},... | collective-permute-start | bytes 245768 | tf_op jit(solution)/shard_map/ppermute | solution.py:153
  82.9 2.2 %collective-permute-start.29 = (bf16[32,1280]{1,0:T(8,128)(2,1)S(1)}, bf16[32,1280]{1,0:T(8,128)(2,1)S(1)}, u32[]{:S(2)}, u32[]{:S(2)}) collective-permute-start(bf16[32,1280]{1,0:T(8,128)(2,1)S(1)} %get-tuple-element.43), channel_id=1, source_target_pairs={{0,8},{1,9},{2,10},{3,11},{4,12},{5,13},{6,14},{7,15},{8,0},{9,1},... | collective-permute-start | bytes 245768 | tf_op jit(solution)/shard_map/ppermute | solution.py:153
  85.3 2.1 %collective-permute-start.30 = (bf16[32,1280]{1,0:T(8,128)(2,1)S(1)}, bf16[32,1280]{1,0:T(8,128)(2,1)S(1)}, u32[]{:S(2)}, u32[]{:S(2)}) collective-permute-start(bf16[32,1280]{1,0:T(8,128)(2,1)S(1)} %get-tuple-element.42), channel_id=1, source_target_pairs={{0,12},{1,13},{2,14},{3,15},{4,8},{5,9},{6,10},{7,11},{8,4},{9,5},... | collective-permute-start | bytes 245768 | tf_op jit(solution)/shard_map/ppermute | solution.py:153
  89.2 3.5 %collective-permute-done.29 = bf16[32,1280]{1,0:T(8,128)(2,1)S(1)} collective-permute-done((bf16[32,1280]{1,0:T(8,128)(2,1)S(1)}, bf16[32,1280]{1,0:T(8,128)(2,1)S(1)}, u32[]{:S(2)}, u32[]{:S(2)}) %collective-permute-start.29) | collective-permute-done | bytes 81952 | tf_op jit(solution)/shard_map/ppermute | solution.py:153
  (97 shorter events, 26.8 us)
Async XLA Ops:
  0.6 57.5 %collective-permute-start.19 = (bf16[384,2560]{1,0:T(8,128)(2,1)}, bf16[384,2560]{1,0:T(8,128)(2,1)}, u32[]{:S(2)}, u32[]{:S(2)}) collective-permute-start(bf16[384,2560]{1,0:T(8,128)(2,1)} %bitcast.77), channel_id=1, source_target_pairs={{0,1},{1,0},{2,3},{3,2},{4,5},{5,4},{6,7},{7,6},{8,9},{9,8},{10,11... | collective-permute-start | bytes 5898248 | tf_op jit(solution)/shard_map/ppermute | solution.py:153
  8.0 7.9 %collective-permute-start.12 = (bf16[2,48,256]{2,1,0:T(8,128)(2,1)S(1)}, bf16[2,48,256]{2,1,0:T(8,128)(2,1)S(1)}, u32[]{:S(2)}, u32[]{:S(2)}) collective-permute-start(bf16[2,48,256]{2,1,0:T(8,128)(2,1)S(1)} %get-tuple-element.49), channel_id=1, source_target_pairs={{0,12},{1,13},{2,14},{3,15},{4,8},{5,9},{6,10},{7,11},{8,4},{9,5},... | collective-permute-start | bytes 147464 | tf_op jit(solution)/shard_map/ppermute | solution.py:153
  12.8 7.0 %collective-permute-start.11 = (bf16[2,48,256]{2,1,0:T(8,128)(2,1)S(1)}, bf16[2,48,256]{2,1,0:T(8,128)(2,1)S(1)}, u32[]{:S(2)}, u32[]{:S(2)}) collective-permute-start(bf16[2,48,256]{2,1,0:T(8,128)(2,1)S(1)} %get-tuple-element.49), channel_id=1, source_target_pairs={{0,8},{1,9},{2,10},{3,11},{4,12},{5,13},{6,14},{7,15},{8,0},{9,1},... | collective-permute-start | bytes 147464 | tf_op jit(solution)/shard_map/ppermute | solution.py:153
  12.8 10.6 %collective-permute-start.2 = (bf16[48,896]{1,0:T(8,128)(2,1)S(1)}, bf16[48,896]{1,0:T(8,128)(2,1)S(1)}, u32[]{:S(2)}, u32[]{:S(2)}) collective-permute-start(bf16[48,896]{1,0:T(8,128)(2,1)S(1)} %get-tuple-element.37), channel_id=1, source_target_pairs={{0,8},{1,9},{2,10},{3,11},{4,12},{5,13},{6,14},{7,15},{8,0},{9,1},... | collective-permute-start | bytes 258056 | tf_op jit(solution)/shard_map/ppermute | solution.py:153
  15.8 9.1 %collective-permute-start.3 = (bf16[48,896]{1,0:T(8,128)(2,1)S(1)}, bf16[48,896]{1,0:T(8,128)(2,1)S(1)}, u32[]{:S(2)}, u32[]{:S(2)}) collective-permute-start(bf16[48,896]{1,0:T(8,128)(2,1)S(1)} %get-tuple-element.34), channel_id=1, source_target_pairs={{0,12},{1,13},{2,14},{3,15},{4,8},{5,9},{6,10},{7,11},{8,4},{9,5},... | collective-permute-start | bytes 258056 | tf_op jit(solution)/shard_map/ppermute | solution.py:153
  15.9 9.7 %collective-permute-start = (bf16[48,896]{1,0:T(8,128)(2,1)S(1)}, bf16[48,896]{1,0:T(8,128)(2,1)S(1)}, u32[]{:S(2)}, u32[]{:S(2)}) collective-permute-start(bf16[48,896]{1,0:T(8,128)(2,1)S(1)} %get-tuple-element.35), channel_id=1, source_target_pairs={{0,4},{1,5},{2,6},{3,7},{4,0},{5,1},{6,2},{7,3},{8,12},{9,13},{10,... | collective-permute-start | bytes 258056 | tf_op jit(solution)/shard_map/ppermute | solution.py:153
  19.8 7.4 %collective-permute-start.10 = (bf16[2,48,256]{2,1,0:T(8,128)(2,1)S(1)}, bf16[2,48,256]{2,1,0:T(8,128)(2,1)S(1)}, u32[]{:S(2)}, u32[]{:S(2)}) collective-permute-start(bf16[2,48,256]{2,1,0:T(8,128)(2,1)S(1)} %get-tuple-element.49), channel_id=1, source_target_pairs={{0,4},{1,5},{2,6},{3,7},{4,0},{5,1},{6,2},{7,3},{8,12},{9,13},{10,... | collective-permute-start | bytes 147464 | tf_op jit(solution)/shard_map/ppermute | solution.py:153
  25.0 13.4 %collective-permute-start.7 = (bf16[96,896]{1,0:T(8,128)(2,1)S(1)}, bf16[96,896]{1,0:T(8,128)(2,1)S(1)}, u32[]{:S(2)}, u32[]{:S(2)}) collective-permute-start(bf16[96,896]{1,0:T(8,128)(2,1)S(1)} %constant_dynamic-update-slice_fusion.refs_2_), channel_id=1, source_target_pairs={{0,2},{1,3},{2,0},{3,1},{4,6},{5,7},{6,4},{7,5},{8,10},{9,11},{10,... | collective-permute-start | bytes 516104 | tf_op jit(solution)/shard_map/ppermute | solution.py:153
  25.6 13.2 %collective-permute-start.5 = (bf16[96,896]{1,0:T(8,128)(2,1)S(1)}, bf16[96,896]{1,0:T(8,128)(2,1)S(1)}, u32[]{:S(2)}, u32[]{:S(2)}) collective-permute-start(bf16[96,896]{1,0:T(8,128)(2,1)S(1)} %pad_maximum_fusion.2.refs_0_), channel_id=1, source_target_pairs={{0,2},{1,3},{2,0},{3,1},{4,6},{5,7},{6,4},{7,5},{8,10},{9,11},{10,... | collective-permute-start | bytes 516104 | tf_op jit(solution)/shard_map/ppermute | solution.py:153
  27.2 10.5 %collective-permute-start.13 = (bf16[2,2,48,256]{3,2,1,0:T(8,128)(2,1)S(1)}, bf16[2,2,48,256]{3,2,1,0:T(8,128)(2,1)S(1)}, u32[]{:S(2)}, u32[]{:S(2)}) collective-permute-start(bf16[2,2,48,256]{3,2,1,0:T(8,128)(2,1)S(1)} %pad_maximum_fusion.3.refs_8_), channel_id=1, source_target_pairs={{0,2},{1,3},{2,0},{3,1},{4,6},{5,7},{6,4},{7,5},{8,10},{9,11},{10,... | collective-permute-start | bytes 294920 | tf_op jit(solution)/shard_map/ppermute | solution.py:153
  29.0 9.9 %collective-permute-start.4 = (bf16[96,896]{1,0:T(8,128)(2,1)S(1)}, bf16[96,896]{1,0:T(8,128)(2,1)S(1)}, u32[]{:S(2)}, u32[]{:S(2)}) collective-permute-start(bf16[96,896]{1,0:T(8,128)(2,1)S(1)} %constant_dynamic-update-slice_fusion.refs_2_), channel_id=1, source_target_pairs={{0,1},{1,0},{2,3},{3,2},{4,5},{5,4},{6,7},{7,6},{8,9},{9,8},{10,11... | collective-permute-start | bytes 516104 | tf_op jit(solution)/shard_map/ppermute | solution.py:153
  39.6 13.2 %collective-permute-start.18 = (f32[16,48]{1,0:T(8,128)S(1)}, f32[16,48]{1,0:T(8,128)S(1)}, u32[]{:S(2)}, u32[]{:S(2)}) collective-permute-start(f32[16,48]{1,0:T(8,128)S(1)} %pad_maximum_fusion.8.pairs.refs_4_), channel_id=1, source_target_pairs={{0,1},{1,0},{2,3},{3,2},{4,5},{5,4},{6,7},{7,6},{8,9},{9,8},{10,11... | collective-permute-start | bytes 9224 | tf_op jit(solution)/shard_map/ppermute | solution.py:153
  51.0 5.9 %collective-permute-start.17 = (bf16[2,48,256]{2,1,0:T(8,128)(2,1)S(1)}, bf16[2,48,256]{2,1,0:T(8,128)(2,1)S(1)}, u32[]{:S(2)}, u32[]{:S(2)}) collective-permute-start(bf16[2,48,256]{2,1,0:T(8,128)(2,1)S(1)} %get-tuple-element.22), channel_id=1, source_target_pairs={{0,12},{1,13},{2,14},{3,15},{4,8},{5,9},{6,10},{7,11},{8,4},{9,5},... | collective-permute-start | bytes 147464 | tf_op jit(solution)/shard_map/ppermute | solution.py:153
  60.6 8.9 %collective-permute-start.20 = (bf16[32,896]{1,0:T(8,128)(2,1)S(1)}, bf16[32,896]{1,0:T(8,128)(2,1)S(1)}, u32[]{:S(2)}, u32[]{:S(2)}) collective-permute-start(bf16[32,896]{1,0:T(8,128)(2,1)S(1)} %get-tuple-element.33), channel_id=1, source_target_pairs={{0,4},{1,5},{2,6},{3,7},{4,0},{5,1},{6,2},{7,3},{8,12},{9,13},{10,... | collective-permute-start | bytes 172040 | tf_op jit(solution)/shard_map/ppermute | solution.py:153
  60.6 8.9 %collective-permute-start.21 = (bf16[32,896]{1,0:T(8,128)(2,1)S(1)}, bf16[32,896]{1,0:T(8,128)(2,1)S(1)}, u32[]{:S(2)}, u32[]{:S(2)}) collective-permute-start(bf16[32,896]{1,0:T(8,128)(2,1)S(1)} %get-tuple-element.32), channel_id=1, source_target_pairs={{0,8},{1,9},{2,10},{3,11},{4,12},{5,13},{6,14},{7,15},{8,0},{9,1},... | collective-permute-start | bytes 172040 | tf_op jit(solution)/shard_map/ppermute | solution.py:153
  62.8 6.7 %collective-permute-start.22 = (bf16[32,896]{1,0:T(8,128)(2,1)S(1)}, bf16[32,896]{1,0:T(8,128)(2,1)S(1)}, u32[]{:S(2)}, u32[]{:S(2)}) collective-permute-start(bf16[32,896]{1,0:T(8,128)(2,1)S(1)} %get-tuple-element.31), channel_id=1, source_target_pairs={{0,12},{1,13},{2,14},{3,15},{4,8},{5,9},{6,10},{7,11},{8,4},{9,5},... | collective-permute-start | bytes 172040 | tf_op jit(solution)/shard_map/ppermute | solution.py:153
  67.4 10.7 %collective-permute-start.23 = (bf16[4,32,1280]{2,1,0:T(8,128)(2,1)S(1)}, bf16[4,32,1280]{2,1,0:T(8,128)(2,1)S(1)}, u32[]{:S(2)}, u32[]{:S(2)}) collective-permute-start(bf16[4,32,1280]{2,1,0:T(8,128)(2,1)S(1)} %bitcast.87), channel_id=1, source_target_pairs={{0,2},{1,3},{2,0},{3,1},{4,6},{5,7},{6,4},{7,5},{8,10},{9,11},{10,... | collective-permute-start | bytes 983048 | tf_op jit(solution)/shard_map/ppermute | solution.py:153
  68.7 14.0 %collective-permute-start.27 = (bf16[4,32,1280]{2,1,0:T(8,128)(2,1)S(1)}, bf16[4,32,1280]{2,1,0:T(8,128)(2,1)S(1)}, u32[]{:S(2)}, u32[]{:S(2)}) collective-permute-start(bf16[4,32,1280]{2,1,0:T(8,128)(2,1)S(1)} %bitcast.86), channel_id=1, source_target_pairs={{0,2},{1,3},{2,0},{3,1},{4,6},{5,7},{6,4},{7,5},{8,10},{9,11},{10,... | collective-permute-start | bytes 983048 | tf_op jit(solution)/shard_map/ppermute | solution.py:153
  78.2 7.1 %collective-permute-start.24 = (bf16[32,1280]{1,0:T(8,128)(2,1)S(1)}, bf16[32,1280]{1,0:T(8,128)(2,1)S(1)}, u32[]{:S(2)}, u32[]{:S(2)}) collective-permute-start(bf16[32,1280]{1,0:T(8,128)(2,1)S(1)} %get-tuple-element.38), channel_id=1, source_target_pairs={{0,4},{1,5},{2,6},{3,7},{4,0},{5,1},{6,2},{7,3},{8,12},{9,13},{10,... | collective-permute-start | bytes 245768 | tf_op jit(solution)/shard_map/ppermute | solution.py:153
  78.3 10.2 %collective-permute-start.25 = (bf16[32,1280]{1,0:T(8,128)(2,1)S(1)}, bf16[32,1280]{1,0:T(8,128)(2,1)S(1)}, u32[]{:S(2)}, u32[]{:S(2)}) collective-permute-start(bf16[32,1280]{1,0:T(8,128)(2,1)S(1)} %get-tuple-element.40), channel_id=1, source_target_pairs={{0,8},{1,9},{2,10},{3,11},{4,12},{5,13},{6,14},{7,15},{8,0},{9,1},... | collective-permute-start | bytes 245768 | tf_op jit(solution)/shard_map/ppermute | solution.py:153
  80.5 8.0 %collective-permute-start.26 = (bf16[32,1280]{1,0:T(8,128)(2,1)S(1)}, bf16[32,1280]{1,0:T(8,128)(2,1)S(1)}, u32[]{:S(2)}, u32[]{:S(2)}) collective-permute-start(bf16[32,1280]{1,0:T(8,128)(2,1)S(1)} %get-tuple-element.39), channel_id=1, source_target_pairs={{0,12},{1,13},{2,14},{3,15},{4,8},{5,9},{6,10},{7,11},{8,4},{9,5},... | collective-permute-start | bytes 245768 | tf_op jit(solution)/shard_map/ppermute | solution.py:153
  82.8 6.3 %collective-permute-start.28 = (bf16[32,1280]{1,0:T(8,128)(2,1)S(1)}, bf16[32,1280]{1,0:T(8,128)(2,1)S(1)}, u32[]{:S(2)}, u32[]{:S(2)}) collective-permute-start(bf16[32,1280]{1,0:T(8,128)(2,1)S(1)} %get-tuple-element.41), channel_id=1, source_target_pairs={{0,4},{1,5},{2,6},{3,7},{4,0},{5,1},{6,2},{7,3},{8,12},{9,13},{10,... | collective-permute-start | bytes 245768 | tf_op jit(solution)/shard_map/ppermute | solution.py:153
  82.9 9.8 %collective-permute-start.29 = (bf16[32,1280]{1,0:T(8,128)(2,1)S(1)}, bf16[32,1280]{1,0:T(8,128)(2,1)S(1)}, u32[]{:S(2)}, u32[]{:S(2)}) collective-permute-start(bf16[32,1280]{1,0:T(8,128)(2,1)S(1)} %get-tuple-element.43), channel_id=1, source_target_pairs={{0,8},{1,9},{2,10},{3,11},{4,12},{5,13},{6,14},{7,15},{8,0},{9,1},... | collective-permute-start | bytes 245768 | tf_op jit(solution)/shard_map/ppermute | solution.py:153
  85.3 7.3 %collective-permute-start.30 = (bf16[32,1280]{1,0:T(8,128)(2,1)S(1)}, bf16[32,1280]{1,0:T(8,128)(2,1)S(1)}, u32[]{:S(2)}, u32[]{:S(2)}) collective-permute-start(bf16[32,1280]{1,0:T(8,128)(2,1)S(1)} %get-tuple-element.42), channel_id=1, source_target_pairs={{0,12},{1,13},{2,14},{3,15},{4,8},{5,9},{6,10},{7,11},{8,4},{9,5},... | collective-permute-start | bytes 245768 | tf_op jit(solution)/shard_map/ppermute | solution.py:153
  (19 other events, 90.8 us)

commit v6 on v5

--- a/solution.py
+++ b/solution.py
@@ -15,6 +15,7 @@
 LIMIT = 24 * 1024 * 1024
 VMEM = pl.BlockSpec(memory_space=pltpu.VMEM)
 SMEM = pl.BlockSpec(memory_space=pltpu.SMEM)
+ANY = pl.BlockSpec(memory_space=pl.ANY)
 BF16 = jnp.bfloat16
 F32 = jnp.float32
 
@@ -28,12 +29,13 @@
     return lax.broadcasted_iota(jnp.int32, shape, dim)
 
 
-def call(body, shapes, flops, size, *args, spaces=None):
+def call(body, shapes, flops, size, spaces, scratch, *args):
     return pl.pallas_call(
         body,
         out_shape=shapes,
-        in_specs=spaces or [VMEM] * len(args),
-        out_specs=jax.tree.map(lambda _: VMEM, shapes),
+        in_specs=spaces,
+        out_specs=[VMEM] * len(shapes),
+        scratch_shapes=scratch,
         compiler_params=pltpu.CompilerParams(vmem_limit_bytes=LIMIT),
         cost_estimate=pl.CostEstimate(flops=flops, bytes_accessed=size, transcendentals=0),
     )(*args)
@@ -55,51 +57,77 @@
     return names, weights
 
 
-def y_kernel(groups, core, cot, sketch, pairs, *outs):
+def load(pairs, sems):
+    copies = [pltpu.make_async_copy(src, dst, sems.at[i]) for i, (src, dst) in enumerate(pairs)]
+    for copy in copies:
+        copy.start()
+    return copies
+
+
+def y_kernel(groups, core, cot_at, sketch_at, ids_at, probs_at, *refs):
+    outs, pairs, (cot, sketch, ids, probs, sems) = refs[:groups], refs[groups], refs[groups + 1 :]
     rows = cot.shape[0]
     tok = pairs.shape[1]
     top = rows // tok
     rank = sketch.shape[0]
     lanes = outs[0].shape[1]
+    parts = 4
+    piece = rows // parts
+    sources = [(ids_at, ids), (probs_at, probs), (sketch_at, sketch)]
+    for i in range(parts):
+        cut = pl.ds(i * piece, piece)
+        sources.append((cot_at.at[cut], cot.at[cut]))
+    copies = load(sources, sems)
+    copies[0].wait()
+    copies[1].wait()
+    pairs[:top] = ids[...].astype(F32)
+    pairs[top:] = probs[...]
+    names, weights = pair_columns(pairs[:top], pairs[top:])
+    copies[2].wait()
     high = sketch[...].astype(BF16)
     low = (sketch[...] - high.astype(F32)).astype(BF16)
-    pair = dot(cot[...], high, 1, 1) + dot(cot[...], low, 1, 1)
-    names, weights = pair_columns(pairs[:top], pairs[top:])
-    pair = (pair * weights).astype(BF16)
     lane = iota((rank, lanes), 1)
-    tiled = dot(pair, (iota((rank, lanes), 0) == lane % rank).astype(BF16), 1, 0)
+    tile = (iota((rank, lanes), 0) == lane % rank).astype(BF16)
     block = iota((1, lanes), 1) // rank * groups
-    for i, out in enumerate(outs):
-        name = block + (core[0] ^ i) if groups == 2 else block
-        y = jnp.where(names == name.astype(F32), tiled, 0.0)
-        out[...] = jnp.sum(y.reshape(tok, top, lanes), axis=1).astype(BF16)
+    for i in range(parts):
+        copies[3 + i].wait()
+        here = slice(i * piece, (i + 1) * piece)
+        there = slice(i * piece // top, (i + 1) * piece // top)
+        pair = dot(cot[here], high, 1, 1) + dot(cot[here], low, 1, 1)
+        tiled = dot((pair * weights[here]).astype(BF16), tile, 1, 0)
+        for j, out in enumerate(outs):
+            name = block + (core[0] ^ j) if groups == 2 else block
+            y = jnp.where(names[here] == name.astype(F32), tiled, 0.0)
+            out[there] = jnp.sum(y.reshape(piece // top, top, lanes), axis=1).astype(BF16)
 
 
 def z_kernel(n, *refs):
-    xs, ys, columns, zs = refs[: 2 * n], refs[2 * n : 3 * n], refs[3 * n], refs[3 * n + 1 :]
-    total = 0.0
-    for b in range(n):
+    xs, ys, columns, zs = refs[: 2 * n], refs[2 * n : -8], refs[-8], refs[-7:-3]
+    x, y, sems = refs[-3:]
+    rows = xs[0].shape[0]
+    tok = zs[0].shape[1]
+    each = rows // tok
+    sources = [(x_at, x.at[pl.ds(i * rows, rows)]) for i, x_at in enumerate(xs)]
+    for b, y_at in enumerate(ys):
+        for i in range(SLICES // each):
+            for core in range(2):
+                block = 2 * (b * (SLICES // each) + i) + core
+                sources.append((y_at.at[pl.ds(i * each, each), core], y.at[block]))
+    for copy in load(sources, sems):
+        copy.wait()
+    total = dot(y[...].reshape(x.shape[0], -1), x[...], 0, 0).astype(BF16)
+    columns[...] = total
+    part = dot(x[: 2 * SLICES * tok], total, 1, 1).astype(BF16)
+    for j in range(SLICES):
         for core in range(2):
-            y = ys[b][:, core].reshape(-1, columns.shape[0])
-            total = total + dot(y, xs[2 * b + core][...], 0, 0)
-    total = total.astype(BF16)
-    columns[...] = total
-    tok = zs[0].shape[1]
-    each = xs[0].shape[0] // tok
-    for core in range(2):
-        for b in range(len(zs) // each):
-            part = dot(xs[2 * b + core][...], total, 1, 1).astype(BF16)
-            for i in range(each):
-                zs[b * each + i][core] = part[i * tok : (i + 1) * tok]
-
-
-def spread_kernel(groups, at, *refs):
-    zs, pairs, outs = refs[:SLICES], refs[SLICES : SLICES + 2], refs[SLICES + 2 : -1]
-    work = refs[-1]
+            start = ((j // each * 2 + core) * each + j % each) * tok
+            zs[j][core] = part[start : start + tok]
+
+
+def spread_rows(groups, at, zs, pairs, work, spread, low, rank):
     _, tok, lanes = zs[0].shape
     top = pairs[0].shape[0] // 2
     rows = tok * top
-    rank = outs[0].shape[0] // SLICES
     block = iota((1, lanes), 1) // rank * groups + (at[0] if groups == 2 else 0)
     for core in range(2):
         z = zs[0][core].astype(F32)
@@ -109,21 +137,43 @@
         z = jnp.broadcast_to(z[:, None], (tok, top, lanes)).reshape(rows, lanes)
         z = jnp.where(names == block.astype(F32), z * weights, 0.0).astype(BF16)
         work[:, core * rows : (core + 1) * rows] = z.T
+    for r in range(low):
+        for j in range(SLICES):
+            start = pl.multiple_of((j * low + (at[1] ^ r)) * rank, rank)
+            spread[(r * SLICES + j) * rank : (r * SLICES + j + 1) * rank] = work[
+                pl.ds(start, rank)
+            ]
+
+
+def cot_copies(start, mine, other, cot, sems):
+    rows, size = mine.shape[0], cot.shape[1]
+    cut = pl.ds(start, size)
+    sources = [(mine.at[:, cut], cot.at[pl.ds(0, rows)])]
+    return load(sources + [(other.at[:, cut], cot.at[pl.ds(rows, rows)])], sems)
+
+
+def terms(spread, cot, outs):
+    size = outs[0].shape[0]
+    part = dot(spread[...], cot[...], 1, 0).astype(BF16)
     for r, out in enumerate(outs):
-        for j in range(SLICES):
-            start = pl.multiple_of((j * len(outs) + (at[1] ^ r)) * rank, rank)
-            out[j * rank : (j + 1) * rank] = work[pl.ds(start, rank)]
-
-
-def part_kernel(spread, mine, other, *outs):
-    rows = mine.shape[0]
-    start = 0
-    for out in outs:
-        size = out.shape[1]
-        part = dot(spread[:, :rows], mine[:, start : start + size], 1, 0)
-        part = part + dot(spread[:, rows:], other[:, start : start + size], 1, 0)
-        out[...] = part.astype(BF16)
-        start += size
+        out[...] = part[r * size : (r + 1) * size]
+
+
+def first_kernel(groups, at, z0, z1, z2, z3, own, pair, mine, other, spread, *refs):
+    outs, (work, cot, sems) = refs[:-3], refs[-3:]
+    copies = cot_copies(0, mine, other, cot, sems)
+    rank = outs[0].shape[0] // SLICES
+    spread_rows(groups, at, (z0, z1, z2, z3), (own, pair), work, spread, len(outs), rank)
+    for copy in copies:
+        copy.wait()
+    terms(spread, cot, outs)
+
+
+def next_kernel(start, spread, mine, other, *refs):
+    outs, (cot, sems) = refs[:-2], refs[-2:]
+    for copy in cot_copies(start, mine, other, cot, sems):
+        copy.wait()
+    terms(spread, cot, outs)
 
 
 def shards(tokens, expert_ids, route_probs, cotangents, sketch):
@@ -164,23 +214,30 @@
         other = exchange(lax.dynamic_slice_in_dim(cot, (1 - half) * part, part, axis=1), 1)
     else:
         mine, other = cot, exchange(cot, 1)
-    pairs = jnp.concatenate([expert_ids.T.astype(F32), route_probs.T], axis=0)
-    pairs = [pairs, exchange(pairs, 1)]
-
-    y = call(
+
+    *y, pairs = call(
         functools.partial(y_kernel, groups),
-        [shape((tok, lanes), BF16)] * groups,
+        [shape((tok, lanes), BF16)] * groups + [shape((2 * top, tok), F32)],
         4 * rows * hidden * rank,
         2 * rows * hidden,
+        [SMEM] + [ANY] * 4,
+        [
+            pltpu.VMEM((rows, hidden), BF16),
+            pltpu.VMEM((rank, hidden), F32),
+            pltpu.VMEM((top, tok), jnp.int32),
+            pltpu.VMEM((top, tok), F32),
+            pltpu.SemaphoreType.DMA((7,)),
+        ],
         core.reshape(1),
         cot,
         sketch.T,
-        pairs[0],
-        spaces=[SMEM] + [VMEM] * 3,
+        expert_ids.T,
+        route_probs.T,
     )
-    y = jnp.stack([y[0], exchange(y[-1], 1)])
-    ys = [y] + [exchange(y, j * line) for j in range(1, SLICES)]
-    ys = [jnp.stack(ys[i : i + 2]) for i in range(0, SLICES, 2)]
+    send, xs = lax.optimization_barrier((y[-1], xs))
+    pairs = [pairs, exchange(pairs, 1)]
+    y = jnp.stack([y[0], exchange(send, 1)])
+    ys = [jnp.stack([y] + [exchange(y, j * line) for j in range(1, SLICES)])]
     step = 2
     while step < line:
         ys = ys + [exchange(b, step) for b in ys]
@@ -190,10 +247,16 @@
 
     if n_dp == 1:
         columns, *zs = call(
-            functools.partial(z_kernel, len(ys)),
+            functools.partial(z_kernel, len(xs) // 2),
             [shape((lanes, share), BF16)] + [shape((2, tok, lanes), BF16)] * SLICES,
             2 * count * tok * lanes * share * 3 // 2,
             2 * count * tok * (lanes + share),
+            [ANY] * (len(xs) + len(ys)),
+            [
+                pltpu.VMEM((count * tok, share), BF16),
+                pltpu.VMEM((len(xs), 2, tok, lanes), BF16),
+                pltpu.SemaphoreType.DMA((2 * len(xs),)),
+            ],
             *xs,
             *ys,
         )
@@ -209,33 +272,41 @@
         ]
     zs = zs[:1] + [exchange(zs[j], j * line) for j in range(1, SLICES)]
 
-    spread = pl.pallas_call(
-        functools.partial(spread_kernel, groups),
-        out_shape=[shape((SLICES * rank, 2 * rows), BF16)] * low,
-        in_specs=[SMEM] + [VMEM] * (SLICES + 2),
-        out_specs=[VMEM] * low,
-        scratch_shapes=[pltpu.VMEM((lanes, 2 * rows), BF16)],
-        compiler_params=pltpu.CompilerParams(vmem_limit_bytes=LIMIT),
-        cost_estimate=pl.CostEstimate(
-            flops=0, bytes_accessed=8 * rows * lanes, transcendentals=0
-        ),
-    )(jnp.stack([core, lower]), *zs, *pairs)
     piece = part // CHUNKS
-    terms = [
-        call(
-            part_kernel,
-            [shape((SLICES * rank, piece), BF16)] * CHUNKS,
-            4 * rows * SLICES * rank * part,
-            4 * rows * part,
-            s,
-            mine,
-            other,
+    flops = 4 * rows * SLICES * rank * piece
+    outs = [shape((SLICES * rank, piece), BF16)] * low
+    work = [pltpu.VMEM((2 * rows, piece), BF16), pltpu.SemaphoreType.DMA((2,))]
+    spread, *blocks = call(
+        functools.partial(first_kernel, groups),
+        [shape((lanes, 2 * rows), BF16)] + outs,
+        flops,
+        4 * rows * piece,
+        [SMEM] + [VMEM] * (SLICES + 2) + [ANY] * 2,
+        [pltpu.VMEM((lanes, 2 * rows), BF16)] + work,
+        jnp.stack([core, lower]),
+        *zs,
+        *pairs,
+        mine,
+        other,
+    )
+    chunks = [blocks]
+    for chunk in range(1, CHUNKS):
+        chunks.append(
+            call(
+                functools.partial(next_kernel, chunk * piece),
+                outs,
+                flops,
+                4 * rows * piece,
+                [VMEM] + [ANY] * 2,
+                work,
+                spread,
+                mine,
+                other,
+            )
         )
-        for s in spread[::-1]
-    ][::-1]
     sums = []
-    for chunk in range(CHUNKS):
-        blocks = [term[chunk].reshape(SLICES, rank, piece) for term in terms]
+    for chunk in chunks:
+        blocks = [term.reshape(SLICES, rank, piece) for term in chunk]
         step = 2
         while len(blocks) > 1:
             blocks = [
@@ -255,15 +326,17 @@
             total = total + other.astype(F32)
         totals.append(total)
 
-    columns, _ = lax.optimization_barrier((columns, terms[0]))
+    columns, _ = lax.optimization_barrier((columns, chunks[-1][0]))
     parts = columns.reshape(SLICES, n_expert // SLICES // groups, rank, share)
     parts = lax.dynamic_index_in_dim(parts, own % (n_expert // SLICES) // groups, 1, False)
     parts = [lax.dynamic_index_in_dim(parts, place ^ j, 0, False) for j in range(SLICES)]
     parts = jnp.stack(parts[:1] + [exchange(parts[j], j * line) for j in range(1, SLICES)])
     parts = [lax.dynamic_index_in_dim(parts, place ^ j, 0, False) for j in range(SLICES)]
     range_rows = jnp.concatenate(parts, axis=1).astype(F32)
+    range_rows, _ = lax.optimization_barrier((range_rows, sums[0]))
     gram = lax.dot_general(range_rows, range_rows, (((1,), (1,)), ((), ())), precision=HIGH)
     lower = jnp.linalg.cholesky(gram)
+    lower, _ = lax.optimization_barrier((lower, sums[-1]))
     inverse = jax.scipy.linalg.solve_triangular(lower, jnp.eye(rank, dtype=F32), lower=True)
     kept = lax.dynamic_slice_in_dim(range_rows, half * (width // n_dp), width // n_dp, axis=1)
     basis = jnp.dot(inverse * math.sqrt(width), kept, precision=HIGH)

time: 94.2 us -> 93.9 us (level)
  Pallas kernels: 10.8 us -> 13.2 us
  other arithmetic: 9.13 us -> 7.82 us
  waiting for transfers between devices: 27.7 us -> 26.6 us
    pallas_call x5 -> x4, Pallas kernels: 10.8 us -> 13.2 us  [call(): pl.pallas_call(body, out_shape=shapes, in_specs=spaces, out_specs=[VMEM]...]
    unnamed x25 -> x18, local copies, waits for them, and re-layouts: 8.84 us -> 7.07 us
    ppermute x31 -> x30, waiting for transfers between devices: 27.7 us -> 26.6 us  [exchange(): return lax.ppermute(block, AXES, [(i, i ^ step) for i in range(count)])]
    dynamic_slice x1, local copies, waits for them, and re-layouts: 0.03 us -> 1.04 us  [shards(): lax.dynamic_slice_in_dim(tokens, (place ^ j) * share, share, axis=1)]
    ppermute x31 -> x30, starting transfers between devices: 34.1 us -> 34.1 us  [exchange(): return lax.ppermute(block, AXES, [(i, i ^ step) for i in range(count)])]
  transfers between devices with their start and end apart: 31 -> 30, of which waited for: 13 -> 13; matrix products, arithmetic and copies ran while one was open for 11% -> 8% of each run, Pallas kernels for 9% -> 9%
where the time goes in v6:
time: 93.9 us; the launch traced here: 93.5 us
  starting transfers between devices  34.1 us (36%)
  waiting for transfers between devices  26.6 us (28%)
  Pallas kernels  13.2 us (14%)
  local copies, waits for them, and re-layouts  8.31 us (9%)
  other arithmetic  7.82 us (8%)
  matrix products  2.57 us (3%)
    ppermute x30, starting transfers between devices, exchange(): return lax.ppermute(block, AXES, [(i, i ^ step) for i in range(count)])  34.1 us
    ppermute x30, waiting for transfers between devices, exchange(): return lax.ppermute(block, AXES, [(i, i ^ step) for i in range(count)])  26.6 us
    pallas_call x4, Pallas kernels, call(): pl.pallas_call(body, out_shape=shapes, in_specs=spaces, out_specs=[VMEM]...  13.2 us
    unnamed x18, local copies, waits for them, and re-layouts  7.07 us
    another operation x3, other arithmetic, shards(): lower = jnp.linalg.cholesky(gram)  3.6 us
    another operation x2, other arithmetic, shards(): jax.scipy.linalg.solve_triangular(lower, jnp.eye(rank, dtype=F32), lower=...  2.44 us
  transfers between devices with their start and end apart: 30, of which 13 were waited for; matrix products, arithmetic and copies ran while one was open for 8% of the time, Pallas kernels for 9%

profile of v6, /device:TPU:0, one launch (start us, length us, event | category | flops | bytes accessed | tf_op | source)
XLA Modules:
  0.0 93.5 jit_solution(10208353657514543127)
XLA Ops:
  2.2 2.7 %collective-permute-start = (bf16[48,896]{1,0:T(8,128)(2,1)S(1)}, bf16[48,896]{1,0:T(8,128)(2,1)S(1)}, u32[]{:S(2)}, u32[]{:S(2)}) collective-permute-start(bf16[48,896]{1,0:T(8,128)(2,1)S(1)} %get-tuple-element.45), channel_id=1, source_target_pairs={{0,4},{1,5},{2,6},{3,7},{4,0},{5,1},{6,2},{7,3},{8,12},{9,13},{10,... | collective-permute-start | bytes 258056 | tf_op jit(solution)/shard_map/ppermute | solution.py:203
  4.9 2.5 %collective-permute-start.2 = (bf16[48,896]{1,0:T(8,128)(2,1)S(1)}, bf16[48,896]{1,0:T(8,128)(2,1)S(1)}, u32[]{:S(2)}, u32[]{:S(2)}) collective-permute-start(bf16[48,896]{1,0:T(8,128)(2,1)S(1)} %get-tuple-element.47), channel_id=1, source_target_pairs={{0,12},{1,13},{2,14},{3,15},{4,8},{5,9},{6,10},{7,11},{8,4},{9,5},... | collective-permute-start | bytes 258056 | tf_op jit(solution)/shard_map/ppermute | solution.py:203
  7.5 1.5 %copy-done = bf16[48,8,2560]{2,1,0:T(8,128)(2,1)S(1)} copy-done((bf16[48,8,2560]{2,1,0:T(8,128)(2,1)S(1)}, bf16[48,8,2560]{2,1,0:T(8,128)(2,1)}, u32[]{:S(2)}) %copy-start) | copy-done | bytes 1966104
  11.4 5.0 %shard_map.68 = (bf16[48,256]{1,0:T(8,128)(2,1)S(1)}, bf16[48,256]{1,0:T(8,128)(2,1)S(1)}, f32[16,48]{1,0:T(8,128)S(1)}) custom-call(s32[1]{0:T(128)} %bitcast.core, bf16[384,2560]{1,0:T(8,128)(2,1)S(1)} %bitcast.80, f32[32,2560]{1,0:T(8,128)S(1)} %bitcast.83, s32[8,48]{1,0:T(8,128)S(1)} %bitcast.88, f32[8,48]{1,0:T(8,128)S(1)} %bitcast.89), custom_call_target="tpu_custom_call" | custom-call | flops 125829120 | bytes 1966080 | tf_op jit(solution)/shard_map/pallas_call | solution.py:33
  17.7 3.0 %collective-permute-start.12 = (bf16[2,48,256]{2,1,0:T(8,128)(2,1)S(1)}, bf16[2,48,256]{2,1,0:T(8,128)(2,1)S(1)}, u32[]{:S(2)}, u32[]{:S(2)}) collective-permute-start(bf16[2,48,256]{2,1,0:T(8,128)(2,1)S(1)} %get-tuple-element.59), channel_id=1, source_target_pairs={{0,12},{1,13},{2,14},{3,15},{4,8},{5,9},{6,10},{7,11},{8,4},{9,5},... | collective-permute-start | bytes 147464 | tf_op jit(solution)/shard_map/ppermute | solution.py:203
  22.2 1.6 %collective-permute-done.12 = bf16[2,48,256]{2,1,0:T(8,128)(2,1)S(1)} collective-permute-done((bf16[2,48,256]{2,1,0:T(8,128)(2,1)S(1)}, bf16[2,48,256]{2,1,0:T(8,128)(2,1)S(1)}, u32[]{:S(2)}, u32[]{:S(2)}) %collective-permute-start.12) | collective-permute-done | bytes 49184 | tf_op jit(solution)/shard_map/ppermute | solution.py:203
  23.8 1.4 %collective-permute-start.5 = (bf16[96,896]{1,0:T(8,128)(2,1)S(1)}, bf16[96,896]{1,0:T(8,128)(2,1)S(1)}, u32[]{:S(2)}, u32[]{:S(2)}) collective-permute-start(bf16[96,896]{1,0:T(8,128)(2,1)S(1)} %pad_maximum_fusion.2.refs_0_), channel_id=1, source_target_pairs={{0,2},{1,3},{2,0},{3,1},{4,6},{5,7},{6,4},{7,5},{8,10},{9,11},{10,... | collective-permute-start | bytes 516104 | tf_op jit(solution)/shard_map/ppermute | solution.py:203
  26.1 1.5 %collective-permute-start.7 = (bf16[96,896]{1,0:T(8,128)(2,1)S(1)}, bf16[96,896]{1,0:T(8,128)(2,1)S(1)}, u32[]{:S(2)}, u32[]{:S(2)}) collective-permute-start(bf16[96,896]{1,0:T(8,128)(2,1)S(1)} %pad_maximum_fusion.3.refs_2_), channel_id=1, source_target_pairs={{0,2},{1,3},{2,0},{3,1},{4,6},{5,7},{6,4},{7,5},{8,10},{9,11},{10,... | collective-permute-start | bytes 516104 | tf_op jit(solution)/shard_map/ppermute | solution.py:203
  28.3 2.7 %collective-permute-done.5.refs_4_ = bf16[96,896]{1,0:T(8,128)(2,1)S(1)} collective-permute-done((bf16[96,896]{1,0:T(8,128)(2,1)S(1)}, bf16[96,896]{1,0:T(8,128)(2,1)S(1)}, u32[]{:S(2)}, u32[]{:S(2)}) %collective-permute-start.5) | collective-permute-done | bytes 172064 | tf_op jit(solution)/shard_map/ppermute | solution.py:203
  31.6 3.0 %collective-permute-done.7.refs_6_ = bf16[96,896]{1,0:T(8,128)(2,1)S(1)} collective-permute-done((bf16[96,896]{1,0:T(8,128)(2,1)S(1)}, bf16[96,896]{1,0:T(8,128)(2,1)S(1)}, u32[]{:S(2)}, u32[]{:S(2)}) %collective-permute-start.7) | collective-permute-done | bytes 172064 | tf_op jit(solution)/shard_map/ppermute | solution.py:203
  39.0 3.1 %shard_map.69 = (bf16[256,896]{1,0:T(8,128)(2,1)S(1)}, bf16[2,48,256]{2,1,0:T(8,128)(2,1)S(1)}, bf16[2,48,256]{2,1,0:T(8,128)(2,1)S(1)}, bf16[2,48,256]{2,1,0:T(8,128)(2,1)S(1)}, bf16[2,48,256]{2,1,0:T(8,128)(2,1)S(1)}) custom-call(bf16[96,896]{1,0:T(8,128)(2,1)S(1)} %pad_maximum_fusion.2.refs_0_, bf16[96,896]{1,0:T(8,128)(2,1)S(1)} %collective-permute-done.3.refs_1_, ...), custom_call_target="tpu_custom_call" | custom-call | flops 528482304 | bytes 1769472 | tf_op jit(solution)/shard_map/pallas_call | solution.py:33
  42.8 3.0 %collective-permute-start.15 = (bf16[2,48,256]{2,1,0:T(8,128)(2,1)S(1)}, bf16[2,48,256]{2,1,0:T(8,128)(2,1)S(1)}, u32[]{:S(2)}, u32[]{:S(2)}) collective-permute-start(bf16[2,48,256]{2,1,0:T(8,128)(2,1)S(1)} %get-tuple-element.29), channel_id=1, source_target_pairs={{0,8},{1,9},{2,10},{3,11},{4,12},{5,13},{6,14},{7,15},{8,0},{9,1},... | collective-permute-start | bytes 147464 | tf_op jit(solution)/shard_map/ppermute | solution.py:203
  46.6 2.1 %collective-permute-done.15.z2 = bf16[2,48,256]{2,1,0:T(8,128)(2,1)S(1)} collective-permute-done((bf16[2,48,256]{2,1,0:T(8,128)(2,1)S(1)}, bf16[2,48,256]{2,1,0:T(8,128)(2,1)S(1)}, u32[]{:S(2)}, u32[]{:S(2)}) %collective-permute-start.15) | collective-permute-done | bytes 49184 | tf_op jit(solution)/shard_map/ppermute | solution.py:203
  48.8 3.0 %collective-permute-done.16.z3 = bf16[2,48,256]{2,1,0:T(8,128)(2,1)S(1)} collective-permute-done((bf16[2,48,256]{2,1,0:T(8,128)(2,1)S(1)}, bf16[2,48,256]{2,1,0:T(8,128)(2,1)S(1)}, u32[]{:S(2)}, u32[]{:S(2)}) %collective-permute-start.16) | collective-permute-done | bytes 49184 | tf_op jit(solution)/shard_map/ppermute | solution.py:203
  51.7 3.1 %shard_map.70 = (bf16[256,768]{1,0:T(8,128)(2,1)S(1)}, bf16[128,1280]{1,0:T(8,128)(2,1)S(1)}, bf16[128,1280]{1,0:T(8,128)(2,1)S(1)}) custom-call(s32[2]{0:T(128)S(1)} %pad_add_fusion.at, bf16[2,48,256]{2,1,0:T(8,128)(2,1)S(1)} %get-tuple-element.27.z0, bf16[2,48,256]{2,1,0:T(8,128)(2,1)S(1)} %collective-permute-done.14.z1, ...), custom_call_target="tpu_custom_call" | custom-call | flops 251658240 | bytes 1966080 | tf_op jit(solution)/shard_map/pallas_call | solution.py:33
  54.9 2.0 %shard_map.71 = (bf16[128,1280]{1,0:T(8,128)(2,1)S(1)}, bf16[128,1280]{1,0:T(8,128)(2,1)S(1)}) custom-call(bf16[256,768]{1,0:T(8,128)(2,1)S(1)} %get-tuple-element.32.spread, bf16[384,2560]{1,0:T(8,128)(2,1)S(1)} %bitcast.82, bf16[384,2560]{1,0:T(8,128)(2,1)} %collective-permute-done.18.other), custom_call_target="tpu_custom_call" | custom-call | flops 251658240 | bytes 1966080 | tf_op jit(solution)/shard_map/pallas_call | solution.py:33
  57.7 3.6 %collective-permute-start.19 = (bf16[32,896]{1,0:T(8,128)(2,1)S(1)}, bf16[32,896]{1,0:T(8,128)(2,1)S(1)}, u32[]{:S(2)}, u32[]{:S(2)}) collective-permute-start(bf16[32,896]{1,0:T(8,128)(2,1)S(1)} %get-tuple-element.43), channel_id=1, source_target_pairs={{0,4},{1,5},{2,6},{3,7},{4,0},{5,1},{6,2},{7,3},{8,12},{9,13},{10,... | collective-permute-start | bytes 172040 | tf_op jit(solution)/shard_map/ppermute | solution.py:203
  61.3 1.5 %collective-permute-start.22 = (bf16[4,32,1280]{2,1,0:T(8,128)(2,1)S(1)}, bf16[4,32,1280]{2,1,0:T(8,128)(2,1)S(1)}, u32[]{:S(2)}, u32[]{:S(2)}) collective-permute-start(bf16[4,32,1280]{2,1,0:T(8,128)(2,1)S(1)} %bitcast.91), channel_id=1, source_target_pairs={{0,2},{1,3},{2,0},{3,1},{4,6},{5,7},{6,4},{7,5},{8,10},{9,11},{10,... | collective-permute-start | bytes 983048 | tf_op jit(solution)/shard_map/ppermute | solution.py:203
  64.1 7.4 %collective-permute-done.22 = bf16[4,32,1280]{2,1,0:T(8,128)(2,1)S(1)} collective-permute-done((bf16[4,32,1280]{2,1,0:T(8,128)(2,1)S(1)}, bf16[4,32,1280]{2,1,0:T(8,128)(2,1)S(1)}, u32[]{:S(2)}, u32[]{:S(2)}) %collective-permute-start.22) | collective-permute-done | bytes 327712 | tf_op jit(solution)/shard_map/ppermute | solution.py:203
  72.2 2.9 %cholesky.17 = f32[32,32]{1,0:T(8,128)S(1)} custom-call(f32[32,32]{1,0:T(8,128)S(1)} %fusion.22), custom_call_target="Cholesky" | custom-call | tf_op jit(solution)/shard_map/jit(cholesky)/cholesky | solution.py:338
  76.7 2.4 %custom-call.7 = f32[1,32,32]{1,2,0:T(8,128)S(1)} custom-call(f32[1,32,32]{2,1,0:T(8,128)S(1)} %select_bitcast_fusion), custom_call_target="InvertDiagBlocksLowerTriangular" | custom-call | tf_op jit(solution)/shard_map/jit(_solve_triangular)/triangular_solve | solution.py:340
  81.1 2.6 %collective-permute-start.27 = (bf16[32,1280]{1,0:T(8,128)(2,1)S(1)}, bf16[32,1280]{1,0:T(8,128)(2,1)S(1)}, u32[]{:S(2)}, u32[]{:S(2)}) collective-permute-start(bf16[32,1280]{1,0:T(8,128)(2,1)S(1)} %get-tuple-element.51), channel_id=1, source_target_pairs={{0,4},{1,5},{2,6},{3,7},{4,0},{5,1},{6,2},{7,3},{8,12},{9,13},{10,... | collective-permute-start | bytes 245768 | tf_op jit(solution)/shard_map/ppermute | solution.py:203
  86.5 2.9 %collective-permute-start.24 = (bf16[32,1280]{1,0:T(8,128)(2,1)S(1)}, bf16[32,1280]{1,0:T(8,128)(2,1)S(1)}, u32[]{:S(2)}, u32[]{:S(2)}) collective-permute-start(bf16[32,1280]{1,0:T(8,128)(2,1)S(1)} %get-tuple-element.48), channel_id=1, source_target_pairs={{0,4},{1,5},{2,6},{3,7},{4,0},{5,1},{6,2},{7,3},{8,12},{9,13},{10,... | collective-permute-start | bytes 245768 | tf_op jit(solution)/shard_map/ppermute | solution.py:203
  90.1 1.6 %collective-permute-done.25 = bf16[32,1280]{1,0:T(8,128)(2,1)S(1)} collective-permute-done((bf16[32,1280]{1,0:T(8,128)(2,1)S(1)}, bf16[32,1280]{1,0:T(8,128)(2,1)S(1)}, u32[]{:S(2)}, u32[]{:S(2)}) %collective-permute-start.25) | collective-permute-done | bytes 81952 | tf_op jit(solution)/shard_map/ppermute | solution.py:203
  (86 shorter events, 26.3 us)
Async XLA Ops:
  0.6 51.1 %collective-permute-start.18 = (bf16[384,2560]{1,0:T(8,128)(2,1)}, bf16[384,2560]{1,0:T(8,128)(2,1)}, u32[]{:S(2)}, u32[]{:S(2)}) collective-permute-start(bf16[384,2560]{1,0:T(8,128)(2,1)} %bitcast.79), channel_id=1, source_target_pairs={{0,1},{1,0},{2,3},{3,2},{4,5},{5,4},{6,7},{7,6},{8,9},{9,8},{10,11... | collective-permute-start | bytes 5898248 | tf_op jit(solution)/shard_map/ppermute | solution.py:203
  2.2 14.2 %collective-permute-start = (bf16[48,896]{1,0:T(8,128)(2,1)S(1)}, bf16[48,896]{1,0:T(8,128)(2,1)S(1)}, u32[]{:S(2)}, u32[]{:S(2)}) collective-permute-start(bf16[48,896]{1,0:T(8,128)(2,1)S(1)} %get-tuple-element.45), channel_id=1, source_target_pairs={{0,4},{1,5},{2,6},{3,7},{4,0},{5,1},{6,2},{7,3},{8,12},{9,13},{10,... | collective-permute-start | bytes 258056 | tf_op jit(solution)/shard_map/ppermute | solution.py:203
  4.9 11.5 %collective-permute-start.2 = (bf16[48,896]{1,0:T(8,128)(2,1)S(1)}, bf16[48,896]{1,0:T(8,128)(2,1)S(1)}, u32[]{:S(2)}, u32[]{:S(2)}) collective-permute-start(bf16[48,896]{1,0:T(8,128)(2,1)S(1)} %get-tuple-element.47), channel_id=1, source_target_pairs={{0,12},{1,13},{2,14},{3,15},{4,8},{5,9},{6,10},{7,11},{8,4},{9,5},... | collective-permute-start | bytes 258056 | tf_op jit(solution)/shard_map/ppermute | solution.py:203
  7.4 9.1 %collective-permute-start.1 = (bf16[48,896]{1,0:T(8,128)(2,1)S(1)}, bf16[48,896]{1,0:T(8,128)(2,1)S(1)}, u32[]{:S(2)}, u32[]{:S(2)}) collective-permute-start(bf16[48,896]{1,0:T(8,128)(2,1)S(1)} %get-tuple-element.44), channel_id=1, source_target_pairs={{0,8},{1,9},{2,10},{3,11},{4,12},{5,13},{6,14},{7,15},{8,0},{9,1},... | collective-permute-start | bytes 258056 | tf_op jit(solution)/shard_map/ppermute | solution.py:203
  17.7 6.1 %collective-permute-start.12 = (bf16[2,48,256]{2,1,0:T(8,128)(2,1)S(1)}, bf16[2,48,256]{2,1,0:T(8,128)(2,1)S(1)}, u32[]{:S(2)}, u32[]{:S(2)}) collective-permute-start(bf16[2,48,256]{2,1,0:T(8,128)(2,1)S(1)} %get-tuple-element.59), channel_id=1, source_target_pairs={{0,12},{1,13},{2,14},{3,15},{4,8},{5,9},{6,10},{7,11},{8,4},{9,5},... | collective-permute-start | bytes 147464 | tf_op jit(solution)/shard_map/ppermute | solution.py:203
  21.1 6.6 %collective-permute-start.10 = (bf16[2,48,256]{2,1,0:T(8,128)(2,1)S(1)}, bf16[2,48,256]{2,1,0:T(8,128)(2,1)S(1)}, u32[]{:S(2)}, u32[]{:S(2)}) collective-permute-start(bf16[2,48,256]{2,1,0:T(8,128)(2,1)S(1)} %get-tuple-element.59), channel_id=1, source_target_pairs={{0,4},{1,5},{2,6},{3,7},{4,0},{5,1},{6,2},{7,3},{8,12},{9,13},{10,... | collective-permute-start | bytes 147464 | tf_op jit(solution)/shard_map/ppermute | solution.py:203
  22.2 6.1 %collective-permute-start.3 = (bf16[96,896]{1,0:T(8,128)(2,1)S(1)}, bf16[96,896]{1,0:T(8,128)(2,1)S(1)}, u32[]{:S(2)}, u32[]{:S(2)}) collective-permute-start(bf16[96,896]{1,0:T(8,128)(2,1)S(1)} %pad_maximum_fusion.2.refs_0_), channel_id=1, source_target_pairs={{0,1},{1,0},{2,3},{3,2},{4,5},{5,4},{6,7},{7,6},{8,9},{9,8},{10,11... | collective-permute-start | bytes 516104 | tf_op jit(solution)/shard_map/ppermute | solution.py:203
  23.8 7.1 %collective-permute-start.5 = (bf16[96,896]{1,0:T(8,128)(2,1)S(1)}, bf16[96,896]{1,0:T(8,128)(2,1)S(1)}, u32[]{:S(2)}, u32[]{:S(2)}) collective-permute-start(bf16[96,896]{1,0:T(8,128)(2,1)S(1)} %pad_maximum_fusion.2.refs_0_), channel_id=1, source_target_pairs={{0,2},{1,3},{2,0},{3,1},{4,6},{5,7},{6,4},{7,5},{8,10},{9,11},{10,... | collective-permute-start | bytes 516104 | tf_op jit(solution)/shard_map/ppermute | solution.py:203
  26.1 8.5 %collective-permute-start.7 = (bf16[96,896]{1,0:T(8,128)(2,1)S(1)}, bf16[96,896]{1,0:T(8,128)(2,1)S(1)}, u32[]{:S(2)}, u32[]{:S(2)}) collective-permute-start(bf16[96,896]{1,0:T(8,128)(2,1)S(1)} %pad_maximum_fusion.3.refs_2_), channel_id=1, source_target_pairs={{0,2},{1,3},{2,0},{3,1},{4,6},{5,7},{6,4},{7,5},{8,10},{9,11},{10,... | collective-permute-start | bytes 516104 | tf_op jit(solution)/shard_map/ppermute | solution.py:203
  27.7 9.5 %collective-permute-start.13 = (bf16[4,2,48,256]{3,2,1,0:T(8,128)(2,1)S(1)}, bf16[4,2,48,256]{3,2,1,0:T(8,128)(2,1)S(1)}, u32[]{:S(2)}, u32[]{:S(2)}) collective-permute-start(bf16[4,2,48,256]{3,2,1,0:T(8,128)(2,1)S(1)} %pad_maximum_fusion.1.refs_8_), channel_id=1, source_target_pairs={{0,2},{1,3},{2,0},{3,1},{4,6},{5,7},{6,4},{7,5},{8,10},{9,11},{10,... | collective-permute-start | bytes 589832 | tf_op jit(solution)/shard_map/ppermute | solution.py:203
  28.3 7.0 %collective-permute-start.4 = (bf16[96,896]{1,0:T(8,128)(2,1)S(1)}, bf16[96,896]{1,0:T(8,128)(2,1)}, u32[]{:S(2)}, u32[]{:S(2)}) collective-permute-start(bf16[96,896]{1,0:T(8,128)(2,1)S(1)} %pad_maximum_fusion.3.refs_2_), channel_id=1, source_target_pairs={{0,1},{1,0},{2,3},{3,2},{4,5},{5,4},{6,7},{7,6},{8,9},{9,8},{10,11... | collective-permute-start | bytes 516104 | tf_op jit(solution)/shard_map/ppermute | solution.py:203
  30.9 6.2 %collective-permute-start.6 = (bf16[96,896]{1,0:T(8,128)(2,1)S(1)}, bf16[96,896]{1,0:T(8,128)(2,1)}, u32[]{:S(2)}, u32[]{:S(2)}) collective-permute-start(bf16[96,896]{1,0:T(8,128)(2,1)S(1)} %collective-permute-done.5.refs_4_), channel_id=1, source_target_pairs={{0,1},{1,0},{2,3},{3,2},{4,5},{5,4},{6,7},{7,6},{8,9},{9,8},{10,11... | collective-permute-start | bytes 516104 | tf_op jit(solution)/shard_map/ppermute | solution.py:203
  35.3 11.3 %collective-permute-start.17 = (f32[16,48]{1,0:T(8,128)S(1)}, f32[16,48]{1,0:T(8,128)S(1)}, u32[]{:S(2)}, u32[]{:S(2)}) collective-permute-start(f32[16,48]{1,0:T(8,128)S(1)} %get-tuple-element.31.own), channel_id=1, source_target_pairs={{0,1},{1,0},{2,3},{3,2},{4,5},{5,4},{6,7},{7,6},{8,9},{9,8},{10,11... | collective-permute-start | bytes 9224 | tf_op jit(solution)/shard_map/ppermute | solution.py:203
  56.9 6.5 %collective-permute-start.21 = (bf16[32,896]{1,0:T(8,128)(2,1)S(1)}, bf16[32,896]{1,0:T(8,128)(2,1)S(1)}, u32[]{:S(2)}, u32[]{:S(2)}) collective-permute-start(bf16[32,896]{1,0:T(8,128)(2,1)S(1)} %get-tuple-element.41), channel_id=1, source_target_pairs={{0,12},{1,13},{2,14},{3,15},{4,8},{5,9},{6,10},{7,11},{8,4},{9,5},... | collective-permute-start | bytes 172040 | tf_op jit(solution)/shard_map/ppermute | solution.py:203
  57.7 6.3 %collective-permute-start.20 = (bf16[32,896]{1,0:T(8,128)(2,1)S(1)}, bf16[32,896]{1,0:T(8,128)(2,1)S(1)}, u32[]{:S(2)}, u32[]{:S(2)}) collective-permute-start(bf16[32,896]{1,0:T(8,128)(2,1)S(1)} %get-tuple-element.42), channel_id=1, source_target_pairs={{0,8},{1,9},{2,10},{3,11},{4,12},{5,13},{6,14},{7,15},{8,0},{9,1},... | collective-permute-start | bytes 172040 | tf_op jit(solution)/shard_map/ppermute | solution.py:203
  57.7 6.3 %collective-permute-start.19 = (bf16[32,896]{1,0:T(8,128)(2,1)S(1)}, bf16[32,896]{1,0:T(8,128)(2,1)S(1)}, u32[]{:S(2)}, u32[]{:S(2)}) collective-permute-start(bf16[32,896]{1,0:T(8,128)(2,1)S(1)} %get-tuple-element.43), channel_id=1, source_target_pairs={{0,4},{1,5},{2,6},{3,7},{4,0},{5,1},{6,2},{7,3},{8,12},{9,13},{10,... | collective-permute-start | bytes 172040 | tf_op jit(solution)/shard_map/ppermute | solution.py:203
  61.3 10.2 %collective-permute-start.22 = (bf16[4,32,1280]{2,1,0:T(8,128)(2,1)S(1)}, bf16[4,32,1280]{2,1,0:T(8,128)(2,1)S(1)}, u32[]{:S(2)}, u32[]{:S(2)}) collective-permute-start(bf16[4,32,1280]{2,1,0:T(8,128)(2,1)S(1)} %bitcast.91), channel_id=1, source_target_pairs={{0,2},{1,3},{2,0},{3,1},{4,6},{5,7},{6,4},{7,5},{8,10},{9,11},{10,... | collective-permute-start | bytes 983048 | tf_op jit(solution)/shard_map/ppermute | solution.py:203
  62.8 13.7 %collective-permute-start.23 = (bf16[4,32,1280]{2,1,0:T(8,128)(2,1)S(1)}, bf16[4,32,1280]{2,1,0:T(8,128)(2,1)S(1)}, u32[]{:S(2)}, u32[]{:S(2)}) collective-permute-start(bf16[4,32,1280]{2,1,0:T(8,128)(2,1)S(1)} %bitcast.90), channel_id=1, source_target_pairs={{0,2},{1,3},{2,0},{3,1},{4,6},{5,7},{6,4},{7,5},{8,10},{9,11},{10,... | collective-permute-start | bytes 983048 | tf_op jit(solution)/shard_map/ppermute | solution.py:203
  79.3 7.2 %collective-permute-start.29 = (bf16[32,1280]{1,0:T(8,128)(2,1)S(1)}, bf16[32,1280]{1,0:T(8,128)(2,1)S(1)}, u32[]{:S(2)}, u32[]{:S(2)}) collective-permute-start(bf16[32,1280]{1,0:T(8,128)(2,1)S(1)} %get-tuple-element.52), channel_id=1, source_target_pairs={{0,12},{1,13},{2,14},{3,15},{4,8},{5,9},{6,10},{7,11},{8,4},{9,5},... | collective-permute-start | bytes 245768 | tf_op jit(solution)/shard_map/ppermute | solution.py:203
  80.1 9.3 %collective-permute-start.28 = (bf16[32,1280]{1,0:T(8,128)(2,1)S(1)}, bf16[32,1280]{1,0:T(8,128)(2,1)S(1)}, u32[]{:S(2)}, u32[]{:S(2)}) collective-permute-start(bf16[32,1280]{1,0:T(8,128)(2,1)S(1)} %get-tuple-element.53), channel_id=1, source_target_pairs={{0,8},{1,9},{2,10},{3,11},{4,12},{5,13},{6,14},{7,15},{8,0},{9,1},... | collective-permute-start | bytes 245768 | tf_op jit(solution)/shard_map/ppermute | solution.py:203
  81.1 8.3 %collective-permute-start.27 = (bf16[32,1280]{1,0:T(8,128)(2,1)S(1)}, bf16[32,1280]{1,0:T(8,128)(2,1)S(1)}, u32[]{:S(2)}, u32[]{:S(2)}) collective-permute-start(bf16[32,1280]{1,0:T(8,128)(2,1)S(1)} %get-tuple-element.51), channel_id=1, source_target_pairs={{0,4},{1,5},{2,6},{3,7},{4,0},{5,1},{6,2},{7,3},{8,12},{9,13},{10,... | collective-permute-start | bytes 245768 | tf_op jit(solution)/shard_map/ppermute | solution.py:203
  83.7 6.3 %collective-permute-start.26 = (bf16[32,1280]{1,0:T(8,128)(2,1)S(1)}, bf16[32,1280]{1,0:T(8,128)(2,1)S(1)}, u32[]{:S(2)}, u32[]{:S(2)}) collective-permute-start(bf16[32,1280]{1,0:T(8,128)(2,1)S(1)} %get-tuple-element.49), channel_id=1, source_target_pairs={{0,12},{1,13},{2,14},{3,15},{4,8},{5,9},{6,10},{7,11},{8,4},{9,5},... | collective-permute-start | bytes 245768 | tf_op jit(solution)/shard_map/ppermute | solution.py:203
  84.5 7.2 %collective-permute-start.25 = (bf16[32,1280]{1,0:T(8,128)(2,1)S(1)}, bf16[32,1280]{1,0:T(8,128)(2,1)S(1)}, u32[]{:S(2)}, u32[]{:S(2)}) collective-permute-start(bf16[32,1280]{1,0:T(8,128)(2,1)S(1)} %get-tuple-element.50), channel_id=1, source_target_pairs={{0,8},{1,9},{2,10},{3,11},{4,12},{5,13},{6,14},{7,15},{8,0},{9,1},... | collective-permute-start | bytes 245768 | tf_op jit(solution)/shard_map/ppermute | solution.py:203
  86.5 6.0 %collective-permute-start.24 = (bf16[32,1280]{1,0:T(8,128)(2,1)S(1)}, bf16[32,1280]{1,0:T(8,128)(2,1)S(1)}, u32[]{:S(2)}, u32[]{:S(2)}) collective-permute-start(bf16[32,1280]{1,0:T(8,128)(2,1)S(1)} %get-tuple-element.48), channel_id=1, source_target_pairs={{0,4},{1,5},{2,6},{3,7},{4,0},{5,1},{6,2},{7,3},{8,12},{9,13},{10,... | collective-permute-start | bytes 245768 | tf_op jit(solution)/shard_map/ppermute | solution.py:203
  (15 other events, 68.0 us)

commit v7 on v6

--- a/solution.py
+++ b/solution.py
@@ -12,10 +12,10 @@
 HIGH = lax.Precision.HIGHEST
 CHUNKS = 2
 SLICES = 4
-LIMIT = 24 * 1024 * 1024
+LIMIT = 12 * 1024 * 1024
 VMEM = pl.BlockSpec(memory_space=pltpu.VMEM)
 SMEM = pl.BlockSpec(memory_space=pltpu.SMEM)
-ANY = pl.BlockSpec(memory_space=pl.ANY)
+HBM = pl.BlockSpec(memory_space=pltpu.HBM)
 BF16 = jnp.bfloat16
 F32 = jnp.float32
 
@@ -220,7 +220,7 @@
         [shape((tok, lanes), BF16)] * groups + [shape((2 * top, tok), F32)],
         4 * rows * hidden * rank,
         2 * rows * hidden,
-        [SMEM] + [ANY] * 4,
+        [SMEM] + [HBM] * 4,
         [
             pltpu.VMEM((rows, hidden), BF16),
             pltpu.VMEM((rank, hidden), F32),
@@ -251,7 +251,7 @@
             [shape((lanes, share), BF16)] + [shape((2, tok, lanes), BF16)] * SLICES,
             2 * count * tok * lanes * share * 3 // 2,
             2 * count * tok * (lanes + share),
-            [ANY] * (len(xs) + len(ys)),
+            [HBM] * (len(xs) + len(ys)),
             [
                 pltpu.VMEM((count * tok, share), BF16),
                 pltpu.VMEM((len(xs), 2, tok, lanes), BF16),
@@ -271,6 +271,7 @@
             for i in (0, tok)
         ]
     zs = zs[:1] + [exchange(zs[j], j * line) for j in range(1, SLICES)]
+    columns, _ = lax.optimization_barrier((columns, zs[1]))
 
     piece = part // CHUNKS
     flops = 4 * rows * SLICES * rank * piece
@@ -281,7 +282,7 @@
         [shape((lanes, 2 * rows), BF16)] + outs,
         flops,
         4 * rows * piece,
-        [SMEM] + [VMEM] * (SLICES + 2) + [ANY] * 2,
+        [SMEM] + [VMEM] * (SLICES + 2) + [HBM] * 2,
         [pltpu.VMEM((lanes, 2 * rows), BF16)] + work,
         jnp.stack([core, lower]),
         *zs,
@@ -297,7 +298,7 @@
                 outs,
                 flops,
                 4 * rows * piece,
-                [VMEM] + [ANY] * 2,
+                [VMEM] + [HBM] * 2,
                 work,
                 spread,
                 mine,
@@ -326,17 +327,14 @@
             total = total + other.astype(F32)
         totals.append(total)
 
-    columns, _ = lax.optimization_barrier((columns, chunks[-1][0]))
     parts = columns.reshape(SLICES, n_expert // SLICES // groups, rank, share)
     parts = lax.dynamic_index_in_dim(parts, own % (n_expert // SLICES) // groups, 1, False)
     parts = [lax.dynamic_index_in_dim(parts, place ^ j, 0, False) for j in range(SLICES)]
     parts = jnp.stack(parts[:1] + [exchange(parts[j], j * line) for j in range(1, SLICES)])
     parts = [lax.dynamic_index_in_dim(parts, place ^ j, 0, False) for j in range(SLICES)]
     range_rows = jnp.concatenate(parts, axis=1).astype(F32)
-    range_rows, _ = lax.optimization_barrier((range_rows, sums[0]))
     gram = lax.dot_general(range_rows, range_rows, (((1,), (1,)), ((), ())), precision=HIGH)
     lower = jnp.linalg.cholesky(gram)
-    lower, _ = lax.optimization_barrier((lower, sums[-1]))
     inverse = jax.scipy.linalg.solve_triangular(lower, jnp.eye(rank, dtype=F32), lower=True)
     kept = lax.dynamic_slice_in_dim(range_rows, half * (width // n_dp), width // n_dp, axis=1)
     basis = jnp.dot(inverse * math.sqrt(width), kept, precision=HIGH)

time: 93.9 us -> 88.2 us (0.939)
  waiting for transfers between devices: 26.6 us -> 22.6 us
  local copies, waits for them, and re-layouts: 8.31 us -> 5.14 us
  starting transfers between devices: 34.1 us -> 36.1 us
    ppermute x30, waiting for transfers between devices: 26.6 us -> 22.6 us  [exchange(): return lax.ppermute(block, AXES, [(i, i ^ step) for i in range(count)])]
    unnamed x18 -> x10, local copies, waits for them, and re-layouts: 7.07 us -> 3.9 us
    ppermute x30, starting transfers between devices: 34.1 us -> 36.1 us  [exchange(): return lax.ppermute(block, AXES, [(i, i ^ step) for i in range(count)])]
  transfers between devices with their start and end apart: 30 -> 30, of which waited for: 13 -> 12; matrix products, arithmetic and copies ran while one was open for 8% -> 10% of each run, Pallas kernels for 9% -> 11%
where the time goes in v7:
time: 88.2 us; the launch traced here: 87.8 us
  starting transfers between devices  36.1 us (41%)
  waiting for transfers between devices  22.6 us (26%)
  Pallas kernels  13.2 us (15%)
  other arithmetic  7.78 us (9%)
  local copies, waits for them, and re-layouts  5.14 us (6%)
  matrix products  2.06 us (2%)
  between operations  0.92 us (1%)
    ppermute x30, starting transfers between devices, exchange(): return lax.ppermute(block, AXES, [(i, i ^ step) for i in range(count)])  36.1 us
    ppermute x30, waiting for transfers between devices, exchange(): return lax.ppermute(block, AXES, [(i, i ^ step) for i in range(count)])  22.6 us
    pallas_call x4, Pallas kernels, call(): pl.pallas_call(body, out_shape=shapes, in_specs=spaces, out_specs=[VMEM]...  13.2 us
    unnamed x10, local copies, waits for them, and re-layouts  3.9 us
    another operation x3, other arithmetic, shards(): lower = jnp.linalg.cholesky(gram)  3.6 us
    another operation x2, other arithmetic, shards(): jax.scipy.linalg.solve_triangular(lower, jnp.eye(rank, dtype=F32), lower=...  3.09 us
  transfers between devices with their start and end apart: 30, of which 12 were waited for; matrix products, arithmetic and copies ran while one was open for 10% of the time, Pallas kernels for 11%

profile of v7, /device:TPU:0, one launch (start us, length us, event | category | flops | bytes accessed | tf_op | source)
XLA Modules:
  0.0 87.8 jit_solution(12057040633915051313)
XLA Ops:
  1.7 4.1 %collective-permute-start.1 = (bf16[48,896]{1,0:T(8,128)(2,1)S(1)}, bf16[48,896]{1,0:T(8,128)(2,1)S(1)}, u32[]{:S(2)}, u32[]{:S(2)}) collective-permute-start(bf16[48,896]{1,0:T(8,128)(2,1)S(1)} %get-tuple-element.40), channel_id=1, source_target_pairs={{0,8},{1,9},{2,10},{3,11},{4,12},{5,13},{6,14},{7,15},{8,0},{9,1},... | collective-permute-start | bytes 258056 | tf_op jit(solution)/shard_map/ppermute | solution.py:203
  7.4 1.5 %copy-done = bf16[48,8,2560]{2,1,0:T(8,128)(2,1)S(1)} copy-done((bf16[48,8,2560]{2,1,0:T(8,128)(2,1)S(1)}, bf16[48,8,2560]{2,1,0:T(8,128)(2,1)}, u32[]{:S(2)}) %copy-start) | copy-done | bytes 1966104
  11.3 5.0 %shard_map.68 = (bf16[48,256]{1,0:T(8,128)(2,1)S(1)}, bf16[48,256]{1,0:T(8,128)(2,1)S(1)}, f32[16,48]{1,0:T(8,128)S(1)}) custom-call(s32[1]{0:T(128)} %bitcast.core, bf16[384,2560]{1,0:T(8,128)(2,1)S(1)} %bitcast.77, f32[32,2560]{1,0:T(8,128)S(1)} %bitcast.80, s32[8,48]{1,0:T(8,128)S(1)} %bitcast.85, f32[8,48]{1,0:T(8,128)S(1)} %bitcast.86), custom_call_target="tpu_custom_call" | custom-call | flops 125829120 | bytes 1966080 | tf_op jit(solution)/shard_map/pallas_call | solution.py:33
  17.8 3.0 %collective-permute-start.12 = (bf16[2,48,256]{2,1,0:T(8,128)(2,1)S(1)}, bf16[2,48,256]{2,1,0:T(8,128)(2,1)S(1)}, u32[]{:S(2)}, u32[]{:S(2)}) collective-permute-start(bf16[2,48,256]{2,1,0:T(8,128)(2,1)S(1)} %get-tuple-element.55), channel_id=1, source_target_pairs={{0,12},{1,13},{2,14},{3,15},{4,8},{5,9},{6,10},{7,11},{8,4},{9,5},... | collective-permute-start | bytes 147464 | tf_op jit(solution)/shard_map/ppermute | solution.py:203
  26.6 1.6 %collective-permute-start.13 = (bf16[4,2,48,256]{3,2,1,0:T(8,128)(2,1)S(1)}, bf16[4,2,48,256]{3,2,1,0:T(8,128)(2,1)S(1)}, u32[]{:S(2)}, u32[]{:S(2)}) collective-permute-start(bf16[4,2,48,256]{3,2,1,0:T(8,128)(2,1)S(1)} %pad_maximum_fusion.2.refs_8_), channel_id=1, source_target_pairs={{0,2},{1,3},{2,0},{3,1},{4,6},{5,7},{6,4},{7,5},{8,10},{9,11},{10,... | collective-permute-start | bytes 589832 | tf_op jit(solution)/shard_map/ppermute | solution.py:203
  29.6 3.7 %collective-permute-done.7.refs_6_ = bf16[96,896]{1,0:T(8,128)(2,1)S(1)} collective-permute-done((bf16[96,896]{1,0:T(8,128)(2,1)S(1)}, bf16[96,896]{1,0:T(8,128)(2,1)S(1)}, u32[]{:S(2)}, u32[]{:S(2)}) %collective-permute-start.7) | collective-permute-done | bytes 172064 | tf_op jit(solution)/shard_map/ppermute | solution.py:203
  33.8 2.2 %collective-permute-done.13.refs_9_ = bf16[4,2,48,256]{3,2,1,0:T(8,128)(2,1)S(1)} collective-permute-done((bf16[4,2,48,256]{3,2,1,0:T(8,128)(2,1)S(1)}, bf16[4,2,48,256]{3,2,1,0:T(8,128)(2,1)S(1)}, u32[]{:S(2)}, u32[]{:S(2)}) %collective-permute-start.13) | collective-permute-done | bytes 196640 | tf_op jit(solution)/shard_map/ppermute | solution.py:203
  36.0 3.1 %shard_map.69 = (bf16[256,896]{1,0:T(8,128)(2,1)S(1)}, bf16[2,48,256]{2,1,0:T(8,128)(2,1)S(1)}, bf16[2,48,256]{2,1,0:T(8,128)(2,1)S(1)}, bf16[2,48,256]{2,1,0:T(8,128)(2,1)S(1)}, bf16[2,48,256]{2,1,0:T(8,128)(2,1)S(1)}) custom-call(bf16[96,896]{1,0:T(8,128)(2,1)S(1)} %pad_maximum_fusion.3.refs_0_, bf16[96,896]{1,0:T(8,128)(2,1)S(1)} %collective-permute-done.3.refs_1_, ...), custom_call_target="tpu_custom_call" | custom-call | flops 528482304 | bytes 1769472 | tf_op jit(solution)/shard_map/pallas_call | solution.py:33
  40.0 3.2 %collective-permute-done.14.z1 = bf16[2,48,256]{2,1,0:T(8,128)(2,1)S(1)} collective-permute-done((bf16[2,48,256]{2,1,0:T(8,128)(2,1)S(1)}, bf16[2,48,256]{2,1,0:T(8,128)(2,1)S(1)}, u32[]{:S(2)}, u32[]{:S(2)}) %collective-permute-start.14) | collective-permute-done | bytes 49184 | tf_op jit(solution)/shard_map/ppermute | solution.py:203
  44.2 2.6 %collective-permute-start.16 = (bf16[32,896]{1,0:T(8,128)(2,1)S(1)}, bf16[32,896]{1,0:T(8,128)(2,1)S(1)}, u32[]{:S(2)}, u32[]{:S(2)}) collective-permute-start(bf16[32,896]{1,0:T(8,128)(2,1)S(1)} %get-tuple-element.38), channel_id=1, source_target_pairs={{0,8},{1,9},{2,10},{3,11},{4,12},{5,13},{6,14},{7,15},{8,0},{9,1},... | collective-permute-start | bytes 172040 | tf_op jit(solution)/shard_map/ppermute | solution.py:203
  47.8 1.9 %collective-permute-start.18 = (bf16[2,48,256]{2,1,0:T(8,128)(2,1)S(1)}, bf16[2,48,256]{2,1,0:T(8,128)(2,1)S(1)}, u32[]{:S(2)}, u32[]{:S(2)}) collective-permute-start(bf16[2,48,256]{2,1,0:T(8,128)(2,1)S(1)} %get-tuple-element.28), channel_id=1, source_target_pairs={{0,8},{1,9},{2,10},{3,11},{4,12},{5,13},{6,14},{7,15},{8,0},{9,1},... | collective-permute-start | bytes 147464 | tf_op jit(solution)/shard_map/ppermute | solution.py:203
  49.7 2.5 %collective-permute-done.16 = bf16[32,896]{1,0:T(8,128)(2,1)S(1)} collective-permute-done((bf16[32,896]{1,0:T(8,128)(2,1)S(1)}, bf16[32,896]{1,0:T(8,128)(2,1)S(1)}, u32[]{:S(2)}, u32[]{:S(2)}) %collective-permute-start.16) | collective-permute-done | bytes 57376 | tf_op jit(solution)/shard_map/ppermute | solution.py:203
  52.2 2.0 %collective-permute-start.19 = (bf16[2,48,256]{2,1,0:T(8,128)(2,1)S(1)}, bf16[2,48,256]{2,1,0:T(8,128)(2,1)S(1)}, u32[]{:S(2)}, u32[]{:S(2)}) collective-permute-start(bf16[2,48,256]{2,1,0:T(8,128)(2,1)S(1)} %get-tuple-element.29), channel_id=1, source_target_pairs={{0,12},{1,13},{2,14},{3,15},{4,8},{5,9},{6,10},{7,11},{8,4},{9,5},... | collective-permute-start | bytes 147464 | tf_op jit(solution)/shard_map/ppermute | solution.py:203
  54.6 2.9 %cholesky.17 = f32[32,32]{1,0:T(8,128)S(1)} custom-call(f32[32,32]{1,0:T(8,128)S(1)} %fusion.24), custom_call_target="Cholesky" | custom-call | tf_op jit(solution)/shard_map/jit(cholesky)/cholesky | solution.py:337
  58.9 2.4 %custom-call.7 = f32[1,32,32]{1,2,0:T(8,128)S(1)} custom-call(f32[1,32,32]{2,1,0:T(8,128)S(1)} %fusion.21), custom_call_target="InvertDiagBlocksLowerTriangular" | custom-call | tf_op jit(solution)/shard_map/jit(_solve_triangular)/triangular_solve | solution.py:338
  61.4 3.1 %shard_map.70 = (bf16[256,768]{1,0:T(8,128)(2,1)S(1)}, bf16[128,1280]{1,0:T(8,128)(2,1)S(1)}, bf16[128,1280]{1,0:T(8,128)(2,1)S(1)}) custom-call(s32[2]{0:T(128)S(1)} %pad_add_fusion.at, bf16[2,48,256]{2,1,0:T(8,128)(2,1)S(1)} %get-tuple-element.27.z0, bf16[2,48,256]{2,1,0:T(8,128)(2,1)S(1)} %collective-permute-done.14.z1, ...), custom_call_target="tpu_custom_call" | custom-call | flops 251658240 | bytes 1966080 | tf_op jit(solution)/shard_map/pallas_call | solution.py:33
  64.5 1.6 %collective-permute-start.22 = (bf16[4,32,1280]{2,1,0:T(8,128)(2,1)S(1)}, bf16[4,32,1280]{2,1,0:T(8,128)(2,1)S(1)}, u32[]{:S(2)}, u32[]{:S(2)}) collective-permute-start(bf16[4,32,1280]{2,1,0:T(8,128)(2,1)S(1)} %bitcast.88), channel_id=1, source_target_pairs={{0,2},{1,3},{2,0},{3,1},{4,6},{5,7},{6,4},{7,5},{8,10},{9,11},{10,... | collective-permute-start | bytes 983048 | tf_op jit(solution)/shard_map/ppermute | solution.py:203
  67.4 2.0 %shard_map.71 = (bf16[128,1280]{1,0:T(8,128)(2,1)S(1)}, bf16[128,1280]{1,0:T(8,128)(2,1)S(1)}) custom-call(bf16[256,768]{1,0:T(8,128)(2,1)S(1)} %get-tuple-element.33.spread, bf16[384,2560]{1,0:T(8,128)(2,1)S(1)} %bitcast.79, bf16[384,2560]{1,0:T(8,128)(2,1)} %collective-permute-done.21.other), custom_call_target="tpu_custom_call" | custom-call | flops 251658240 | bytes 1966080 | tf_op jit(solution)/shard_map/pallas_call | solution.py:33
  69.9 4.1 %collective-permute-done.22 = bf16[4,32,1280]{2,1,0:T(8,128)(2,1)S(1)} collective-permute-done((bf16[4,32,1280]{2,1,0:T(8,128)(2,1)S(1)}, bf16[4,32,1280]{2,1,0:T(8,128)(2,1)S(1)}, u32[]{:S(2)}, u32[]{:S(2)}) %collective-permute-start.22) | collective-permute-done | bytes 327712 | tf_op jit(solution)/shard_map/ppermute | solution.py:203
  74.2 1.6 %collective-permute-start.24 = (bf16[32,1280]{1,0:T(8,128)(2,1)S(1)}, bf16[32,1280]{1,0:T(8,128)(2,1)S(1)}, u32[]{:S(2)}, u32[]{:S(2)}) collective-permute-start(bf16[32,1280]{1,0:T(8,128)(2,1)S(1)} %get-tuple-element.46), channel_id=1, source_target_pairs={{0,8},{1,9},{2,10},{3,11},{4,12},{5,13},{6,14},{7,15},{8,0},{9,1},... | collective-permute-start | bytes 245768 | tf_op jit(solution)/shard_map/ppermute | solution.py:203
  75.9 2.7 %collective-permute-start.25 = (bf16[32,1280]{1,0:T(8,128)(2,1)S(1)}, bf16[32,1280]{1,0:T(8,128)(2,1)S(1)}, u32[]{:S(2)}, u32[]{:S(2)}) collective-permute-start(bf16[32,1280]{1,0:T(8,128)(2,1)S(1)} %get-tuple-element.45), channel_id=1, source_target_pairs={{0,12},{1,13},{2,14},{3,15},{4,8},{5,9},{6,10},{7,11},{8,4},{9,5},... | collective-permute-start | bytes 245768 | tf_op jit(solution)/shard_map/ppermute | solution.py:203
  78.8 1.6 %collective-permute-start.28 = (bf16[32,1280]{1,0:T(8,128)(2,1)S(1)}, bf16[32,1280]{1,0:T(8,128)(2,1)S(1)}, u32[]{:S(2)}, u32[]{:S(2)}) collective-permute-start(bf16[32,1280]{1,0:T(8,128)(2,1)S(1)} %get-tuple-element.49), channel_id=1, source_target_pairs={{0,8},{1,9},{2,10},{3,11},{4,12},{5,13},{6,14},{7,15},{8,0},{9,1},... | collective-permute-start | bytes 245768 | tf_op jit(solution)/shard_map/ppermute | solution.py:203
  80.4 2.7 %collective-permute-start.29 = (bf16[32,1280]{1,0:T(8,128)(2,1)S(1)}, bf16[32,1280]{1,0:T(8,128)(2,1)S(1)}, u32[]{:S(2)}, u32[]{:S(2)}) collective-permute-start(bf16[32,1280]{1,0:T(8,128)(2,1)S(1)} %get-tuple-element.48), channel_id=1, source_target_pairs={{0,12},{1,13},{2,14},{3,15},{4,8},{5,9},{6,10},{7,11},{8,4},{9,5},... | collective-permute-start | bytes 245768 | tf_op jit(solution)/shard_map/ppermute | solution.py:203
  84.7 2.1 %collective-permute-done.29 = bf16[32,1280]{1,0:T(8,128)(2,1)S(1)} collective-permute-done((bf16[32,1280]{1,0:T(8,128)(2,1)S(1)}, bf16[32,1280]{1,0:T(8,128)(2,1)S(1)}, u32[]{:S(2)}, u32[]{:S(2)}) %collective-permute-start.29) | collective-permute-done | bytes 81952 | tf_op jit(solution)/shard_map/ppermute | solution.py:203
  (76 shorter events, 23.5 us)
Async XLA Ops:
  1.7 14.6 %collective-permute-start.1 = (bf16[48,896]{1,0:T(8,128)(2,1)S(1)}, bf16[48,896]{1,0:T(8,128)(2,1)S(1)}, u32[]{:S(2)}, u32[]{:S(2)}) collective-permute-start(bf16[48,896]{1,0:T(8,128)(2,1)S(1)} %get-tuple-element.40), channel_id=1, source_target_pairs={{0,8},{1,9},{2,10},{3,11},{4,12},{5,13},{6,14},{7,15},{8,0},{9,1},... | collective-permute-start | bytes 258056 | tf_op jit(solution)/shard_map/ppermute | solution.py:203
  5.8 10.5 %collective-permute-start.2 = (bf16[48,896]{1,0:T(8,128)(2,1)S(1)}, bf16[48,896]{1,0:T(8,128)(2,1)S(1)}, u32[]{:S(2)}, u32[]{:S(2)}) collective-permute-start(bf16[48,896]{1,0:T(8,128)(2,1)S(1)} %get-tuple-element.43), channel_id=1, source_target_pairs={{0,12},{1,13},{2,14},{3,15},{4,8},{5,9},{6,10},{7,11},{8,4},{9,5},... | collective-permute-start | bytes 258056 | tf_op jit(solution)/shard_map/ppermute | solution.py:203
  7.2 9.2 %collective-permute-start = (bf16[48,896]{1,0:T(8,128)(2,1)S(1)}, bf16[48,896]{1,0:T(8,128)(2,1)S(1)}, u32[]{:S(2)}, u32[]{:S(2)}) collective-permute-start(bf16[48,896]{1,0:T(8,128)(2,1)S(1)} %get-tuple-element.41), channel_id=1, source_target_pairs={{0,4},{1,5},{2,6},{3,7},{4,0},{5,1},{6,2},{7,3},{8,12},{9,13},{10,... | collective-permute-start | bytes 258056 | tf_op jit(solution)/shard_map/ppermute | solution.py:203
  7.4 53.9 %collective-permute-start.21 = (bf16[384,2560]{1,0:T(8,128)(2,1)}, bf16[384,2560]{1,0:T(8,128)(2,1)}, u32[]{:S(2)}, u32[]{:S(2)}) collective-permute-start(bf16[384,2560]{1,0:T(8,128)(2,1)} %bitcast.76), channel_id=1, source_target_pairs={{0,1},{1,0},{2,3},{3,2},{4,5},{5,4},{6,7},{7,6},{8,9},{9,8},{10,11... | collective-permute-start | bytes 5898248 | tf_op jit(solution)/shard_map/ppermute | solution.py:203
  17.8 6.5 %collective-permute-start.12 = (bf16[2,48,256]{2,1,0:T(8,128)(2,1)S(1)}, bf16[2,48,256]{2,1,0:T(8,128)(2,1)S(1)}, u32[]{:S(2)}, u32[]{:S(2)}) collective-permute-start(bf16[2,48,256]{2,1,0:T(8,128)(2,1)S(1)} %get-tuple-element.55), channel_id=1, source_target_pairs={{0,12},{1,13},{2,14},{3,15},{4,8},{5,9},{6,10},{7,11},{8,4},{9,5},... | collective-permute-start | bytes 147464 | tf_op jit(solution)/shard_map/ppermute | solution.py:203
  20.8 5.0 %collective-permute-start.10 = (bf16[2,48,256]{2,1,0:T(8,128)(2,1)S(1)}, bf16[2,48,256]{2,1,0:T(8,128)(2,1)S(1)}, u32[]{:S(2)}, u32[]{:S(2)}) collective-permute-start(bf16[2,48,256]{2,1,0:T(8,128)(2,1)S(1)} %get-tuple-element.55), channel_id=1, source_target_pairs={{0,4},{1,5},{2,6},{3,7},{4,0},{5,1},{6,2},{7,3},{8,12},{9,13},{10,... | collective-permute-start | bytes 147464 | tf_op jit(solution)/shard_map/ppermute | solution.py:203
  21.3 5.3 %collective-permute-start.11 = (bf16[2,48,256]{2,1,0:T(8,128)(2,1)S(1)}, bf16[2,48,256]{2,1,0:T(8,128)(2,1)S(1)}, u32[]{:S(2)}, u32[]{:S(2)}) collective-permute-start(bf16[2,48,256]{2,1,0:T(8,128)(2,1)S(1)} %get-tuple-element.55), channel_id=1, source_target_pairs={{0,8},{1,9},{2,10},{3,11},{4,12},{5,13},{6,14},{7,15},{8,0},{9,1},... | collective-permute-start | bytes 147464 | tf_op jit(solution)/shard_map/ppermute | solution.py:203
  22.3 7.3 %collective-permute-start.5 = (bf16[96,896]{1,0:T(8,128)(2,1)S(1)}, bf16[96,896]{1,0:T(8,128)(2,1)S(1)}, u32[]{:S(2)}, u32[]{:S(2)}) collective-permute-start(bf16[96,896]{1,0:T(8,128)(2,1)S(1)} %pad_maximum_fusion.3.refs_0_), channel_id=1, source_target_pairs={{0,2},{1,3},{2,0},{3,1},{4,6},{5,7},{6,4},{7,5},{8,10},{9,11},{10,... | collective-permute-start | bytes 516104 | tf_op jit(solution)/shard_map/ppermute | solution.py:203
  24.3 9.0 %collective-permute-start.7 = (bf16[96,896]{1,0:T(8,128)(2,1)S(1)}, bf16[96,896]{1,0:T(8,128)(2,1)S(1)}, u32[]{:S(2)}, u32[]{:S(2)}) collective-permute-start(bf16[96,896]{1,0:T(8,128)(2,1)S(1)} %pad_maximum_fusion.4.refs_2_), channel_id=1, source_target_pairs={{0,2},{1,3},{2,0},{3,1},{4,6},{5,7},{6,4},{7,5},{8,10},{9,11},{10,... | collective-permute-start | bytes 516104 | tf_op jit(solution)/shard_map/ppermute | solution.py:203
  25.8 7.5 %collective-permute-start.3 = (bf16[96,896]{1,0:T(8,128)(2,1)S(1)}, bf16[96,896]{1,0:T(8,128)(2,1)S(1)}, u32[]{:S(2)}, u32[]{:S(2)}) collective-permute-start(bf16[96,896]{1,0:T(8,128)(2,1)S(1)} %pad_maximum_fusion.3.refs_0_), channel_id=1, source_target_pairs={{0,1},{1,0},{2,3},{3,2},{4,5},{5,4},{6,7},{7,6},{8,9},{9,8},{10,11... | collective-permute-start | bytes 516104 | tf_op jit(solution)/shard_map/ppermute | solution.py:203
  26.6 9.3 %collective-permute-start.13 = (bf16[4,2,48,256]{3,2,1,0:T(8,128)(2,1)S(1)}, bf16[4,2,48,256]{3,2,1,0:T(8,128)(2,1)S(1)}, u32[]{:S(2)}, u32[]{:S(2)}) collective-permute-start(bf16[4,2,48,256]{3,2,1,0:T(8,128)(2,1)S(1)} %pad_maximum_fusion.2.refs_8_), channel_id=1, source_target_pairs={{0,2},{1,3},{2,0},{3,1},{4,6},{5,7},{6,4},{7,5},{8,10},{9,11},{10,... | collective-permute-start | bytes 589832 | tf_op jit(solution)/shard_map/ppermute | solution.py:203
  40.0 21.3 %collective-permute-start.20 = (f32[16,48]{1,0:T(8,128)S(1)}, f32[16,48]{1,0:T(8,128)S(1)}, u32[]{:S(2)}, u32[]{:S(2)}) collective-permute-start(f32[16,48]{1,0:T(8,128)S(1)} %get-tuple-element.30.own), channel_id=1, source_target_pairs={{0,1},{1,0},{2,3},{3,2},{4,5},{5,4},{6,7},{7,6},{8,9},{9,8},{10,11... | collective-permute-start | bytes 9224 | tf_op jit(solution)/shard_map/ppermute | solution.py:203
  44.2 8.0 %collective-permute-start.16 = (bf16[32,896]{1,0:T(8,128)(2,1)S(1)}, bf16[32,896]{1,0:T(8,128)(2,1)S(1)}, u32[]{:S(2)}, u32[]{:S(2)}) collective-permute-start(bf16[32,896]{1,0:T(8,128)(2,1)S(1)} %get-tuple-element.38), channel_id=1, source_target_pairs={{0,8},{1,9},{2,10},{3,11},{4,12},{5,13},{6,14},{7,15},{8,0},{9,1},... | collective-permute-start | bytes 172040 | tf_op jit(solution)/shard_map/ppermute | solution.py:203
  46.8 7.4 %collective-permute-start.17 = (bf16[32,896]{1,0:T(8,128)(2,1)S(1)}, bf16[32,896]{1,0:T(8,128)(2,1)S(1)}, u32[]{:S(2)}, u32[]{:S(2)}) collective-permute-start(bf16[32,896]{1,0:T(8,128)(2,1)S(1)} %get-tuple-element.37), channel_id=1, source_target_pairs={{0,12},{1,13},{2,14},{3,15},{4,8},{5,9},{6,10},{7,11},{8,4},{9,5},... | collective-permute-start | bytes 172040 | tf_op jit(solution)/shard_map/ppermute | solution.py:203
  47.8 13.5 %collective-permute-start.18 = (bf16[2,48,256]{2,1,0:T(8,128)(2,1)S(1)}, bf16[2,48,256]{2,1,0:T(8,128)(2,1)S(1)}, u32[]{:S(2)}, u32[]{:S(2)}) collective-permute-start(bf16[2,48,256]{2,1,0:T(8,128)(2,1)S(1)} %get-tuple-element.28), channel_id=1, source_target_pairs={{0,8},{1,9},{2,10},{3,11},{4,12},{5,13},{6,14},{7,15},{8,0},{9,1},... | collective-permute-start | bytes 147464 | tf_op jit(solution)/shard_map/ppermute | solution.py:203
  52.2 9.1 %collective-permute-start.19 = (bf16[2,48,256]{2,1,0:T(8,128)(2,1)S(1)}, bf16[2,48,256]{2,1,0:T(8,128)(2,1)S(1)}, u32[]{:S(2)}, u32[]{:S(2)}) collective-permute-start(bf16[2,48,256]{2,1,0:T(8,128)(2,1)S(1)} %get-tuple-element.29), channel_id=1, source_target_pairs={{0,12},{1,13},{2,14},{3,15},{4,8},{5,9},{6,10},{7,11},{8,4},{9,5},... | collective-permute-start | bytes 147464 | tf_op jit(solution)/shard_map/ppermute | solution.py:203
  64.5 9.5 %collective-permute-start.22 = (bf16[4,32,1280]{2,1,0:T(8,128)(2,1)S(1)}, bf16[4,32,1280]{2,1,0:T(8,128)(2,1)S(1)}, u32[]{:S(2)}, u32[]{:S(2)}) collective-permute-start(bf16[4,32,1280]{2,1,0:T(8,128)(2,1)S(1)} %bitcast.88), channel_id=1, source_target_pairs={{0,2},{1,3},{2,0},{3,1},{4,6},{5,7},{6,4},{7,5},{8,10},{9,11},{10,... | collective-permute-start | bytes 983048 | tf_op jit(solution)/shard_map/ppermute | solution.py:203
  69.3 9.3 %collective-permute-start.26 = (bf16[4,32,1280]{2,1,0:T(8,128)(2,1)S(1)}, bf16[4,32,1280]{2,1,0:T(8,128)(2,1)S(1)}, u32[]{:S(2)}, u32[]{:S(2)}) collective-permute-start(bf16[4,32,1280]{2,1,0:T(8,128)(2,1)S(1)} %bitcast.87), channel_id=1, source_target_pairs={{0,2},{1,3},{2,0},{3,1},{4,6},{5,7},{6,4},{7,5},{8,10},{9,11},{10,... | collective-permute-start | bytes 983048 | tf_op jit(solution)/shard_map/ppermute | solution.py:203
  74.2 6.3 %collective-permute-start.23 = (bf16[32,1280]{1,0:T(8,128)(2,1)S(1)}, bf16[32,1280]{1,0:T(8,128)(2,1)S(1)}, u32[]{:S(2)}, u32[]{:S(2)}) collective-permute-start(bf16[32,1280]{1,0:T(8,128)(2,1)S(1)} %get-tuple-element.44), channel_id=1, source_target_pairs={{0,4},{1,5},{2,6},{3,7},{4,0},{5,1},{6,2},{7,3},{8,12},{9,13},{10,... | collective-permute-start | bytes 245768 | tf_op jit(solution)/shard_map/ppermute | solution.py:203
  74.2 9.0 %collective-permute-start.24 = (bf16[32,1280]{1,0:T(8,128)(2,1)S(1)}, bf16[32,1280]{1,0:T(8,128)(2,1)S(1)}, u32[]{:S(2)}, u32[]{:S(2)}) collective-permute-start(bf16[32,1280]{1,0:T(8,128)(2,1)S(1)} %get-tuple-element.46), channel_id=1, source_target_pairs={{0,8},{1,9},{2,10},{3,11},{4,12},{5,13},{6,14},{7,15},{8,0},{9,1},... | collective-permute-start | bytes 245768 | tf_op jit(solution)/shard_map/ppermute | solution.py:203
  75.9 7.3 %collective-permute-start.25 = (bf16[32,1280]{1,0:T(8,128)(2,1)S(1)}, bf16[32,1280]{1,0:T(8,128)(2,1)S(1)}, u32[]{:S(2)}, u32[]{:S(2)}) collective-permute-start(bf16[32,1280]{1,0:T(8,128)(2,1)S(1)} %get-tuple-element.45), channel_id=1, source_target_pairs={{0,12},{1,13},{2,14},{3,15},{4,8},{5,9},{6,10},{7,11},{8,4},{9,5},... | collective-permute-start | bytes 245768 | tf_op jit(solution)/shard_map/ppermute | solution.py:203
  78.7 5.0 %collective-permute-start.27 = (bf16[32,1280]{1,0:T(8,128)(2,1)S(1)}, bf16[32,1280]{1,0:T(8,128)(2,1)S(1)}, u32[]{:S(2)}, u32[]{:S(2)}) collective-permute-start(bf16[32,1280]{1,0:T(8,128)(2,1)S(1)} %get-tuple-element.47), channel_id=1, source_target_pairs={{0,4},{1,5},{2,6},{3,7},{4,0},{5,1},{6,2},{7,3},{8,12},{9,13},{10,... | collective-permute-start | bytes 245768 | tf_op jit(solution)/shard_map/ppermute | solution.py:203
  78.8 5.9 %collective-permute-start.28 = (bf16[32,1280]{1,0:T(8,128)(2,1)S(1)}, bf16[32,1280]{1,0:T(8,128)(2,1)S(1)}, u32[]{:S(2)}, u32[]{:S(2)}) collective-permute-start(bf16[32,1280]{1,0:T(8,128)(2,1)S(1)} %get-tuple-element.49), channel_id=1, source_target_pairs={{0,8},{1,9},{2,10},{3,11},{4,12},{5,13},{6,14},{7,15},{8,0},{9,1},... | collective-permute-start | bytes 245768 | tf_op jit(solution)/shard_map/ppermute | solution.py:203
  80.4 6.3 %collective-permute-start.29 = (bf16[32,1280]{1,0:T(8,128)(2,1)S(1)}, bf16[32,1280]{1,0:T(8,128)(2,1)S(1)}, u32[]{:S(2)}, u32[]{:S(2)}) collective-permute-start(bf16[32,1280]{1,0:T(8,128)(2,1)S(1)} %get-tuple-element.48), channel_id=1, source_target_pairs={{0,12},{1,13},{2,14},{3,15},{4,8},{5,9},{6,10},{7,11},{8,4},{9,5},... | collective-permute-start | bytes 245768 | tf_op jit(solution)/shard_map/ppermute | solution.py:203
  (11 other events, 58.3 us)

commit v8 on v7

--- a/solution.py
+++ b/solution.py
@@ -9,10 +9,10 @@
 from jax.sharding import PartitionSpec as P
 
 AXES = ("expert", "dp")
-HIGH = lax.Precision.HIGHEST
 CHUNKS = 2
 SLICES = 4
 LIMIT = 12 * 1024 * 1024
+LARGE = 56 * 1024 * 1024
 VMEM = pl.BlockSpec(memory_space=pltpu.VMEM)
 SMEM = pl.BlockSpec(memory_space=pltpu.SMEM)
 HBM = pl.BlockSpec(memory_space=pltpu.HBM)
@@ -29,16 +29,40 @@
     return lax.broadcasted_iota(jnp.int32, shape, dim)
 
 
-def call(body, shapes, flops, size, spaces, scratch, *args):
+def call(body, shapes, spaces, scratch, *args, limit=LIMIT):
     return pl.pallas_call(
         body,
         out_shape=shapes,
         in_specs=spaces,
         out_specs=[VMEM] * len(shapes),
         scratch_shapes=scratch,
-        compiler_params=pltpu.CompilerParams(vmem_limit_bytes=LIMIT),
-        cost_estimate=pl.CostEstimate(flops=flops, bytes_accessed=size, transcendentals=0),
+        compiler_params=pltpu.CompilerParams(vmem_limit_bytes=limit),
+        cost_estimate=pl.CostEstimate(flops=1, bytes_accessed=1, transcendentals=0),
     )(*args)
+
+
+def pieces(value, count):
+    terms = []
+    for _ in range(count):
+        terms.append(value.astype(BF16))
+        value = value - terms[-1].astype(F32)
+    return terms
+
+
+def pack(z, columns):
+    tiles = [z[:, i : i + 128] for i in range(0, z.shape[1], 128)]
+    tiles += [columns[:, i : i + 128] for i in range(0, columns.shape[1], 128)]
+    return jnp.concatenate(tiles, axis=0)
+
+
+def unpack_z(rows, size, lanes):
+    tiles = [rows[i * size : (i + 1) * size] for i in range(lanes // 128)]
+    return jnp.concatenate(tiles, axis=1)
+
+
+def unpack_columns(rows, start, rank):
+    tiles = [rows[i : i + rank] for i in range(start, rows.shape[0], rank)]
+    return jnp.concatenate(tiles, axis=1)
 
 
 def pair_columns(ids, probs):
@@ -101,11 +125,12 @@
             out[there] = jnp.sum(y.reshape(piece // top, top, lanes), axis=1).astype(BF16)
 
 
-def z_kernel(n, *refs):
-    xs, ys, columns, zs = refs[: 2 * n], refs[2 * n : -8], refs[-8], refs[-7:-3]
-    x, y, sems = refs[-3:]
+def z_kernel(n, low, at, *refs):
+    xs, ys, outs = refs[: 2 * n], refs[2 * n : -8], refs[-8:-4]
+    x, y, columns, sems = refs[-4:]
     rows = xs[0].shape[0]
-    tok = zs[0].shape[1]
+    _, _, tok, lanes = y.shape
+    rank = lanes // (SLICES * low)
     each = rows // tok
     sources = [(x_at, x.at[pl.ds(i * rows, rows)]) for i, x_at in enumerate(xs)]
     for b, y_at in enumerate(ys):
@@ -118,21 +143,75 @@
     total = dot(y[...].reshape(x.shape[0], -1), x[...], 0, 0).astype(BF16)
     columns[...] = total
     part = dot(x[: 2 * SLICES * tok], total, 1, 1).astype(BF16)
-    for j in range(SLICES):
-        for core in range(2):
-            start = ((j // each * 2 + core) * each + j % each) * tok
-            zs[j][core] = part[start : start + tok]
-
-
-def spread_rows(groups, at, zs, pairs, work, spread, low, rank):
-    _, tok, lanes = zs[0].shape
+    for j, out in enumerate(outs):
+        starts = [((j // each * 2 + core) * each + j % each) * tok for core in range(2)]
+        z = jnp.concatenate([part[start : start + tok] for start in starts], axis=0)
+        expert = (at[2] ^ j) * low + at[1]
+        out[...] = pack(z, columns[pl.ds(pl.multiple_of(expert * rank, rank), rank)])
+
+
+def inverse_kernel(start, at, p0, p1, p2, p3, inverse, basis, columns):
+    rank = inverse.shape[0]
+    _, _, share = columns.shape
+    gram = 0.0
+    for j, packed in enumerate((p0, p1, p2, p3)):
+        block = unpack_columns(packed[...], start, rank)
+        columns[at[2] ^ j] = block
+        gram = gram + dot(block, block, 1, 1)
+    row = iota((rank, 128), 0)
+    lane = iota((rank, 128), 1)
+    eye = (row + rank == lane).astype(F32)
+    work = jnp.concatenate([gram, jnp.zeros((rank, 128 - rank), F32)], axis=1) + eye
+    for first in range(0, rank, 4):
+        heads = [work[first + i : first + i + 1] for i in range(4)]
+        sides = [
+            jnp.broadcast_to(work[:, first + i : first + i + 1], (rank, 128)) for i in range(4)
+        ]
+        taken = 0.0
+        for i in range(4):
+            pivot = first + i
+            factor = sides[i] / sides[i][pivot : pivot + 1]
+            factor = jnp.where(row > pivot, factor, 0.0)
+            taken = taken + factor * heads[i]
+            for k in range(i + 1, 4):
+                sides[k] = sides[k] - factor * sides[k][pivot : pivot + 1]
+                heads[k] = heads[k] - factor[first + k : first + k + 1] * heads[i]
+        work = work - taken
+    diagonal = jnp.sum(jnp.where(row == lane, work, 0.0), axis=1, keepdims=True)
+    result = work[:, rank : 2 * rank] * lax.rsqrt(diagonal)
+    inverse[...] = result
+    scaled = result * math.sqrt(SLICES * share)
+    scaled = jnp.concatenate(pieces(scaled, 3), axis=0)
+    count = basis.shape[1] // share
+    for i in range(count):
+        out = dot(scaled, columns[at[3] * count + i], 1, 0)
+        out = out[:rank] + out[rank : 2 * rank] + out[2 * rank :]
+        basis[:, i * share : (i + 1) * share] = out
+
+
+def coeffs_kernel(scale, inverse, *refs):
+    blocks, out = refs[:-1], refs[-1]
+    rank, size = blocks[0].shape
+    left = jnp.concatenate(pieces(inverse[...] * scale, 3), axis=0)
+    left = jnp.concatenate([left] * SLICES, axis=1)
+    for i in range(len(blocks) // SLICES):
+        right = jnp.concatenate([b[...] for b in blocks[i * SLICES : (i + 1) * SLICES]], axis=0)
+        part = dot(left, right, 1, 0)
+        out[:, i * size : (i + 1) * size] = part[:rank] + part[rank : 2 * rank] + part[2 * rank :]
+
+
+def spread_rows(groups, at, packed, pairs, work, spread, low, rank):
+    lanes = work.shape[0]
+    tok = pairs[0].shape[1]
     top = pairs[0].shape[0] // 2
     rows = tok * top
+    size = 2 * tok * lanes // 128
+    total = 0.0
+    for block in packed:
+        total = total + unpack_z(block[:size], 2 * tok, lanes).astype(F32)
     block = iota((1, lanes), 1) // rank * groups + (at[0] if groups == 2 else 0)
     for core in range(2):
-        z = zs[0][core].astype(F32)
-        for other in zs[1:]:
-            z = z + other[core].astype(F32)
+        z = total[core * tok : (core + 1) * tok]
         names, weights = pair_columns(pairs[core][:top], pairs[core][top:])
         z = jnp.broadcast_to(z[:, None], (tok, top, lanes)).reshape(rows, lanes)
         z = jnp.where(names == block.astype(F32), z * weights, 0.0).astype(BF16)
@@ -191,12 +270,11 @@
     lanes = count // 2 * rank
     part = hidden // n_dp
     scale = 1.0 / math.sqrt(rows)
-    own = lax.axis_index("expert")
     half = lax.axis_index("dp")
     me = lax.axis_index(AXES)
     core = me % 2
     place = me // line
-    lower = me // 2 % low
+    at = jnp.stack([core, me // 2 % low, place, half])
     shape = jax.ShapeDtypeStruct
 
     def exchange(block, step):
@@ -218,8 +296,6 @@
     *y, pairs = call(
         functools.partial(y_kernel, groups),
         [shape((tok, lanes), BF16)] * groups + [shape((2 * top, tok), F32)],
-        4 * rows * hidden * rank,
-        2 * rows * hidden,
         [SMEM] + [HBM] * 4,
         [
             pltpu.VMEM((rows, hidden), BF16),
@@ -228,11 +304,12 @@
             pltpu.VMEM((top, tok), F32),
             pltpu.SemaphoreType.DMA((7,)),
         ],
-        core.reshape(1),
+        at,
         cot,
         sketch.T,
         expert_ids.T,
         route_probs.T,
+        limit=LARGE,
     )
     send, xs = lax.optimization_barrier((y[-1], xs))
     pairs = [pairs, exchange(pairs, 1)]
@@ -245,18 +322,20 @@
         step *= 2
     xs = [b for x in xs for b in (x, exchange(x, 1))]
 
+    size = 2 * tok * lanes // 128
+    packed = size + rank * share // 128
     if n_dp == 1:
-        columns, *zs = call(
-            functools.partial(z_kernel, len(xs) // 2),
-            [shape((lanes, share), BF16)] + [shape((2, tok, lanes), BF16)] * SLICES,
-            2 * count * tok * lanes * share * 3 // 2,
-            2 * count * tok * (lanes + share),
-            [HBM] * (len(xs) + len(ys)),
+        zs = call(
+            functools.partial(z_kernel, len(xs) // 2, low),
+            [shape((packed, 128), BF16)] * SLICES,
+            [SMEM] + [HBM] * (len(xs) + len(ys)),
             [
                 pltpu.VMEM((count * tok, share), BF16),
                 pltpu.VMEM((len(xs), 2, tok, lanes), BF16),
+                pltpu.VMEM((lanes, share), BF16),
                 pltpu.SemaphoreType.DMA((2 * len(xs),)),
             ],
+            at,
             *xs,
             *ys,
         )
@@ -266,29 +345,33 @@
         right = jnp.stack(right).reshape(-1, 2, 2, tok, share).swapaxes(1, 2)
         columns = dot(left, right.reshape(-1, share), 0, 0).astype(BF16)
         zs = [
-            jnp.stack([dot(x[i : i + tok], columns, 1, 1).astype(BF16) for x in xs[b : b + 2]])
+            jnp.concatenate([dot(x[i : i + tok], columns, 1, 1) for x in xs[b : b + 2]], axis=0)
             for b in (0, 2)
             for i in (0, tok)
         ]
-    zs = zs[:1] + [exchange(zs[j], j * line) for j in range(1, SLICES)]
-    columns, _ = lax.optimization_barrier((columns, zs[1]))
+        zs = [
+            pack(
+                z.astype(BF16),
+                lax.dynamic_slice_in_dim(columns, ((place ^ j) * low + at[1]) * rank, rank, axis=0),
+            )
+            for j, z in enumerate(zs)
+        ]
+    zs = list(zs[:1]) + [exchange(zs[j], j * line) for j in range(1, SLICES)]
 
     piece = part // CHUNKS
-    flops = 4 * rows * SLICES * rank * piece
     outs = [shape((SLICES * rank, piece), BF16)] * low
     work = [pltpu.VMEM((2 * rows, piece), BF16), pltpu.SemaphoreType.DMA((2,))]
     spread, *blocks = call(
         functools.partial(first_kernel, groups),
         [shape((lanes, 2 * rows), BF16)] + outs,
-        flops,
-        4 * rows * piece,
         [SMEM] + [VMEM] * (SLICES + 2) + [HBM] * 2,
         [pltpu.VMEM((lanes, 2 * rows), BF16)] + work,
-        jnp.stack([core, lower]),
+        at,
         *zs,
         *pairs,
         mine,
         other,
+        limit=LARGE,
     )
     chunks = [blocks]
     for chunk in range(1, CHUNKS):
@@ -296,15 +379,23 @@
             call(
                 functools.partial(next_kernel, chunk * piece),
                 outs,
-                flops,
-                4 * rows * piece,
                 [VMEM] + [HBM] * 2,
                 work,
                 spread,
                 mine,
                 other,
+                limit=LARGE,
             )
         )
+    zs, _ = lax.optimization_barrier((zs, chunks[-1][0]))
+    inverse, basis = call(
+        functools.partial(inverse_kernel, size),
+        [shape((rank, rank), F32), shape((rank, width // n_dp), F32)],
+        [SMEM] + [VMEM] * SLICES,
+        [pltpu.VMEM((SLICES, rank, share), BF16)],
+        at,
+        *zs,
+    )
     sums = []
     for chunk in chunks:
         blocks = [term.reshape(SLICES, rank, piece) for term in chunk]
@@ -316,30 +407,20 @@
             ]
             step *= 2
         sums.append(blocks[0])
-    totals = []
+    sums[0], inverse = lax.optimization_barrier((sums[0], inverse))
+    blocks = []
     for block in sums:
-        gone = [
-            exchange(lax.dynamic_index_in_dim(block, place ^ j, 0, False), j * line)
-            for j in range(1, SLICES)
-        ]
-        total = lax.dynamic_index_in_dim(block, place, 0, False).astype(F32)
-        for other in gone:
-            total = total + other.astype(F32)
-        totals.append(total)
-
-    parts = columns.reshape(SLICES, n_expert // SLICES // groups, rank, share)
-    parts = lax.dynamic_index_in_dim(parts, own % (n_expert // SLICES) // groups, 1, False)
-    parts = [lax.dynamic_index_in_dim(parts, place ^ j, 0, False) for j in range(SLICES)]
-    parts = jnp.stack(parts[:1] + [exchange(parts[j], j * line) for j in range(1, SLICES)])
-    parts = [lax.dynamic_index_in_dim(parts, place ^ j, 0, False) for j in range(SLICES)]
-    range_rows = jnp.concatenate(parts, axis=1).astype(F32)
-    gram = lax.dot_general(range_rows, range_rows, (((1,), (1,)), ((), ())), precision=HIGH)
-    lower = jnp.linalg.cholesky(gram)
-    inverse = jax.scipy.linalg.solve_triangular(lower, jnp.eye(rank, dtype=F32), lower=True)
-    kept = lax.dynamic_slice_in_dim(range_rows, half * (width // n_dp), width // n_dp, axis=1)
-    basis = jnp.dot(inverse * math.sqrt(width), kept, precision=HIGH)
-    coeffs = [jnp.dot(inverse * scale, total, precision=HIGH) for total in totals]
-    return basis[None], jnp.concatenate(coeffs, axis=1)[None]
+        own = [lax.dynamic_index_in_dim(block, place ^ j, 0, False) for j in range(SLICES)]
+        blocks += own[:1] + [exchange(own[j], j * line) for j in range(1, SLICES)]
+    [coeffs] = call(
+        functools.partial(coeffs_kernel, scale),
+        [shape((rank, part), F32)],
+        [VMEM] * (1 + len(blocks)),
+        [],
+        inverse,
+        *blocks,
+    )
+    return basis[None], coeffs[None]
 
 
 def solution(mesh):

time: 88.2 us -> 89.3 us (1.012)
  Pallas kernels: 13.2 us -> 22 us
  waiting for transfers between devices: 22.6 us -> 28.8 us
  other arithmetic: 7.78 us -> 2.53 us
  starting transfers between devices: 36.1 us -> 31.5 us
  matrix products: 2.06 us -> 0 us
  local copies, waits for them, and re-layouts: 5.14 us -> 3.15 us
    pallas_call x4 -> x6, Pallas kernels: 13.2 us -> 22 us  [call(): pl.pallas_call(body, out_shape=shapes, in_specs=spaces, out_specs=[VMEM]...]
    ppermute x30 -> x27, waiting for transfers between devices: 22.6 us -> 28.8 us  [exchange(): return lax.ppermute(block, AXES, [(i, i ^ step) for i in range(count)])]
    another operation x7 -> x1, other arithmetic: 6.8 us -> 0.58 us  [shards(): at = jnp.stack([core, me // 2 % low, place, half])]
    ppermute x30 -> x27, starting transfers between devices: 36.1 us -> 31.5 us  [exchange(): return lax.ppermute(block, AXES, [(i, i ^ step) for i in range(count)])]
    dot_general x4 -> x0, matrix products: 1.87 us -> none  [the longest x1 1.11 us: shards(): basis = jnp.dot(inverse * math.sqrt(width), kept, precision=HIGH)]
    unnamed x10 -> x30, local copies, waits for them, and re-layouts: 3.9 us -> 2.04 us
    convert_element_type x2, other arithmetic: 0.15 us -> 1.14 us  [shards(): (keep.astype(F32) + exchange(send, step).astype(F32)).astype(BF16)]
  transfers between devices with their start and end apart: 30 -> 27, of which waited for: 12 -> 12; matrix products, arithmetic and copies ran while one was open for 10% -> 4% of each run, Pallas kernels for 11% -> 14%
where the time goes in v8:
time: 89.3 us; the launch traced here: 88.9 us
  starting transfers between devices  31.5 us (35%)
  waiting for transfers between devices  28.8 us (32%)
  Pallas kernels  22 us (25%)
  local copies, waits for them, and re-layouts  3.15 us (4%)
  other arithmetic  2.53 us (3%)
    ppermute x27, starting transfers between devices, exchange(): return lax.ppermute(block, AXES, [(i, i ^ step) for i in range(count)])  31.5 us
    ppermute x27, waiting for transfers between devices, exchange(): return lax.ppermute(block, AXES, [(i, i ^ step) for i in range(count)])  28.8 us
    pallas_call x6, Pallas kernels, call(): pl.pallas_call(body, out_shape=shapes, in_specs=spaces, out_specs=[VMEM]...  22 us
    unnamed x30, local copies, waits for them, and re-layouts  2.04 us
  transfers between devices with their start and end apart: 27, of which 12 were waited for; matrix products, arithmetic and copies ran while one was open for 4% of the time, Pallas kernels for 14%

profile of v8, /device:TPU:0, one launch (start us, length us, event | category | flops | bytes accessed | tf_op | source)
XLA Modules:
  0.0 88.9 jit_solution(18042894550040503996)
XLA Ops:
  2.2 3.7 %collective-permute-start.1 = (bf16[48,896]{1,0:T(8,128)(2,1)S(1)}, bf16[48,896]{1,0:T(8,128)(2,1)S(1)}, u32[]{:S(2)}, u32[]{:S(2)}) collective-permute-start(bf16[48,896]{1,0:T(8,128)(2,1)S(1)} %get-tuple-element.48), channel_id=1, source_target_pairs={{0,8},{1,9},{2,10},{3,11},{4,12},{5,13},{6,14},{7,15},{8,0},{9,1},... | collective-permute-start | bytes 258056 | tf_op jit(solution)/shard_map/ppermute | solution.py:281
  5.9 1.6 %collective-permute-start = (bf16[48,896]{1,0:T(8,128)(2,1)S(1)}, bf16[48,896]{1,0:T(8,128)(2,1)S(1)}, u32[]{:S(2)}, u32[]{:S(2)}) collective-permute-start(bf16[48,896]{1,0:T(8,128)(2,1)S(1)} %get-tuple-element.49), channel_id=1, source_target_pairs={{0,4},{1,5},{2,6},{3,7},{4,0},{5,1},{6,2},{7,3},{8,12},{9,13},{10,... | collective-permute-start | bytes 258056 | tf_op jit(solution)/shard_map/ppermute | solution.py:281
  8.1 5.8 %shard_map.68 = (bf16[48,256]{1,0:T(8,128)(2,1)}, bf16[48,256]{1,0:T(8,128)(2,1)}, f32[16,48]{1,0:T(8,128)}) custom-call(s32[4]{0:T(128)} %pad_add_fusion.core.at, bf16[384,2560]{1,0:T(8,128)(2,1)} %bitcast.39, f32[32,2560]{1,0:T(8,128)} %bitcast.42, s32[8,48]{1,0:T(8,128)} %bitcast.51, f32[8,48]{1,0:T(8,128)} %bitcast.52), custom_call_target="tpu_custom_call" | custom-call | flops 1 | bytes 1 | tf_op jit(solution)/shard_map/pallas_call | solution.py:33
  14.1 1.4 %collective-permute-done.9 = bf16[48,256]{1,0:T(8,128)(2,1)S(1)} collective-permute-done((bf16[48,256]{1,0:T(8,128)(2,1)}, bf16[48,256]{1,0:T(8,128)(2,1)S(1)}, u32[]{:S(2)}, u32[]{:S(2)}) %collective-permute-start.9) | collective-permute-done | bytes 24608 | tf_op jit(solution)/shard_map/ppermute | solution.py:281
  16.2 3.2 %collective-permute-start.11 = (bf16[2,48,256]{2,1,0:T(8,128)(2,1)S(1)}, bf16[2,48,256]{2,1,0:T(8,128)(2,1)S(1)}, u32[]{:S(2)}, u32[]{:S(2)}) collective-permute-start(bf16[2,48,256]{2,1,0:T(8,128)(2,1)S(1)} %get-tuple-element.61), channel_id=1, source_target_pairs={{0,8},{1,9},{2,10},{3,11},{4,12},{5,13},{6,14},{7,15},{8,0},{9,1},... | collective-permute-start | bytes 147464 | tf_op jit(solution)/shard_map/ppermute | solution.py:281
  21.0 1.5 %collective-permute-start.5 = (bf16[96,896]{1,0:T(8,128)(2,1)S(1)}, bf16[96,896]{1,0:T(8,128)(2,1)S(1)}, u32[]{:S(2)}, u32[]{:S(2)}) collective-permute-start(bf16[96,896]{1,0:T(8,128)(2,1)S(1)} %pad_maximum_fusion.1.refs_0_), channel_id=1, source_target_pairs={{0,2},{1,3},{2,0},{3,1},{4,6},{5,7},{6,4},{7,5},{8,10},{9,11},{10,... | collective-permute-start | bytes 516104 | tf_op jit(solution)/shard_map/ppermute | solution.py:281
  23.5 1.5 %collective-permute-start.7 = (bf16[96,896]{1,0:T(8,128)(2,1)S(1)}, bf16[96,896]{1,0:T(8,128)(2,1)S(1)}, u32[]{:S(2)}, u32[]{:S(2)}) collective-permute-start(bf16[96,896]{1,0:T(8,128)(2,1)S(1)} %pad_maximum_fusion.2.refs_2_), channel_id=1, source_target_pairs={{0,2},{1,3},{2,0},{3,1},{4,6},{5,7},{6,4},{7,5},{8,10},{9,11},{10,... | collective-permute-start | bytes 516104 | tf_op jit(solution)/shard_map/ppermute | solution.py:281
  25.0 1.4 %collective-permute-done.12 = bf16[2,48,256]{2,1,0:T(8,128)(2,1)S(1)} collective-permute-done((bf16[2,48,256]{2,1,0:T(8,128)(2,1)S(1)}, bf16[2,48,256]{2,1,0:T(8,128)(2,1)S(1)}, u32[]{:S(2)}, u32[]{:S(2)}) %collective-permute-start.12) | collective-permute-done | bytes 49184 | tf_op jit(solution)/shard_map/ppermute | solution.py:281
  26.5 1.6 %collective-permute-start.13 = (bf16[4,2,48,256]{3,2,1,0:T(8,128)(2,1)S(1)}, bf16[4,2,48,256]{3,2,1,0:T(8,128)(2,1)S(1)}, u32[]{:S(2)}, u32[]{:S(2)}) collective-permute-start(bf16[4,2,48,256]{3,2,1,0:T(8,128)(2,1)S(1)} %pad_maximum_fusion.refs_8_), channel_id=1, source_target_pairs={{0,2},{1,3},{2,0},{3,1},{4,6},{5,7},{6,4},{7,5},{8,10},{9,11},{10,... | collective-permute-start | bytes 589832 | tf_op jit(solution)/shard_map/ppermute | solution.py:281
  28.6 3.0 %collective-permute-done.7.refs_6_ = bf16[96,896]{1,0:T(8,128)(2,1)S(1)} collective-permute-done((bf16[96,896]{1,0:T(8,128)(2,1)S(1)}, bf16[96,896]{1,0:T(8,128)(2,1)S(1)}, u32[]{:S(2)}, u32[]{:S(2)}) %collective-permute-start.7) | collective-permute-done | bytes 172064 | tf_op jit(solution)/shard_map/ppermute | solution.py:281
  31.6 3.2 %collective-permute-done.13.refs_9_ = bf16[4,2,48,256]{3,2,1,0:T(8,128)(2,1)S(1)} collective-permute-done((bf16[4,2,48,256]{3,2,1,0:T(8,128)(2,1)S(1)}, bf16[4,2,48,256]{3,2,1,0:T(8,128)(2,1)S(1)}, u32[]{:S(2)}, u32[]{:S(2)}) %collective-permute-start.13) | collective-permute-done | bytes 196640 | tf_op jit(solution)/shard_map/ppermute | solution.py:281
  34.8 3.7 %shard_map.69 = (bf16[416,128]{1,0:T(8,128)(2,1)S(1)}, bf16[416,128]{1,0:T(8,128)(2,1)S(1)}, bf16[416,128]{1,0:T(8,128)(2,1)S(1)}, bf16[416,128]{1,0:T(8,128)(2,1)S(1)}) custom-call(s32[4]{0:T(128)S(1)} %copy-done.8, bf16[96,896]{1,0:T(8,128)(2,1)S(1)} %pad_maximum_fusion.1.refs_0_, bf16[96,896]{1,0:T(8,128)(2,1)S(1)} %collective-permute-done.3.refs_1_, ...), custom_call_target="tpu_custom_call" | custom-call | flops 1 | bytes 1 | tf_op jit(solution)/shard_map/pallas_call | solution.py:33
  39.6 3.2 %collective-permute-start.15 = (bf16[416,128]{1,0:T(8,128)(2,1)S(1)}, bf16[416,128]{1,0:T(8,128)(2,1)S(1)}, u32[]{:S(2)}, u32[]{:S(2)}) collective-permute-start(bf16[416,128]{1,0:T(8,128)(2,1)S(1)} %get-tuple-element.32), channel_id=1, source_target_pairs={{0,8},{1,9},{2,10},{3,11},{4,12},{5,13},{6,14},{7,15},{8,0},{9,1},... | collective-permute-start | bytes 319496 | tf_op jit(solution)/shard_map/ppermute | solution.py:281
  45.2 6.1 %collective-permute-done.15.z2.p2 = bf16[416,128]{1,0:T(8,128)(2,1)S(1)} collective-permute-done((bf16[416,128]{1,0:T(8,128)(2,1)S(1)}, bf16[416,128]{1,0:T(8,128)(2,1)S(1)}, u32[]{:S(2)}, u32[]{:S(2)}) %collective-permute-start.15) | collective-permute-done | bytes 106528 | tf_op jit(solution)/shard_map/ppermute | solution.py:281
  52.6 4.2 %shard_map.70 = (bf16[256,768]{1,0:T(8,128)(2,1)}, bf16[128,1280]{1,0:T(8,128)(2,1)}, bf16[128,1280]{1,0:T(8,128)(2,1)}) custom-call(s32[4]{0:T(128)} %pad_add_fusion.core.at, bf16[416,128]{1,0:T(8,128)(2,1)} %copy-done, bf16[416,128]{1,0:T(8,128)(2,1)} %copy-done.2, bf16[416,128]{1,0:T(8,128)(2,1)} %copy-done.4, bf16[416,128]{1,0:T(8,128)(2,1)} %copy-done.6, ...), custom_call_target="tpu_custom_call" | custom-call | flops 1 | bytes 1 | tf_op jit(solution)/shard_map/pallas_call | solution.py:33
  56.9 4.1 %shard_map.71 = (bf16[128,1280]{1,0:T(8,128)(2,1)}, bf16[128,1280]{1,0:T(8,128)(2,1)}) custom-call(bf16[256,768]{1,0:T(8,128)(2,1)} %get-tuple-element.35.spread, bf16[384,2560]{1,0:T(8,128)(2,1)} %bitcast.41, bf16[384,2560]{1,0:T(8,128)(2,1)} %copy-done.10), custom_call_target="tpu_custom_call" | custom-call | flops 1 | bytes 1 | tf_op jit(solution)/shard_map/pallas_call | solution.py:33
  60.9 1.6 %collective-permute-start.23 = (bf16[4,32,1280]{2,1,0:T(8,128)(2,1)}, bf16[4,32,1280]{2,1,0:T(8,128)(2,1)S(1)}, u32[]{:S(2)}, u32[]{:S(2)}) collective-permute-start(bf16[4,32,1280]{2,1,0:T(8,128)(2,1)} %bitcast.55), channel_id=1, source_target_pairs={{0,2},{1,3},{2,0},{3,1},{4,6},{5,7},{6,4},{7,5},{8,10},{9,11},{10,... | collective-permute-start | bytes 983048 | tf_op jit(solution)/shard_map/ppermute | solution.py:281
  63.0 3.3 %shard_map.72 = (f32[32,32]{1,0:T(8,128)S(1)}, f32[32,3584]{1,0:T(8,128)}) custom-call(s32[4]{0:T(128)S(1)} %copy-done.9, bf16[416,128]{1,0:T(8,128)(2,1)S(1)} %copy-done.1, bf16[416,128]{1,0:T(8,128)(2,1)S(1)} %copy-done.3, bf16[416,128]{1,0:T(8,128)(2,1)S(1)} %copy-done.5, bf16[416,128]{1,0:T(8,128)(2,1)S(1)} %copy-done.7), custom_call_target="tpu_custom_call" | custom-call | flops 1 | bytes 1 | tf_op jit(solution)/shard_map/pallas_call | solution.py:33
  66.3 5.5 %collective-permute-done.23 = bf16[4,32,1280]{2,1,0:T(8,128)(2,1)S(1)} collective-permute-done((bf16[4,32,1280]{2,1,0:T(8,128)(2,1)}, bf16[4,32,1280]{2,1,0:T(8,128)(2,1)S(1)}, u32[]{:S(2)}, u32[]{:S(2)}) %collective-permute-start.23) | collective-permute-done | bytes 327712 | tf_op jit(solution)/shard_map/ppermute | solution.py:281
  74.1 2.1 %collective-permute-start.25 = (bf16[32,1280]{1,0:T(8,128)(2,1)S(1)}, bf16[32,1280]{1,0:T(8,128)(2,1)S(1)}, u32[]{:S(2)}, u32[]{:S(2)}) collective-permute-start(bf16[32,1280]{1,0:T(8,128)(2,1)S(1)} %get-tuple-element.53), channel_id=1, source_target_pairs={{0,8},{1,9},{2,10},{3,11},{4,12},{5,13},{6,14},{7,15},{8,0},{9,1},... | collective-permute-start | bytes 245768 | tf_op jit(solution)/shard_map/ppermute | solution.py:281
  78.8 1.5 %collective-permute-start.21 = (bf16[32,1280]{1,0:T(8,128)(2,1)S(1)}, bf16[32,1280]{1,0:T(8,128)(2,1)S(1)}, u32[]{:S(2)}, u32[]{:S(2)}) collective-permute-start(bf16[32,1280]{1,0:T(8,128)(2,1)S(1)} %get-tuple-element.57), channel_id=1, source_target_pairs={{0,8},{1,9},{2,10},{3,11},{4,12},{5,13},{6,14},{7,15},{8,0},{9,1},... | collective-permute-start | bytes 245768 | tf_op jit(solution)/shard_map/ppermute | solution.py:281
  80.2 2.1 %collective-permute-start.20 = (bf16[32,1280]{1,0:T(8,128)(2,1)S(1)}, bf16[32,1280]{1,0:T(8,128)(2,1)S(1)}, u32[]{:S(2)}, u32[]{:S(2)}) collective-permute-start(bf16[32,1280]{1,0:T(8,128)(2,1)S(1)} %get-tuple-element.58), channel_id=1, source_target_pairs={{0,4},{1,5},{2,6},{3,7},{4,0},{5,1},{6,2},{7,3},{8,12},{9,13},{10,... | collective-permute-start | bytes 245768 | tf_op jit(solution)/shard_map/ppermute | solution.py:281
  82.4 3.4 %collective-permute-done.25.refs_6_ = bf16[32,1280]{1,0:T(8,128)(2,1)S(1)} collective-permute-done((bf16[32,1280]{1,0:T(8,128)(2,1)S(1)}, bf16[32,1280]{1,0:T(8,128)(2,1)S(1)}, u32[]{:S(2)}, u32[]{:S(2)}) %collective-permute-start.25) | collective-permute-done | bytes 81952 | tf_op jit(solution)/shard_map/ppermute | solution.py:281
  85.8 2.0 %collective-permute-done.21.refs_2_ = bf16[32,1280]{1,0:T(8,128)(2,1)S(1)} collective-permute-done((bf16[32,1280]{1,0:T(8,128)(2,1)S(1)}, bf16[32,1280]{1,0:T(8,128)(2,1)S(1)}, u32[]{:S(2)}, u32[]{:S(2)}) %collective-permute-start.21) | collective-permute-done | bytes 81952 | tf_op jit(solution)/shard_map/ppermute | solution.py:281
  (76 shorter events, 17.4 us)
Async XLA Ops:
  0.6 50.6 %collective-permute-start.18 = (bf16[384,2560]{1,0:T(8,128)(2,1)}, bf16[384,2560]{1,0:T(8,128)(2,1)S(1)}, u32[]{:S(2)}, u32[]{:S(2)}) collective-permute-start(bf16[384,2560]{1,0:T(8,128)(2,1)} %bitcast.38), channel_id=1, source_target_pairs={{0,1},{1,0},{2,3},{3,2},{4,5},{5,4},{6,7},{7,6},{8,9},{9,8},{10,11... | collective-permute-start | bytes 5898248 | tf_op jit(solution)/shard_map/ppermute | solution.py:281
  2.2 11.8 %collective-permute-start.1 = (bf16[48,896]{1,0:T(8,128)(2,1)S(1)}, bf16[48,896]{1,0:T(8,128)(2,1)S(1)}, u32[]{:S(2)}, u32[]{:S(2)}) collective-permute-start(bf16[48,896]{1,0:T(8,128)(2,1)S(1)} %get-tuple-element.48), channel_id=1, source_target_pairs={{0,8},{1,9},{2,10},{3,11},{4,12},{5,13},{6,14},{7,15},{8,0},{9,1},... | collective-permute-start | bytes 258056 | tf_op jit(solution)/shard_map/ppermute | solution.py:281
  5.9 8.0 %collective-permute-start = (bf16[48,896]{1,0:T(8,128)(2,1)S(1)}, bf16[48,896]{1,0:T(8,128)(2,1)S(1)}, u32[]{:S(2)}, u32[]{:S(2)}) collective-permute-start(bf16[48,896]{1,0:T(8,128)(2,1)S(1)} %get-tuple-element.49), channel_id=1, source_target_pairs={{0,4},{1,5},{2,6},{3,7},{4,0},{5,1},{6,2},{7,3},{8,12},{9,13},{10,... | collective-permute-start | bytes 258056 | tf_op jit(solution)/shard_map/ppermute | solution.py:281
  7.5 6.5 %collective-permute-start.2 = (bf16[48,896]{1,0:T(8,128)(2,1)S(1)}, bf16[48,896]{1,0:T(8,128)(2,1)S(1)}, u32[]{:S(2)}, u32[]{:S(2)}) collective-permute-start(bf16[48,896]{1,0:T(8,128)(2,1)S(1)} %get-tuple-element.51), channel_id=1, source_target_pairs={{0,12},{1,13},{2,14},{3,15},{4,8},{5,9},{6,10},{7,11},{8,4},{9,5},... | collective-permute-start | bytes 258056 | tf_op jit(solution)/shard_map/ppermute | solution.py:281
  16.2 6.5 %collective-permute-start.11 = (bf16[2,48,256]{2,1,0:T(8,128)(2,1)S(1)}, bf16[2,48,256]{2,1,0:T(8,128)(2,1)S(1)}, u32[]{:S(2)}, u32[]{:S(2)}) collective-permute-start(bf16[2,48,256]{2,1,0:T(8,128)(2,1)S(1)} %get-tuple-element.61), channel_id=1, source_target_pairs={{0,8},{1,9},{2,10},{3,11},{4,12},{5,13},{6,14},{7,15},{8,0},{9,1},... | collective-permute-start | bytes 147464 | tf_op jit(solution)/shard_map/ppermute | solution.py:281
  19.5 4.1 %collective-permute-start.10 = (bf16[2,48,256]{2,1,0:T(8,128)(2,1)S(1)}, bf16[2,48,256]{2,1,0:T(8,128)(2,1)S(1)}, u32[]{:S(2)}, u32[]{:S(2)}) collective-permute-start(bf16[2,48,256]{2,1,0:T(8,128)(2,1)S(1)} %get-tuple-element.61), channel_id=1, source_target_pairs={{0,4},{1,5},{2,6},{3,7},{4,0},{5,1},{6,2},{7,3},{8,12},{9,13},{10,... | collective-permute-start | bytes 147464 | tf_op jit(solution)/shard_map/ppermute | solution.py:281
  20.6 5.9 %collective-permute-start.12 = (bf16[2,48,256]{2,1,0:T(8,128)(2,1)S(1)}, bf16[2,48,256]{2,1,0:T(8,128)(2,1)S(1)}, u32[]{:S(2)}, u32[]{:S(2)}) collective-permute-start(bf16[2,48,256]{2,1,0:T(8,128)(2,1)S(1)} %get-tuple-element.61), channel_id=1, source_target_pairs={{0,12},{1,13},{2,14},{3,15},{4,8},{5,9},{6,10},{7,11},{8,4},{9,5},... | collective-permute-start | bytes 147464 | tf_op jit(solution)/shard_map/ppermute | solution.py:281
  21.0 7.1 %collective-permute-start.5 = (bf16[96,896]{1,0:T(8,128)(2,1)S(1)}, bf16[96,896]{1,0:T(8,128)(2,1)S(1)}, u32[]{:S(2)}, u32[]{:S(2)}) collective-permute-start(bf16[96,896]{1,0:T(8,128)(2,1)S(1)} %pad_maximum_fusion.1.refs_0_), channel_id=1, source_target_pairs={{0,2},{1,3},{2,0},{3,1},{4,6},{5,7},{6,4},{7,5},{8,10},{9,11},{10,... | collective-permute-start | bytes 516104 | tf_op jit(solution)/shard_map/ppermute | solution.py:281
  22.7 5.4 %collective-permute-start.3 = (bf16[96,896]{1,0:T(8,128)(2,1)S(1)}, bf16[96,896]{1,0:T(8,128)(2,1)S(1)}, u32[]{:S(2)}, u32[]{:S(2)}) collective-permute-start(bf16[96,896]{1,0:T(8,128)(2,1)S(1)} %pad_maximum_fusion.1.refs_0_), channel_id=1, source_target_pairs={{0,1},{1,0},{2,3},{3,2},{4,5},{5,4},{6,7},{7,6},{8,9},{9,8},{10,11... | collective-permute-start | bytes 516104 | tf_op jit(solution)/shard_map/ppermute | solution.py:281
  23.5 8.1 %collective-permute-start.7 = (bf16[96,896]{1,0:T(8,128)(2,1)S(1)}, bf16[96,896]{1,0:T(8,128)(2,1)S(1)}, u32[]{:S(2)}, u32[]{:S(2)}) collective-permute-start(bf16[96,896]{1,0:T(8,128)(2,1)S(1)} %pad_maximum_fusion.2.refs_2_), channel_id=1, source_target_pairs={{0,2},{1,3},{2,0},{3,1},{4,6},{5,7},{6,4},{7,5},{8,10},{9,11},{10,... | collective-permute-start | bytes 516104 | tf_op jit(solution)/shard_map/ppermute | solution.py:281
  26.5 8.3 %collective-permute-start.13 = (bf16[4,2,48,256]{3,2,1,0:T(8,128)(2,1)S(1)}, bf16[4,2,48,256]{3,2,1,0:T(8,128)(2,1)S(1)}, u32[]{:S(2)}, u32[]{:S(2)}) collective-permute-start(bf16[4,2,48,256]{3,2,1,0:T(8,128)(2,1)S(1)} %pad_maximum_fusion.refs_8_), channel_id=1, source_target_pairs={{0,2},{1,3},{2,0},{3,1},{4,6},{5,7},{6,4},{7,5},{8,10},{9,11},{10,... | collective-permute-start | bytes 589832 | tf_op jit(solution)/shard_map/ppermute | solution.py:281
  28.1 3.6 %collective-permute-start.4 = (bf16[96,896]{1,0:T(8,128)(2,1)S(1)}, bf16[96,896]{1,0:T(8,128)(2,1)S(1)}, u32[]{:S(2)}, u32[]{:S(2)}) collective-permute-start(bf16[96,896]{1,0:T(8,128)(2,1)S(1)} %pad_maximum_fusion.2.refs_2_), channel_id=1, source_target_pairs={{0,1},{1,0},{2,3},{3,2},{4,5},{5,4},{6,7},{7,6},{8,9},{9,8},{10,11... | collective-permute-start | bytes 516104 | tf_op jit(solution)/shard_map/ppermute | solution.py:281
  28.1 6.7 %collective-permute-start.6 = (bf16[96,896]{1,0:T(8,128)(2,1)S(1)}, bf16[96,896]{1,0:T(8,128)(2,1)S(1)}, u32[]{:S(2)}, u32[]{:S(2)}) collective-permute-start(bf16[96,896]{1,0:T(8,128)(2,1)S(1)} %collective-permute-done.5.refs_4_), channel_id=1, source_target_pairs={{0,1},{1,0},{2,3},{3,2},{4,5},{5,4},{6,7},{7,6},{8,9},{9,8},{10,11... | collective-permute-start | bytes 516104 | tf_op jit(solution)/shard_map/ppermute | solution.py:281
  39.1 6.0 %collective-permute-start.14 = (bf16[416,128]{1,0:T(8,128)(2,1)S(1)}, bf16[416,128]{1,0:T(8,128)(2,1)S(1)}, u32[]{:S(2)}, u32[]{:S(2)}) collective-permute-start(bf16[416,128]{1,0:T(8,128)(2,1)S(1)} %get-tuple-element.31), channel_id=1, source_target_pairs={{0,4},{1,5},{2,6},{3,7},{4,0},{5,1},{6,2},{7,3},{8,12},{9,13},{10,... | collective-permute-start | bytes 319496 | tf_op jit(solution)/shard_map/ppermute | solution.py:281
  39.6 11.6 %collective-permute-start.15 = (bf16[416,128]{1,0:T(8,128)(2,1)S(1)}, bf16[416,128]{1,0:T(8,128)(2,1)S(1)}, u32[]{:S(2)}, u32[]{:S(2)}) collective-permute-start(bf16[416,128]{1,0:T(8,128)(2,1)S(1)} %get-tuple-element.32), channel_id=1, source_target_pairs={{0,8},{1,9},{2,10},{3,11},{4,12},{5,13},{6,14},{7,15},{8,0},{9,1},... | collective-permute-start | bytes 319496 | tf_op jit(solution)/shard_map/ppermute | solution.py:281
  42.8 8.4 %collective-permute-start.16 = (bf16[416,128]{1,0:T(8,128)(2,1)S(1)}, bf16[416,128]{1,0:T(8,128)(2,1)S(1)}, u32[]{:S(2)}, u32[]{:S(2)}) collective-permute-start(bf16[416,128]{1,0:T(8,128)(2,1)S(1)} %get-tuple-element.33), channel_id=1, source_target_pairs={{0,12},{1,13},{2,14},{3,15},{4,8},{5,9},{6,10},{7,11},{8,4},{9,5},... | collective-permute-start | bytes 319496 | tf_op jit(solution)/shard_map/ppermute | solution.py:281
  60.9 10.9 %collective-permute-start.23 = (bf16[4,32,1280]{2,1,0:T(8,128)(2,1)}, bf16[4,32,1280]{2,1,0:T(8,128)(2,1)S(1)}, u32[]{:S(2)}, u32[]{:S(2)}) collective-permute-start(bf16[4,32,1280]{2,1,0:T(8,128)(2,1)} %bitcast.55), channel_id=1, source_target_pairs={{0,2},{1,3},{2,0},{3,1},{4,6},{5,7},{6,4},{7,5},{8,10},{9,11},{10,... | collective-permute-start | bytes 983048 | tf_op jit(solution)/shard_map/ppermute | solution.py:281
  62.5 14.9 %collective-permute-start.19 = (bf16[4,32,1280]{2,1,0:T(8,128)(2,1)S(1)}, bf16[4,32,1280]{2,1,0:T(8,128)(2,1)S(1)}, u32[]{:S(2)}, u32[]{:S(2)}) collective-permute-start(bf16[4,32,1280]{2,1,0:T(8,128)(2,1)S(1)} %bitcast.54), channel_id=1, source_target_pairs={{0,2},{1,3},{2,0},{3,1},{4,6},{5,7},{6,4},{7,5},{8,10},{9,11},{10,... | collective-permute-start | bytes 983048 | tf_op jit(solution)/shard_map/ppermute | solution.py:281
  73.0 7.3 %collective-permute-start.26 = (bf16[32,1280]{1,0:T(8,128)(2,1)S(1)}, bf16[32,1280]{1,0:T(8,128)(2,1)S(1)}, u32[]{:S(2)}, u32[]{:S(2)}) collective-permute-start(bf16[32,1280]{1,0:T(8,128)(2,1)S(1)} %get-tuple-element.52), channel_id=1, source_target_pairs={{0,12},{1,13},{2,14},{3,15},{4,8},{5,9},{6,10},{7,11},{8,4},{9,5},... | collective-permute-start | bytes 245768 | tf_op jit(solution)/shard_map/ppermute | solution.py:281
  74.1 11.7 %collective-permute-start.25 = (bf16[32,1280]{1,0:T(8,128)(2,1)S(1)}, bf16[32,1280]{1,0:T(8,128)(2,1)S(1)}, u32[]{:S(2)}, u32[]{:S(2)}) collective-permute-start(bf16[32,1280]{1,0:T(8,128)(2,1)S(1)} %get-tuple-element.53), channel_id=1, source_target_pairs={{0,8},{1,9},{2,10},{3,11},{4,12},{5,13},{6,14},{7,15},{8,0},{9,1},... | collective-permute-start | bytes 245768 | tf_op jit(solution)/shard_map/ppermute | solution.py:281
  76.2 9.6 %collective-permute-start.24 = (bf16[32,1280]{1,0:T(8,128)(2,1)S(1)}, bf16[32,1280]{1,0:T(8,128)(2,1)S(1)}, u32[]{:S(2)}, u32[]{:S(2)}) collective-permute-start(bf16[32,1280]{1,0:T(8,128)(2,1)S(1)} %get-tuple-element.54), channel_id=1, source_target_pairs={{0,4},{1,5},{2,6},{3,7},{4,0},{5,1},{6,2},{7,3},{8,12},{9,13},{10,... | collective-permute-start | bytes 245768 | tf_op jit(solution)/shard_map/ppermute | solution.py:281
  77.6 8.2 %collective-permute-start.22 = (bf16[32,1280]{1,0:T(8,128)(2,1)S(1)}, bf16[32,1280]{1,0:T(8,128)(2,1)S(1)}, u32[]{:S(2)}, u32[]{:S(2)}) collective-permute-start(bf16[32,1280]{1,0:T(8,128)(2,1)S(1)} %get-tuple-element.56), channel_id=1, source_target_pairs={{0,12},{1,13},{2,14},{3,15},{4,8},{5,9},{6,10},{7,11},{8,4},{9,5},... | collective-permute-start | bytes 245768 | tf_op jit(solution)/shard_map/ppermute | solution.py:281
  78.8 9.0 %collective-permute-start.21 = (bf16[32,1280]{1,0:T(8,128)(2,1)S(1)}, bf16[32,1280]{1,0:T(8,128)(2,1)S(1)}, u32[]{:S(2)}, u32[]{:S(2)}) collective-permute-start(bf16[32,1280]{1,0:T(8,128)(2,1)S(1)} %get-tuple-element.57), channel_id=1, source_target_pairs={{0,8},{1,9},{2,10},{3,11},{4,12},{5,13},{6,14},{7,15},{8,0},{9,1},... | collective-permute-start | bytes 245768 | tf_op jit(solution)/shard_map/ppermute | solution.py:281
  80.2 7.6 %collective-permute-start.20 = (bf16[32,1280]{1,0:T(8,128)(2,1)S(1)}, bf16[32,1280]{1,0:T(8,128)(2,1)S(1)}, u32[]{:S(2)}, u32[]{:S(2)}) collective-permute-start(bf16[32,1280]{1,0:T(8,128)(2,1)S(1)} %get-tuple-element.58), channel_id=1, source_target_pairs={{0,4},{1,5},{2,6},{3,7},{4,0},{5,1},{6,2},{7,3},{8,12},{9,13},{10,... | collective-permute-start | bytes 245768 | tf_op jit(solution)/shard_map/ppermute | solution.py:281
  (18 other events, 131.4 us)

commit v9 on v8

v9 whole, which is shorter than its diff:
```python
import functools
import math

import jax
import jax.numpy as jnp
from jax import lax
from jax.experimental import pallas as pl
from jax.experimental.pallas import tpu as pltpu
from jax.sharding import PartitionSpec as P

AXES = ("expert", "dp")
CHUNKS = 2
SLICES = 4
LIMIT = 12 * 1024 * 1024
LARGE = 56 * 1024 * 1024
VMEM = pl.BlockSpec(memory_space=pltpu.VMEM)
HBM = pl.BlockSpec(memory_space=pltpu.HBM)
BF16 = jnp.bfloat16
F32 = jnp.float32


def dot(left, right, left_dim, right_dim):
    dims = (((left_dim,), (right_dim,)), ((), ()))
    return lax.dot_general(left, right, dims, preferred_element_type=F32)


def iota(shape, dim):
    return lax.broadcasted_iota(jnp.int32, shape, dim)


def position():
    half = lax.axis_index("dp")
    me = lax.axis_index("expert") * lax.axis_size("dp") + half
    line = lax.axis_size("expert") * lax.axis_size("dp") // SLICES
    return me % 2, me // 2 % (line // 2), me // line, half


def call(body, shapes, spaces, scratch, *args, limit=LIMIT):
    return pl.pallas_call(
        body,
        out_shape=shapes,
        in_specs=spaces,
        out_specs=[VMEM] * len(shapes),
        scratch_shapes=scratch,
        compiler_params=pltpu.CompilerParams(vmem_limit_bytes=limit),
        cost_estimate=pl.CostEstimate(flops=1, bytes_accessed=1, transcendentals=0),
    )(*args)


def pieces(value, count):
    terms = []
    for _ in range(count):
        terms.append(value.astype(BF16))
        value = value - terms[-1].astype(F32)
    return terms


def pack(z, columns):
    tiles = [z[:, i : i + 128] for i in range(0, z.shape[1], 128)]
    tiles += [columns[:, i : i + 128] for i in range(0, columns.shape[1], 128)]
    return jnp.concatenate(tiles, axis=0)


def unpack_z(rows, size, lanes):
    tiles = [rows[i * size : (i + 1) * size] for i in range(lanes // 128)]
    return jnp.concatenate(tiles, axis=1)


def unpack_columns(rows, start, rank):
    tiles = [rows[i : i + rank] for i in range(start, rows.shape[0], rank)]
    return jnp.concatenate(tiles, axis=1)


def pair_columns(ids, probs):
    top, tok = ids.shape
    rows = tok * top
    pick = (iota((rows, tok), 0) // top == iota((rows, tok), 1)).astype(BF16)
    here = iota((rows, top), 0) % top == iota((rows, top), 1)
    names = dot(pick, ids.astype(BF16), 1, 1)
    weights, rest = jnp.zeros((rows, top), F32), probs
    for _ in range(3):
        piece = rest.astype(BF16)
        weights = weights + dot(pick, piece, 1, 1)
        rest = rest - piece.astype(F32)
    names = jnp.sum(jnp.where(here, names, 0.0), axis=1, keepdims=True)
    weights = jnp.sum(jnp.where(here, weights, 0.0), axis=1, keepdims=True)
    return names, weights


def load(pairs, sems):
    copies = [pltpu.make_async_copy(src, dst, sems.at[i]) for i, (src, dst) in enumerate(pairs)]
    for copy in copies:
        copy.start()
    return copies


def first_kernel(groups, tokens, cot_at, sketch_at, ids_at, probs_at, *refs):
    outs, pairs, (cot, sketch, ids, probs, sems, x_sems) = refs[:SLICES], refs[SLICES], refs[5:]
    core, _, place, _ = position()
    rows, hidden = cot.shape
    tok = pairs.shape[1]
    top = rows // tok
    rank = sketch.shape[0]
    share = tokens.shape[1] // SLICES
    lanes = (outs[0].shape[1] - share) // groups
    parts = 5
    piece = hidden // parts
    sources = [(ids_at, ids), (probs_at, probs), (sketch_at, sketch)]
    for i in range(parts):
        cut = pl.ds(i * piece, piece)
        sources.append((cot_at.at[:, cut], cot.at[:, cut]))
    copies = load(sources, sems)
    sources = []
    for j, out in enumerate(outs):
        cut = pl.ds(pl.multiple_of((place ^ j) * share, share), share)
        sources.append((tokens.at[:, cut], out.at[:, pl.ds(lanes, share)]))
    x_copies = load(sources, x_sems)
    copies[0].wait()
    copies[1].wait()
    pairs[:top] = ids[...].astype(F32)
    pairs[top:] = probs[...]
    names, weights = pair_columns(pairs[:top], pairs[top:])
    copies[2].wait()
    both = jnp.concatenate(pieces(sketch[...], 2), axis=0)
    pair = 0.0
    for i in range(parts):
        copies[3 + i].wait()
        here = slice(i * piece, (i + 1) * piece)
        pair = pair + dot(cot[:, here], both[:, here], 1, 1)
    pair = (pair[:, :rank] + pair[:, rank:]) * weights
    lane = iota((rank, lanes), 1)
    tiled = dot(pair.astype(BF16), (iota((rank, lanes), 0) == lane % rank).astype(BF16), 1, 0)
    block = iota((1, lanes), 1) // rank * groups
    for i in range(groups):
        name = block + (core ^ i) if groups == 2 else block
        y = jnp.where(names == name.astype(F32), tiled, 0.0)
        y = jnp.sum(y.reshape(tok, top, lanes), axis=1).astype(BF16)
        for out in outs:
            out[:, i * (lanes + share) : i * (lanes + share) + lanes] = y
    for copy in x_copies:
        copy.wait()


def gather(near, far, x, y, sems):
    share, lanes = x.shape[1], y.shape[1]
    rows = near[0].shape[0]
    sources = []
    for i, (a, b) in enumerate(zip(near, far)):
        cut = pl.ds(2 * i * rows, rows)
        sources.append((a.at[:, pl.ds(0, lanes)], y.at[cut]))
        sources.append((a.at[:, pl.ds(lanes, share)], x.at[cut]))
        cut = pl.ds((2 * i + 1) * rows, rows)
        sources.append((b.at[:, pl.ds(0, share)], x.at[cut]))
        sources.append((b.at[:, pl.ds(share, lanes)], y.at[cut]))
    for copy in load(sources, sems):
        copy.wait()


def columns_kernel(n, *refs):
    out, x, y, sems = refs[2 * n :]
    gather(refs[:n], refs[n : 2 * n], x, y, sems)
    out[...] = dot(y[...], x[...], 0, 0)


def z_kernel(n, low, part, near_x, far_x, *refs):
    outs, (x, y, columns, sems) = refs[2 * n : -4], refs[-4:]
    _, lower, place, _ = position()
    gather(refs[:n], refs[n : 2 * n], x, y, sems)
    rank = columns.shape[0] // (SLICES * low)
    share = x.shape[1]
    lanes = y.shape[1]
    rows = near_x.shape[0]
    tok = rows // 2
    total = (part[...] + dot(y[...], x[...], 0, 0)).astype(BF16)
    columns[...] = total
    own = jnp.concatenate([near_x[:, lanes : lanes + share], far_x[:, :share]], axis=0)
    halves = [dot(own, total, 1, 1), dot(x[: 2 * rows], total, 1, 1)]
    for j, out in enumerate(outs):
        half = halves[j // 2].astype(BF16)
        start = j % 2 * tok
        z = jnp.concatenate([half[start : start + tok], half[rows + start :][:tok]], axis=0)
        expert = (place ^ j) * low + lower
        out[...] = pack(z, columns[pl.ds(pl.multiple_of(expert * rank, rank), rank)])


def inverse_kernel(start, p0, p1, p2, p3, inverse, basis, columns):
    _, _, place, half = position()
    rank = inverse.shape[0]
    _, _, share = columns.shape
    gram = 0.0
    for j, packed in enumerate((p0, p1, p2, p3)):
        block = unpack_columns(packed[...], start, rank)
        columns[place ^ j] = block
        gram = gram + dot(block, block, 1, 1)
    row = iota((rank, 128), 0)
    lane = iota((rank, 128), 1)
    eye = (row + rank == lane).astype(F32)
    work = jnp.concatenate([gram, jnp.zeros((rank, 128 - rank), F32)], axis=1) + eye
    for first in range(0, rank, 4):
        heads = [work[first + i : first + i + 1] for i in range(4)]
        sides = [
            jnp.broadcast_to(work[:, first + i : first + i + 1], (rank, 128)) for i in range(4)
        ]
        taken = 0.0
        for i in range(4):
            pivot = first + i
            factor = sides[i] / sides[i][pivot : pivot + 1]
            factor = jnp.where(row > pivot, factor, 0.0)
            taken = taken + factor * heads[i]
            for k in range(i + 1, 4):
                sides[k] = sides[k] - factor * sides[k][pivot : pivot + 1]
                heads[k] = heads[k] - factor[first + k : first + k + 1] * heads[i]
        work = work - taken
    diagonal = jnp.sum(jnp.where(row == lane, work, 0.0), axis=1, keepdims=True)
    result = work[:, rank : 2 * rank] * lax.rsqrt(diagonal)
    inverse[...] = result
    scaled = result * math.sqrt(SLICES * share)
    scaled = jnp.concatenate(pieces(scaled, 3), axis=0)
    count = basis.shape[1] // share
    for i in range(count):
        out = dot(scaled, columns[half * count + i], 1, 0)
        out = out[:rank] + out[rank : 2 * rank] + out[2 * rank :]
        basis[:, i * share : (i + 1) * share] = out


def coeffs_kernel(scale, inverse, *refs):
    blocks, out = refs[:-1], refs[-1]
    rank, size = blocks[0].shape
    left = jnp.concatenate(pieces(inverse[...] * scale, 3), axis=0)
    left = jnp.concatenate([left] * SLICES, axis=1)
    for i in range(len(blocks) // SLICES):
        right = jnp.concatenate([b[...] for b in blocks[i * SLICES : (i + 1) * SLICES]], axis=0)
        part = dot(left, right, 1, 0)
        out[:, i * size : (i + 1) * size] = part[:rank] + part[rank : 2 * rank] + part[2 * rank :]


def mask_kernel(groups, own, pair, out):
    core = position()[0]
    lanes, rows = out.shape
    rows = rows // 2
    top, tok = own.shape[0] // 2, own.shape[1]
    rank = lanes // (lax.axis_size("expert") // groups)
    pick = (iota((tok, rows), 1) // top == iota((tok, rows), 0)).astype(BF16)
    here = iota((top, rows), 1) % top == iota((top, rows), 0)
    block = iota((lanes, 1), 0) // rank * groups + (core if groups == 2 else 0)
    for i, pairs in enumerate((own, pair)):
        names = dot(pairs[:top].astype(BF16), pick, 1, 0)
        weights = sum(dot(piece, pick, 1, 0) for piece in pieces(pairs[top:], 3))
        names = jnp.sum(jnp.where(here, names, 0.0), axis=0, keepdims=True)
        weights = jnp.sum(jnp.where(here, weights, 0.0), axis=0, keepdims=True)
        masked = jnp.where(names == block.astype(F32), weights, 0.0)
        out[:, i * rows : (i + 1) * rows] = masked


def terms_kernel(low, tok, z0, z1, z2, z3, mask, mine, other, *refs):
    outs, (work, spread) = refs[:-2], refs[-2:]
    lower = position()[1]
    lanes, rows = mask.shape
    rows = rows // 2
    rank = lanes // (SLICES * low)
    size = 2 * tok * lanes // 128
    z = 0.0
    for block in (z0, z1, z2, z3):
        z = z + unpack_z(block[:size], 2 * tok, lanes).astype(F32)
    repeat = iota((2 * tok, 2 * rows), 1) // (rows // tok) == iota((2 * tok, 2 * rows), 0)
    z = dot(z.astype(BF16), repeat.astype(BF16), 0, 0)
    work[...] = (z * mask[...]).astype(BF16)
    for r in range(low):
        for j in range(SLICES):
            start = pl.multiple_of((j * low + (lower ^ r)) * rank, rank)
            spread[(r * SLICES + j) * rank : (r * SLICES + j + 1) * rank] = work[
                pl.ds(start, rank)
            ]
    for chunk in range(len(outs) // low):
        block, width = outs[chunk * low].shape
        here = slice(chunk * width, (chunk + 1) * width)
        part = dot(spread[:, :rows], mine[:, here], 1, 0)
        part = (part + dot(spread[:, rows:], other[:, here], 1, 0)).astype(BF16)
        for r in range(low):
            outs[chunk * low + r][...] = part[r * block : (r + 1) * block]


def shards(tokens, expert_ids, route_probs, cotangents, sketch):
    n_expert = lax.axis_size("expert")
    n_dp = lax.axis_size("dp")
    count = n_expert * n_dp
    line = count // SLICES
    low = line // 2
    groups = 2 // n_dp
    tok, width = tokens.shape
    top = expert_ids.shape[1]
    hidden, rank = sketch.shape
    rows = tok * top
    share = width // SLICES
    lanes = count // 2 * rank
    part = hidden // n_dp
    scale = 1.0 / math.sqrt(rows)
    _, lower, place, half = position()
    limit = LIMIT if n_dp == 1 else LARGE
    shape = jax.ShapeDtypeStruct

    def exchange(block, step):
        return lax.ppermute(block, AXES, [(i, i ^ step) for i in range(count)])

    cot = cotangents.reshape(rows, hidden)
    if n_dp > 1:
        mine = lax.dynamic_slice_in_dim(cot, half * part, part, axis=1)
        other = exchange(lax.dynamic_slice_in_dim(cot, (1 - half) * part, part, axis=1), 1)
    else:
        mine, other = cot, exchange(cot, 1)

    *blocks, pairs = call(
        functools.partial(first_kernel, groups),
        [shape((tok, groups * lanes + share), BF16)] * SLICES + [shape((2 * top, tok), F32)],
        [HBM] * 5,
        [
            pltpu.VMEM((rows, hidden), BF16),
            pltpu.VMEM((rank, hidden), F32),
            pltpu.VMEM((top, tok), jnp.int32),
            pltpu.VMEM((top, tok), F32),
            pltpu.SemaphoreType.DMA((8,)),
            pltpu.SemaphoreType.DMA((SLICES,)),
        ],
        tokens,
        cot,
        sketch.T,
        expert_ids.T,
        route_probs.T,
        limit=LARGE,
    )
    blocks = blocks[:1] + [exchange(blocks[j], j * line) for j in range(1, SLICES)]
    pairs = [pairs, exchange(pairs, 1)]
    near = [[jnp.concatenate(blocks[i : i + 2], axis=0)] for i in range(0, SLICES, 2)]
    step = 2
    while step < line:
        near = [side + [exchange(b, step) for b in side] for side in near]
        step *= 2
    n = len(near[0])
    skip = lanes if groups == 2 else 0

    size = 2 * tok * lanes // 128
    far = [exchange(b[:, skip:], 1) for b in near[0]]
    if n_dp == 1:
        work = [
            pltpu.VMEM((4 * n * tok, share), BF16),
            pltpu.VMEM((4 * n * tok, lanes), BF16),
            pltpu.SemaphoreType.DMA((4 * n,)),
        ]
        [columns] = call(
            functools.partial(columns_kernel, n),
            [shape((lanes, share), F32)],
            [HBM] * (2 * n),
            work,
            *near[0],
            *far,
        )
        near[1], columns = lax.optimization_barrier((near[1], columns))
        zs = call(
            functools.partial(z_kernel, n, low),
            [shape((size + rank * share // 128, 128), BF16)] * SLICES,
            [VMEM] * 3 + [HBM] * (2 * n),
            work[:2] + [pltpu.VMEM((lanes, share), BF16)] + work[2:],
            columns,
            near[0][0],
            far[0],
            *near[1],
            *[exchange(b[:, skip:], 1) for b in near[1]],
        )
    else:
        far = [far, [exchange(b[:, skip:], 1) for b in near[1]]]
        rows_all = jnp.concatenate(near[0] + far[0] + near[1] + far[1], axis=0)
        columns = dot(rows_all[:, :lanes], rows_all[:, lanes:], 0, 0).astype(BF16)
        zs = []
        for j in range(SLICES):
            here = slice(j % 2 * tok, (j % 2 + 1) * tok)
            x = jnp.concatenate([near[j // 2][0][here], far[j // 2][0][here]], axis=0)
            start = ((place ^ j) * low + lower) * rank
            own = lax.dynamic_slice_in_dim(columns, start, rank, axis=0)
            zs.append(pack(dot(x[:, lanes:], columns, 1, 1).astype(BF16), own))
    zs = list(zs[:1]) + [exchange(zs[j], j * line) for j in range(1, SLICES)]

    [mask] = call(
        functools.partial(mask_kernel, groups),
        [shape((lanes, 2 * rows), F32)],
        [VMEM] * 2,
        [],
        *pairs,
        limit=limit,
    )
    piece = part // CHUNKS
    terms = call(
        functools.partial(terms_kernel, low, tok),
        [shape((SLICES * rank, piece), BF16)] * (low * CHUNKS),
        [VMEM] * (SLICES + 3),
        [pltpu.VMEM((lanes, 2 * rows), BF16)] * 2,
        *zs,
        mask,
        mine,
        other,
        limit=limit,
    )
    zs, _ = lax.optimization_barrier((zs, terms[-1]))
    inverse, basis = call(
        functools.partial(inverse_kernel, size),
        [shape((rank, rank), F32), shape((rank, width // n_dp), F32)],
        [VMEM] * SLICES,
        [pltpu.VMEM((SLICES, rank, share), BF16)],
        *zs,
    )
    sums = []
    for chunk in range(CHUNKS):
        blocks = terms[chunk * low : (chunk + 1) * low]
        blocks = [term.reshape(SLICES, rank, piece) for term in blocks]
        step = 2
        while len(blocks) > 1:
            blocks = [
                (keep.astype(F32) + exchange(send, step).astype(F32)).astype(BF16)
                for keep, send in zip(blocks[::2], blocks[1::2])
            ]
            step *= 2
        sums.append(blocks[0])
    sums[0], inverse = lax.optimization_barrier((sums[0], inverse))
    blocks = []
    for block in sums:
        own = [lax.dynamic_index_in_dim(block, place ^ j, 0, False) for j in range(SLICES)]
        blocks += own[:1] + [exchange(own[j], j * line) for j in range(1, SLICES)]
    [coeffs] = call(
        functools.partial(coeffs_kernel, scale),
        [shape((rank, part), F32)],
        [VMEM] * (1 + len(blocks)),
        [],
        inverse,
        *blocks,
    )
    return basis[None], coeffs[None]


def solution(mesh):
    in_specs = (
        P(("group", "expert", "dp"), None),
        P(("group", "expert", "dp"), None),
        P(("group", "expert", "dp"), None),
        P(("group", "expert", "dp"), None, None),
        P(),
    )
    out_specs = (P(("group", "expert"), None, "dp"), P(("group", "expert"), None, "dp"))
    return jax.shard_map(shards, mesh=mesh, in_specs=in_specs, out_specs=out_specs, check_vma=False)
```

time: 89.3 us -> 74.3 us (0.83)
  Pallas kernels: 22 us -> 11.1 us
  waiting for transfers between devices: 28.8 us -> 34 us
  starting transfers between devices: 31.5 us -> 26.9 us
  other arithmetic: 2.53 us -> 0.15 us
  local copies, waits for them, and re-layouts: 3.15 us -> 1.12 us
    pallas_call x6 -> x7, Pallas kernels: 22 us -> 11.1 us  [call(): pl.pallas_call(body, out_shape=shapes, in_specs=spaces, out_specs=[VMEM]...]
    ppermute x27 -> x22, waiting for transfers between devices: 28.8 us -> 34 us  [exchange(): return lax.ppermute(block, AXES, [(i, i ^ step) for i in range(count)])]
    ppermute x27 -> x22, starting transfers between devices: 31.5 us -> 26.9 us  [exchange(): return lax.ppermute(block, AXES, [(i, i ^ step) for i in range(count)])]
    another operation x3 -> x0, other arithmetic: 1.35 us -> none  [the longest x2 0.77 us: shards(): ys = [jnp.stack([y] + [exchange(y, j * line) for j in range(1, SLICES)])]]
    unnamed x30 -> x6, local copies, waits for them, and re-layouts: 2.04 us -> 0.94 us
    dynamic_slice x1 -> x0, local copies, waits for them, and re-layouts: 1.04 us -> none  [shards(): lax.dynamic_slice_in_dim(tokens, (place ^ j) * share, share, axis=1)]
    convert_element_type x2, other arithmetic: 1.14 us -> 0.15 us  [shards(): (keep.astype(F32) + exchange(send, step).astype(F32)).astype(BF16)]
  transfers between devices with their start and end apart: 27 -> 22, of which waited for: 12 -> 15; matrix products, arithmetic and copies ran while one was open for 4% -> 2% of each run, Pallas kernels for 14% -> 11%
where the time goes in v9:
time: 74.3 us; the launch traced here: 74.1 us
  waiting for transfers between devices  34 us (46%)
  starting transfers between devices  26.9 us (36%)
  Pallas kernels  11.1 us (15%)
  local copies, waits for them, and re-layouts  1.12 us (2%)
  between operations  0.79 us (1%)
    ppermute x22, waiting for transfers between devices, exchange(): return lax.ppermute(block, AXES, [(i, i ^ step) for i in range(count)])  34 us
    ppermute x22, starting transfers between devices, exchange(): return lax.ppermute(block, AXES, [(i, i ^ step) for i in range(count)])  26.9 us
    pallas_call x7, Pallas kernels, call(): pl.pallas_call(body, out_shape=shapes, in_specs=spaces, out_specs=[VMEM]...  11.1 us
  transfers between devices with their start and end apart: 22, of which 15 were waited for; matrix products, arithmetic and copies ran while one was open for 2% of the time, Pallas kernels for 11%

profile of v9, /device:TPU:0, one launch (start us, length us, event | category | flops | bytes accessed | tf_op | source)
XLA Modules:
  0.0 74.1 jit_solution(5254125050544610686)
XLA Ops:
  1.1 3.8 %shard_map.68 = (bf16[48,1408]{1,0:T(8,128)(2,1)}, bf16[48,1408]{1,0:T(8,128)(2,1)}, bf16[48,1408]{1,0:T(8,128)(2,1)}, bf16[48,1408]{1,0:T(8,128)(2,1)}, f32[16,48]{1,0:T(8,128)}) custom-call(bf16[48,3584]{1,0:T(8,128)(2,1)} %tokens.1, bf16[384,2560]{1,0:T(8,128)(2,1)} %bitcast.29, f32[32,2560]{1,0:T(8,128)} %bitcast.35, s32[8,48]{1,0:T(8,128)} %bitcast.37, ...), custom_call_target="tpu_custom_call" | custom-call | flops 1 | bytes 1 | tf_op jit(solution)/shard_map/pallas_call | solution.py:39
  5.0 2.7 %collective-permute-start.3 = (bf16[48,1408]{1,0:T(8,128)(2,1)}, bf16[48,1408]{1,0:T(8,128)(2,1)S(1)}, u32[]{:S(2)}, u32[]{:S(2)}) collective-permute-start(bf16[48,1408]{1,0:T(8,128)(2,1)} %get-tuple-element.29), channel_id=1, source_target_pairs={{0,4},{1,5},{2,6},{3,7},{4,0},{5,1},{6,2},{7,3},{8,12},{9,13},{10,... | collective-permute-start | bytes 405512 | tf_op jit(solution)/shard_map/ppermute | solution.py:303
  7.6 2.6 %collective-permute-start = (bf16[48,1408]{1,0:T(8,128)(2,1)}, bf16[48,1408]{1,0:T(8,128)(2,1)S(1)}, u32[]{:S(2)}, u32[]{:S(2)}) collective-permute-start(bf16[48,1408]{1,0:T(8,128)(2,1)} %get-tuple-element.26), channel_id=1, source_target_pairs={{0,8},{1,9},{2,10},{3,11},{4,12},{5,13},{6,14},{7,15},{8,0},{9,1},... | collective-permute-start | bytes 405512 | tf_op jit(solution)/shard_map/ppermute | solution.py:303
  10.2 0.9 %constant_dynamic-update-slice_fusion.3 = bf16[96,1408]{1,0:T(8,128)(2,1)S(1)} fusion(bf16[48,1408]{1,0:T(8,128)(2,1)} %get-tuple-element.28), kind=kLoop, calls=%fused_computation.15 | loop fusion | bytes 270336
  11.1 3.3 %collective-permute-done.3 = bf16[48,1408]{1,0:T(8,128)(2,1)S(1)} collective-permute-done((bf16[48,1408]{1,0:T(8,128)(2,1)}, bf16[48,1408]{1,0:T(8,128)(2,1)S(1)}, u32[]{:S(2)}, u32[]{:S(2)}) %collective-permute-start.3) | collective-permute-done | bytes 135200 | tf_op jit(solution)/shard_map/ppermute | solution.py:303
  14.5 1.8 %collective-permute-start.4 = (bf16[96,1408]{1,0:T(8,128)(2,1)S(1)}, bf16[96,1408]{1,0:T(8,128)(2,1)S(1)}, u32[]{:S(2)}, u32[]{:S(2)}) collective-permute-start(bf16[96,1408]{1,0:T(8,128)(2,1)S(1)} %constant_dynamic-update-slice_fusion.2.refs_0_.near_x), channel_id=1, source_target_pairs={{0,2},{1,3},{2,0},{3,1},{4,6},{5,7},{6,4},{7,5},{8,10},{9,11},{10,... | collective-permute-start | bytes 811016 | tf_op jit(solution)/shard_map/ppermute | solution.py:303
  16.2 4.7 %collective-permute-done = bf16[48,1408]{1,0:T(8,128)(2,1)S(1)} collective-permute-done((bf16[48,1408]{1,0:T(8,128)(2,1)}, bf16[48,1408]{1,0:T(8,128)(2,1)S(1)}, u32[]{:S(2)}, u32[]{:S(2)}) %collective-permute-start) | collective-permute-done | bytes 135200 | tf_op jit(solution)/shard_map/ppermute | solution.py:303
  21.0 1.6 %collective-permute-start.2 = (bf16[96,1408]{1,0:T(8,128)(2,1)S(1)}, bf16[96,1408]{1,0:T(8,128)(2,1)S(1)}, u32[]{:S(2)}, u32[]{:S(2)}) collective-permute-start(bf16[96,1408]{1,0:T(8,128)(2,1)S(1)} %constant_dynamic-update-slice_fusion.refs_0_), channel_id=1, source_target_pairs={{0,2},{1,3},{2,0},{3,1},{4,6},{5,7},{6,4},{7,5},{8,10},{9,11},{10,... | collective-permute-start | bytes 811016 | tf_op jit(solution)/shard_map/ppermute | solution.py:303
  25.2 3.4 %collective-permute-done.2.refs_1_ = bf16[96,1408]{1,0:T(8,128)(2,1)S(1)} collective-permute-done((bf16[96,1408]{1,0:T(8,128)(2,1)S(1)}, bf16[96,1408]{1,0:T(8,128)(2,1)S(1)}, u32[]{:S(2)}, u32[]{:S(2)}) %collective-permute-start.2) | collective-permute-done | bytes 270368 | tf_op jit(solution)/shard_map/ppermute | solution.py:303
  31.4 4.1 %collective-permute-start.10 = (bf16[416,128]{1,0:T(8,128)(2,1)S(1)}, bf16[416,128]{1,0:T(8,128)(2,1)S(1)}, u32[]{:S(2)}, u32[]{:S(2)}) collective-permute-start(bf16[416,128]{1,0:T(8,128)(2,1)S(1)} %get-tuple-element.35), channel_id=1, source_target_pairs={{0,8},{1,9},{2,10},{3,11},{4,12},{5,13},{6,14},{7,15},{8,0},{9,1},... | collective-permute-start | bytes 319496 | tf_op jit(solution)/shard_map/ppermute | solution.py:303
  35.5 1.4 %collective-permute-start.11 = (bf16[416,128]{1,0:T(8,128)(2,1)S(1)}, bf16[416,128]{1,0:T(8,128)(2,1)S(1)}, u32[]{:S(2)}, u32[]{:S(2)}) collective-permute-start(bf16[416,128]{1,0:T(8,128)(2,1)S(1)} %get-tuple-element.36), channel_id=1, source_target_pairs={{0,12},{1,13},{2,14},{3,15},{4,8},{5,9},{6,10},{7,11},{8,4},{9,5},... | collective-permute-start | bytes 319496 | tf_op jit(solution)/shard_map/ppermute | solution.py:303
  36.8 1.2 %collective-permute-done.12.pair = f32[16,48]{1,0:T(8,128)S(1)} collective-permute-done((f32[16,48]{1,0:T(8,128)S(1)}, f32[16,48]{1,0:T(8,128)S(1)}, u32[]{:S(2)}, u32[]{:S(2)}) %collective-permute-start.12) | collective-permute-done | bytes 3104 | tf_op jit(solution)/shard_map/ppermute | solution.py:303
  38.2 5.6 %collective-permute-done.10.z2.p2 = bf16[416,128]{1,0:T(8,128)(2,1)S(1)} collective-permute-done((bf16[416,128]{1,0:T(8,128)(2,1)S(1)}, bf16[416,128]{1,0:T(8,128)(2,1)S(1)}, u32[]{:S(2)}, u32[]{:S(2)}) %collective-permute-start.10) | collective-permute-done | bytes 106528 | tf_op jit(solution)/shard_map/ppermute | solution.py:303
  43.8 1.0 %collective-permute-done.9.z1.p1 = bf16[416,128]{1,0:T(8,128)(2,1)S(1)} collective-permute-done((bf16[416,128]{1,0:T(8,128)(2,1)S(1)}, bf16[416,128]{1,0:T(8,128)(2,1)S(1)}, u32[]{:S(2)}, u32[]{:S(2)}) %collective-permute-start.9) | collective-permute-done | bytes 106528 | tf_op jit(solution)/shard_map/ppermute | solution.py:303
  44.8 1.8 %shard_map.72 = (bf16[128,1280]{1,0:T(8,128)(2,1)S(1)}, bf16[128,1280]{1,0:T(8,128)(2,1)S(1)}, bf16[128,1280]{1,0:T(8,128)(2,1)S(1)}, bf16[128,1280]{1,0:T(8,128)(2,1)S(1)}) custom-call(bf16[416,128]{1,0:T(8,128)(2,1)S(1)} %get-tuple-element.39.z0.p0, bf16[416,128]{1,0:T(8,128)(2,1)S(1)} %collective-permute-done.9.z1.p1, ...), custom_call_target="tpu_custom_call" | custom-call | flops 1 | bytes 1 | tf_op jit(solution)/shard_map/pallas_call | solution.py:39
  46.6 1.6 %collective-permute-start.18 = (bf16[4,32,1280]{2,1,0:T(8,128)(2,1)S(1)}, bf16[4,32,1280]{2,1,0:T(8,128)(2,1)S(1)}, u32[]{:S(2)}, u32[]{:S(2)}) collective-permute-start(bf16[4,32,1280]{2,1,0:T(8,128)(2,1)S(1)} %bitcast.34), channel_id=1, source_target_pairs={{0,2},{1,3},{2,0},{3,1},{4,6},{5,7},{6,4},{7,5},{8,10},{9,11},{10,... | collective-permute-start | bytes 983048 | tf_op jit(solution)/shard_map/ppermute | solution.py:303
  48.7 2.7 %shard_map.73 = (f32[32,32]{1,0:T(8,128)S(1)}, f32[32,3584]{1,0:T(8,128)}) custom-call(bf16[416,128]{1,0:T(8,128)(2,1)S(1)} %get-tuple-element.39.z0.p0, bf16[416,128]{1,0:T(8,128)(2,1)S(1)} %collective-permute-done.9.z1.p1, bf16[416,128]{1,0:T(8,128)(2,1)S(1)} %collective-permute-done.10.z2.p2, bf16[416,128]{1,0:T(8,128)(2,1)S(1)} %collective-permute-done.11.z3.p3), custom_call_target="tpu_custom_call" | custom-call | flops 1 | bytes 1 | tf_op jit(solution)/shard_map/pallas_call | solution.py:39
  51.4 5.9 %collective-permute-done.18 = bf16[4,32,1280]{2,1,0:T(8,128)(2,1)S(1)} collective-permute-done((bf16[4,32,1280]{2,1,0:T(8,128)(2,1)S(1)}, bf16[4,32,1280]{2,1,0:T(8,128)(2,1)S(1)}, u32[]{:S(2)}, u32[]{:S(2)}) %collective-permute-start.18) | collective-permute-done | bytes 327712 | tf_op jit(solution)/shard_map/ppermute | solution.py:303
  57.5 1.6 %collective-permute-start.19 = (bf16[32,1280]{1,0:T(8,128)(2,1)S(1)}, bf16[32,1280]{1,0:T(8,128)(2,1)S(1)}, u32[]{:S(2)}, u32[]{:S(2)}) collective-permute-start(bf16[32,1280]{1,0:T(8,128)(2,1)S(1)} %get-tuple-element.52), channel_id=1, source_target_pairs={{0,4},{1,5},{2,6},{3,7},{4,0},{5,1},{6,2},{7,3},{8,12},{9,13},{10,... | collective-permute-start | bytes 245768 | tf_op jit(solution)/shard_map/ppermute | solution.py:303
  59.8 2.1 %collective-permute-start.21 = (bf16[32,1280]{1,0:T(8,128)(2,1)S(1)}, bf16[32,1280]{1,0:T(8,128)(2,1)S(1)}, u32[]{:S(2)}, u32[]{:S(2)}) collective-permute-start(bf16[32,1280]{1,0:T(8,128)(2,1)S(1)} %get-tuple-element.50), channel_id=1, source_target_pairs={{0,12},{1,13},{2,14},{3,15},{4,8},{5,9},{6,10},{7,11},{8,4},{9,5},... | collective-permute-start | bytes 245768 | tf_op jit(solution)/shard_map/ppermute | solution.py:303
  62.4 2.4 %collective-permute-start.15 = (bf16[32,1280]{1,0:T(8,128)(2,1)S(1)}, bf16[32,1280]{1,0:T(8,128)(2,1)S(1)}, u32[]{:S(2)}, u32[]{:S(2)}) collective-permute-start(bf16[32,1280]{1,0:T(8,128)(2,1)S(1)} %get-tuple-element.56), channel_id=1, source_target_pairs={{0,4},{1,5},{2,6},{3,7},{4,0},{5,1},{6,2},{7,3},{8,12},{9,13},{10,... | collective-permute-start | bytes 245768 | tf_op jit(solution)/shard_map/ppermute | solution.py:303
  65.1 2.1 %collective-permute-start.17 = (bf16[32,1280]{1,0:T(8,128)(2,1)S(1)}, bf16[32,1280]{1,0:T(8,128)(2,1)S(1)}, u32[]{:S(2)}, u32[]{:S(2)}) collective-permute-start(bf16[32,1280]{1,0:T(8,128)(2,1)S(1)} %get-tuple-element.54), channel_id=1, source_target_pairs={{0,12},{1,13},{2,14},{3,15},{4,8},{5,9},{6,10},{7,11},{8,4},{9,5},... | collective-permute-start | bytes 245768 | tf_op jit(solution)/shard_map/ppermute | solution.py:303
  67.9 5.2 %collective-permute-done.16.refs_2_ = bf16[32,1280]{1,0:T(8,128)(2,1)S(1)} collective-permute-done((bf16[32,1280]{1,0:T(8,128)(2,1)S(1)}, bf16[32,1280]{1,0:T(8,128)(2,1)S(1)}, u32[]{:S(2)}, u32[]{:S(2)}) %collective-permute-start.16) | collective-permute-done | bytes 81952 | tf_op jit(solution)/shard_map/ppermute | solution.py:303
  73.0 1.1 %shard_map.74 = f32[32,2560]{1,0:T(8,128)} custom-call(f32[32,32]{1,0:T(8,128)S(1)} %get-tuple-element.47.inverse, bf16[32,1280]{1,0:T(8,128)(2,1)S(1)} %get-tuple-element.57.refs_0_, bf16[32,1280]{1,0:T(8,128)(2,1)S(1)} %collective-permute-done.15.refs_1_, bf16[32,1280]{1,0:T(8,128)(2,1)S(1)} %collective-permute-done.16.refs_2_, ...), custom_call_target="tpu_custom_call" | custom-call | flops 1 | bytes 1 | tf_op jit(solution)/shard_map/pallas_call | solution.py:39
  (43 shorter events, 9.0 us)
Async XLA Ops:
  0.6 44.2 %collective-permute-start.13 = (bf16[384,2560]{1,0:T(8,128)(2,1)}, bf16[384,2560]{1,0:T(8,128)(2,1)S(1)}, u32[]{:S(2)}, u32[]{:S(2)}) collective-permute-start(bf16[384,2560]{1,0:T(8,128)(2,1)} %bitcast.28), channel_id=1, source_target_pairs={{0,1},{1,0},{2,3},{3,2},{4,5},{5,4},{6,7},{7,6},{8,9},{9,8},{10,11... | collective-permute-start | bytes 5898248 | tf_op jit(solution)/shard_map/ppermute | solution.py:303
  5.0 9.5 %collective-permute-start.3 = (bf16[48,1408]{1,0:T(8,128)(2,1)}, bf16[48,1408]{1,0:T(8,128)(2,1)S(1)}, u32[]{:S(2)}, u32[]{:S(2)}) collective-permute-start(bf16[48,1408]{1,0:T(8,128)(2,1)} %get-tuple-element.29), channel_id=1, source_target_pairs={{0,4},{1,5},{2,6},{3,7},{4,0},{5,1},{6,2},{7,3},{8,12},{9,13},{10,... | collective-permute-start | bytes 405512 | tf_op jit(solution)/shard_map/ppermute | solution.py:303
  7.6 13.4 %collective-permute-start = (bf16[48,1408]{1,0:T(8,128)(2,1)}, bf16[48,1408]{1,0:T(8,128)(2,1)S(1)}, u32[]{:S(2)}, u32[]{:S(2)}) collective-permute-start(bf16[48,1408]{1,0:T(8,128)(2,1)} %get-tuple-element.26), channel_id=1, source_target_pairs={{0,8},{1,9},{2,10},{3,11},{4,12},{5,13},{6,14},{7,15},{8,0},{9,1},... | collective-permute-start | bytes 405512 | tf_op jit(solution)/shard_map/ppermute | solution.py:303
  10.2 10.8 %collective-permute-start.1 = (bf16[48,1408]{1,0:T(8,128)(2,1)}, bf16[48,1408]{1,0:T(8,128)(2,1)S(1)}, u32[]{:S(2)}, u32[]{:S(2)}) collective-permute-start(bf16[48,1408]{1,0:T(8,128)(2,1)} %get-tuple-element.27), channel_id=1, source_target_pairs={{0,12},{1,13},{2,14},{3,15},{4,8},{5,9},{6,10},{7,11},{8,4},{9,5},... | collective-permute-start | bytes 405512 | tf_op jit(solution)/shard_map/ppermute | solution.py:303
  14.5 8.5 %collective-permute-start.4 = (bf16[96,1408]{1,0:T(8,128)(2,1)S(1)}, bf16[96,1408]{1,0:T(8,128)(2,1)S(1)}, u32[]{:S(2)}, u32[]{:S(2)}) collective-permute-start(bf16[96,1408]{1,0:T(8,128)(2,1)S(1)} %constant_dynamic-update-slice_fusion.2.refs_0_.near_x), channel_id=1, source_target_pairs={{0,2},{1,3},{2,0},{3,1},{4,6},{5,7},{6,4},{7,5},{8,10},{9,11},{10,... | collective-permute-start | bytes 811016 | tf_op jit(solution)/shard_map/ppermute | solution.py:303
  21.0 7.5 %collective-permute-start.2 = (bf16[96,1408]{1,0:T(8,128)(2,1)S(1)}, bf16[96,1408]{1,0:T(8,128)(2,1)S(1)}, u32[]{:S(2)}, u32[]{:S(2)}) collective-permute-start(bf16[96,1408]{1,0:T(8,128)(2,1)S(1)} %constant_dynamic-update-slice_fusion.refs_0_), channel_id=1, source_target_pairs={{0,2},{1,3},{2,0},{3,1},{4,6},{5,7},{6,4},{7,5},{8,10},{9,11},{10,... | collective-permute-start | bytes 811016 | tf_op jit(solution)/shard_map/ppermute | solution.py:303
  22.6 1.5 %collective-permute-start.5 = (bf16[96,1152]{1,0:T(8,128)(2,1)S(1)}, bf16[96,1152]{1,0:T(8,128)(2,1)S(1)}, u32[]{:S(2)}, u32[]{:S(2)}) collective-permute-start(bf16[96,1152]{1,0:T(8,128)(2,1)S(1)} %slice.16), channel_id=1, source_target_pairs={{0,1},{1,0},{2,3},{3,2},{4,5},{5,4},{6,7},{7,6},{8,9},{9,8},{10,11... | collective-permute-start | bytes 663560 | tf_op jit(solution)/shard_map/ppermute | solution.py:303
  23.0 1.5 %collective-permute-start.6 = (bf16[96,1152]{1,0:T(8,128)(2,1)S(1)}, bf16[96,1152]{1,0:T(8,128)(2,1)S(1)}, u32[]{:S(2)}, u32[]{:S(2)}) collective-permute-start(bf16[96,1152]{1,0:T(8,128)(2,1)S(1)} %slice.17), channel_id=1, source_target_pairs={{0,1},{1,0},{2,3},{3,2},{4,5},{5,4},{6,7},{7,6},{8,9},{9,8},{10,11... | collective-permute-start | bytes 663560 | tf_op jit(solution)/shard_map/ppermute | solution.py:303
  25.2 11.6 %copy-start.1 = (f32[16,48]{1,0:T(8,128)S(1)}, f32[16,48]{1,0:T(8,128)}, u32[]{:S(2)}) copy-start(f32[16,48]{1,0:T(8,128)} %get-tuple-element.37.own) | copy-start | bytes 9220
  25.2 19.6 %copy-start = (bf16[48,8,2560]{2,1,0:T(8,128)(2,1)S(1)}, bf16[48,8,2560]{2,1,0:T(8,128)(2,1)}, u32[]{:S(2)}) copy-start(bf16[48,8,2560]{2,1,0:T(8,128)(2,1)} %param.8) | copy-start | bytes 5898244
  28.6 1.5 %collective-permute-start.7 = (bf16[96,1152]{1,0:T(8,128)(2,1)S(1)}, bf16[96,1152]{1,0:T(8,128)(2,1)S(1)}, u32[]{:S(2)}, u32[]{:S(2)}) collective-permute-start(bf16[96,1152]{1,0:T(8,128)(2,1)S(1)} %slice.14), channel_id=1, source_target_pairs={{0,1},{1,0},{2,3},{3,2},{4,5},{5,4},{6,7},{7,6},{8,9},{9,8},{10,11... | collective-permute-start | bytes 663560 | tf_op jit(solution)/shard_map/ppermute | solution.py:303
  28.7 1.8 %collective-permute-start.8 = (bf16[96,1152]{1,0:T(8,128)(2,1)S(1)}, bf16[96,1152]{1,0:T(8,128)(2,1)S(1)}, u32[]{:S(2)}, u32[]{:S(2)}) collective-permute-start(bf16[96,1152]{1,0:T(8,128)(2,1)S(1)} %slice.15), channel_id=1, source_target_pairs={{0,1},{1,0},{2,3},{3,2},{4,5},{5,4},{6,7},{7,6},{8,9},{9,8},{10,11... | collective-permute-start | bytes 663560 | tf_op jit(solution)/shard_map/ppermute | solution.py:303
  31.4 12.5 %collective-permute-start.10 = (bf16[416,128]{1,0:T(8,128)(2,1)S(1)}, bf16[416,128]{1,0:T(8,128)(2,1)S(1)}, u32[]{:S(2)}, u32[]{:S(2)}) collective-permute-start(bf16[416,128]{1,0:T(8,128)(2,1)S(1)} %get-tuple-element.35), channel_id=1, source_target_pairs={{0,8},{1,9},{2,10},{3,11},{4,12},{5,13},{6,14},{7,15},{8,0},{9,1},... | collective-permute-start | bytes 319496 | tf_op jit(solution)/shard_map/ppermute | solution.py:303
  35.5 8.4 %collective-permute-start.11 = (bf16[416,128]{1,0:T(8,128)(2,1)S(1)}, bf16[416,128]{1,0:T(8,128)(2,1)S(1)}, u32[]{:S(2)}, u32[]{:S(2)}) collective-permute-start(bf16[416,128]{1,0:T(8,128)(2,1)S(1)} %get-tuple-element.36), channel_id=1, source_target_pairs={{0,12},{1,13},{2,14},{3,15},{4,8},{5,9},{6,10},{7,11},{8,4},{9,5},... | collective-permute-start | bytes 319496 | tf_op jit(solution)/shard_map/ppermute | solution.py:303
  36.8 8.0 %collective-permute-start.9 = (bf16[416,128]{1,0:T(8,128)(2,1)S(1)}, bf16[416,128]{1,0:T(8,128)(2,1)S(1)}, u32[]{:S(2)}, u32[]{:S(2)}) collective-permute-start(bf16[416,128]{1,0:T(8,128)(2,1)S(1)} %get-tuple-element.34), channel_id=1, source_target_pairs={{0,4},{1,5},{2,6},{3,7},{4,0},{5,1},{6,2},{7,3},{8,12},{9,13},{10,... | collective-permute-start | bytes 319496 | tf_op jit(solution)/shard_map/ppermute | solution.py:303
  36.8 1.2 %collective-permute-start.12 = (f32[16,48]{1,0:T(8,128)S(1)}, f32[16,48]{1,0:T(8,128)S(1)}, u32[]{:S(2)}, u32[]{:S(2)}) collective-permute-start(f32[16,48]{1,0:T(8,128)S(1)} %copy-done.1), channel_id=1, source_target_pairs={{0,1},{1,0},{2,3},{3,2},{4,5},{5,4},{6,7},{7,6},{8,9},{9,8},{10,11... | collective-permute-start | bytes 9224 | tf_op jit(solution)/shard_map/ppermute | solution.py:303
  46.6 10.7 %collective-permute-start.18 = (bf16[4,32,1280]{2,1,0:T(8,128)(2,1)S(1)}, bf16[4,32,1280]{2,1,0:T(8,128)(2,1)S(1)}, u32[]{:S(2)}, u32[]{:S(2)}) collective-permute-start(bf16[4,32,1280]{2,1,0:T(8,128)(2,1)S(1)} %bitcast.34), channel_id=1, source_target_pairs={{0,2},{1,3},{2,0},{3,1},{4,6},{5,7},{6,4},{7,5},{8,10},{9,11},{10,... | collective-permute-start | bytes 983048 | tf_op jit(solution)/shard_map/ppermute | solution.py:303
  48.2 14.1 %collective-permute-start.14 = (bf16[4,32,1280]{2,1,0:T(8,128)(2,1)S(1)}, bf16[4,32,1280]{2,1,0:T(8,128)(2,1)S(1)}, u32[]{:S(2)}, u32[]{:S(2)}) collective-permute-start(bf16[4,32,1280]{2,1,0:T(8,128)(2,1)S(1)} %bitcast.33), channel_id=1, source_target_pairs={{0,2},{1,3},{2,0},{3,1},{4,6},{5,7},{6,4},{7,5},{8,10},{9,11},{10,... | collective-permute-start | bytes 983048 | tf_op jit(solution)/shard_map/ppermute | solution.py:303
  57.5 7.7 %collective-permute-start.19 = (bf16[32,1280]{1,0:T(8,128)(2,1)S(1)}, bf16[32,1280]{1,0:T(8,128)(2,1)S(1)}, u32[]{:S(2)}, u32[]{:S(2)}) collective-permute-start(bf16[32,1280]{1,0:T(8,128)(2,1)S(1)} %get-tuple-element.52), channel_id=1, source_target_pairs={{0,4},{1,5},{2,6},{3,7},{4,0},{5,1},{6,2},{7,3},{8,12},{9,13},{10,... | collective-permute-start | bytes 245768 | tf_op jit(solution)/shard_map/ppermute | solution.py:303
  59.0 8.3 %collective-permute-start.20 = (bf16[32,1280]{1,0:T(8,128)(2,1)S(1)}, bf16[32,1280]{1,0:T(8,128)(2,1)S(1)}, u32[]{:S(2)}, u32[]{:S(2)}) collective-permute-start(bf16[32,1280]{1,0:T(8,128)(2,1)S(1)} %get-tuple-element.51), channel_id=1, source_target_pairs={{0,8},{1,9},{2,10},{3,11},{4,12},{5,13},{6,14},{7,15},{8,0},{9,1},... | collective-permute-start | bytes 245768 | tf_op jit(solution)/shard_map/ppermute | solution.py:303
  59.8 7.5 %collective-permute-start.21 = (bf16[32,1280]{1,0:T(8,128)(2,1)S(1)}, bf16[32,1280]{1,0:T(8,128)(2,1)S(1)}, u32[]{:S(2)}, u32[]{:S(2)}) collective-permute-start(bf16[32,1280]{1,0:T(8,128)(2,1)S(1)} %get-tuple-element.50), channel_id=1, source_target_pairs={{0,12},{1,13},{2,14},{3,15},{4,8},{5,9},{6,10},{7,11},{8,4},{9,5},... | collective-permute-start | bytes 245768 | tf_op jit(solution)/shard_map/ppermute | solution.py:303
  62.4 5.4 %collective-permute-start.15 = (bf16[32,1280]{1,0:T(8,128)(2,1)S(1)}, bf16[32,1280]{1,0:T(8,128)(2,1)S(1)}, u32[]{:S(2)}, u32[]{:S(2)}) collective-permute-start(bf16[32,1280]{1,0:T(8,128)(2,1)S(1)} %get-tuple-element.56), channel_id=1, source_target_pairs={{0,4},{1,5},{2,6},{3,7},{4,0},{5,1},{6,2},{7,3},{8,12},{9,13},{10,... | collective-permute-start | bytes 245768 | tf_op jit(solution)/shard_map/ppermute | solution.py:303
  64.8 8.2 %collective-permute-start.16 = (bf16[32,1280]{1,0:T(8,128)(2,1)S(1)}, bf16[32,1280]{1,0:T(8,128)(2,1)S(1)}, u32[]{:S(2)}, u32[]{:S(2)}) collective-permute-start(bf16[32,1280]{1,0:T(8,128)(2,1)S(1)} %get-tuple-element.55), channel_id=1, source_target_pairs={{0,8},{1,9},{2,10},{3,11},{4,12},{5,13},{6,14},{7,15},{8,0},{9,1},... | collective-permute-start | bytes 245768 | tf_op jit(solution)/shard_map/ppermute | solution.py:303
  65.1 7.9 %collective-permute-start.17 = (bf16[32,1280]{1,0:T(8,128)(2,1)S(1)}, bf16[32,1280]{1,0:T(8,128)(2,1)S(1)}, u32[]{:S(2)}, u32[]{:S(2)}) collective-permute-start(bf16[32,1280]{1,0:T(8,128)(2,1)S(1)} %get-tuple-element.54), channel_id=1, source_target_pairs={{0,12},{1,13},{2,14},{3,15},{4,8},{5,9},{6,10},{7,11},{8,4},{9,5},... | collective-permute-start | bytes 245768 | tf_op jit(solution)/shard_map/ppermute | solution.py:303

commit v10 on v9

--- a/solution.py
+++ b/solution.py
@@ -9,7 +9,6 @@
 from jax.sharding import PartitionSpec as P
 
 AXES = ("expert", "dp")
-CHUNKS = 2
 SLICES = 4
 LIMIT = 12 * 1024 * 1024
 LARGE = 56 * 1024 * 1024
@@ -169,18 +168,17 @@
     rank = columns.shape[0] // (SLICES * low)
     share = x.shape[1]
     lanes = y.shape[1]
-    rows = near_x.shape[0]
-    tok = rows // 2
+    tok = near_x.shape[0] // 2
     total = (part[...] + dot(y[...], x[...], 0, 0)).astype(BF16)
     columns[...] = total
-    own = jnp.concatenate([near_x[:, lanes : lanes + share], far_x[:, :share]], axis=0)
-    halves = [dot(own, total, 1, 1), dot(x[: 2 * rows], total, 1, 1)]
+    own = [near_x[:tok, lanes : lanes + share], far_x[:tok, :share]]
+    own += [near_x[tok:, lanes : lanes + share], far_x[tok:, :share]]
+    own += [x[: 2 * tok], x[n * tok : (n + 2) * tok]]
+    z = dot(jnp.concatenate(own, axis=0), total, 1, 1).astype(BF16)
     for j, out in enumerate(outs):
-        half = halves[j // 2].astype(BF16)
-        start = j % 2 * tok
-        z = jnp.concatenate([half[start : start + tok], half[rows + start :][:tok]], axis=0)
         expert = (place ^ j) * low + lower
-        out[...] = pack(z, columns[pl.ds(pl.multiple_of(expert * rank, rank), rank)])
+        own = columns[pl.ds(pl.multiple_of(expert * rank, rank), rank)]
+        out[...] = pack(z[2 * j * tok : 2 * (j + 1) * tok], own)
 
 
 def inverse_kernel(start, p0, p1, p2, p3, inverse, basis, columns):
@@ -225,13 +223,16 @@
 
 def coeffs_kernel(scale, inverse, *refs):
     blocks, out = refs[:-1], refs[-1]
-    rank, size = blocks[0].shape
+    rank = inverse.shape[0]
     left = jnp.concatenate(pieces(inverse[...] * scale, 3), axis=0)
     left = jnp.concatenate([left] * SLICES, axis=1)
-    for i in range(len(blocks) // SLICES):
-        right = jnp.concatenate([b[...] for b in blocks[i * SLICES : (i + 1) * SLICES]], axis=0)
+    start = 0
+    for i in range(0, len(blocks), SLICES):
+        right = jnp.concatenate([b[...] for b in blocks[i : i + SLICES]], axis=0)
         part = dot(left, right, 1, 0)
-        out[:, i * size : (i + 1) * size] = part[:rank] + part[rank : 2 * rank] + part[2 * rank :]
+        part = part[:rank] + part[rank : 2 * rank] + part[2 * rank :]
+        out[:, start : start + right.shape[1]] = part
+        start += right.shape[1]
 
 
 def mask_kernel(groups, own, pair, out):
@@ -271,13 +272,15 @@
             spread[(r * SLICES + j) * rank : (r * SLICES + j + 1) * rank] = work[
                 pl.ds(start, rank)
             ]
-    for chunk in range(len(outs) // low):
-        block, width = outs[chunk * low].shape
-        here = slice(chunk * width, (chunk + 1) * width)
+    start = 0
+    for chunk in range(0, len(outs), low):
+        block, width = outs[chunk].shape
+        here = slice(start, start + width)
         part = dot(spread[:, :rows], mine[:, here], 1, 0)
         part = (part + dot(spread[:, rows:], other[:, here], 1, 0)).astype(BF16)
         for r in range(low):
-            outs[chunk * low + r][...] = part[r * block : (r + 1) * block]
+            outs[chunk + r][...] = part[r * block : (r + 1) * block]
+        start += width
 
 
 def shards(tokens, expert_ids, route_probs, cotangents, sketch):
@@ -330,12 +333,13 @@
     )
     blocks = blocks[:1] + [exchange(blocks[j], j * line) for j in range(1, SLICES)]
     pairs = [pairs, exchange(pairs, 1)]
-    near = [[jnp.concatenate(blocks[i : i + 2], axis=0)] for i in range(0, SLICES, 2)]
+    near = [[jnp.concatenate(blocks[:2], axis=0)], [blocks[2]], [blocks[3]]]
     step = 2
     while step < line:
         near = [side + [exchange(b, step) for b in side] for side in near]
         step *= 2
     n = len(near[0])
+    late = near[1] + near[2]
     skip = lanes if groups == 2 else 0
 
     size = 2 * tok * lanes // 128
@@ -354,29 +358,29 @@
             *near[0],
             *far,
         )
-        near[1], columns = lax.optimization_barrier((near[1], columns))
+        late[-1], columns = lax.optimization_barrier((late[-1], columns))
         zs = call(
-            functools.partial(z_kernel, n, low),
+            functools.partial(z_kernel, 2 * n, low),
             [shape((size + rank * share // 128, 128), BF16)] * SLICES,
-            [VMEM] * 3 + [HBM] * (2 * n),
-            work[:2] + [pltpu.VMEM((lanes, share), BF16)] + work[2:],
+            [VMEM] * 3 + [HBM] * (4 * n),
+            work[:2]
+            + [pltpu.VMEM((lanes, share), BF16), pltpu.SemaphoreType.DMA((8 * n,))],
             columns,
             near[0][0],
             far[0],
-            *near[1],
-            *[exchange(b[:, skip:], 1) for b in near[1]],
+            *late,
+            *[exchange(b[:, skip:], 1) for b in late],
         )
     else:
-        far = [far, [exchange(b[:, skip:], 1) for b in near[1]]]
-        rows_all = jnp.concatenate(near[0] + far[0] + near[1] + far[1], axis=0)
+        far += [exchange(b[:, skip:], 1) for b in late]
+        rows_all = jnp.concatenate(near[0] + late + far, axis=0)
         columns = dot(rows_all[:, :lanes], rows_all[:, lanes:], 0, 0).astype(BF16)
         zs = []
-        for j in range(SLICES):
-            here = slice(j % 2 * tok, (j % 2 + 1) * tok)
-            x = jnp.concatenate([near[j // 2][0][here], far[j // 2][0][here]], axis=0)
+        for j, (b, i) in enumerate([(0, 0), (0, tok), (n, 0), (2 * n, 0)]):
+            x = [side[b][i : i + tok, lanes:] for side in (near[0] + late, far)]
             start = ((place ^ j) * low + lower) * rank
             own = lax.dynamic_slice_in_dim(columns, start, rank, axis=0)
-            zs.append(pack(dot(x[:, lanes:], columns, 1, 1).astype(BF16), own))
+            zs.append(pack(dot(jnp.concatenate(x, axis=0), columns, 1, 1).astype(BF16), own))
     zs = list(zs[:1]) + [exchange(zs[j], j * line) for j in range(1, SLICES)]
 
     [mask] = call(
@@ -387,10 +391,11 @@
         *pairs,
         limit=limit,
     )
-    piece = part // CHUNKS
+    piece = part // 128 * 3 // 10 * 128
+    chunks = [part - 2 * piece, piece, piece]
     terms = call(
         functools.partial(terms_kernel, low, tok),
-        [shape((SLICES * rank, piece), BF16)] * (low * CHUNKS),
+        [shape((SLICES * rank, chunk), BF16) for chunk in chunks for _ in range(low)],
         [VMEM] * (SLICES + 3),
         [pltpu.VMEM((lanes, 2 * rows), BF16)] * 2,
         *zs,
@@ -408,9 +413,9 @@
         *zs,
     )
     sums = []
-    for chunk in range(CHUNKS):
-        blocks = terms[chunk * low : (chunk + 1) * low]
-        blocks = [term.reshape(SLICES, rank, piece) for term in blocks]
+    for i in range(len(chunks)):
+        blocks = terms[i * low : (i + 1) * low]
+        blocks = [term.reshape(SLICES, rank, chunks[i]) for term in blocks]
         step = 2
         while len(blocks) > 1:
             blocks = [

time: 74.3 us -> 81.3 us (1.094)
  starting transfers between devices: 26.9 us -> 34.5 us
  waiting for transfers between devices: 34 us -> 33.1 us
    ppermute x22 -> x29, starting transfers between devices: 26.9 us -> 34.5 us  [exchange(): return lax.ppermute(block, AXES, [(i, i ^ step) for i in range(count)])]
    ppermute x22 -> x29, waiting for transfers between devices: 34 us -> 33.1 us  [exchange(): return lax.ppermute(block, AXES, [(i, i ^ step) for i in range(count)])]
  transfers between devices with their start and end apart: 22 -> 29, of which waited for: 15 -> 12; matrix products, arithmetic and copies ran while one was open for 2% -> 2% of each run, Pallas kernels for 11% -> 10%
where the time goes in v10:
time: 81.3 us; the launch traced here: 81.1 us
  starting transfers between devices  34.5 us (42%)
  waiting for transfers between devices  33.1 us (41%)
  Pallas kernels  11.4 us (14%)
  local copies, waits for them, and re-layouts  1.1 us (1%)
  between operations  0.83 us (1%)
    ppermute x29, starting transfers between devices, exchange(): return lax.ppermute(block, AXES, [(i, i ^ step) for i in range(count)])  34.5 us
    ppermute x29, waiting for transfers between devices, exchange(): return lax.ppermute(block, AXES, [(i, i ^ step) for i in range(count)])  33.1 us
    pallas_call x7, Pallas kernels, call(): pl.pallas_call(body, out_shape=shapes, in_specs=spaces, out_specs=[VMEM]...  11.4 us
  transfers between devices with their start and end apart: 29, of which 12 were waited for; matrix products, arithmetic and copies ran while one was open for 2% of the time, Pallas kernels for 10%

profile of v10, /device:TPU:0, one launch (start us, length us, event | category | flops | bytes accessed | tf_op | source)
XLA Modules:
  0.0 81.1 jit_solution(3604625561899141660)
XLA Ops:
  1.1 3.8 %shard_map.68 = (bf16[48,1408]{1,0:T(8,128)(2,1)}, bf16[48,1408]{1,0:T(8,128)(2,1)}, bf16[48,1408]{1,0:T(8,128)(2,1)}, bf16[48,1408]{1,0:T(8,128)(2,1)}, f32[16,48]{1,0:T(8,128)}) custom-call(bf16[48,3584]{1,0:T(8,128)(2,1)} %tokens.1, bf16[384,2560]{1,0:T(8,128)(2,1)} %bitcast.40, f32[32,2560]{1,0:T(8,128)} %bitcast.48, s32[8,48]{1,0:T(8,128)} %bitcast.50, ...), custom_call_target="tpu_custom_call" | custom-call | flops 1 | bytes 1 | tf_op jit(solution)/shard_map/pallas_call | solution.py:38
  5.0 2.7 %collective-permute-start.2 = (bf16[48,1408]{1,0:T(8,128)(2,1)}, bf16[48,1408]{1,0:T(8,128)(2,1)S(1)}, u32[]{:S(2)}, u32[]{:S(2)}) collective-permute-start(bf16[48,1408]{1,0:T(8,128)(2,1)} %get-tuple-element.29), channel_id=1, source_target_pairs={{0,4},{1,5},{2,6},{3,7},{4,0},{5,1},{6,2},{7,3},{8,12},{9,13},{10,... | collective-permute-start | bytes 405512 | tf_op jit(solution)/shard_map/ppermute | solution.py:306
  8.5 3.5 %collective-permute-done.2 = bf16[48,1408]{1,0:T(8,128)(2,1)S(1)} collective-permute-done((bf16[48,1408]{1,0:T(8,128)(2,1)}, bf16[48,1408]{1,0:T(8,128)(2,1)S(1)}, u32[]{:S(2)}, u32[]{:S(2)}) %collective-permute-start.2) | collective-permute-done | bytes 135200 | tf_op jit(solution)/shard_map/ppermute | solution.py:306
  12.1 1.7 %collective-permute-start.3 = (bf16[96,1408]{1,0:T(8,128)(2,1)S(1)}, bf16[96,1408]{1,0:T(8,128)(2,1)S(1)}, u32[]{:S(2)}, u32[]{:S(2)}) collective-permute-start(bf16[96,1408]{1,0:T(8,128)(2,1)S(1)} %constant_dynamic-update-slice_fusion.refs_0_.near_x), channel_id=1, source_target_pairs={{0,2},{1,3},{2,0},{3,1},{4,6},{5,7},{6,4},{7,5},{8,10},{9,11},{10,... | collective-permute-start | bytes 811016 | tf_op jit(solution)/shard_map/ppermute | solution.py:306
  13.8 2.6 %collective-permute-start.6 = (bf16[48,1408]{1,0:T(8,128)(2,1)}, bf16[48,1408]{1,0:T(8,128)(2,1)S(1)}, u32[]{:S(2)}, u32[]{:S(2)}) collective-permute-start(bf16[48,1408]{1,0:T(8,128)(2,1)} %get-tuple-element.31), channel_id=1, source_target_pairs={{0,8},{1,9},{2,10},{3,11},{4,12},{5,13},{6,14},{7,15},{8,0},{9,1},... | collective-permute-start | bytes 405512 | tf_op jit(solution)/shard_map/ppermute | solution.py:306
  17.9 2.6 %collective-permute-done.3.refs_1_ = bf16[96,1408]{1,0:T(8,128)(2,1)S(1)} collective-permute-done((bf16[96,1408]{1,0:T(8,128)(2,1)S(1)}, bf16[96,1408]{1,0:T(8,128)(2,1)S(1)}, u32[]{:S(2)}, u32[]{:S(2)}) %collective-permute-start.3) | collective-permute-done | bytes 270368 | tf_op jit(solution)/shard_map/ppermute | solution.py:306
  20.6 6.2 %collective-permute-done.6.refs_0_ = bf16[48,1408]{1,0:T(8,128)(2,1)S(1)} collective-permute-done((bf16[48,1408]{1,0:T(8,128)(2,1)}, bf16[48,1408]{1,0:T(8,128)(2,1)S(1)}, u32[]{:S(2)}, u32[]{:S(2)}) %collective-permute-start.6) | collective-permute-done | bytes 135200 | tf_op jit(solution)/shard_map/ppermute | solution.py:306
  27.3 1.5 %collective-permute-start.1 = (bf16[48,1408]{1,0:T(8,128)(2,1)S(1)}, bf16[48,1408]{1,0:T(8,128)(2,1)S(1)}, u32[]{:S(2)}, u32[]{:S(2)}) collective-permute-start(bf16[48,1408]{1,0:T(8,128)(2,1)S(1)} %collective-permute-done.refs_2_), channel_id=1, source_target_pairs={{0,2},{1,3},{2,0},{3,1},{4,6},{5,7},{6,4},{7,5},{8,10},{9,11},{10,... | collective-permute-start | bytes 405512 | tf_op jit(solution)/shard_map/ppermute | solution.py:306
  28.9 3.0 %collective-permute-done.7.refs_1_ = bf16[48,1408]{1,0:T(8,128)(2,1)S(1)} collective-permute-done((bf16[48,1408]{1,0:T(8,128)(2,1)S(1)}, bf16[48,1408]{1,0:T(8,128)(2,1)S(1)}, u32[]{:S(2)}, u32[]{:S(2)}) %collective-permute-start.7) | collective-permute-done | bytes 135200 | tf_op jit(solution)/shard_map/ppermute | solution.py:306
  35.8 1.6 %collective-permute-start.12 = (bf16[416,128]{1,0:T(8,128)(2,1)S(1)}, bf16[416,128]{1,0:T(8,128)(2,1)S(1)}, u32[]{:S(2)}, u32[]{:S(2)}) collective-permute-start(bf16[416,128]{1,0:T(8,128)(2,1)S(1)} %get-tuple-element.34), channel_id=1, source_target_pairs={{0,4},{1,5},{2,6},{3,7},{4,0},{5,1},{6,2},{7,3},{8,12},{9,13},{10,... | collective-permute-start | bytes 319496 | tf_op jit(solution)/shard_map/ppermute | solution.py:306
  37.4 3.3 %collective-permute-start.13 = (bf16[416,128]{1,0:T(8,128)(2,1)S(1)}, bf16[416,128]{1,0:T(8,128)(2,1)S(1)}, u32[]{:S(2)}, u32[]{:S(2)}) collective-permute-start(bf16[416,128]{1,0:T(8,128)(2,1)S(1)} %get-tuple-element.35), channel_id=1, source_target_pairs={{0,8},{1,9},{2,10},{3,11},{4,12},{5,13},{6,14},{7,15},{8,0},{9,1},... | collective-permute-start | bytes 319496 | tf_op jit(solution)/shard_map/ppermute | solution.py:306
  42.1 6.9 %collective-permute-done.13.z2.p2 = bf16[416,128]{1,0:T(8,128)(2,1)S(1)} collective-permute-done((bf16[416,128]{1,0:T(8,128)(2,1)S(1)}, bf16[416,128]{1,0:T(8,128)(2,1)S(1)}, u32[]{:S(2)}, u32[]{:S(2)}) %collective-permute-start.13) | collective-permute-done | bytes 106528 | tf_op jit(solution)/shard_map/ppermute | solution.py:306
  49.1 1.8 %shard_map.72 = (bf16[128,1024]{1,0:T(8,128)(2,1)S(1)}, bf16[128,1024]{1,0:T(8,128)(2,1)S(1)}, bf16[128,768]{1,0:T(8,128)(2,1)S(1)}, bf16[128,768]{1,0:T(8,128)(...) custom-call(bf16[416,128]{1,0:T(8,128)(2,1)S(1)} %get-tuple-element.39.z0.p0, ...), custom_call_target="tpu_custom_call" | custom-call | flops 1 | bytes 1 | tf_op jit(solution)/shard_map/pallas_call | solution.py:38
  51.4 1.5 %collective-permute-start.21 = (bf16[4,32,768]{2,1,0:T(8,128)(2,1)S(1)}, bf16[4,32,768]{2,1,0:T(8,128)(2,1)S(1)}, u32[]{:S(2)}, u32[]{:S(2)}) collective-permute-start(bf16[4,32,768]{2,1,0:T(8,128)(2,1)S(1)} %bitcast.46), channel_id=1, source_target_pairs={{0,2},{1,3},{2,0},{3,1},{4,6},{5,7},{6,4},{7,5},{8,10},{9,11},{10,... | collective-permute-start | bytes 589832 | tf_op jit(solution)/shard_map/ppermute | solution.py:306
  53.5 2.7 %shard_map.73 = (f32[32,32]{1,0:T(8,128)S(1)}, f32[32,3584]{1,0:T(8,128)}) custom-call(bf16[416,128]{1,0:T(8,128)(2,1)S(1)} %get-tuple-element.39.z0.p0, bf16[416,128]{1,0:T(8,128)(2,1)S(1)} %collective-permute-done.12.z1.p1, bf16[416,128]{1,0:T(8,128)(2,1)S(1)} %collective-permute-done.13.z2.p2, bf16[416,128]{1,0:T(8,128)(2,1)S(1)} %collective-permute-done.14.z3.p3), custom_call_target="tpu_custom_call" | custom-call | flops 1 | bytes 1 | tf_op jit(solution)/shard_map/pallas_call | solution.py:38
  56.2 2.6 %collective-permute-done.25 = bf16[4,32,768]{2,1,0:T(8,128)(2,1)S(1)} collective-permute-done((bf16[4,32,768]{2,1,0:T(8,128)(2,1)S(1)}, bf16[4,32,768]{2,1,0:T(8,128)(2,1)S(1)}, u32[]{:S(2)}, u32[]{:S(2)}) %collective-permute-start.25) | collective-permute-done | bytes 196640 | tf_op jit(solution)/shard_map/ppermute | solution.py:306
  58.8 2.1 %collective-permute-start.26 = (bf16[32,768]{1,0:T(8,128)(2,1)S(1)}, bf16[32,768]{1,0:T(8,128)(2,1)S(1)}, u32[]{:S(2)}, u32[]{:S(2)}) collective-permute-start(bf16[32,768]{1,0:T(8,128)(2,1)S(1)} %get-tuple-element.58), channel_id=1, source_target_pairs={{0,4},{1,5},{2,6},{3,7},{4,0},{5,1},{6,2},{7,3},{8,12},{9,13},{10,... | collective-permute-start | bytes 147464 | tf_op jit(solution)/shard_map/ppermute | solution.py:306
  61.0 1.4 %collective-permute-start.27 = (bf16[32,768]{1,0:T(8,128)(2,1)S(1)}, bf16[32,768]{1,0:T(8,128)(2,1)S(1)}, u32[]{:S(2)}, u32[]{:S(2)}) collective-permute-start(bf16[32,768]{1,0:T(8,128)(2,1)S(1)} %get-tuple-element.57), channel_id=1, source_target_pairs={{0,8},{1,9},{2,10},{3,11},{4,12},{5,13},{6,14},{7,15},{8,0},{9,1},... | collective-permute-start | bytes 147464 | tf_op jit(solution)/shard_map/ppermute | solution.py:306
  63.7 1.5 %collective-permute-start.22 = (bf16[32,768]{1,0:T(8,128)(2,1)S(1)}, bf16[32,768]{1,0:T(8,128)(2,1)S(1)}, u32[]{:S(2)}, u32[]{:S(2)}) collective-permute-start(bf16[32,768]{1,0:T(8,128)(2,1)S(1)} %get-tuple-element.62), channel_id=1, source_target_pairs={{0,4},{1,5},{2,6},{3,7},{4,0},{5,1},{6,2},{7,3},{8,12},{9,13},{10,... | collective-permute-start | bytes 147464 | tf_op jit(solution)/shard_map/ppermute | solution.py:306
  66.2 2.9 %collective-permute-start.18 = (bf16[32,1024]{1,0:T(8,128)(2,1)S(1)}, bf16[32,1024]{1,0:T(8,128)(2,1)S(1)}, u32[]{:S(2)}, u32[]{:S(2)}) collective-permute-start(bf16[32,1024]{1,0:T(8,128)(2,1)S(1)} %get-tuple-element.54), channel_id=1, source_target_pairs={{0,4},{1,5},{2,6},{3,7},{4,0},{5,1},{6,2},{7,3},{8,12},{9,13},{10,... | collective-permute-start | bytes 196616 | tf_op jit(solution)/shard_map/ppermute | solution.py:306
  70.2 1.4 %collective-permute-start.20 = (bf16[32,1024]{1,0:T(8,128)(2,1)S(1)}, bf16[32,1024]{1,0:T(8,128)(2,1)S(1)}, u32[]{:S(2)}, u32[]{:S(2)}) collective-permute-start(bf16[32,1024]{1,0:T(8,128)(2,1)S(1)} %get-tuple-element.52), channel_id=1, source_target_pairs={{0,12},{1,13},{2,14},{3,15},{4,8},{5,9},{6,10},{7,11},{8,4},{9,5},... | collective-permute-start | bytes 196616 | tf_op jit(solution)/shard_map/ppermute | solution.py:306
  71.6 2.0 %collective-permute-start.23 = (bf16[32,768]{1,0:T(8,128)(2,1)S(1)}, bf16[32,768]{1,0:T(8,128)(2,1)S(1)}, u32[]{:S(2)}, u32[]{:S(2)}) collective-permute-start(bf16[32,768]{1,0:T(8,128)(2,1)S(1)} %get-tuple-element.61), channel_id=1, source_target_pairs={{0,8},{1,9},{2,10},{3,11},{4,12},{5,13},{6,14},{7,15},{8,0},{9,1},... | collective-permute-start | bytes 147464 | tf_op jit(solution)/shard_map/ppermute | solution.py:306
  73.6 1.4 %collective-permute-start.24 = (bf16[32,768]{1,0:T(8,128)(2,1)S(1)}, bf16[32,768]{1,0:T(8,128)(2,1)S(1)}, u32[]{:S(2)}, u32[]{:S(2)}) collective-permute-start(bf16[32,768]{1,0:T(8,128)(2,1)S(1)} %get-tuple-element.60), channel_id=1, source_target_pairs={{0,12},{1,13},{2,14},{3,15},{4,8},{5,9},{6,10},{7,11},{8,4},{9,5},... | collective-permute-start | bytes 147464 | tf_op jit(solution)/shard_map/ppermute | solution.py:306
  75.0 5.0 %collective-permute-done.23.refs_6_ = bf16[32,768]{1,0:T(8,128)(2,1)S(1)} collective-permute-done((bf16[32,768]{1,0:T(8,128)(2,1)S(1)}, bf16[32,768]{1,0:T(8,128)(2,1)S(1)}, u32[]{:S(2)}, u32[]{:S(2)}) %collective-permute-start.23) | collective-permute-done | bytes 49184 | tf_op jit(solution)/shard_map/ppermute | solution.py:306
  (59 shorter events, 14.6 us)
Async XLA Ops:
  0.6 48.4 %collective-permute-start.16 = (bf16[384,2560]{1,0:T(8,128)(2,1)}, bf16[384,2560]{1,0:T(8,128)(2,1)S(1)}, u32[]{:S(2)}, u32[]{:S(2)}) collective-permute-start(bf16[384,2560]{1,0:T(8,128)(2,1)} %bitcast.39), channel_id=1, source_target_pairs={{0,1},{1,0},{2,3},{3,2},{4,5},{5,4},{6,7},{7,6},{8,9},{9,8},{10,11... | collective-permute-start | bytes 5898248 | tf_op jit(solution)/shard_map/ppermute | solution.py:306
  5.0 7.1 %collective-permute-start.2 = (bf16[48,1408]{1,0:T(8,128)(2,1)}, bf16[48,1408]{1,0:T(8,128)(2,1)S(1)}, u32[]{:S(2)}, u32[]{:S(2)}) collective-permute-start(bf16[48,1408]{1,0:T(8,128)(2,1)} %get-tuple-element.29), channel_id=1, source_target_pairs={{0,4},{1,5},{2,6},{3,7},{4,0},{5,1},{6,2},{7,3},{8,12},{9,13},{10,... | collective-permute-start | bytes 405512 | tf_op jit(solution)/shard_map/ppermute | solution.py:306
  12.1 8.4 %collective-permute-start.3 = (bf16[96,1408]{1,0:T(8,128)(2,1)S(1)}, bf16[96,1408]{1,0:T(8,128)(2,1)S(1)}, u32[]{:S(2)}, u32[]{:S(2)}) collective-permute-start(bf16[96,1408]{1,0:T(8,128)(2,1)S(1)} %constant_dynamic-update-slice_fusion.refs_0_.near_x), channel_id=1, source_target_pairs={{0,2},{1,3},{2,0},{3,1},{4,6},{5,7},{6,4},{7,5},{8,10},{9,11},{10,... | collective-permute-start | bytes 811016 | tf_op jit(solution)/shard_map/ppermute | solution.py:306
  13.8 13.0 %collective-permute-start.6 = (bf16[48,1408]{1,0:T(8,128)(2,1)}, bf16[48,1408]{1,0:T(8,128)(2,1)S(1)}, u32[]{:S(2)}, u32[]{:S(2)}) collective-permute-start(bf16[48,1408]{1,0:T(8,128)(2,1)} %get-tuple-element.31), channel_id=1, source_target_pairs={{0,8},{1,9},{2,10},{3,11},{4,12},{5,13},{6,14},{7,15},{8,0},{9,1},... | collective-permute-start | bytes 405512 | tf_op jit(solution)/shard_map/ppermute | solution.py:306
  16.4 10.9 %collective-permute-start = (bf16[48,1408]{1,0:T(8,128)(2,1)}, bf16[48,1408]{1,0:T(8,128)(2,1)S(1)}, u32[]{:S(2)}, u32[]{:S(2)}) collective-permute-start(bf16[48,1408]{1,0:T(8,128)(2,1)} %get-tuple-element.27), channel_id=1, source_target_pairs={{0,12},{1,13},{2,14},{3,15},{4,8},{5,9},{6,10},{7,11},{8,4},{9,5},... | collective-permute-start | bytes 405512 | tf_op jit(solution)/shard_map/ppermute | solution.py:306
  17.8 14.1 %collective-permute-start.4 = (bf16[96,1152]{1,0:T(8,128)(2,1)S(1)}, bf16[96,1152]{1,0:T(8,128)(2,1)S(1)}, u32[]{:S(2)}, u32[]{:S(2)}) collective-permute-start(bf16[96,1152]{1,0:T(8,128)(2,1)S(1)} %slice.24), channel_id=1, source_target_pairs={{0,1},{1,0},{2,3},{3,2},{4,5},{5,4},{6,7},{7,6},{8,9},{9,8},{10,11... | collective-permute-start | bytes 663560 | tf_op jit(solution)/shard_map/ppermute | solution.py:306
  20.5 12.0 %collective-permute-start.5 = (bf16[96,1152]{1,0:T(8,128)(2,1)S(1)}, bf16[96,1152]{1,0:T(8,128)(2,1)S(1)}, u32[]{:S(2)}, u32[]{:S(2)}) collective-permute-start(bf16[96,1152]{1,0:T(8,128)(2,1)S(1)} %slice.25), channel_id=1, source_target_pairs={{0,1},{1,0},{2,3},{3,2},{4,5},{5,4},{6,7},{7,6},{8,9},{9,8},{10,11... | collective-permute-start | bytes 663560 | tf_op jit(solution)/shard_map/ppermute | solution.py:306
  26.8 5.0 %collective-permute-start.7 = (bf16[48,1408]{1,0:T(8,128)(2,1)S(1)}, bf16[48,1408]{1,0:T(8,128)(2,1)S(1)}, u32[]{:S(2)}, u32[]{:S(2)}) collective-permute-start(bf16[48,1408]{1,0:T(8,128)(2,1)S(1)} %collective-permute-done.6.refs_0_), channel_id=1, source_target_pairs={{0,2},{1,3},{2,0},{3,1},{4,6},{5,7},{6,4},{7,5},{8,10},{9,11},{10,... | collective-permute-start | bytes 405512 | tf_op jit(solution)/shard_map/ppermute | solution.py:306
  27.3 5.9 %collective-permute-start.1 = (bf16[48,1408]{1,0:T(8,128)(2,1)S(1)}, bf16[48,1408]{1,0:T(8,128)(2,1)S(1)}, u32[]{:S(2)}, u32[]{:S(2)}) collective-permute-start(bf16[48,1408]{1,0:T(8,128)(2,1)S(1)} %collective-permute-done.refs_2_), channel_id=1, source_target_pairs={{0,2},{1,3},{2,0},{3,1},{4,6},{5,7},{6,4},{7,5},{8,10},{9,11},{10,... | collective-permute-start | bytes 405512 | tf_op jit(solution)/shard_map/ppermute | solution.py:306
  35.8 6.3 %collective-permute-start.12 = (bf16[416,128]{1,0:T(8,128)(2,1)S(1)}, bf16[416,128]{1,0:T(8,128)(2,1)S(1)}, u32[]{:S(2)}, u32[]{:S(2)}) collective-permute-start(bf16[416,128]{1,0:T(8,128)(2,1)S(1)} %get-tuple-element.34), channel_id=1, source_target_pairs={{0,4},{1,5},{2,6},{3,7},{4,0},{5,1},{6,2},{7,3},{8,12},{9,13},{10,... | collective-permute-start | bytes 319496 | tf_op jit(solution)/shard_map/ppermute | solution.py:306
  37.4 11.6 %collective-permute-start.13 = (bf16[416,128]{1,0:T(8,128)(2,1)S(1)}, bf16[416,128]{1,0:T(8,128)(2,1)S(1)}, u32[]{:S(2)}, u32[]{:S(2)}) collective-permute-start(bf16[416,128]{1,0:T(8,128)(2,1)S(1)} %get-tuple-element.35), channel_id=1, source_target_pairs={{0,8},{1,9},{2,10},{3,11},{4,12},{5,13},{6,14},{7,15},{8,0},{9,1},... | collective-permute-start | bytes 319496 | tf_op jit(solution)/shard_map/ppermute | solution.py:306
  40.7 8.4 %collective-permute-start.14 = (bf16[416,128]{1,0:T(8,128)(2,1)S(1)}, bf16[416,128]{1,0:T(8,128)(2,1)S(1)}, u32[]{:S(2)}, u32[]{:S(2)}) collective-permute-start(bf16[416,128]{1,0:T(8,128)(2,1)S(1)} %get-tuple-element.36), channel_id=1, source_target_pairs={{0,12},{1,13},{2,14},{3,15},{4,8},{5,9},{6,10},{7,11},{8,4},{9,5},... | collective-permute-start | bytes 319496 | tf_op jit(solution)/shard_map/ppermute | solution.py:306
  50.9 7.9 %collective-permute-start.25 = (bf16[4,32,768]{2,1,0:T(8,128)(2,1)S(1)}, bf16[4,32,768]{2,1,0:T(8,128)(2,1)S(1)}, u32[]{:S(2)}, u32[]{:S(2)}) collective-permute-start(bf16[4,32,768]{2,1,0:T(8,128)(2,1)S(1)} %bitcast.47), channel_id=1, source_target_pairs={{0,2},{1,3},{2,0},{3,1},{4,6},{5,7},{6,4},{7,5},{8,10},{9,11},{10,... | collective-permute-start | bytes 589832 | tf_op jit(solution)/shard_map/ppermute | solution.py:306
  51.4 12.2 %collective-permute-start.21 = (bf16[4,32,768]{2,1,0:T(8,128)(2,1)S(1)}, bf16[4,32,768]{2,1,0:T(8,128)(2,1)S(1)}, u32[]{:S(2)}, u32[]{:S(2)}) collective-permute-start(bf16[4,32,768]{2,1,0:T(8,128)(2,1)S(1)} %bitcast.46), channel_id=1, source_target_pairs={{0,2},{1,3},{2,0},{3,1},{4,6},{5,7},{6,4},{7,5},{8,10},{9,11},{10,... | collective-permute-start | bytes 589832 | tf_op jit(solution)/shard_map/ppermute | solution.py:306
  52.9 13.2 %collective-permute-start.17 = (bf16[4,32,1024]{2,1,0:T(8,128)(2,1)S(1)}, bf16[4,32,1024]{2,1,0:T(8,128)(2,1)S(1)}, u32[]{:S(2)}, u32[]{:S(2)}) collective-permute-start(bf16[4,32,1024]{2,1,0:T(8,128)(2,1)S(1)} %bitcast.45), channel_id=1, source_target_pairs={{0,2},{1,3},{2,0},{3,1},{4,6},{5,7},{6,4},{7,5},{8,10},{9,11},{10,... | collective-permute-start | bytes 786440 | tf_op jit(solution)/shard_map/ppermute | solution.py:306
  58.8 10.2 %collective-permute-start.26 = (bf16[32,768]{1,0:T(8,128)(2,1)S(1)}, bf16[32,768]{1,0:T(8,128)(2,1)S(1)}, u32[]{:S(2)}, u32[]{:S(2)}) collective-permute-start(bf16[32,768]{1,0:T(8,128)(2,1)S(1)} %get-tuple-element.58), channel_id=1, source_target_pairs={{0,4},{1,5},{2,6},{3,7},{4,0},{5,1},{6,2},{7,3},{8,12},{9,13},{10,... | collective-permute-start | bytes 147464 | tf_op jit(solution)/shard_map/ppermute | solution.py:306
  61.0 9.2 %collective-permute-start.27 = (bf16[32,768]{1,0:T(8,128)(2,1)S(1)}, bf16[32,768]{1,0:T(8,128)(2,1)S(1)}, u32[]{:S(2)}, u32[]{:S(2)}) collective-permute-start(bf16[32,768]{1,0:T(8,128)(2,1)S(1)} %get-tuple-element.57), channel_id=1, source_target_pairs={{0,8},{1,9},{2,10},{3,11},{4,12},{5,13},{6,14},{7,15},{8,0},{9,1},... | collective-permute-start | bytes 147464 | tf_op jit(solution)/shard_map/ppermute | solution.py:306
  62.3 9.3 %collective-permute-start.28 = (bf16[32,768]{1,0:T(8,128)(2,1)S(1)}, bf16[32,768]{1,0:T(8,128)(2,1)S(1)}, u32[]{:S(2)}, u32[]{:S(2)}) collective-permute-start(bf16[32,768]{1,0:T(8,128)(2,1)S(1)} %get-tuple-element.56), channel_id=1, source_target_pairs={{0,12},{1,13},{2,14},{3,15},{4,8},{5,9},{6,10},{7,11},{8,4},{9,5},... | collective-permute-start | bytes 147464 | tf_op jit(solution)/shard_map/ppermute | solution.py:306
  63.7 9.9 %collective-permute-start.22 = (bf16[32,768]{1,0:T(8,128)(2,1)S(1)}, bf16[32,768]{1,0:T(8,128)(2,1)S(1)}, u32[]{:S(2)}, u32[]{:S(2)}) collective-permute-start(bf16[32,768]{1,0:T(8,128)(2,1)S(1)} %get-tuple-element.62), channel_id=1, source_target_pairs={{0,4},{1,5},{2,6},{3,7},{4,0},{5,1},{6,2},{7,3},{8,12},{9,13},{10,... | collective-permute-start | bytes 147464 | tf_op jit(solution)/shard_map/ppermute | solution.py:306
  66.2 13.8 %collective-permute-start.18 = (bf16[32,1024]{1,0:T(8,128)(2,1)S(1)}, bf16[32,1024]{1,0:T(8,128)(2,1)S(1)}, u32[]{:S(2)}, u32[]{:S(2)}) collective-permute-start(bf16[32,1024]{1,0:T(8,128)(2,1)S(1)} %get-tuple-element.54), channel_id=1, source_target_pairs={{0,4},{1,5},{2,6},{3,7},{4,0},{5,1},{6,2},{7,3},{8,12},{9,13},{10,... | collective-permute-start | bytes 196616 | tf_op jit(solution)/shard_map/ppermute | solution.py:306
  69.1 10.9 %collective-permute-start.19 = (bf16[32,1024]{1,0:T(8,128)(2,1)S(1)}, bf16[32,1024]{1,0:T(8,128)(2,1)S(1)}, u32[]{:S(2)}, u32[]{:S(2)}) collective-permute-start(bf16[32,1024]{1,0:T(8,128)(2,1)S(1)} %get-tuple-element.53), channel_id=1, source_target_pairs={{0,8},{1,9},{2,10},{3,11},{4,12},{5,13},{6,14},{7,15},{8,0},{9,1},... | collective-permute-start | bytes 196616 | tf_op jit(solution)/shard_map/ppermute | solution.py:306
  70.2 9.9 %collective-permute-start.20 = (bf16[32,1024]{1,0:T(8,128)(2,1)S(1)}, bf16[32,1024]{1,0:T(8,128)(2,1)S(1)}, u32[]{:S(2)}, u32[]{:S(2)}) collective-permute-start(bf16[32,1024]{1,0:T(8,128)(2,1)S(1)} %get-tuple-element.52), channel_id=1, source_target_pairs={{0,12},{1,13},{2,14},{3,15},{4,8},{5,9},{6,10},{7,11},{8,4},{9,5},... | collective-permute-start | bytes 196616 | tf_op jit(solution)/shard_map/ppermute | solution.py:306
  71.6 8.4 %collective-permute-start.23 = (bf16[32,768]{1,0:T(8,128)(2,1)S(1)}, bf16[32,768]{1,0:T(8,128)(2,1)S(1)}, u32[]{:S(2)}, u32[]{:S(2)}) collective-permute-start(bf16[32,768]{1,0:T(8,128)(2,1)S(1)} %get-tuple-element.61), channel_id=1, source_target_pairs={{0,8},{1,9},{2,10},{3,11},{4,12},{5,13},{6,14},{7,15},{8,0},{9,1},... | collective-permute-start | bytes 147464 | tf_op jit(solution)/shard_map/ppermute | solution.py:306
  73.6 6.4 %collective-permute-start.24 = (bf16[32,768]{1,0:T(8,128)(2,1)S(1)}, bf16[32,768]{1,0:T(8,128)(2,1)S(1)}, u32[]{:S(2)}, u32[]{:S(2)}) collective-permute-start(bf16[32,768]{1,0:T(8,128)(2,1)S(1)} %get-tuple-element.60), channel_id=1, source_target_pairs={{0,12},{1,13},{2,14},{3,15},{4,8},{5,9},{6,10},{7,11},{8,4},{9,5},... | collective-permute-start | bytes 147464 | tf_op jit(solution)/shard_map/ppermute | solution.py:306
  (7 other events, 32.3 us)

commit v11 on v9

--- a/solution.py
+++ b/solution.py
@@ -53,22 +53,6 @@
         terms.append(value.astype(BF16))
         value = value - terms[-1].astype(F32)
     return terms
-
-
-def pack(z, columns):
-    tiles = [z[:, i : i + 128] for i in range(0, z.shape[1], 128)]
-    tiles += [columns[:, i : i + 128] for i in range(0, columns.shape[1], 128)]
-    return jnp.concatenate(tiles, axis=0)
-
-
-def unpack_z(rows, size, lanes):
-    tiles = [rows[i * size : (i + 1) * size] for i in range(lanes // 128)]
-    return jnp.concatenate(tiles, axis=1)
-
-
-def unpack_columns(rows, start, rank):
-    tiles = [rows[i : i + rank] for i in range(start, rows.shape[0], rank)]
-    return jnp.concatenate(tiles, axis=1)
 
 
 def pair_columns(ids, probs):
@@ -131,10 +115,11 @@
     lane = iota((rank, lanes), 1)
     tiled = dot(pair.astype(BF16), (iota((rank, lanes), 0) == lane % rank).astype(BF16), 1, 0)
     block = iota((1, lanes), 1) // rank * groups
+    pick = (iota((rows, tok), 0) // top == iota((rows, tok), 1)).astype(BF16)
     for i in range(groups):
         name = block + (core ^ i) if groups == 2 else block
-        y = jnp.where(names == name.astype(F32), tiled, 0.0)
-        y = jnp.sum(y.reshape(tok, top, lanes), axis=1).astype(BF16)
+        y = jnp.where(names == name.astype(F32), tiled, 0.0).astype(BF16)
+        y = dot(pick, y, 0, 0).astype(BF16)
         for out in outs:
             out[:, i * (lanes + share) : i * (lanes + share) + lanes] = y
     for copy in x_copies:
@@ -175,23 +160,23 @@
     columns[...] = total
     own = jnp.concatenate([near_x[:, lanes : lanes + share], far_x[:, :share]], axis=0)
     halves = [dot(own, total, 1, 1), dot(x[: 2 * rows], total, 1, 1)]
-    for j, out in enumerate(outs):
+    for j in range(SLICES):
         half = halves[j // 2].astype(BF16)
         start = j % 2 * tok
-        z = jnp.concatenate([half[start : start + tok], half[rows + start :][:tok]], axis=0)
+        outs[j][:tok] = half[start : start + tok]
+        outs[j][tok:] = half[rows + start : rows + start + tok]
         expert = (place ^ j) * low + lower
-        out[...] = pack(z, columns[pl.ds(pl.multiple_of(expert * rank, rank), rank)])
-
-
-def inverse_kernel(start, p0, p1, p2, p3, inverse, basis, columns):
+        outs[SLICES + j][...] = columns[pl.ds(pl.multiple_of(expert * rank, rank), rank)]
+
+
+def inverse_kernel(c0, c1, c2, c3, inverse, basis, columns):
     _, _, place, half = position()
     rank = inverse.shape[0]
     _, _, share = columns.shape
     gram = 0.0
-    for j, packed in enumerate((p0, p1, p2, p3)):
-        block = unpack_columns(packed[...], start, rank)
-        columns[place ^ j] = block
-        gram = gram + dot(block, block, 1, 1)
+    for j, block in enumerate((c0, c1, c2, c3)):
+        columns[place ^ j] = block[...]
+        gram = gram + dot(block[...], block[...], 1, 1)
     row = iota((rank, 128), 0)
     lane = iota((rank, 128), 1)
     eye = (row + rank == lane).astype(F32)
@@ -258,10 +243,9 @@
     lanes, rows = mask.shape
     rows = rows // 2
     rank = lanes // (SLICES * low)
-    size = 2 * tok * lanes // 128
     z = 0.0
     for block in (z0, z1, z2, z3):
-        z = z + unpack_z(block[:size], 2 * tok, lanes).astype(F32)
+        z = z + block[...].astype(F32)
     repeat = iota((2 * tok, 2 * rows), 1) // (rows // tok) == iota((2 * tok, 2 * rows), 0)
     z = dot(z.astype(BF16), repeat.astype(BF16), 0, 0)
     work[...] = (z * mask[...]).astype(BF16)
@@ -303,11 +287,6 @@
         return lax.ppermute(block, AXES, [(i, i ^ step) for i in range(count)])
 
     cot = cotangents.reshape(rows, hidden)
-    if n_dp > 1:
-        mine = lax.dynamic_slice_in_dim(cot, half * part, part, axis=1)
-        other = exchange(lax.dynamic_slice_in_dim(cot, (1 - half) * part, part, axis=1), 1)
-    else:
-        mine, other = cot, exchange(cot, 1)
 
     *blocks, pairs = call(
         functools.partial(first_kernel, groups),
@@ -329,7 +308,15 @@
         limit=LARGE,
     )
     blocks = blocks[:1] + [exchange(blocks[j], j * line) for j in range(1, SLICES)]
+
+    pairs, send = lax.optimization_barrier((pairs, cot))
     pairs = [pairs, exchange(pairs, 1)]
+    mine = cot
+    if n_dp > 1:
+        mine = lax.dynamic_slice_in_dim(cot, half * part, part, axis=1)
+        send = lax.dynamic_slice_in_dim(send, (1 - half) * part, part, axis=1)
+    other = exchange(send, 1)
+
     near = [[jnp.concatenate(blocks[i : i + 2], axis=0)] for i in range(0, SLICES, 2)]
     step = 2
     while step < line:
@@ -338,7 +325,6 @@
     n = len(near[0])
     skip = lanes if groups == 2 else 0
 
-    size = 2 * tok * lanes // 128
     far = [exchange(b[:, skip:], 1) for b in near[0]]
     if n_dp == 1:
         work = [
@@ -357,7 +343,7 @@
         near[1], columns = lax.optimization_barrier((near[1], columns))
         zs = call(
             functools.partial(z_kernel, n, low),
-            [shape((size + rank * share // 128, 128), BF16)] * SLICES,
+            [shape((2 * tok, lanes), BF16)] * SLICES + [shape((rank, share), BF16)] * SLICES,
             [VMEM] * 3 + [HBM] * (2 * n),
             work[:2] + [pltpu.VMEM((lanes, share), BF16)] + work[2:],
             columns,
@@ -370,13 +356,15 @@
         far = [far, [exchange(b[:, skip:], 1) for b in near[1]]]
         rows_all = jnp.concatenate(near[0] + far[0] + near[1] + far[1], axis=0)
         columns = dot(rows_all[:, :lanes], rows_all[:, lanes:], 0, 0).astype(BF16)
-        zs = []
+        zs, own = [], []
         for j in range(SLICES):
             here = slice(j % 2 * tok, (j % 2 + 1) * tok)
             x = jnp.concatenate([near[j // 2][0][here], far[j // 2][0][here]], axis=0)
             start = ((place ^ j) * low + lower) * rank
-            own = lax.dynamic_slice_in_dim(columns, start, rank, axis=0)
-            zs.append(pack(dot(x[:, lanes:], columns, 1, 1).astype(BF16), own))
+            own.append(lax.dynamic_slice_in_dim(columns, start, rank, axis=0))
+            zs.append(dot(x[:, lanes:], columns, 1, 1).astype(BF16))
+        zs = zs + own
+    columns = zs[SLICES:]
     zs = list(zs[:1]) + [exchange(zs[j], j * line) for j in range(1, SLICES)]
 
     [mask] = call(
@@ -399,13 +387,14 @@
         other,
         limit=limit,
     )
-    zs, _ = lax.optimization_barrier((zs, terms[-1]))
+    columns, _ = lax.optimization_barrier((columns, exchange(terms[0][:16, :128], 1)))
+    columns = list(columns[:1]) + [exchange(columns[j], j * line) for j in range(1, SLICES)]
     inverse, basis = call(
-        functools.partial(inverse_kernel, size),
+        inverse_kernel,
         [shape((rank, rank), F32), shape((rank, width // n_dp), F32)],
         [VMEM] * SLICES,
         [pltpu.VMEM((SLICES, rank, share), BF16)],
-        *zs,
+        *columns,
     )
     sums = []
     for chunk in range(CHUNKS):
@@ -419,7 +408,7 @@
             ]
             step *= 2
         sums.append(blocks[0])
-    sums[0], inverse = lax.optimization_barrier((sums[0], inverse))
+    sums[-1], inverse = lax.optimization_barrier((sums[-1], inverse))
     blocks = []
     for block in sums:
         own = [lax.dynamic_index_in_dim(block, place ^ j, 0, False) for j in range(SLICES)]

time: 74.3 us -> 74.4 us (level)
  starting transfers between devices: 26.9 us -> 30.7 us
  waiting for transfers between devices: 34 us -> 30.3 us
    ppermute x22 -> x25, starting transfers between devices: 26.9 us -> 30.7 us  [exchange(): return lax.ppermute(block, AXES, [(i, i ^ step) for i in range(count)])]
    ppermute x22 -> x25, waiting for transfers between devices: 34 us -> 30.3 us  [exchange(): return lax.ppermute(block, AXES, [(i, i ^ step) for i in range(count)])]
  transfers between devices with their start and end apart: 22 -> 25, of which waited for: 15 -> 16; matrix products, arithmetic and copies ran while one was open for 2% -> 2% of each run, Pallas kernels for 11% -> 6%
where the time goes in v11:
time: 74.4 us; the launch traced here: 74.2 us
  starting transfers between devices  30.7 us (41%)
  waiting for transfers between devices  30.3 us (41%)
  Pallas kernels  11.2 us (15%)
  local copies, waits for them, and re-layouts  1.11 us (1%)
  between operations  0.82 us (1%)
    ppermute x25, starting transfers between devices, exchange(): return lax.ppermute(block, AXES, [(i, i ^ step) for i in range(count)])  30.7 us
    ppermute x25, waiting for transfers between devices, exchange(): return lax.ppermute(block, AXES, [(i, i ^ step) for i in range(count)])  30.3 us
    pallas_call x7, Pallas kernels, call(): pl.pallas_call(body, out_shape=shapes, in_specs=spaces, out_specs=[VMEM]...  11.2 us
  transfers between devices with their start and end apart: 25, of which 16 were waited for; matrix products, arithmetic and copies ran while one was open for 2% of the time, Pallas kernels for 6%

profile of v11, /device:TPU:0, one launch (start us, length us, event | category | flops | bytes accessed | tf_op | source)
XLA Modules:
  0.0 74.2 jit_solution(12198044009128348780)
XLA Ops:
  0.6 3.9 %shard_map.68 = (bf16[48,1408]{1,0:T(8,128)(2,1)}, bf16[48,1408]{1,0:T(8,128)(2,1)}, bf16[48,1408]{1,0:T(8,128)(2,1)}, bf16[48,1408]{1,0:T(8,128)(2,1)}, f32[16,48]{1,0:T(8,128)}) custom-call(bf16[48,3584]{1,0:T(8,128)(2,1)} %tokens.1, bf16[384,2560]{1,0:T(8,128)(2,1)} %bitcast.28, f32[32,2560]{1,0:T(8,128)} %bitcast.35, s32[8,48]{1,0:T(8,128)} %bitcast.37, ...), custom_call_target="tpu_custom_call" | custom-call | flops 1 | bytes 1 | tf_op jit(solution)/shard_map/pallas_call | solution.py:39
  5.1 2.7 %collective-permute-start.3 = (bf16[48,1408]{1,0:T(8,128)(2,1)}, bf16[48,1408]{1,0:T(8,128)(2,1)S(1)}, u32[]{:S(2)}, u32[]{:S(2)}) collective-permute-start(bf16[48,1408]{1,0:T(8,128)(2,1)} %get-tuple-element.35), channel_id=1, source_target_pairs={{0,4},{1,5},{2,6},{3,7},{4,0},{5,1},{6,2},{7,3},{8,12},{9,13},{10,... | collective-permute-start | bytes 405512 | tf_op jit(solution)/shard_map/ppermute | solution.py:287
  7.8 2.6 %collective-permute-start = (bf16[48,1408]{1,0:T(8,128)(2,1)}, bf16[48,1408]{1,0:T(8,128)(2,1)S(1)}, u32[]{:S(2)}, u32[]{:S(2)}) collective-permute-start(bf16[48,1408]{1,0:T(8,128)(2,1)} %get-tuple-element.32), channel_id=1, source_target_pairs={{0,8},{1,9},{2,10},{3,11},{4,12},{5,13},{6,14},{7,15},{8,0},{9,1},... | collective-permute-start | bytes 405512 | tf_op jit(solution)/shard_map/ppermute | solution.py:287
  11.3 3.2 %collective-permute-done.3 = bf16[48,1408]{1,0:T(8,128)(2,1)S(1)} collective-permute-done((bf16[48,1408]{1,0:T(8,128)(2,1)}, bf16[48,1408]{1,0:T(8,128)(2,1)S(1)}, u32[]{:S(2)}, u32[]{:S(2)}) %collective-permute-start.3) | collective-permute-done | bytes 135200 | tf_op jit(solution)/shard_map/ppermute | solution.py:287
  14.5 1.8 %collective-permute-start.4 = (bf16[96,1408]{1,0:T(8,128)(2,1)S(1)}, bf16[96,1408]{1,0:T(8,128)(2,1)S(1)}, u32[]{:S(2)}, u32[]{:S(2)}) collective-permute-start(bf16[96,1408]{1,0:T(8,128)(2,1)S(1)} %constant_dynamic-update-slice_fusion.2.refs_0_.near_x), channel_id=1, source_target_pairs={{0,2},{1,3},{2,0},{3,1},{4,6},{5,7},{6,4},{7,5},{8,10},{9,11},{10,... | collective-permute-start | bytes 811016 | tf_op jit(solution)/shard_map/ppermute | solution.py:287
  16.3 4.9 %collective-permute-done = bf16[48,1408]{1,0:T(8,128)(2,1)S(1)} collective-permute-done((bf16[48,1408]{1,0:T(8,128)(2,1)}, bf16[48,1408]{1,0:T(8,128)(2,1)S(1)}, u32[]{:S(2)}, u32[]{:S(2)}) %collective-permute-start) | collective-permute-done | bytes 135200 | tf_op jit(solution)/shard_map/ppermute | solution.py:287
  21.2 1.6 %collective-permute-start.2 = (bf16[96,1408]{1,0:T(8,128)(2,1)S(1)}, bf16[96,1408]{1,0:T(8,128)(2,1)S(1)}, u32[]{:S(2)}, u32[]{:S(2)}) collective-permute-start(bf16[96,1408]{1,0:T(8,128)(2,1)S(1)} %constant_dynamic-update-slice_fusion.refs_0_), channel_id=1, source_target_pairs={{0,2},{1,3},{2,0},{3,1},{4,6},{5,7},{6,4},{7,5},{8,10},{9,11},{10,... | collective-permute-start | bytes 811016 | tf_op jit(solution)/shard_map/ppermute | solution.py:287
  25.3 3.2 %collective-permute-done.2.refs_1_ = bf16[96,1408]{1,0:T(8,128)(2,1)S(1)} collective-permute-done((bf16[96,1408]{1,0:T(8,128)(2,1)S(1)}, bf16[96,1408]{1,0:T(8,128)(2,1)S(1)}, u32[]{:S(2)}, u32[]{:S(2)}) %collective-permute-start.2) | collective-permute-done | bytes 270368 | tf_op jit(solution)/shard_map/ppermute | solution.py:287
  31.3 3.2 %collective-permute-start.12 = (bf16[96,256]{1,0:T(8,128)(2,1)S(1)}, bf16[96,256]{1,0:T(8,128)(2,1)S(1)}, u32[]{:S(2)}, u32[]{:S(2)}) collective-permute-start(bf16[96,256]{1,0:T(8,128)(2,1)S(1)} %get-tuple-element.49), channel_id=1, source_target_pairs={{0,4},{1,5},{2,6},{3,7},{4,0},{5,1},{6,2},{7,3},{8,12},{9,13},{10,... | collective-permute-start | bytes 147464 | tf_op jit(solution)/shard_map/ppermute | solution.py:287
  35.6 1.4 %collective-permute-start.14 = (bf16[96,256]{1,0:T(8,128)(2,1)S(1)}, bf16[96,256]{1,0:T(8,128)(2,1)S(1)}, u32[]{:S(2)}, u32[]{:S(2)}) collective-permute-start(bf16[96,256]{1,0:T(8,128)(2,1)S(1)} %get-tuple-element.51), channel_id=1, source_target_pairs={{0,12},{1,13},{2,14},{3,15},{4,8},{5,9},{6,10},{7,11},{8,4},{9,5},... | collective-permute-start | bytes 147464 | tf_op jit(solution)/shard_map/ppermute | solution.py:287
  38.4 3.2 %collective-permute-done.13.z2 = bf16[96,256]{1,0:T(8,128)(2,1)S(1)} collective-permute-done((bf16[96,256]{1,0:T(8,128)(2,1)S(1)}, bf16[96,256]{1,0:T(8,128)(2,1)S(1)}, u32[]{:S(2)}, u32[]{:S(2)}) %collective-permute-start.13) | collective-permute-done | bytes 49184 | tf_op jit(solution)/shard_map/ppermute | solution.py:287
  41.6 1.8 %shard_map.73 = (bf16[128,1280]{1,0:T(8,128)(2,1)S(1)}, bf16[128,1280]{1,0:T(8,128)(2,1)S(1)}, bf16[128,1280]{1,0:T(8,128)(2,1)S(1)}, bf16[128,1280]{1,0:T(8,128)(2,1)S(1)}) custom-call(bf16[96,256]{1,0:T(8,128)(2,1)S(1)} %get-tuple-element.48.z0, bf16[96,256]{1,0:T(8,128)(2,1)S(1)} %collective-permute-done.12.z1, ...), custom_call_target="tpu_custom_call" | custom-call | flops 1 | bytes 1 | tf_op jit(solution)/shard_map/pallas_call | solution.py:39
  43.4 1.6 %collective-permute-start.18 = (bf16[4,32,1280]{2,1,0:T(8,128)(2,1)S(1)}, bf16[4,32,1280]{2,1,0:T(8,128)(2,1)S(1)}, u32[]{:S(2)}, u32[]{:S(2)}) collective-permute-start(bf16[4,32,1280]{2,1,0:T(8,128)(2,1)S(1)} %bitcast.34), channel_id=1, source_target_pairs={{0,2},{1,3},{2,0},{3,1},{4,6},{5,7},{6,4},{7,5},{8,10},{9,11},{10,... | collective-permute-start | bytes 983048 | tf_op jit(solution)/shard_map/ppermute | solution.py:287
  44.9 2.0 %collective-permute-start.10 = (bf16[32,896]{1,0:T(8,128)(2,1)S(1)}, bf16[32,896]{1,0:T(8,128)(2,1)S(1)}, u32[]{:S(2)}, u32[]{:S(2)}) collective-permute-start(bf16[32,896]{1,0:T(8,128)(2,1)S(1)} %get-tuple-element.45), channel_id=1, source_target_pairs={{0,8},{1,9},{2,10},{3,11},{4,12},{5,13},{6,14},{7,15},{8,0},{9,1},... | collective-permute-start | bytes 172040 | tf_op jit(solution)/shard_map/ppermute | solution.py:287
  47.0 1.6 %collective-permute-start.11 = (bf16[32,896]{1,0:T(8,128)(2,1)S(1)}, bf16[32,896]{1,0:T(8,128)(2,1)S(1)}, u32[]{:S(2)}, u32[]{:S(2)}) collective-permute-start(bf16[32,896]{1,0:T(8,128)(2,1)S(1)} %get-tuple-element.46), channel_id=1, source_target_pairs={{0,12},{1,13},{2,14},{3,15},{4,8},{5,9},{6,10},{7,11},{8,4},{9,5},... | collective-permute-start | bytes 172040 | tf_op jit(solution)/shard_map/ppermute | solution.py:287
  48.6 3.1 %collective-permute-done.10.c2 = bf16[32,896]{1,0:T(8,128)(2,1)S(1)} collective-permute-done((bf16[32,896]{1,0:T(8,128)(2,1)S(1)}, bf16[32,896]{1,0:T(8,128)(2,1)S(1)}, u32[]{:S(2)}, u32[]{:S(2)}) %collective-permute-start.10) | collective-permute-done | bytes 57376 | tf_op jit(solution)/shard_map/ppermute | solution.py:287
  51.7 1.4 %collective-permute-done.11.c3 = bf16[32,896]{1,0:T(8,128)(2,1)S(1)} collective-permute-done((bf16[32,896]{1,0:T(8,128)(2,1)S(1)}, bf16[32,896]{1,0:T(8,128)(2,1)S(1)}, u32[]{:S(2)}, u32[]{:S(2)}) %collective-permute-start.11) | collective-permute-done | bytes 57376 | tf_op jit(solution)/shard_map/ppermute | solution.py:287
  53.3 2.7 %shard_map.71 = (f32[32,32]{1,0:T(8,128)S(1)}, f32[32,3584]{1,0:T(8,128)}) custom-call(bf16[32,896]{1,0:T(8,128)(2,1)S(1)} %get-tuple-element.43.c0, bf16[32,896]{1,0:T(8,128)(2,1)S(1)} %collective-permute-done.9.c1, bf16[32,896]{1,0:T(8,128)(2,1)S(1)} %collective-permute-done.10.c2, bf16[32,896]{1,0:T(8,128)(2,1)S(1)} %collective-permute-done.11.c3), custom_call_target="tpu_custom_call" | custom-call | flops 1 | bytes 1 | tf_op jit(solution)/shard_map/pallas_call | solution.py:39
  56.8 2.4 %collective-permute-start.20 = (bf16[32,1280]{1,0:T(8,128)(2,1)S(1)}, bf16[32,1280]{1,0:T(8,128)(2,1)S(1)}, u32[]{:S(2)}, u32[]{:S(2)}) collective-permute-start(bf16[32,1280]{1,0:T(8,128)(2,1)S(1)} %get-tuple-element.67), channel_id=1, source_target_pairs={{0,8},{1,9},{2,10},{3,11},{4,12},{5,13},{6,14},{7,15},{8,0},{9,1},... | collective-permute-start | bytes 245768 | tf_op jit(solution)/shard_map/ppermute | solution.py:287
  59.3 1.9 %collective-permute-start.21 = (bf16[32,1280]{1,0:T(8,128)(2,1)S(1)}, bf16[32,1280]{1,0:T(8,128)(2,1)S(1)}, u32[]{:S(2)}, u32[]{:S(2)}) collective-permute-start(bf16[32,1280]{1,0:T(8,128)(2,1)S(1)} %get-tuple-element.66), channel_id=1, source_target_pairs={{0,12},{1,13},{2,14},{3,15},{4,8},{5,9},{6,10},{7,11},{8,4},{9,5},... | collective-permute-start | bytes 245768 | tf_op jit(solution)/shard_map/ppermute | solution.py:287
  61.2 2.4 %collective-permute-done.17 = bf16[4,32,1280]{2,1,0:T(8,128)(2,1)S(1)} collective-permute-done((bf16[4,32,1280]{2,1,0:T(8,128)(2,1)S(1)}, bf16[4,32,1280]{2,1,0:T(8,128)(2,1)S(1)}, u32[]{:S(2)}, u32[]{:S(2)}) %collective-permute-start.17) | collective-permute-done | bytes 327712 | tf_op jit(solution)/shard_map/ppermute | solution.py:287
  64.8 2.0 %collective-permute-start.23 = (bf16[32,1280]{1,0:T(8,128)(2,1)S(1)}, bf16[32,1280]{1,0:T(8,128)(2,1)S(1)}, u32[]{:S(2)}, u32[]{:S(2)}) collective-permute-start(bf16[32,1280]{1,0:T(8,128)(2,1)S(1)} %get-tuple-element.63), channel_id=1, source_target_pairs={{0,8},{1,9},{2,10},{3,11},{4,12},{5,13},{6,14},{7,15},{8,0},{9,1},... | collective-permute-start | bytes 245768 | tf_op jit(solution)/shard_map/ppermute | solution.py:287
  69.1 2.3 %collective-permute-done.23.refs_6_ = bf16[32,1280]{1,0:T(8,128)(2,1)S(1)} collective-permute-done((bf16[32,1280]{1,0:T(8,128)(2,1)S(1)}, bf16[32,1280]{1,0:T(8,128)(2,1)S(1)}, u32[]{:S(2)}, u32[]{:S(2)}) %collective-permute-start.23) | collective-permute-done | bytes 81952 | tf_op jit(solution)/shard_map/ppermute | solution.py:287
  71.4 1.8 %collective-permute-done.24.refs_7_ = bf16[32,1280]{1,0:T(8,128)(2,1)S(1)} collective-permute-done((bf16[32,1280]{1,0:T(8,128)(2,1)S(1)}, bf16[32,1280]{1,0:T(8,128)(2,1)S(1)}, u32[]{:S(2)}, u32[]{:S(2)}) %collective-permute-start.24) | collective-permute-done | bytes 81952 | tf_op jit(solution)/shard_map/ppermute | solution.py:287
  (49 shorter events, 14.8 us)
Async XLA Ops:
  4.6 37.0 %collective-permute-start.16 = (bf16[384,2560]{1,0:T(8,128)(2,1)S(1)}, bf16[384,2560]{1,0:T(8,128)(2,1)S(1)}, u32[]{:S(2)}, u32[]{:S(2)}) collective-permute-start(bf16[384,2560]{1,0:T(8,128)(2,1)S(1)} %bitcast.29), channel_id=1, source_target_pairs={{0,1},{1,0},{2,3},{3,2},{4,5},{5,4},{6,7},{7,6},{8,9},{9,8},{10,11... | collective-permute-start | bytes 5898248 | tf_op jit(solution)/shard_map/ppermute | solution.py:287
  5.1 9.4 %collective-permute-start.3 = (bf16[48,1408]{1,0:T(8,128)(2,1)}, bf16[48,1408]{1,0:T(8,128)(2,1)S(1)}, u32[]{:S(2)}, u32[]{:S(2)}) collective-permute-start(bf16[48,1408]{1,0:T(8,128)(2,1)} %get-tuple-element.35), channel_id=1, source_target_pairs={{0,4},{1,5},{2,6},{3,7},{4,0},{5,1},{6,2},{7,3},{8,12},{9,13},{10,... | collective-permute-start | bytes 405512 | tf_op jit(solution)/shard_map/ppermute | solution.py:287
  7.8 13.4 %collective-permute-start = (bf16[48,1408]{1,0:T(8,128)(2,1)}, bf16[48,1408]{1,0:T(8,128)(2,1)S(1)}, u32[]{:S(2)}, u32[]{:S(2)}) collective-permute-start(bf16[48,1408]{1,0:T(8,128)(2,1)} %get-tuple-element.32), channel_id=1, source_target_pairs={{0,8},{1,9},{2,10},{3,11},{4,12},{5,13},{6,14},{7,15},{8,0},{9,1},... | collective-permute-start | bytes 405512 | tf_op jit(solution)/shard_map/ppermute | solution.py:287
  10.3 10.8 %collective-permute-start.1 = (bf16[48,1408]{1,0:T(8,128)(2,1)}, bf16[48,1408]{1,0:T(8,128)(2,1)S(1)}, u32[]{:S(2)}, u32[]{:S(2)}) collective-permute-start(bf16[48,1408]{1,0:T(8,128)(2,1)} %get-tuple-element.33), channel_id=1, source_target_pairs={{0,12},{1,13},{2,14},{3,15},{4,8},{5,9},{6,10},{7,11},{8,4},{9,5},... | collective-permute-start | bytes 405512 | tf_op jit(solution)/shard_map/ppermute | solution.py:287
  14.5 8.4 %collective-permute-start.4 = (bf16[96,1408]{1,0:T(8,128)(2,1)S(1)}, bf16[96,1408]{1,0:T(8,128)(2,1)S(1)}, u32[]{:S(2)}, u32[]{:S(2)}) collective-permute-start(bf16[96,1408]{1,0:T(8,128)(2,1)S(1)} %constant_dynamic-update-slice_fusion.2.refs_0_.near_x), channel_id=1, source_target_pairs={{0,2},{1,3},{2,0},{3,1},{4,6},{5,7},{6,4},{7,5},{8,10},{9,11},{10,... | collective-permute-start | bytes 811016 | tf_op jit(solution)/shard_map/ppermute | solution.py:287
  21.2 7.3 %collective-permute-start.2 = (bf16[96,1408]{1,0:T(8,128)(2,1)S(1)}, bf16[96,1408]{1,0:T(8,128)(2,1)S(1)}, u32[]{:S(2)}, u32[]{:S(2)}) collective-permute-start(bf16[96,1408]{1,0:T(8,128)(2,1)S(1)} %constant_dynamic-update-slice_fusion.refs_0_), channel_id=1, source_target_pairs={{0,2},{1,3},{2,0},{3,1},{4,6},{5,7},{6,4},{7,5},{8,10},{9,11},{10,... | collective-permute-start | bytes 811016 | tf_op jit(solution)/shard_map/ppermute | solution.py:287
  22.8 1.5 %collective-permute-start.5 = (bf16[96,1152]{1,0:T(8,128)(2,1)S(1)}, bf16[96,1152]{1,0:T(8,128)(2,1)S(1)}, u32[]{:S(2)}, u32[]{:S(2)}) collective-permute-start(bf16[96,1152]{1,0:T(8,128)(2,1)S(1)} %slice.17), channel_id=1, source_target_pairs={{0,1},{1,0},{2,3},{3,2},{4,5},{5,4},{6,7},{7,6},{8,9},{9,8},{10,11... | collective-permute-start | bytes 663560 | tf_op jit(solution)/shard_map/ppermute | solution.py:287
  22.9 1.7 %collective-permute-start.6 = (bf16[96,1152]{1,0:T(8,128)(2,1)S(1)}, bf16[96,1152]{1,0:T(8,128)(2,1)S(1)}, u32[]{:S(2)}, u32[]{:S(2)}) collective-permute-start(bf16[96,1152]{1,0:T(8,128)(2,1)S(1)} %slice.18), channel_id=1, source_target_pairs={{0,1},{1,0},{2,3},{3,2},{4,5},{5,4},{6,7},{7,6},{8,9},{9,8},{10,11... | collective-permute-start | bytes 663560 | tf_op jit(solution)/shard_map/ppermute | solution.py:287
  28.5 1.5 %collective-permute-start.7 = (bf16[96,1152]{1,0:T(8,128)(2,1)S(1)}, bf16[96,1152]{1,0:T(8,128)(2,1)S(1)}, u32[]{:S(2)}, u32[]{:S(2)}) collective-permute-start(bf16[96,1152]{1,0:T(8,128)(2,1)S(1)} %slice.15), channel_id=1, source_target_pairs={{0,1},{1,0},{2,3},{3,2},{4,5},{5,4},{6,7},{7,6},{8,9},{9,8},{10,11... | collective-permute-start | bytes 663560 | tf_op jit(solution)/shard_map/ppermute | solution.py:287
  28.6 1.8 %collective-permute-start.8 = (bf16[96,1152]{1,0:T(8,128)(2,1)S(1)}, bf16[96,1152]{1,0:T(8,128)(2,1)S(1)}, u32[]{:S(2)}, u32[]{:S(2)}) collective-permute-start(bf16[96,1152]{1,0:T(8,128)(2,1)S(1)} %slice.16), channel_id=1, source_target_pairs={{0,1},{1,0},{2,3},{3,2},{4,5},{5,4},{6,7},{7,6},{8,9},{9,8},{10,11... | collective-permute-start | bytes 663560 | tf_op jit(solution)/shard_map/ppermute | solution.py:287
  31.3 7.1 %collective-permute-start.12 = (bf16[96,256]{1,0:T(8,128)(2,1)S(1)}, bf16[96,256]{1,0:T(8,128)(2,1)S(1)}, u32[]{:S(2)}, u32[]{:S(2)}) collective-permute-start(bf16[96,256]{1,0:T(8,128)(2,1)S(1)} %get-tuple-element.49), channel_id=1, source_target_pairs={{0,4},{1,5},{2,6},{3,7},{4,0},{5,1},{6,2},{7,3},{8,12},{9,13},{10,... | collective-permute-start | bytes 147464 | tf_op jit(solution)/shard_map/ppermute | solution.py:287
  34.5 7.1 %collective-permute-start.13 = (bf16[96,256]{1,0:T(8,128)(2,1)S(1)}, bf16[96,256]{1,0:T(8,128)(2,1)S(1)}, u32[]{:S(2)}, u32[]{:S(2)}) collective-permute-start(bf16[96,256]{1,0:T(8,128)(2,1)S(1)} %get-tuple-element.50), channel_id=1, source_target_pairs={{0,8},{1,9},{2,10},{3,11},{4,12},{5,13},{6,14},{7,15},{8,0},{9,1},... | collective-permute-start | bytes 147464 | tf_op jit(solution)/shard_map/ppermute | solution.py:287
  35.6 6.0 %collective-permute-start.14 = (bf16[96,256]{1,0:T(8,128)(2,1)S(1)}, bf16[96,256]{1,0:T(8,128)(2,1)S(1)}, u32[]{:S(2)}, u32[]{:S(2)}) collective-permute-start(bf16[96,256]{1,0:T(8,128)(2,1)S(1)} %get-tuple-element.51), channel_id=1, source_target_pairs={{0,12},{1,13},{2,14},{3,15},{4,8},{5,9},{6,10},{7,11},{8,4},{9,5},... | collective-permute-start | bytes 147464 | tf_op jit(solution)/shard_map/ppermute | solution.py:287
  43.4 13.2 %collective-permute-start.18 = (bf16[4,32,1280]{2,1,0:T(8,128)(2,1)S(1)}, bf16[4,32,1280]{2,1,0:T(8,128)(2,1)S(1)}, u32[]{:S(2)}, u32[]{:S(2)}) collective-permute-start(bf16[4,32,1280]{2,1,0:T(8,128)(2,1)S(1)} %bitcast.34), channel_id=1, source_target_pairs={{0,2},{1,3},{2,0},{3,1},{4,6},{5,7},{6,4},{7,5},{8,10},{9,11},{10,... | collective-permute-start | bytes 983048 | tf_op jit(solution)/shard_map/ppermute | solution.py:287
  44.9 6.7 %collective-permute-start.10 = (bf16[32,896]{1,0:T(8,128)(2,1)S(1)}, bf16[32,896]{1,0:T(8,128)(2,1)S(1)}, u32[]{:S(2)}, u32[]{:S(2)}) collective-permute-start(bf16[32,896]{1,0:T(8,128)(2,1)S(1)} %get-tuple-element.45), channel_id=1, source_target_pairs={{0,8},{1,9},{2,10},{3,11},{4,12},{5,13},{6,14},{7,15},{8,0},{9,1},... | collective-permute-start | bytes 172040 | tf_op jit(solution)/shard_map/ppermute | solution.py:287
  47.0 6.1 %collective-permute-start.11 = (bf16[32,896]{1,0:T(8,128)(2,1)S(1)}, bf16[32,896]{1,0:T(8,128)(2,1)S(1)}, u32[]{:S(2)}, u32[]{:S(2)}) collective-permute-start(bf16[32,896]{1,0:T(8,128)(2,1)S(1)} %get-tuple-element.46), channel_id=1, source_target_pairs={{0,12},{1,13},{2,14},{3,15},{4,8},{5,9},{6,10},{7,11},{8,4},{9,5},... | collective-permute-start | bytes 172040 | tf_op jit(solution)/shard_map/ppermute | solution.py:287
  48.5 4.8 %collective-permute-start.9 = (bf16[32,896]{1,0:T(8,128)(2,1)S(1)}, bf16[32,896]{1,0:T(8,128)(2,1)S(1)}, u32[]{:S(2)}, u32[]{:S(2)}) collective-permute-start(bf16[32,896]{1,0:T(8,128)(2,1)S(1)} %get-tuple-element.44), channel_id=1, source_target_pairs={{0,4},{1,5},{2,6},{3,7},{4,0},{5,1},{6,2},{7,3},{8,12},{9,13},{10,... | collective-permute-start | bytes 172040 | tf_op jit(solution)/shard_map/ppermute | solution.py:287
  56.1 7.5 %collective-permute-start.17 = (bf16[4,32,1280]{2,1,0:T(8,128)(2,1)S(1)}, bf16[4,32,1280]{2,1,0:T(8,128)(2,1)S(1)}, u32[]{:S(2)}, u32[]{:S(2)}) collective-permute-start(bf16[4,32,1280]{2,1,0:T(8,128)(2,1)S(1)} %bitcast.33), channel_id=1, source_target_pairs={{0,2},{1,3},{2,0},{3,1},{4,6},{5,7},{6,4},{7,5},{8,10},{9,11},{10,... | collective-permute-start | bytes 983048 | tf_op jit(solution)/shard_map/ppermute | solution.py:287
  56.7 10.1 %collective-permute-start.19 = (bf16[32,1280]{1,0:T(8,128)(2,1)S(1)}, bf16[32,1280]{1,0:T(8,128)(2,1)S(1)}, u32[]{:S(2)}, u32[]{:S(2)}) collective-permute-start(bf16[32,1280]{1,0:T(8,128)(2,1)S(1)} %get-tuple-element.68), channel_id=1, source_target_pairs={{0,4},{1,5},{2,6},{3,7},{4,0},{5,1},{6,2},{7,3},{8,12},{9,13},{10,... | collective-permute-start | bytes 245768 | tf_op jit(solution)/shard_map/ppermute | solution.py:287
  56.8 11.3 %collective-permute-start.20 = (bf16[32,1280]{1,0:T(8,128)(2,1)S(1)}, bf16[32,1280]{1,0:T(8,128)(2,1)S(1)}, u32[]{:S(2)}, u32[]{:S(2)}) collective-permute-start(bf16[32,1280]{1,0:T(8,128)(2,1)S(1)} %get-tuple-element.67), channel_id=1, source_target_pairs={{0,8},{1,9},{2,10},{3,11},{4,12},{5,13},{6,14},{7,15},{8,0},{9,1},... | collective-permute-start | bytes 245768 | tf_op jit(solution)/shard_map/ppermute | solution.py:287
  59.3 8.9 %collective-permute-start.21 = (bf16[32,1280]{1,0:T(8,128)(2,1)S(1)}, bf16[32,1280]{1,0:T(8,128)(2,1)S(1)}, u32[]{:S(2)}, u32[]{:S(2)}) collective-permute-start(bf16[32,1280]{1,0:T(8,128)(2,1)S(1)} %get-tuple-element.66), channel_id=1, source_target_pairs={{0,12},{1,13},{2,14},{3,15},{4,8},{5,9},{6,10},{7,11},{8,4},{9,5},... | collective-permute-start | bytes 245768 | tf_op jit(solution)/shard_map/ppermute | solution.py:287
  63.7 5.4 %collective-permute-start.22 = (bf16[32,1280]{1,0:T(8,128)(2,1)S(1)}, bf16[32,1280]{1,0:T(8,128)(2,1)S(1)}, u32[]{:S(2)}, u32[]{:S(2)}) collective-permute-start(bf16[32,1280]{1,0:T(8,128)(2,1)S(1)} %get-tuple-element.64), channel_id=1, source_target_pairs={{0,4},{1,5},{2,6},{3,7},{4,0},{5,1},{6,2},{7,3},{8,12},{9,13},{10,... | collective-permute-start | bytes 245768 | tf_op jit(solution)/shard_map/ppermute | solution.py:287
  64.8 6.6 %collective-permute-start.23 = (bf16[32,1280]{1,0:T(8,128)(2,1)S(1)}, bf16[32,1280]{1,0:T(8,128)(2,1)S(1)}, u32[]{:S(2)}, u32[]{:S(2)}) collective-permute-start(bf16[32,1280]{1,0:T(8,128)(2,1)S(1)} %get-tuple-element.63), channel_id=1, source_target_pairs={{0,8},{1,9},{2,10},{3,11},{4,12},{5,13},{6,14},{7,15},{8,0},{9,1},... | collective-permute-start | bytes 245768 | tf_op jit(solution)/shard_map/ppermute | solution.py:287
  66.9 6.3 %collective-permute-start.24 = (bf16[32,1280]{1,0:T(8,128)(2,1)S(1)}, bf16[32,1280]{1,0:T(8,128)(2,1)S(1)}, u32[]{:S(2)}, u32[]{:S(2)}) collective-permute-start(bf16[32,1280]{1,0:T(8,128)(2,1)S(1)} %get-tuple-element.62), channel_id=1, source_target_pairs={{0,12},{1,13},{2,14},{3,15},{4,8},{5,9},{6,10},{7,11},{8,4},{9,5},... | collective-permute-start | bytes 245768 | tf_op jit(solution)/shard_map/ppermute | solution.py:287
  (3 other events, 16.8 us)

commit v12 on v11

--- a/solution.py
+++ b/solution.py
@@ -35,7 +35,7 @@
     return me % 2, me // 2 % (line // 2), me // line, half
 
 
-def call(body, shapes, spaces, scratch, *args, limit=LIMIT):
+def call(body, shapes, spaces, scratch, *args, limit=LIMIT, cost=1):
     return pl.pallas_call(
         body,
         out_shape=shapes,
@@ -43,7 +43,7 @@
         out_specs=[VMEM] * len(shapes),
         scratch_shapes=scratch,
         compiler_params=pltpu.CompilerParams(vmem_limit_bytes=limit),
-        cost_estimate=pl.CostEstimate(flops=1, bytes_accessed=1, transcendentals=0),
+        cost_estimate=pl.CostEstimate(flops=cost, bytes_accessed=cost, transcendentals=0),
     )(*args)
 
 
@@ -387,7 +387,6 @@
         other,
         limit=limit,
     )
-    columns, _ = lax.optimization_barrier((columns, exchange(terms[0][:16, :128], 1)))
     columns = list(columns[:1]) + [exchange(columns[j], j * line) for j in range(1, SLICES)]
     inverse, basis = call(
         inverse_kernel,
@@ -395,6 +394,7 @@
         [VMEM] * SLICES,
         [pltpu.VMEM((SLICES, rank, share), BF16)],
         *columns,
+        cost=10_000_000,
     )
     sums = []
     for chunk in range(CHUNKS):

time: 74.4 us -> 74.4 us (level)
  no operation moved by 1% of the time
where the time goes in v12:
time: 74.4 us; the launch traced here: 74.2 us
  starting transfers between devices  30.7 us (41%)
  waiting for transfers between devices  30.3 us (41%)
  Pallas kernels  11.2 us (15%)
  local copies, waits for them, and re-layouts  1.11 us (1%)
  between operations  0.82 us (1%)
    ppermute x25, starting transfers between devices, exchange(): return lax.ppermute(block, AXES, [(i, i ^ step) for i in range(count)])  30.7 us
    ppermute x25, waiting for transfers between devices, exchange(): return lax.ppermute(block, AXES, [(i, i ^ step) for i in range(count)])  30.3 us
    pallas_call x7, Pallas kernels, call(): pl.pallas_call(body, out_shape=shapes, in_specs=spaces, out_specs=[VMEM]...  11.2 us
  transfers between devices with their start and end apart: 25, of which 16 were waited for; matrix products, arithmetic and copies ran while one was open for 2% of the time, Pallas kernels for 6%

profile of v12, /device:TPU:0, one launch (start us, length us, event | category | flops | bytes accessed | tf_op | source)
XLA Modules:
  0.0 74.2 jit_solution(12198044009128348780)
XLA Ops:
  0.6 3.9 %shard_map.68 = (bf16[48,1408]{1,0:T(8,128)(2,1)}, bf16[48,1408]{1,0:T(8,128)(2,1)}, bf16[48,1408]{1,0:T(8,128)(2,1)}, bf16[48,1408]{1,0:T(8,128)(2,1)}, f32[16,48]{1,0:T(8,128)}) custom-call(bf16[48,3584]{1,0:T(8,128)(2,1)} %tokens.1, bf16[384,2560]{1,0:T(8,128)(2,1)} %bitcast.28, f32[32,2560]{1,0:T(8,128)} %bitcast.35, s32[8,48]{1,0:T(8,128)} %bitcast.37, ...), custom_call_target="tpu_custom_call" | custom-call | flops 1 | bytes 1 | tf_op jit(solution)/shard_map/pallas_call | solution.py:39
  5.1 2.7 %collective-permute-start.3 = (bf16[48,1408]{1,0:T(8,128)(2,1)}, bf16[48,1408]{1,0:T(8,128)(2,1)S(1)}, u32[]{:S(2)}, u32[]{:S(2)}) collective-permute-start(bf16[48,1408]{1,0:T(8,128)(2,1)} %get-tuple-element.31), channel_id=1, source_target_pairs={{0,4},{1,5},{2,6},{3,7},{4,0},{5,1},{6,2},{7,3},{8,12},{9,13},{10,... | collective-permute-start | bytes 405512 | tf_op jit(solution)/shard_map/ppermute | solution.py:287
  7.8 2.6 %collective-permute-start = (bf16[48,1408]{1,0:T(8,128)(2,1)}, bf16[48,1408]{1,0:T(8,128)(2,1)S(1)}, u32[]{:S(2)}, u32[]{:S(2)}) collective-permute-start(bf16[48,1408]{1,0:T(8,128)(2,1)} %get-tuple-element.28), channel_id=1, source_target_pairs={{0,8},{1,9},{2,10},{3,11},{4,12},{5,13},{6,14},{7,15},{8,0},{9,1},... | collective-permute-start | bytes 405512 | tf_op jit(solution)/shard_map/ppermute | solution.py:287
  11.3 3.2 %collective-permute-done.3 = bf16[48,1408]{1,0:T(8,128)(2,1)S(1)} collective-permute-done((bf16[48,1408]{1,0:T(8,128)(2,1)}, bf16[48,1408]{1,0:T(8,128)(2,1)S(1)}, u32[]{:S(2)}, u32[]{:S(2)}) %collective-permute-start.3) | collective-permute-done | bytes 135200 | tf_op jit(solution)/shard_map/ppermute | solution.py:287
  14.5 1.8 %collective-permute-start.4 = (bf16[96,1408]{1,0:T(8,128)(2,1)S(1)}, bf16[96,1408]{1,0:T(8,128)(2,1)S(1)}, u32[]{:S(2)}, u32[]{:S(2)}) collective-permute-start(bf16[96,1408]{1,0:T(8,128)(2,1)S(1)} %constant_dynamic-update-slice_fusion.2.refs_0_.near_x), channel_id=1, source_target_pairs={{0,2},{1,3},{2,0},{3,1},{4,6},{5,7},{6,4},{7,5},{8,10},{9,11},{10,... | collective-permute-start | bytes 811016 | tf_op jit(solution)/shard_map/ppermute | solution.py:287
  16.3 4.9 %collective-permute-done = bf16[48,1408]{1,0:T(8,128)(2,1)S(1)} collective-permute-done((bf16[48,1408]{1,0:T(8,128)(2,1)}, bf16[48,1408]{1,0:T(8,128)(2,1)S(1)}, u32[]{:S(2)}, u32[]{:S(2)}) %collective-permute-start) | collective-permute-done | bytes 135200 | tf_op jit(solution)/shard_map/ppermute | solution.py:287
  21.2 1.6 %collective-permute-start.2 = (bf16[96,1408]{1,0:T(8,128)(2,1)S(1)}, bf16[96,1408]{1,0:T(8,128)(2,1)S(1)}, u32[]{:S(2)}, u32[]{:S(2)}) collective-permute-start(bf16[96,1408]{1,0:T(8,128)(2,1)S(1)} %constant_dynamic-update-slice_fusion.refs_0_), channel_id=1, source_target_pairs={{0,2},{1,3},{2,0},{3,1},{4,6},{5,7},{6,4},{7,5},{8,10},{9,11},{10,... | collective-permute-start | bytes 811016 | tf_op jit(solution)/shard_map/ppermute | solution.py:287
  25.3 3.2 %collective-permute-done.2.refs_1_ = bf16[96,1408]{1,0:T(8,128)(2,1)S(1)} collective-permute-done((bf16[96,1408]{1,0:T(8,128)(2,1)S(1)}, bf16[96,1408]{1,0:T(8,128)(2,1)S(1)}, u32[]{:S(2)}, u32[]{:S(2)}) %collective-permute-start.2) | collective-permute-done | bytes 270368 | tf_op jit(solution)/shard_map/ppermute | solution.py:287
  31.3 3.2 %collective-permute-start.12 = (bf16[96,256]{1,0:T(8,128)(2,1)S(1)}, bf16[96,256]{1,0:T(8,128)(2,1)S(1)}, u32[]{:S(2)}, u32[]{:S(2)}) collective-permute-start(bf16[96,256]{1,0:T(8,128)(2,1)S(1)} %get-tuple-element.41), channel_id=1, source_target_pairs={{0,4},{1,5},{2,6},{3,7},{4,0},{5,1},{6,2},{7,3},{8,12},{9,13},{10,... | collective-permute-start | bytes 147464 | tf_op jit(solution)/shard_map/ppermute | solution.py:287
  35.6 1.4 %collective-permute-start.14 = (bf16[96,256]{1,0:T(8,128)(2,1)S(1)}, bf16[96,256]{1,0:T(8,128)(2,1)S(1)}, u32[]{:S(2)}, u32[]{:S(2)}) collective-permute-start(bf16[96,256]{1,0:T(8,128)(2,1)S(1)} %get-tuple-element.43), channel_id=1, source_target_pairs={{0,12},{1,13},{2,14},{3,15},{4,8},{5,9},{6,10},{7,11},{8,4},{9,5},... | collective-permute-start | bytes 147464 | tf_op jit(solution)/shard_map/ppermute | solution.py:287
  38.4 3.2 %collective-permute-done.13.z2 = bf16[96,256]{1,0:T(8,128)(2,1)S(1)} collective-permute-done((bf16[96,256]{1,0:T(8,128)(2,1)S(1)}, bf16[96,256]{1,0:T(8,128)(2,1)S(1)}, u32[]{:S(2)}, u32[]{:S(2)}) %collective-permute-start.13) | collective-permute-done | bytes 49184 | tf_op jit(solution)/shard_map/ppermute | solution.py:287
  41.6 1.8 %shard_map.73 = (bf16[128,1280]{1,0:T(8,128)(2,1)S(1)}, bf16[128,1280]{1,0:T(8,128)(2,1)S(1)}, bf16[128,1280]{1,0:T(8,128)(2,1)S(1)}, bf16[128,1280]{1,0:T(8,128)(2,1)S(1)}) custom-call(bf16[96,256]{1,0:T(8,128)(2,1)S(1)} %get-tuple-element.40.z0, bf16[96,256]{1,0:T(8,128)(2,1)S(1)} %collective-permute-done.12.z1, ...), custom_call_target="tpu_custom_call" | custom-call | flops 1 | bytes 1 | tf_op jit(solution)/shard_map/pallas_call | solution.py:39
  43.4 1.6 %collective-permute-start.18 = (bf16[4,32,1280]{2,1,0:T(8,128)(2,1)S(1)}, bf16[4,32,1280]{2,1,0:T(8,128)(2,1)S(1)}, u32[]{:S(2)}, u32[]{:S(2)}) collective-permute-start(bf16[4,32,1280]{2,1,0:T(8,128)(2,1)S(1)} %bitcast.34), channel_id=1, source_target_pairs={{0,2},{1,3},{2,0},{3,1},{4,6},{5,7},{6,4},{7,5},{8,10},{9,11},{10,... | collective-permute-start | bytes 983048 | tf_op jit(solution)/shard_map/ppermute | solution.py:287
  44.9 2.0 %collective-permute-start.10 = (bf16[32,896]{1,0:T(8,128)(2,1)S(1)}, bf16[32,896]{1,0:T(8,128)(2,1)S(1)}, u32[]{:S(2)}, u32[]{:S(2)}) collective-permute-start(bf16[32,896]{1,0:T(8,128)(2,1)S(1)} %get-tuple-element.37), channel_id=1, source_target_pairs={{0,8},{1,9},{2,10},{3,11},{4,12},{5,13},{6,14},{7,15},{8,0},{9,1},... | collective-permute-start | bytes 172040 | tf_op jit(solution)/shard_map/ppermute | solution.py:287
  47.0 1.6 %collective-permute-start.11 = (bf16[32,896]{1,0:T(8,128)(2,1)S(1)}, bf16[32,896]{1,0:T(8,128)(2,1)S(1)}, u32[]{:S(2)}, u32[]{:S(2)}) collective-permute-start(bf16[32,896]{1,0:T(8,128)(2,1)S(1)} %get-tuple-element.38), channel_id=1, source_target_pairs={{0,12},{1,13},{2,14},{3,15},{4,8},{5,9},{6,10},{7,11},{8,4},{9,5},... | collective-permute-start | bytes 172040 | tf_op jit(solution)/shard_map/ppermute | solution.py:287
  48.6 3.1 %collective-permute-done.10.c2 = bf16[32,896]{1,0:T(8,128)(2,1)S(1)} collective-permute-done((bf16[32,896]{1,0:T(8,128)(2,1)S(1)}, bf16[32,896]{1,0:T(8,128)(2,1)S(1)}, u32[]{:S(2)}, u32[]{:S(2)}) %collective-permute-start.10) | collective-permute-done | bytes 57376 | tf_op jit(solution)/shard_map/ppermute | solution.py:287
  51.7 1.4 %collective-permute-done.11.c3 = bf16[32,896]{1,0:T(8,128)(2,1)S(1)} collective-permute-done((bf16[32,896]{1,0:T(8,128)(2,1)S(1)}, bf16[32,896]{1,0:T(8,128)(2,1)S(1)}, u32[]{:S(2)}, u32[]{:S(2)}) %collective-permute-start.11) | collective-permute-done | bytes 57376 | tf_op jit(solution)/shard_map/ppermute | solution.py:287
  53.3 2.7 %shard_map.71 = (f32[32,32]{1,0:T(8,128)S(1)}, f32[32,3584]{1,0:T(8,128)}) custom-call(bf16[32,896]{1,0:T(8,128)(2,1)S(1)} %get-tuple-element.35.c0, bf16[32,896]{1,0:T(8,128)(2,1)S(1)} %collective-permute-done.9.c1, bf16[32,896]{1,0:T(8,128)(2,1)S(1)} %collective-permute-done.10.c2, bf16[32,896]{1,0:T(8,128)(2,1)S(1)} %collective-permute-done.11.c3), custom_call_target="tpu_custom_call" | custom-call | flops 10000000 | bytes 10000000 | tf_op jit(solution)/shard_map/pallas_call | solution.py:39
  56.8 2.4 %collective-permute-start.20 = (bf16[32,1280]{1,0:T(8,128)(2,1)S(1)}, bf16[32,1280]{1,0:T(8,128)(2,1)S(1)}, u32[]{:S(2)}, u32[]{:S(2)}) collective-permute-start(bf16[32,1280]{1,0:T(8,128)(2,1)S(1)} %get-tuple-element.59), channel_id=1, source_target_pairs={{0,8},{1,9},{2,10},{3,11},{4,12},{5,13},{6,14},{7,15},{8,0},{9,1},... | collective-permute-start | bytes 245768 | tf_op jit(solution)/shard_map/ppermute | solution.py:287
  59.3 1.9 %collective-permute-start.21 = (bf16[32,1280]{1,0:T(8,128)(2,1)S(1)}, bf16[32,1280]{1,0:T(8,128)(2,1)S(1)}, u32[]{:S(2)}, u32[]{:S(2)}) collective-permute-start(bf16[32,1280]{1,0:T(8,128)(2,1)S(1)} %get-tuple-element.58), channel_id=1, source_target_pairs={{0,12},{1,13},{2,14},{3,15},{4,8},{5,9},{6,10},{7,11},{8,4},{9,5},... | collective-permute-start | bytes 245768 | tf_op jit(solution)/shard_map/ppermute | solution.py:287
  61.2 2.4 %collective-permute-done.17 = bf16[4,32,1280]{2,1,0:T(8,128)(2,1)S(1)} collective-permute-done((bf16[4,32,1280]{2,1,0:T(8,128)(2,1)S(1)}, bf16[4,32,1280]{2,1,0:T(8,128)(2,1)S(1)}, u32[]{:S(2)}, u32[]{:S(2)}) %collective-permute-start.17) | collective-permute-done | bytes 327712 | tf_op jit(solution)/shard_map/ppermute | solution.py:287
  64.8 2.0 %collective-permute-start.23 = (bf16[32,1280]{1,0:T(8,128)(2,1)S(1)}, bf16[32,1280]{1,0:T(8,128)(2,1)S(1)}, u32[]{:S(2)}, u32[]{:S(2)}) collective-permute-start(bf16[32,1280]{1,0:T(8,128)(2,1)S(1)} %get-tuple-element.55), channel_id=1, source_target_pairs={{0,8},{1,9},{2,10},{3,11},{4,12},{5,13},{6,14},{7,15},{8,0},{9,1},... | collective-permute-start | bytes 245768 | tf_op jit(solution)/shard_map/ppermute | solution.py:287
  69.1 2.3 %collective-permute-done.23.refs_6_ = bf16[32,1280]{1,0:T(8,128)(2,1)S(1)} collective-permute-done((bf16[32,1280]{1,0:T(8,128)(2,1)S(1)}, bf16[32,1280]{1,0:T(8,128)(2,1)S(1)}, u32[]{:S(2)}, u32[]{:S(2)}) %collective-permute-start.23) | collective-permute-done | bytes 81952 | tf_op jit(solution)/shard_map/ppermute | solution.py:287
  71.4 1.8 %collective-permute-done.24.refs_7_ = bf16[32,1280]{1,0:T(8,128)(2,1)S(1)} collective-permute-done((bf16[32,1280]{1,0:T(8,128)(2,1)S(1)}, bf16[32,1280]{1,0:T(8,128)(2,1)S(1)}, u32[]{:S(2)}, u32[]{:S(2)}) %collective-permute-start.24) | collective-permute-done | bytes 81952 | tf_op jit(solution)/shard_map/ppermute | solution.py:287
  (49 shorter events, 14.8 us)
Async XLA Ops:
  4.6 37.0 %collective-permute-start.16 = (bf16[384,2560]{1,0:T(8,128)(2,1)S(1)}, bf16[384,2560]{1,0:T(8,128)(2,1)S(1)}, u32[]{:S(2)}, u32[]{:S(2)}) collective-permute-start(bf16[384,2560]{1,0:T(8,128)(2,1)S(1)} %bitcast.29), channel_id=1, source_target_pairs={{0,1},{1,0},{2,3},{3,2},{4,5},{5,4},{6,7},{7,6},{8,9},{9,8},{10,11... | collective-permute-start | bytes 5898248 | tf_op jit(solution)/shard_map/ppermute | solution.py:287
  5.1 9.4 %collective-permute-start.3 = (bf16[48,1408]{1,0:T(8,128)(2,1)}, bf16[48,1408]{1,0:T(8,128)(2,1)S(1)}, u32[]{:S(2)}, u32[]{:S(2)}) collective-permute-start(bf16[48,1408]{1,0:T(8,128)(2,1)} %get-tuple-element.31), channel_id=1, source_target_pairs={{0,4},{1,5},{2,6},{3,7},{4,0},{5,1},{6,2},{7,3},{8,12},{9,13},{10,... | collective-permute-start | bytes 405512 | tf_op jit(solution)/shard_map/ppermute | solution.py:287
  7.8 13.4 %collective-permute-start = (bf16[48,1408]{1,0:T(8,128)(2,1)}, bf16[48,1408]{1,0:T(8,128)(2,1)S(1)}, u32[]{:S(2)}, u32[]{:S(2)}) collective-permute-start(bf16[48,1408]{1,0:T(8,128)(2,1)} %get-tuple-element.28), channel_id=1, source_target_pairs={{0,8},{1,9},{2,10},{3,11},{4,12},{5,13},{6,14},{7,15},{8,0},{9,1},... | collective-permute-start | bytes 405512 | tf_op jit(solution)/shard_map/ppermute | solution.py:287
  10.3 10.8 %collective-permute-start.1 = (bf16[48,1408]{1,0:T(8,128)(2,1)}, bf16[48,1408]{1,0:T(8,128)(2,1)S(1)}, u32[]{:S(2)}, u32[]{:S(2)}) collective-permute-start(bf16[48,1408]{1,0:T(8,128)(2,1)} %get-tuple-element.29), channel_id=1, source_target_pairs={{0,12},{1,13},{2,14},{3,15},{4,8},{5,9},{6,10},{7,11},{8,4},{9,5},... | collective-permute-start | bytes 405512 | tf_op jit(solution)/shard_map/ppermute | solution.py:287
  14.5 8.4 %collective-permute-start.4 = (bf16[96,1408]{1,0:T(8,128)(2,1)S(1)}, bf16[96,1408]{1,0:T(8,128)(2,1)S(1)}, u32[]{:S(2)}, u32[]{:S(2)}) collective-permute-start(bf16[96,1408]{1,0:T(8,128)(2,1)S(1)} %constant_dynamic-update-slice_fusion.2.refs_0_.near_x), channel_id=1, source_target_pairs={{0,2},{1,3},{2,0},{3,1},{4,6},{5,7},{6,4},{7,5},{8,10},{9,11},{10,... | collective-permute-start | bytes 811016 | tf_op jit(solution)/shard_map/ppermute | solution.py:287
  21.2 7.3 %collective-permute-start.2 = (bf16[96,1408]{1,0:T(8,128)(2,1)S(1)}, bf16[96,1408]{1,0:T(8,128)(2,1)S(1)}, u32[]{:S(2)}, u32[]{:S(2)}) collective-permute-start(bf16[96,1408]{1,0:T(8,128)(2,1)S(1)} %constant_dynamic-update-slice_fusion.refs_0_), channel_id=1, source_target_pairs={{0,2},{1,3},{2,0},{3,1},{4,6},{5,7},{6,4},{7,5},{8,10},{9,11},{10,... | collective-permute-start | bytes 811016 | tf_op jit(solution)/shard_map/ppermute | solution.py:287
  22.8 1.5 %collective-permute-start.5 = (bf16[96,1152]{1,0:T(8,128)(2,1)S(1)}, bf16[96,1152]{1,0:T(8,128)(2,1)S(1)}, u32[]{:S(2)}, u32[]{:S(2)}) collective-permute-start(bf16[96,1152]{1,0:T(8,128)(2,1)S(1)} %slice.16), channel_id=1, source_target_pairs={{0,1},{1,0},{2,3},{3,2},{4,5},{5,4},{6,7},{7,6},{8,9},{9,8},{10,11... | collective-permute-start | bytes 663560 | tf_op jit(solution)/shard_map/ppermute | solution.py:287
  22.9 1.7 %collective-permute-start.6 = (bf16[96,1152]{1,0:T(8,128)(2,1)S(1)}, bf16[96,1152]{1,0:T(8,128)(2,1)S(1)}, u32[]{:S(2)}, u32[]{:S(2)}) collective-permute-start(bf16[96,1152]{1,0:T(8,128)(2,1)S(1)} %slice.17), channel_id=1, source_target_pairs={{0,1},{1,0},{2,3},{3,2},{4,5},{5,4},{6,7},{7,6},{8,9},{9,8},{10,11... | collective-permute-start | bytes 663560 | tf_op jit(solution)/shard_map/ppermute | solution.py:287
  28.5 1.5 %collective-permute-start.7 = (bf16[96,1152]{1,0:T(8,128)(2,1)S(1)}, bf16[96,1152]{1,0:T(8,128)(2,1)S(1)}, u32[]{:S(2)}, u32[]{:S(2)}) collective-permute-start(bf16[96,1152]{1,0:T(8,128)(2,1)S(1)} %slice.14), channel_id=1, source_target_pairs={{0,1},{1,0},{2,3},{3,2},{4,5},{5,4},{6,7},{7,6},{8,9},{9,8},{10,11... | collective-permute-start | bytes 663560 | tf_op jit(solution)/shard_map/ppermute | solution.py:287
  28.6 1.8 %collective-permute-start.8 = (bf16[96,1152]{1,0:T(8,128)(2,1)S(1)}, bf16[96,1152]{1,0:T(8,128)(2,1)S(1)}, u32[]{:S(2)}, u32[]{:S(2)}) collective-permute-start(bf16[96,1152]{1,0:T(8,128)(2,1)S(1)} %slice.15), channel_id=1, source_target_pairs={{0,1},{1,0},{2,3},{3,2},{4,5},{5,4},{6,7},{7,6},{8,9},{9,8},{10,11... | collective-permute-start | bytes 663560 | tf_op jit(solution)/shard_map/ppermute | solution.py:287
  31.3 7.1 %collective-permute-start.12 = (bf16[96,256]{1,0:T(8,128)(2,1)S(1)}, bf16[96,256]{1,0:T(8,128)(2,1)S(1)}, u32[]{:S(2)}, u32[]{:S(2)}) collective-permute-start(bf16[96,256]{1,0:T(8,128)(2,1)S(1)} %get-tuple-element.41), channel_id=1, source_target_pairs={{0,4},{1,5},{2,6},{3,7},{4,0},{5,1},{6,2},{7,3},{8,12},{9,13},{10,... | collective-permute-start | bytes 147464 | tf_op jit(solution)/shard_map/ppermute | solution.py:287
  34.5 7.1 %collective-permute-start.13 = (bf16[96,256]{1,0:T(8,128)(2,1)S(1)}, bf16[96,256]{1,0:T(8,128)(2,1)S(1)}, u32[]{:S(2)}, u32[]{:S(2)}) collective-permute-start(bf16[96,256]{1,0:T(8,128)(2,1)S(1)} %get-tuple-element.42), channel_id=1, source_target_pairs={{0,8},{1,9},{2,10},{3,11},{4,12},{5,13},{6,14},{7,15},{8,0},{9,1},... | collective-permute-start | bytes 147464 | tf_op jit(solution)/shard_map/ppermute | solution.py:287
  35.6 6.0 %collective-permute-start.14 = (bf16[96,256]{1,0:T(8,128)(2,1)S(1)}, bf16[96,256]{1,0:T(8,128)(2,1)S(1)}, u32[]{:S(2)}, u32[]{:S(2)}) collective-permute-start(bf16[96,256]{1,0:T(8,128)(2,1)S(1)} %get-tuple-element.43), channel_id=1, source_target_pairs={{0,12},{1,13},{2,14},{3,15},{4,8},{5,9},{6,10},{7,11},{8,4},{9,5},... | collective-permute-start | bytes 147464 | tf_op jit(solution)/shard_map/ppermute | solution.py:287
  43.4 13.2 %collective-permute-start.18 = (bf16[4,32,1280]{2,1,0:T(8,128)(2,1)S(1)}, bf16[4,32,1280]{2,1,0:T(8,128)(2,1)S(1)}, u32[]{:S(2)}, u32[]{:S(2)}) collective-permute-start(bf16[4,32,1280]{2,1,0:T(8,128)(2,1)S(1)} %bitcast.34), channel_id=1, source_target_pairs={{0,2},{1,3},{2,0},{3,1},{4,6},{5,7},{6,4},{7,5},{8,10},{9,11},{10,... | collective-permute-start | bytes 983048 | tf_op jit(solution)/shard_map/ppermute | solution.py:287
  44.9 6.7 %collective-permute-start.10 = (bf16[32,896]{1,0:T(8,128)(2,1)S(1)}, bf16[32,896]{1,0:T(8,128)(2,1)S(1)}, u32[]{:S(2)}, u32[]{:S(2)}) collective-permute-start(bf16[32,896]{1,0:T(8,128)(2,1)S(1)} %get-tuple-element.37), channel_id=1, source_target_pairs={{0,8},{1,9},{2,10},{3,11},{4,12},{5,13},{6,14},{7,15},{8,0},{9,1},... | collective-permute-start | bytes 172040 | tf_op jit(solution)/shard_map/ppermute | solution.py:287
  47.0 6.1 %collective-permute-start.11 = (bf16[32,896]{1,0:T(8,128)(2,1)S(1)}, bf16[32,896]{1,0:T(8,128)(2,1)S(1)}, u32[]{:S(2)}, u32[]{:S(2)}) collective-permute-start(bf16[32,896]{1,0:T(8,128)(2,1)S(1)} %get-tuple-element.38), channel_id=1, source_target_pairs={{0,12},{1,13},{2,14},{3,15},{4,8},{5,9},{6,10},{7,11},{8,4},{9,5},... | collective-permute-start | bytes 172040 | tf_op jit(solution)/shard_map/ppermute | solution.py:287
  48.5 4.8 %collective-permute-start.9 = (bf16[32,896]{1,0:T(8,128)(2,1)S(1)}, bf16[32,896]{1,0:T(8,128)(2,1)S(1)}, u32[]{:S(2)}, u32[]{:S(2)}) collective-permute-start(bf16[32,896]{1,0:T(8,128)(2,1)S(1)} %get-tuple-element.36), channel_id=1, source_target_pairs={{0,4},{1,5},{2,6},{3,7},{4,0},{5,1},{6,2},{7,3},{8,12},{9,13},{10,... | collective-permute-start | bytes 172040 | tf_op jit(solution)/shard_map/ppermute | solution.py:287
  56.1 7.5 %collective-permute-start.17 = (bf16[4,32,1280]{2,1,0:T(8,128)(2,1)S(1)}, bf16[4,32,1280]{2,1,0:T(8,128)(2,1)S(1)}, u32[]{:S(2)}, u32[]{:S(2)}) collective-permute-start(bf16[4,32,1280]{2,1,0:T(8,128)(2,1)S(1)} %bitcast.33), channel_id=1, source_target_pairs={{0,2},{1,3},{2,0},{3,1},{4,6},{5,7},{6,4},{7,5},{8,10},{9,11},{10,... | collective-permute-start | bytes 983048 | tf_op jit(solution)/shard_map/ppermute | solution.py:287
  56.7 10.1 %collective-permute-start.19 = (bf16[32,1280]{1,0:T(8,128)(2,1)S(1)}, bf16[32,1280]{1,0:T(8,128)(2,1)S(1)}, u32[]{:S(2)}, u32[]{:S(2)}) collective-permute-start(bf16[32,1280]{1,0:T(8,128)(2,1)S(1)} %get-tuple-element.60), channel_id=1, source_target_pairs={{0,4},{1,5},{2,6},{3,7},{4,0},{5,1},{6,2},{7,3},{8,12},{9,13},{10,... | collective-permute-start | bytes 245768 | tf_op jit(solution)/shard_map/ppermute | solution.py:287
  56.8 11.3 %collective-permute-start.20 = (bf16[32,1280]{1,0:T(8,128)(2,1)S(1)}, bf16[32,1280]{1,0:T(8,128)(2,1)S(1)}, u32[]{:S(2)}, u32[]{:S(2)}) collective-permute-start(bf16[32,1280]{1,0:T(8,128)(2,1)S(1)} %get-tuple-element.59), channel_id=1, source_target_pairs={{0,8},{1,9},{2,10},{3,11},{4,12},{5,13},{6,14},{7,15},{8,0},{9,1},... | collective-permute-start | bytes 245768 | tf_op jit(solution)/shard_map/ppermute | solution.py:287
  59.3 8.9 %collective-permute-start.21 = (bf16[32,1280]{1,0:T(8,128)(2,1)S(1)}, bf16[32,1280]{1,0:T(8,128)(2,1)S(1)}, u32[]{:S(2)}, u32[]{:S(2)}) collective-permute-start(bf16[32,1280]{1,0:T(8,128)(2,1)S(1)} %get-tuple-element.58), channel_id=1, source_target_pairs={{0,12},{1,13},{2,14},{3,15},{4,8},{5,9},{6,10},{7,11},{8,4},{9,5},... | collective-permute-start | bytes 245768 | tf_op jit(solution)/shard_map/ppermute | solution.py:287
  63.7 5.4 %collective-permute-start.22 = (bf16[32,1280]{1,0:T(8,128)(2,1)S(1)}, bf16[32,1280]{1,0:T(8,128)(2,1)S(1)}, u32[]{:S(2)}, u32[]{:S(2)}) collective-permute-start(bf16[32,1280]{1,0:T(8,128)(2,1)S(1)} %get-tuple-element.56), channel_id=1, source_target_pairs={{0,4},{1,5},{2,6},{3,7},{4,0},{5,1},{6,2},{7,3},{8,12},{9,13},{10,... | collective-permute-start | bytes 245768 | tf_op jit(solution)/shard_map/ppermute | solution.py:287
  64.8 6.6 %collective-permute-start.23 = (bf16[32,1280]{1,0:T(8,128)(2,1)S(1)}, bf16[32,1280]{1,0:T(8,128)(2,1)S(1)}, u32[]{:S(2)}, u32[]{:S(2)}) collective-permute-start(bf16[32,1280]{1,0:T(8,128)(2,1)S(1)} %get-tuple-element.55), channel_id=1, source_target_pairs={{0,8},{1,9},{2,10},{3,11},{4,12},{5,13},{6,14},{7,15},{8,0},{9,1},... | collective-permute-start | bytes 245768 | tf_op jit(solution)/shard_map/ppermute | solution.py:287
  66.9 6.3 %collective-permute-start.24 = (bf16[32,1280]{1,0:T(8,128)(2,1)S(1)}, bf16[32,1280]{1,0:T(8,128)(2,1)S(1)}, u32[]{:S(2)}, u32[]{:S(2)}) collective-permute-start(bf16[32,1280]{1,0:T(8,128)(2,1)S(1)} %get-tuple-element.54), channel_id=1, source_target_pairs={{0,12},{1,13},{2,14},{3,15},{4,8},{5,9},{6,10},{7,11},{8,4},{9,5},... | collective-permute-start | bytes 245768 | tf_op jit(solution)/shard_map/ppermute | solution.py:287
  (3 other events, 16.8 us)

commit v13 on v11

--- a/solution.py
+++ b/solution.py
@@ -387,15 +387,6 @@
         other,
         limit=limit,
     )
-    columns, _ = lax.optimization_barrier((columns, exchange(terms[0][:16, :128], 1)))
-    columns = list(columns[:1]) + [exchange(columns[j], j * line) for j in range(1, SLICES)]
-    inverse, basis = call(
-        inverse_kernel,
-        [shape((rank, rank), F32), shape((rank, width // n_dp), F32)],
-        [VMEM] * SLICES,
-        [pltpu.VMEM((SLICES, rank, share), BF16)],
-        *columns,
-    )
     sums = []
     for chunk in range(CHUNKS):
         blocks = terms[chunk * low : (chunk + 1) * low]
@@ -408,11 +399,23 @@
             ]
             step *= 2
         sums.append(blocks[0])
-    sums[-1], inverse = lax.optimization_barrier((sums[-1], inverse))
+    columns = list(columns[:1]) + [exchange(columns[j], j * line) for j in range(1, SLICES)]
     blocks = []
-    for block in sums:
+    for i, block in enumerate(sums):
+        if i == len(sums) - 1:
+            block, inverse = lax.optimization_barrier((block, inverse))
         own = [lax.dynamic_index_in_dim(block, place ^ j, 0, False) for j in range(SLICES)]
-        blocks += own[:1] + [exchange(own[j], j * line) for j in range(1, SLICES)]
+        gone = [exchange(own[j], j * line) for j in range(1, SLICES)]
+        if i == 0:
+            gone[0], *columns = lax.optimization_barrier((gone[0], *columns))
+            inverse, basis = call(
+                inverse_kernel,
+                [shape((rank, rank), F32), shape((rank, width // n_dp), F32)],
+                [VMEM] * SLICES,
+                [pltpu.VMEM((SLICES, rank, share), BF16)],
+                *columns,
+            )
+        blocks += own[:1] + gone
     [coeffs] = call(
         functools.partial(coeffs_kernel, scale),
         [shape((rank, part), F32)],

time: 74.4 us -> 74.9 us (level)
  waiting for transfers between devices: 30.3 us -> 31.3 us
    ppermute x25, waiting for transfers between devices: 30.3 us -> 31.3 us  [exchange(): return lax.ppermute(block, AXES, [(i, i ^ step) for i in range(count)])]
  transfers between devices with their start and end apart: 25 -> 25, of which waited for: 16 -> 15; matrix products, arithmetic and copies ran while one was open for 2% -> 2% of each run, Pallas kernels for 6% -> 6%
where the time goes in v13:
time: 74.9 us; the launch traced here: 74.8 us
  waiting for transfers between devices  31.3 us (42%)
  starting transfers between devices  30.1 us (40%)
  Pallas kernels  11.2 us (15%)
  local copies, waits for them, and re-layouts  1.1 us (1%)
  between operations  0.82 us (1%)
    ppermute x25, waiting for transfers between devices, exchange(): return lax.ppermute(block, AXES, [(i, i ^ step) for i in range(count)])  31.3 us
    ppermute x25, starting transfers between devices, exchange(): return lax.ppermute(block, AXES, [(i, i ^ step) for i in range(count)])  30.1 us
    pallas_call x7, Pallas kernels, call(): pl.pallas_call(body, out_shape=shapes, in_specs=spaces, out_specs=[VMEM]...  11.2 us
  transfers between devices with their start and end apart: 25, of which 15 were waited for; matrix products, arithmetic and copies ran while one was open for 2% of the time, Pallas kernels for 6%

profile of v13, /device:TPU:0, one launch (start us, length us, event | category | flops | bytes accessed | tf_op | source)
XLA Modules:
  0.0 74.8 jit_solution(9333447598887235133)
XLA Ops:
  0.6 3.9 %shard_map.68 = (bf16[48,1408]{1,0:T(8,128)(2,1)}, bf16[48,1408]{1,0:T(8,128)(2,1)}, bf16[48,1408]{1,0:T(8,128)(2,1)}, bf16[48,1408]{1,0:T(8,128)(2,1)}, f32[16,48]{1,0:T(8,128)}) custom-call(bf16[48,3584]{1,0:T(8,128)(2,1)} %tokens.1, bf16[384,2560]{1,0:T(8,128)(2,1)} %bitcast.28, f32[32,2560]{1,0:T(8,128)} %bitcast.35, s32[8,48]{1,0:T(8,128)} %bitcast.37, ...), custom_call_target="tpu_custom_call" | custom-call | flops 1 | bytes 1 | tf_op jit(solution)/shard_map/pallas_call | solution.py:39
  5.1 2.7 %collective-permute-start.3 = (bf16[48,1408]{1,0:T(8,128)(2,1)}, bf16[48,1408]{1,0:T(8,128)(2,1)S(1)}, u32[]{:S(2)}, u32[]{:S(2)}) collective-permute-start(bf16[48,1408]{1,0:T(8,128)(2,1)} %get-tuple-element.36), channel_id=1, source_target_pairs={{0,4},{1,5},{2,6},{3,7},{4,0},{5,1},{6,2},{7,3},{8,12},{9,13},{10,... | collective-permute-start | bytes 405512 | tf_op jit(solution)/shard_map/ppermute | solution.py:287
  7.8 2.6 %collective-permute-start = (bf16[48,1408]{1,0:T(8,128)(2,1)}, bf16[48,1408]{1,0:T(8,128)(2,1)S(1)}, u32[]{:S(2)}, u32[]{:S(2)}) collective-permute-start(bf16[48,1408]{1,0:T(8,128)(2,1)} %get-tuple-element.33), channel_id=1, source_target_pairs={{0,8},{1,9},{2,10},{3,11},{4,12},{5,13},{6,14},{7,15},{8,0},{9,1},... | collective-permute-start | bytes 405512 | tf_op jit(solution)/shard_map/ppermute | solution.py:287
  11.3 3.2 %collective-permute-done.3 = bf16[48,1408]{1,0:T(8,128)(2,1)S(1)} collective-permute-done((bf16[48,1408]{1,0:T(8,128)(2,1)}, bf16[48,1408]{1,0:T(8,128)(2,1)S(1)}, u32[]{:S(2)}, u32[]{:S(2)}) %collective-permute-start.3) | collective-permute-done | bytes 135200 | tf_op jit(solution)/shard_map/ppermute | solution.py:287
  14.5 1.8 %collective-permute-start.4 = (bf16[96,1408]{1,0:T(8,128)(2,1)S(1)}, bf16[96,1408]{1,0:T(8,128)(2,1)S(1)}, u32[]{:S(2)}, u32[]{:S(2)}) collective-permute-start(bf16[96,1408]{1,0:T(8,128)(2,1)S(1)} %constant_dynamic-update-slice_fusion.2.refs_0_.near_x), channel_id=1, source_target_pairs={{0,2},{1,3},{2,0},{3,1},{4,6},{5,7},{6,4},{7,5},{8,10},{9,11},{10,... | collective-permute-start | bytes 811016 | tf_op jit(solution)/shard_map/ppermute | solution.py:287
  16.3 4.9 %collective-permute-done = bf16[48,1408]{1,0:T(8,128)(2,1)S(1)} collective-permute-done((bf16[48,1408]{1,0:T(8,128)(2,1)}, bf16[48,1408]{1,0:T(8,128)(2,1)S(1)}, u32[]{:S(2)}, u32[]{:S(2)}) %collective-permute-start) | collective-permute-done | bytes 135200 | tf_op jit(solution)/shard_map/ppermute | solution.py:287
  21.2 1.6 %collective-permute-start.2 = (bf16[96,1408]{1,0:T(8,128)(2,1)S(1)}, bf16[96,1408]{1,0:T(8,128)(2,1)S(1)}, u32[]{:S(2)}, u32[]{:S(2)}) collective-permute-start(bf16[96,1408]{1,0:T(8,128)(2,1)S(1)} %constant_dynamic-update-slice_fusion.refs_0_), channel_id=1, source_target_pairs={{0,2},{1,3},{2,0},{3,1},{4,6},{5,7},{6,4},{7,5},{8,10},{9,11},{10,... | collective-permute-start | bytes 811016 | tf_op jit(solution)/shard_map/ppermute | solution.py:287
  25.3 3.2 %collective-permute-done.2.refs_1_ = bf16[96,1408]{1,0:T(8,128)(2,1)S(1)} collective-permute-done((bf16[96,1408]{1,0:T(8,128)(2,1)S(1)}, bf16[96,1408]{1,0:T(8,128)(2,1)S(1)}, u32[]{:S(2)}, u32[]{:S(2)}) %collective-permute-start.2) | collective-permute-done | bytes 270368 | tf_op jit(solution)/shard_map/ppermute | solution.py:287
  31.3 4.2 %collective-permute-start.10 = (bf16[96,256]{1,0:T(8,128)(2,1)S(1)}, bf16[96,256]{1,0:T(8,128)(2,1)S(1)}, u32[]{:S(2)}, u32[]{:S(2)}) collective-permute-start(bf16[96,256]{1,0:T(8,128)(2,1)S(1)} %get-tuple-element.42), channel_id=1, source_target_pairs={{0,8},{1,9},{2,10},{3,11},{4,12},{5,13},{6,14},{7,15},{8,0},{9,1},... | collective-permute-start | bytes 147464 | tf_op jit(solution)/shard_map/ppermute | solution.py:287
  35.5 1.4 %collective-permute-start.11 = (bf16[96,256]{1,0:T(8,128)(2,1)S(1)}, bf16[96,256]{1,0:T(8,128)(2,1)S(1)}, u32[]{:S(2)}, u32[]{:S(2)}) collective-permute-start(bf16[96,256]{1,0:T(8,128)(2,1)S(1)} %get-tuple-element.43), channel_id=1, source_target_pairs={{0,12},{1,13},{2,14},{3,15},{4,8},{5,9},{6,10},{7,11},{8,4},{9,5},... | collective-permute-start | bytes 147464 | tf_op jit(solution)/shard_map/ppermute | solution.py:287
  39.1 2.4 %collective-permute-done.11.z3 = bf16[96,256]{1,0:T(8,128)(2,1)S(1)} collective-permute-done((bf16[96,256]{1,0:T(8,128)(2,1)S(1)}, bf16[96,256]{1,0:T(8,128)(2,1)S(1)}, u32[]{:S(2)}, u32[]{:S(2)}) %collective-permute-start.11) | collective-permute-done | bytes 49184 | tf_op jit(solution)/shard_map/ppermute | solution.py:287
  41.5 1.8 %shard_map.72 = (bf16[128,1280]{1,0:T(8,128)(2,1)S(1)}, bf16[128,1280]{1,0:T(8,128)(2,1)S(1)}, bf16[128,1280]{1,0:T(8,128)(2,1)S(1)}, bf16[128,1280]{1,0:T(8,128)(2,1)S(1)}) custom-call(bf16[96,256]{1,0:T(8,128)(2,1)S(1)} %get-tuple-element.40.z0, bf16[96,256]{1,0:T(8,128)(2,1)S(1)} %collective-permute-done.9.z1, ...), custom_call_target="tpu_custom_call" | custom-call | flops 1 | bytes 1 | tf_op jit(solution)/shard_map/pallas_call | solution.py:39
  43.3 1.6 %collective-permute-start.14 = (bf16[4,32,1280]{2,1,0:T(8,128)(2,1)S(1)}, bf16[4,32,1280]{2,1,0:T(8,128)(2,1)S(1)}, u32[]{:S(2)}, u32[]{:S(2)}) collective-permute-start(bf16[4,32,1280]{2,1,0:T(8,128)(2,1)S(1)} %bitcast.34), channel_id=1, source_target_pairs={{0,2},{1,3},{2,0},{3,1},{4,6},{5,7},{6,4},{7,5},{8,10},{9,11},{10,... | collective-permute-start | bytes 983048 | tf_op jit(solution)/shard_map/ppermute | solution.py:287
  45.1 2.4 %collective-permute-start.17 = (bf16[32,896]{1,0:T(8,128)(2,1)S(1)}, bf16[32,896]{1,0:T(8,128)(2,1)S(1)}, u32[]{:S(2)}, u32[]{:S(2)}) collective-permute-start(bf16[32,896]{1,0:T(8,128)(2,1)S(1)} %get-tuple-element.51), channel_id=1, source_target_pairs={{0,8},{1,9},{2,10},{3,11},{4,12},{5,13},{6,14},{7,15},{8,0},{9,1},... | collective-permute-start | bytes 172040 | tf_op jit(solution)/shard_map/ppermute | solution.py:287
  47.4 1.8 %collective-permute-start.18 = (bf16[32,896]{1,0:T(8,128)(2,1)S(1)}, bf16[32,896]{1,0:T(8,128)(2,1)S(1)}, u32[]{:S(2)}, u32[]{:S(2)}) collective-permute-start(bf16[32,896]{1,0:T(8,128)(2,1)S(1)} %get-tuple-element.52), channel_id=1, source_target_pairs={{0,12},{1,13},{2,14},{3,15},{4,8},{5,9},{6,10},{7,11},{8,4},{9,5},... | collective-permute-start | bytes 172040 | tf_op jit(solution)/shard_map/ppermute | solution.py:287
  49.7 4.2 %collective-permute-done.14 = bf16[4,32,1280]{2,1,0:T(8,128)(2,1)S(1)} collective-permute-done((bf16[4,32,1280]{2,1,0:T(8,128)(2,1)S(1)}, bf16[4,32,1280]{2,1,0:T(8,128)(2,1)S(1)}, u32[]{:S(2)}, u32[]{:S(2)}) %collective-permute-start.14) | collective-permute-done | bytes 327712 | tf_op jit(solution)/shard_map/ppermute | solution.py:287
  54.4 4.3 %collective-permute-done.19 = bf16[4,32,1280]{2,1,0:T(8,128)(2,1)S(1)} collective-permute-done((bf16[4,32,1280]{2,1,0:T(8,128)(2,1)S(1)}, bf16[4,32,1280]{2,1,0:T(8,128)(2,1)S(1)}, u32[]{:S(2)}, u32[]{:S(2)}) %collective-permute-start.19) | collective-permute-done | bytes 327712 | tf_op jit(solution)/shard_map/ppermute | solution.py:287
  58.7 1.3 %collective-permute-start.20 = (bf16[32,1280]{1,0:T(8,128)(2,1)S(1)}, bf16[32,1280]{1,0:T(8,128)(2,1)S(1)}, u32[]{:S(2)}, u32[]{:S(2)}) collective-permute-start(bf16[32,1280]{1,0:T(8,128)(2,1)S(1)} %get-tuple-element.69), channel_id=1, source_target_pairs={{0,8},{1,9},{2,10},{3,11},{4,12},{5,13},{6,14},{7,15},{8,0},{9,1},... | collective-permute-start | bytes 245768 | tf_op jit(solution)/shard_map/ppermute | solution.py:287
  60.1 1.7 %collective-permute-start.21 = (bf16[32,1280]{1,0:T(8,128)(2,1)S(1)}, bf16[32,1280]{1,0:T(8,128)(2,1)S(1)}, u32[]{:S(2)}, u32[]{:S(2)}) collective-permute-start(bf16[32,1280]{1,0:T(8,128)(2,1)S(1)} %get-tuple-element.68), channel_id=1, source_target_pairs={{0,12},{1,13},{2,14},{3,15},{4,8},{5,9},{6,10},{7,11},{8,4},{9,5},... | collective-permute-start | bytes 245768 | tf_op jit(solution)/shard_map/ppermute | solution.py:287
  61.7 2.7 %shard_map.73 = (f32[32,32]{1,0:T(8,128)S(1)}, f32[32,3584]{1,0:T(8,128)}) custom-call(bf16[32,896]{1,0:T(8,128)(2,1)S(1)} %get-tuple-element.53.c0, bf16[32,896]{1,0:T(8,128)(2,1)S(1)} %collective-permute-done.16.c1, bf16[32,896]{1,0:T(8,128)(2,1)S(1)} %collective-permute-done.17.c2, bf16[32,896]{1,0:T(8,128)(2,1)S(1)} %collective-permute-done.18.c3), custom_call_target="tpu_custom_call" | custom-call | flops 1 | bytes 1 | tf_op jit(solution)/shard_map/pallas_call | solution.py:39
  65.2 2.2 %collective-permute-start.23 = (bf16[32,1280]{1,0:T(8,128)(2,1)S(1)}, bf16[32,1280]{1,0:T(8,128)(2,1)S(1)}, u32[]{:S(2)}, u32[]{:S(2)}) collective-permute-start(bf16[32,1280]{1,0:T(8,128)(2,1)S(1)} %get-tuple-element.65), channel_id=1, source_target_pairs={{0,8},{1,9},{2,10},{3,11},{4,12},{5,13},{6,14},{7,15},{8,0},{9,1},... | collective-permute-start | bytes 245768 | tf_op jit(solution)/shard_map/ppermute | solution.py:287
  67.4 1.6 %collective-permute-start.24 = (bf16[32,1280]{1,0:T(8,128)(2,1)S(1)}, bf16[32,1280]{1,0:T(8,128)(2,1)S(1)}, u32[]{:S(2)}, u32[]{:S(2)}) collective-permute-start(bf16[32,1280]{1,0:T(8,128)(2,1)S(1)} %get-tuple-element.64), channel_id=1, source_target_pairs={{0,12},{1,13},{2,14},{3,15},{4,8},{5,9},{6,10},{7,11},{8,4},{9,5},... | collective-permute-start | bytes 245768 | tf_op jit(solution)/shard_map/ppermute | solution.py:287
  69.0 1.6 %collective-permute-done.22.refs_5_ = bf16[32,1280]{1,0:T(8,128)(2,1)S(1)} collective-permute-done((bf16[32,1280]{1,0:T(8,128)(2,1)S(1)}, bf16[32,1280]{1,0:T(8,128)(2,1)S(1)}, u32[]{:S(2)}, u32[]{:S(2)}) %collective-permute-start.22) | collective-permute-done | bytes 81952 | tf_op jit(solution)/shard_map/ppermute | solution.py:287
  70.6 2.1 %collective-permute-done.23.refs_6_ = bf16[32,1280]{1,0:T(8,128)(2,1)S(1)} collective-permute-done((bf16[32,1280]{1,0:T(8,128)(2,1)S(1)}, bf16[32,1280]{1,0:T(8,128)(2,1)S(1)}, u32[]{:S(2)}, u32[]{:S(2)}) %collective-permute-start.23) | collective-permute-done | bytes 81952 | tf_op jit(solution)/shard_map/ppermute | solution.py:287
  (49 shorter events, 13.1 us)
Async XLA Ops:
  4.6 36.9 %collective-permute-start.13 = (bf16[384,2560]{1,0:T(8,128)(2,1)S(1)}, bf16[384,2560]{1,0:T(8,128)(2,1)S(1)}, u32[]{:S(2)}, u32[]{:S(2)}) collective-permute-start(bf16[384,2560]{1,0:T(8,128)(2,1)S(1)} %bitcast.29), channel_id=1, source_target_pairs={{0,1},{1,0},{2,3},{3,2},{4,5},{5,4},{6,7},{7,6},{8,9},{9,8},{10,11... | collective-permute-start | bytes 5898248 | tf_op jit(solution)/shard_map/ppermute | solution.py:287
  5.1 9.4 %collective-permute-start.3 = (bf16[48,1408]{1,0:T(8,128)(2,1)}, bf16[48,1408]{1,0:T(8,128)(2,1)S(1)}, u32[]{:S(2)}, u32[]{:S(2)}) collective-permute-start(bf16[48,1408]{1,0:T(8,128)(2,1)} %get-tuple-element.36), channel_id=1, source_target_pairs={{0,4},{1,5},{2,6},{3,7},{4,0},{5,1},{6,2},{7,3},{8,12},{9,13},{10,... | collective-permute-start | bytes 405512 | tf_op jit(solution)/shard_map/ppermute | solution.py:287
  7.8 13.4 %collective-permute-start = (bf16[48,1408]{1,0:T(8,128)(2,1)}, bf16[48,1408]{1,0:T(8,128)(2,1)S(1)}, u32[]{:S(2)}, u32[]{:S(2)}) collective-permute-start(bf16[48,1408]{1,0:T(8,128)(2,1)} %get-tuple-element.33), channel_id=1, source_target_pairs={{0,8},{1,9},{2,10},{3,11},{4,12},{5,13},{6,14},{7,15},{8,0},{9,1},... | collective-permute-start | bytes 405512 | tf_op jit(solution)/shard_map/ppermute | solution.py:287
  10.3 10.8 %collective-permute-start.1 = (bf16[48,1408]{1,0:T(8,128)(2,1)}, bf16[48,1408]{1,0:T(8,128)(2,1)S(1)}, u32[]{:S(2)}, u32[]{:S(2)}) collective-permute-start(bf16[48,1408]{1,0:T(8,128)(2,1)} %get-tuple-element.34), channel_id=1, source_target_pairs={{0,12},{1,13},{2,14},{3,15},{4,8},{5,9},{6,10},{7,11},{8,4},{9,5},... | collective-permute-start | bytes 405512 | tf_op jit(solution)/shard_map/ppermute | solution.py:287
  14.5 8.4 %collective-permute-start.4 = (bf16[96,1408]{1,0:T(8,128)(2,1)S(1)}, bf16[96,1408]{1,0:T(8,128)(2,1)S(1)}, u32[]{:S(2)}, u32[]{:S(2)}) collective-permute-start(bf16[96,1408]{1,0:T(8,128)(2,1)S(1)} %constant_dynamic-update-slice_fusion.2.refs_0_.near_x), channel_id=1, source_target_pairs={{0,2},{1,3},{2,0},{3,1},{4,6},{5,7},{6,4},{7,5},{8,10},{9,11},{10,... | collective-permute-start | bytes 811016 | tf_op jit(solution)/shard_map/ppermute | solution.py:287
  21.2 7.3 %collective-permute-start.2 = (bf16[96,1408]{1,0:T(8,128)(2,1)S(1)}, bf16[96,1408]{1,0:T(8,128)(2,1)S(1)}, u32[]{:S(2)}, u32[]{:S(2)}) collective-permute-start(bf16[96,1408]{1,0:T(8,128)(2,1)S(1)} %constant_dynamic-update-slice_fusion.refs_0_), channel_id=1, source_target_pairs={{0,2},{1,3},{2,0},{3,1},{4,6},{5,7},{6,4},{7,5},{8,10},{9,11},{10,... | collective-permute-start | bytes 811016 | tf_op jit(solution)/shard_map/ppermute | solution.py:287
  22.8 1.5 %collective-permute-start.5 = (bf16[96,1152]{1,0:T(8,128)(2,1)S(1)}, bf16[96,1152]{1,0:T(8,128)(2,1)S(1)}, u32[]{:S(2)}, u32[]{:S(2)}) collective-permute-start(bf16[96,1152]{1,0:T(8,128)(2,1)S(1)} %slice.16), channel_id=1, source_target_pairs={{0,1},{1,0},{2,3},{3,2},{4,5},{5,4},{6,7},{7,6},{8,9},{9,8},{10,11... | collective-permute-start | bytes 663560 | tf_op jit(solution)/shard_map/ppermute | solution.py:287
  22.9 1.7 %collective-permute-start.6 = (bf16[96,1152]{1,0:T(8,128)(2,1)S(1)}, bf16[96,1152]{1,0:T(8,128)(2,1)S(1)}, u32[]{:S(2)}, u32[]{:S(2)}) collective-permute-start(bf16[96,1152]{1,0:T(8,128)(2,1)S(1)} %slice.17), channel_id=1, source_target_pairs={{0,1},{1,0},{2,3},{3,2},{4,5},{5,4},{6,7},{7,6},{8,9},{9,8},{10,11... | collective-permute-start | bytes 663560 | tf_op jit(solution)/shard_map/ppermute | solution.py:287
  28.5 1.5 %collective-permute-start.7 = (bf16[96,1152]{1,0:T(8,128)(2,1)S(1)}, bf16[96,1152]{1,0:T(8,128)(2,1)S(1)}, u32[]{:S(2)}, u32[]{:S(2)}) collective-permute-start(bf16[96,1152]{1,0:T(8,128)(2,1)S(1)} %slice.14), channel_id=1, source_target_pairs={{0,1},{1,0},{2,3},{3,2},{4,5},{5,4},{6,7},{7,6},{8,9},{9,8},{10,11... | collective-permute-start | bytes 663560 | tf_op jit(solution)/shard_map/ppermute | solution.py:287
  28.6 1.8 %collective-permute-start.8 = (bf16[96,1152]{1,0:T(8,128)(2,1)S(1)}, bf16[96,1152]{1,0:T(8,128)(2,1)S(1)}, u32[]{:S(2)}, u32[]{:S(2)}) collective-permute-start(bf16[96,1152]{1,0:T(8,128)(2,1)S(1)} %slice.15), channel_id=1, source_target_pairs={{0,1},{1,0},{2,3},{3,2},{4,5},{5,4},{6,7},{7,6},{8,9},{9,8},{10,11... | collective-permute-start | bytes 663560 | tf_op jit(solution)/shard_map/ppermute | solution.py:287
  31.3 7.8 %collective-permute-start.10 = (bf16[96,256]{1,0:T(8,128)(2,1)S(1)}, bf16[96,256]{1,0:T(8,128)(2,1)S(1)}, u32[]{:S(2)}, u32[]{:S(2)}) collective-permute-start(bf16[96,256]{1,0:T(8,128)(2,1)S(1)} %get-tuple-element.42), channel_id=1, source_target_pairs={{0,8},{1,9},{2,10},{3,11},{4,12},{5,13},{6,14},{7,15},{8,0},{9,1},... | collective-permute-start | bytes 147464 | tf_op jit(solution)/shard_map/ppermute | solution.py:287
  35.5 6.0 %collective-permute-start.11 = (bf16[96,256]{1,0:T(8,128)(2,1)S(1)}, bf16[96,256]{1,0:T(8,128)(2,1)S(1)}, u32[]{:S(2)}, u32[]{:S(2)}) collective-permute-start(bf16[96,256]{1,0:T(8,128)(2,1)S(1)} %get-tuple-element.43), channel_id=1, source_target_pairs={{0,12},{1,13},{2,14},{3,15},{4,8},{5,9},{6,10},{7,11},{8,4},{9,5},... | collective-permute-start | bytes 147464 | tf_op jit(solution)/shard_map/ppermute | solution.py:287
  36.9 4.6 %collective-permute-start.9 = (bf16[96,256]{1,0:T(8,128)(2,1)S(1)}, bf16[96,256]{1,0:T(8,128)(2,1)S(1)}, u32[]{:S(2)}, u32[]{:S(2)}) collective-permute-start(bf16[96,256]{1,0:T(8,128)(2,1)S(1)} %get-tuple-element.41), channel_id=1, source_target_pairs={{0,4},{1,5},{2,6},{3,7},{4,0},{5,1},{6,2},{7,3},{8,12},{9,13},{10,... | collective-permute-start | bytes 147464 | tf_op jit(solution)/shard_map/ppermute | solution.py:287
  43.3 10.6 %collective-permute-start.14 = (bf16[4,32,1280]{2,1,0:T(8,128)(2,1)S(1)}, bf16[4,32,1280]{2,1,0:T(8,128)(2,1)S(1)}, u32[]{:S(2)}, u32[]{:S(2)}) collective-permute-start(bf16[4,32,1280]{2,1,0:T(8,128)(2,1)S(1)} %bitcast.34), channel_id=1, source_target_pairs={{0,2},{1,3},{2,0},{3,1},{4,6},{5,7},{6,4},{7,5},{8,10},{9,11},{10,... | collective-permute-start | bytes 983048 | tf_op jit(solution)/shard_map/ppermute | solution.py:287
  44.8 15.2 %collective-permute-start.16 = (bf16[32,896]{1,0:T(8,128)(2,1)S(1)}, bf16[32,896]{1,0:T(8,128)(2,1)S(1)}, u32[]{:S(2)}, u32[]{:S(2)}) collective-permute-start(bf16[32,896]{1,0:T(8,128)(2,1)S(1)} %get-tuple-element.50), channel_id=1, source_target_pairs={{0,4},{1,5},{2,6},{3,7},{4,0},{5,1},{6,2},{7,3},{8,12},{9,13},{10,... | collective-permute-start | bytes 172040 | tf_op jit(solution)/shard_map/ppermute | solution.py:287
  45.1 16.7 %collective-permute-start.17 = (bf16[32,896]{1,0:T(8,128)(2,1)S(1)}, bf16[32,896]{1,0:T(8,128)(2,1)S(1)}, u32[]{:S(2)}, u32[]{:S(2)}) collective-permute-start(bf16[32,896]{1,0:T(8,128)(2,1)S(1)} %get-tuple-element.51), channel_id=1, source_target_pairs={{0,8},{1,9},{2,10},{3,11},{4,12},{5,13},{6,14},{7,15},{8,0},{9,1},... | collective-permute-start | bytes 172040 | tf_op jit(solution)/shard_map/ppermute | solution.py:287
  47.4 14.3 %collective-permute-start.18 = (bf16[32,896]{1,0:T(8,128)(2,1)S(1)}, bf16[32,896]{1,0:T(8,128)(2,1)S(1)}, u32[]{:S(2)}, u32[]{:S(2)}) collective-permute-start(bf16[32,896]{1,0:T(8,128)(2,1)S(1)} %get-tuple-element.52), channel_id=1, source_target_pairs={{0,12},{1,13},{2,14},{3,15},{4,8},{5,9},{6,10},{7,11},{8,4},{9,5},... | collective-permute-start | bytes 172040 | tf_op jit(solution)/shard_map/ppermute | solution.py:287
  49.2 9.5 %collective-permute-start.19 = (bf16[4,32,1280]{2,1,0:T(8,128)(2,1)S(1)}, bf16[4,32,1280]{2,1,0:T(8,128)(2,1)S(1)}, u32[]{:S(2)}, u32[]{:S(2)}) collective-permute-start(bf16[4,32,1280]{2,1,0:T(8,128)(2,1)S(1)} %bitcast.33), channel_id=1, source_target_pairs={{0,2},{1,3},{2,0},{3,1},{4,6},{5,7},{6,4},{7,5},{8,10},{9,11},{10,... | collective-permute-start | bytes 983048 | tf_op jit(solution)/shard_map/ppermute | solution.py:287
  54.0 7.7 %collective-permute-start.15 = (bf16[32,1280]{1,0:T(8,128)(2,1)S(1)}, bf16[32,1280]{1,0:T(8,128)(2,1)S(1)}, u32[]{:S(2)}, u32[]{:S(2)}) collective-permute-start(bf16[32,1280]{1,0:T(8,128)(2,1)S(1)} %get-tuple-element.71), channel_id=1, source_target_pairs={{0,4},{1,5},{2,6},{3,7},{4,0},{5,1},{6,2},{7,3},{8,12},{9,13},{10,... | collective-permute-start | bytes 245768 | tf_op jit(solution)/shard_map/ppermute | solution.py:287
  58.7 10.2 %collective-permute-start.20 = (bf16[32,1280]{1,0:T(8,128)(2,1)S(1)}, bf16[32,1280]{1,0:T(8,128)(2,1)S(1)}, u32[]{:S(2)}, u32[]{:S(2)}) collective-permute-start(bf16[32,1280]{1,0:T(8,128)(2,1)S(1)} %get-tuple-element.69), channel_id=1, source_target_pairs={{0,8},{1,9},{2,10},{3,11},{4,12},{5,13},{6,14},{7,15},{8,0},{9,1},... | collective-permute-start | bytes 245768 | tf_op jit(solution)/shard_map/ppermute | solution.py:287
  60.1 8.9 %collective-permute-start.21 = (bf16[32,1280]{1,0:T(8,128)(2,1)S(1)}, bf16[32,1280]{1,0:T(8,128)(2,1)S(1)}, u32[]{:S(2)}, u32[]{:S(2)}) collective-permute-start(bf16[32,1280]{1,0:T(8,128)(2,1)S(1)} %get-tuple-element.68), channel_id=1, source_target_pairs={{0,12},{1,13},{2,14},{3,15},{4,8},{5,9},{6,10},{7,11},{8,4},{9,5},... | collective-permute-start | bytes 245768 | tf_op jit(solution)/shard_map/ppermute | solution.py:287
  64.5 6.1 %collective-permute-start.22 = (bf16[32,1280]{1,0:T(8,128)(2,1)S(1)}, bf16[32,1280]{1,0:T(8,128)(2,1)S(1)}, u32[]{:S(2)}, u32[]{:S(2)}) collective-permute-start(bf16[32,1280]{1,0:T(8,128)(2,1)S(1)} %get-tuple-element.66), channel_id=1, source_target_pairs={{0,4},{1,5},{2,6},{3,7},{4,0},{5,1},{6,2},{7,3},{8,12},{9,13},{10,... | collective-permute-start | bytes 245768 | tf_op jit(solution)/shard_map/ppermute | solution.py:287
  65.2 7.4 %collective-permute-start.23 = (bf16[32,1280]{1,0:T(8,128)(2,1)S(1)}, bf16[32,1280]{1,0:T(8,128)(2,1)S(1)}, u32[]{:S(2)}, u32[]{:S(2)}) collective-permute-start(bf16[32,1280]{1,0:T(8,128)(2,1)S(1)} %get-tuple-element.65), channel_id=1, source_target_pairs={{0,8},{1,9},{2,10},{3,11},{4,12},{5,13},{6,14},{7,15},{8,0},{9,1},... | collective-permute-start | bytes 245768 | tf_op jit(solution)/shard_map/ppermute | solution.py:287
  67.4 6.3 %collective-permute-start.24 = (bf16[32,1280]{1,0:T(8,128)(2,1)S(1)}, bf16[32,1280]{1,0:T(8,128)(2,1)S(1)}, u32[]{:S(2)}, u32[]{:S(2)}) collective-permute-start(bf16[32,1280]{1,0:T(8,128)(2,1)S(1)} %get-tuple-element.64), channel_id=1, source_target_pairs={{0,12},{1,13},{2,14},{3,15},{4,8},{5,9},{6,10},{7,11},{8,4},{9,5},... | collective-permute-start | bytes 245768 | tf_op jit(solution)/shard_map/ppermute | solution.py:287
  (3 other events, 16.7 us)

commit v14 on v11

--- a/solution.py
+++ b/solution.py
@@ -387,8 +387,24 @@
         other,
         limit=limit,
     )
-    columns, _ = lax.optimization_barrier((columns, exchange(terms[0][:16, :128], 1)))
     columns = list(columns[:1]) + [exchange(columns[j], j * line) for j in range(1, SLICES)]
+    blocks = []
+    for i in range(CHUNKS):
+        parts = terms[i * low : (i + 1) * low]
+        parts = [term.reshape(SLICES, rank, piece) for term in parts]
+        step = 2
+        while len(parts) > 1:
+            got = [exchange(send, step) for send in parts[1::2]]
+            if i and step == 2:
+                got[0], blocks[2] = lax.optimization_barrier((got[0], blocks[2]))
+            parts = [
+                (keep.astype(F32) + other.astype(F32)).astype(BF16)
+                for keep, other in zip(parts[::2], got)
+            ]
+            step *= 2
+        own = [lax.dynamic_index_in_dim(parts[0], place ^ j, 0, False) for j in range(SLICES)]
+        blocks += own[:1] + [exchange(own[j], j * line) for j in range(1, SLICES)]
+    blocks[-3], *columns = lax.optimization_barrier((blocks[-3], *columns))
     inverse, basis = call(
         inverse_kernel,
         [shape((rank, rank), F32), shape((rank, width // n_dp), F32)],
@@ -396,23 +412,6 @@
         [pltpu.VMEM((SLICES, rank, share), BF16)],
         *columns,
     )
-    sums = []
-    for chunk in range(CHUNKS):
-        blocks = terms[chunk * low : (chunk + 1) * low]
-        blocks = [term.reshape(SLICES, rank, piece) for term in blocks]
-        step = 2
-        while len(blocks) > 1:
-            blocks = [
-                (keep.astype(F32) + exchange(send, step).astype(F32)).astype(BF16)
-                for keep, send in zip(blocks[::2], blocks[1::2])
-            ]
-            step *= 2
-        sums.append(blocks[0])
-    sums[-1], inverse = lax.optimization_barrier((sums[-1], inverse))
-    blocks = []
-    for block in sums:
-        own = [lax.dynamic_index_in_dim(block, place ^ j, 0, False) for j in range(SLICES)]
-        blocks += own[:1] + [exchange(own[j], j * line) for j in range(1, SLICES)]
     [coeffs] = call(
         functools.partial(coeffs_kernel, scale),
         [shape((rank, part), F32)],

time: 74.4 us -> 74.6 us (level)
  starting transfers between devices: 30.7 us -> 29.5 us
  waiting for transfers between devices: 30.3 us -> 31.5 us
    ppermute x25, waiting for transfers between devices: 30.3 us -> 31.5 us  [exchange(): return lax.ppermute(block, AXES, [(i, i ^ step) for i in range(count)])]
    ppermute x25, starting transfers between devices: 30.7 us -> 29.5 us  [exchange(): return lax.ppermute(block, AXES, [(i, i ^ step) for i in range(count)])]
  transfers between devices with their start and end apart: 25 -> 25, of which waited for: 16 -> 13; matrix products, arithmetic and copies ran while one was open for 2% -> 2% of each run, Pallas kernels for 6% -> 6%
where the time goes in v14:
time: 74.6 us; the launch traced here: 74.4 us
  waiting for transfers between devices  31.5 us (42%)
  starting transfers between devices  29.5 us (40%)
  Pallas kernels  11.2 us (15%)
  local copies, waits for them, and re-layouts  1.11 us (1%)
  between operations  0.82 us (1%)
    ppermute x25, waiting for transfers between devices, exchange(): return lax.ppermute(block, AXES, [(i, i ^ step) for i in range(count)])  31.5 us
    ppermute x25, starting transfers between devices, exchange(): return lax.ppermute(block, AXES, [(i, i ^ step) for i in range(count)])  29.5 us
    pallas_call x7, Pallas kernels, call(): pl.pallas_call(body, out_shape=shapes, in_specs=spaces, out_specs=[VMEM]...  11.2 us
  transfers between devices with their start and end apart: 25, of which 13 were waited for; matrix products, arithmetic and copies ran while one was open for 2% of the time, Pallas kernels for 6%

profile of v14, /device:TPU:0, one launch (start us, length us, event | category | flops | bytes accessed | tf_op | source)
XLA Modules:
  0.0 74.4 jit_solution(6804781898076795226)
XLA Ops:
  0.6 3.9 %shard_map.68 = (bf16[48,1408]{1,0:T(8,128)(2,1)}, bf16[48,1408]{1,0:T(8,128)(2,1)}, bf16[48,1408]{1,0:T(8,128)(2,1)}, bf16[48,1408]{1,0:T(8,128)(2,1)}, f32[16,48]{1,0:T(8,128)}) custom-call(bf16[48,3584]{1,0:T(8,128)(2,1)} %tokens.1, bf16[384,2560]{1,0:T(8,128)(2,1)} %bitcast.28, f32[32,2560]{1,0:T(8,128)} %bitcast.35, s32[8,48]{1,0:T(8,128)} %bitcast.37, ...), custom_call_target="tpu_custom_call" | custom-call | flops 1 | bytes 1 | tf_op jit(solution)/shard_map/pallas_call | solution.py:39
  5.1 2.7 %collective-permute-start.3 = (bf16[48,1408]{1,0:T(8,128)(2,1)}, bf16[48,1408]{1,0:T(8,128)(2,1)S(1)}, u32[]{:S(2)}, u32[]{:S(2)}) collective-permute-start(bf16[48,1408]{1,0:T(8,128)(2,1)} %get-tuple-element.36), channel_id=1, source_target_pairs={{0,4},{1,5},{2,6},{3,7},{4,0},{5,1},{6,2},{7,3},{8,12},{9,13},{10,... | collective-permute-start | bytes 405512 | tf_op jit(solution)/shard_map/ppermute | solution.py:287
  7.8 2.6 %collective-permute-start = (bf16[48,1408]{1,0:T(8,128)(2,1)}, bf16[48,1408]{1,0:T(8,128)(2,1)S(1)}, u32[]{:S(2)}, u32[]{:S(2)}) collective-permute-start(bf16[48,1408]{1,0:T(8,128)(2,1)} %get-tuple-element.33), channel_id=1, source_target_pairs={{0,8},{1,9},{2,10},{3,11},{4,12},{5,13},{6,14},{7,15},{8,0},{9,1},... | collective-permute-start | bytes 405512 | tf_op jit(solution)/shard_map/ppermute | solution.py:287
  11.3 3.2 %collective-permute-done.3 = bf16[48,1408]{1,0:T(8,128)(2,1)S(1)} collective-permute-done((bf16[48,1408]{1,0:T(8,128)(2,1)}, bf16[48,1408]{1,0:T(8,128)(2,1)S(1)}, u32[]{:S(2)}, u32[]{:S(2)}) %collective-permute-start.3) | collective-permute-done | bytes 135200 | tf_op jit(solution)/shard_map/ppermute | solution.py:287
  14.5 1.8 %collective-permute-start.4 = (bf16[96,1408]{1,0:T(8,128)(2,1)S(1)}, bf16[96,1408]{1,0:T(8,128)(2,1)S(1)}, u32[]{:S(2)}, u32[]{:S(2)}) collective-permute-start(bf16[96,1408]{1,0:T(8,128)(2,1)S(1)} %constant_dynamic-update-slice_fusion.2.refs_0_.near_x), channel_id=1, source_target_pairs={{0,2},{1,3},{2,0},{3,1},{4,6},{5,7},{6,4},{7,5},{8,10},{9,11},{10,... | collective-permute-start | bytes 811016 | tf_op jit(solution)/shard_map/ppermute | solution.py:287
  16.3 4.9 %collective-permute-done = bf16[48,1408]{1,0:T(8,128)(2,1)S(1)} collective-permute-done((bf16[48,1408]{1,0:T(8,128)(2,1)}, bf16[48,1408]{1,0:T(8,128)(2,1)S(1)}, u32[]{:S(2)}, u32[]{:S(2)}) %collective-permute-start) | collective-permute-done | bytes 135200 | tf_op jit(solution)/shard_map/ppermute | solution.py:287
  21.2 1.6 %collective-permute-start.2 = (bf16[96,1408]{1,0:T(8,128)(2,1)S(1)}, bf16[96,1408]{1,0:T(8,128)(2,1)S(1)}, u32[]{:S(2)}, u32[]{:S(2)}) collective-permute-start(bf16[96,1408]{1,0:T(8,128)(2,1)S(1)} %constant_dynamic-update-slice_fusion.refs_0_), channel_id=1, source_target_pairs={{0,2},{1,3},{2,0},{3,1},{4,6},{5,7},{6,4},{7,5},{8,10},{9,11},{10,... | collective-permute-start | bytes 811016 | tf_op jit(solution)/shard_map/ppermute | solution.py:287
  25.3 3.2 %collective-permute-done.2.refs_1_ = bf16[96,1408]{1,0:T(8,128)(2,1)S(1)} collective-permute-done((bf16[96,1408]{1,0:T(8,128)(2,1)S(1)}, bf16[96,1408]{1,0:T(8,128)(2,1)S(1)}, u32[]{:S(2)}, u32[]{:S(2)}) %collective-permute-start.2) | collective-permute-done | bytes 270368 | tf_op jit(solution)/shard_map/ppermute | solution.py:287
  31.3 4.2 %collective-permute-start.10 = (bf16[96,256]{1,0:T(8,128)(2,1)S(1)}, bf16[96,256]{1,0:T(8,128)(2,1)S(1)}, u32[]{:S(2)}, u32[]{:S(2)}) collective-permute-start(bf16[96,256]{1,0:T(8,128)(2,1)S(1)} %get-tuple-element.42), channel_id=1, source_target_pairs={{0,8},{1,9},{2,10},{3,11},{4,12},{5,13},{6,14},{7,15},{8,0},{9,1},... | collective-permute-start | bytes 147464 | tf_op jit(solution)/shard_map/ppermute | solution.py:287
  35.5 1.4 %collective-permute-start.11 = (bf16[96,256]{1,0:T(8,128)(2,1)S(1)}, bf16[96,256]{1,0:T(8,128)(2,1)S(1)}, u32[]{:S(2)}, u32[]{:S(2)}) collective-permute-start(bf16[96,256]{1,0:T(8,128)(2,1)S(1)} %get-tuple-element.43), channel_id=1, source_target_pairs={{0,12},{1,13},{2,14},{3,15},{4,8},{5,9},{6,10},{7,11},{8,4},{9,5},... | collective-permute-start | bytes 147464 | tf_op jit(solution)/shard_map/ppermute | solution.py:287
  36.9 1.2 %collective-permute-done.12.pair = f32[16,48]{1,0:T(8,128)S(1)} collective-permute-done((f32[16,48]{1,0:T(8,128)S(1)}, f32[16,48]{1,0:T(8,128)S(1)}, u32[]{:S(2)}, u32[]{:S(2)}) %collective-permute-start.12) | collective-permute-done | bytes 3104 | tf_op jit(solution)/shard_map/ppermute | solution.py:287
  39.1 2.4 %collective-permute-done.11.z3 = bf16[96,256]{1,0:T(8,128)(2,1)S(1)} collective-permute-done((bf16[96,256]{1,0:T(8,128)(2,1)S(1)}, bf16[96,256]{1,0:T(8,128)(2,1)S(1)}, u32[]{:S(2)}, u32[]{:S(2)}) %collective-permute-start.11) | collective-permute-done | bytes 49184 | tf_op jit(solution)/shard_map/ppermute | solution.py:287
  41.5 1.8 %shard_map.72 = (bf16[128,1280]{1,0:T(8,128)(2,1)S(1)}, bf16[128,1280]{1,0:T(8,128)(2,1)S(1)}, bf16[128,1280]{1,0:T(8,128)(2,1)S(1)}, bf16[128,1280]{1,0:T(8,128)(2,1)S(1)}) custom-call(bf16[96,256]{1,0:T(8,128)(2,1)S(1)} %get-tuple-element.40.z0, bf16[96,256]{1,0:T(8,128)(2,1)S(1)} %collective-permute-done.9.z1, ...), custom_call_target="tpu_custom_call" | custom-call | flops 1 | bytes 1 | tf_op jit(solution)/shard_map/pallas_call | solution.py:39
  43.3 1.6 %collective-permute-start.15 = (bf16[4,32,1280]{2,1,0:T(8,128)(2,1)S(1)}, bf16[4,32,1280]{2,1,0:T(8,128)(2,1)S(1)}, u32[]{:S(2)}, u32[]{:S(2)}) collective-permute-start(bf16[4,32,1280]{2,1,0:T(8,128)(2,1)S(1)} %bitcast.34), channel_id=1, source_target_pairs={{0,2},{1,3},{2,0},{3,1},{4,6},{5,7},{6,4},{7,5},{8,10},{9,11},{10,... | collective-permute-start | bytes 983048 | tf_op jit(solution)/shard_map/ppermute | solution.py:287
  45.4 8.6 %collective-permute-done.15 = bf16[4,32,1280]{2,1,0:T(8,128)(2,1)S(1)} collective-permute-done((bf16[4,32,1280]{2,1,0:T(8,128)(2,1)S(1)}, bf16[4,32,1280]{2,1,0:T(8,128)(2,1)S(1)}, u32[]{:S(2)}, u32[]{:S(2)}) %collective-permute-start.15) | collective-permute-done | bytes 327712 | tf_op jit(solution)/shard_map/ppermute | solution.py:287
  54.1 1.2 %collective-permute-start.16 = (bf16[32,1280]{1,0:T(8,128)(2,1)S(1)}, bf16[32,1280]{1,0:T(8,128)(2,1)S(1)}, u32[]{:S(2)}, u32[]{:S(2)}) collective-permute-start(bf16[32,1280]{1,0:T(8,128)(2,1)S(1)} %get-tuple-element.71), channel_id=1, source_target_pairs={{0,8},{1,9},{2,10},{3,11},{4,12},{5,13},{6,14},{7,15},{8,0},{9,1},... | collective-permute-start | bytes 245768 | tf_op jit(solution)/shard_map/ppermute | solution.py:287
  55.3 1.5 %collective-permute-start.18 = (bf16[32,896]{1,0:T(8,128)(2,1)S(1)}, bf16[32,896]{1,0:T(8,128)(2,1)S(1)}, u32[]{:S(2)}, u32[]{:S(2)}) collective-permute-start(bf16[32,896]{1,0:T(8,128)(2,1)S(1)} %get-tuple-element.53), channel_id=1, source_target_pairs={{0,4},{1,5},{2,6},{3,7},{4,0},{5,1},{6,2},{7,3},{8,12},{9,13},{10,... | collective-permute-start | bytes 172040 | tf_op jit(solution)/shard_map/ppermute | solution.py:287
  57.3 2.3 %collective-permute-start.20 = (bf16[32,896]{1,0:T(8,128)(2,1)S(1)}, bf16[32,896]{1,0:T(8,128)(2,1)S(1)}, u32[]{:S(2)}, u32[]{:S(2)}) collective-permute-start(bf16[32,896]{1,0:T(8,128)(2,1)S(1)} %get-tuple-element.55), channel_id=1, source_target_pairs={{0,12},{1,13},{2,14},{3,15},{4,8},{5,9},{6,10},{7,11},{8,4},{9,5},... | collective-permute-start | bytes 172040 | tf_op jit(solution)/shard_map/ppermute | solution.py:287
  59.7 1.3 %collective-permute-done.16.refs_2_ = bf16[32,1280]{1,0:T(8,128)(2,1)S(1)} collective-permute-done((bf16[32,1280]{1,0:T(8,128)(2,1)S(1)}, bf16[32,1280]{1,0:T(8,128)(2,1)S(1)}, u32[]{:S(2)}, u32[]{:S(2)}) %collective-permute-start.16) | collective-permute-done | bytes 81952 | tf_op jit(solution)/shard_map/ppermute | solution.py:287
  61.1 2.0 %collective-permute-start.21 = (bf16[32,1280]{1,0:T(8,128)(2,1)S(1)}, bf16[32,1280]{1,0:T(8,128)(2,1)S(1)}, u32[]{:S(2)}, u32[]{:S(2)}) collective-permute-start(bf16[32,1280]{1,0:T(8,128)(2,1)S(1)} %get-tuple-element.69), channel_id=1, source_target_pairs={{0,4},{1,5},{2,6},{3,7},{4,0},{5,1},{6,2},{7,3},{8,12},{9,13},{10,... | collective-permute-start | bytes 245768 | tf_op jit(solution)/shard_map/ppermute | solution.py:287
  63.1 1.6 %collective-permute-start.22 = (bf16[32,1280]{1,0:T(8,128)(2,1)S(1)}, bf16[32,1280]{1,0:T(8,128)(2,1)S(1)}, u32[]{:S(2)}, u32[]{:S(2)}) collective-permute-start(bf16[32,1280]{1,0:T(8,128)(2,1)S(1)} %get-tuple-element.68), channel_id=1, source_target_pairs={{0,12},{1,13},{2,14},{3,15},{4,8},{5,9},{6,10},{7,11},{8,4},{9,5},... | collective-permute-start | bytes 245768 | tf_op jit(solution)/shard_map/ppermute | solution.py:287
  64.8 2.3 %collective-permute-start.24 = (bf16[32,1280]{1,0:T(8,128)(2,1)S(1)}, bf16[32,1280]{1,0:T(8,128)(2,1)S(1)}, u32[]{:S(2)}, u32[]{:S(2)}) collective-permute-start(bf16[32,1280]{1,0:T(8,128)(2,1)S(1)} %get-tuple-element.64), channel_id=1, source_target_pairs={{0,12},{1,13},{2,14},{3,15},{4,8},{5,9},{6,10},{7,11},{8,4},{9,5},... | collective-permute-start | bytes 245768 | tf_op jit(solution)/shard_map/ppermute | solution.py:287
  67.0 2.7 %shard_map.73 = (f32[32,32]{1,0:T(8,128)S(1)}, f32[32,3584]{1,0:T(8,128)}) custom-call(bf16[32,896]{1,0:T(8,128)(2,1)S(1)} %get-tuple-element.56.c0, bf16[32,896]{1,0:T(8,128)(2,1)S(1)} %collective-permute-done.18.c1, bf16[32,896]{1,0:T(8,128)(2,1)S(1)} %collective-permute-done.19.c2, bf16[32,896]{1,0:T(8,128)(2,1)S(1)} %collective-permute-done.20.c3), custom_call_target="tpu_custom_call" | custom-call | flops 1 | bytes 1 | tf_op jit(solution)/shard_map/pallas_call | solution.py:39
  69.8 3.6 %collective-permute-done.23.refs_6_ = bf16[32,1280]{1,0:T(8,128)(2,1)S(1)} collective-permute-done((bf16[32,1280]{1,0:T(8,128)(2,1)S(1)}, bf16[32,1280]{1,0:T(8,128)(2,1)S(1)}, u32[]{:S(2)}, u32[]{:S(2)}) %collective-permute-start.23) | collective-permute-done | bytes 81952 | tf_op jit(solution)/shard_map/ppermute | solution.py:287
  (49 shorter events, 10.2 us)
Async XLA Ops:
  4.6 36.9 %collective-permute-start.13 = (bf16[384,2560]{1,0:T(8,128)(2,1)S(1)}, bf16[384,2560]{1,0:T(8,128)(2,1)S(1)}, u32[]{:S(2)}, u32[]{:S(2)}) collective-permute-start(bf16[384,2560]{1,0:T(8,128)(2,1)S(1)} %bitcast.29), channel_id=1, source_target_pairs={{0,1},{1,0},{2,3},{3,2},{4,5},{5,4},{6,7},{7,6},{8,9},{9,8},{10,11... | collective-permute-start | bytes 5898248 | tf_op jit(solution)/shard_map/ppermute | solution.py:287
  5.1 9.4 %collective-permute-start.3 = (bf16[48,1408]{1,0:T(8,128)(2,1)}, bf16[48,1408]{1,0:T(8,128)(2,1)S(1)}, u32[]{:S(2)}, u32[]{:S(2)}) collective-permute-start(bf16[48,1408]{1,0:T(8,128)(2,1)} %get-tuple-element.36), channel_id=1, source_target_pairs={{0,4},{1,5},{2,6},{3,7},{4,0},{5,1},{6,2},{7,3},{8,12},{9,13},{10,... | collective-permute-start | bytes 405512 | tf_op jit(solution)/shard_map/ppermute | solution.py:287
  7.8 13.4 %collective-permute-start = (bf16[48,1408]{1,0:T(8,128)(2,1)}, bf16[48,1408]{1,0:T(8,128)(2,1)S(1)}, u32[]{:S(2)}, u32[]{:S(2)}) collective-permute-start(bf16[48,1408]{1,0:T(8,128)(2,1)} %get-tuple-element.33), channel_id=1, source_target_pairs={{0,8},{1,9},{2,10},{3,11},{4,12},{5,13},{6,14},{7,15},{8,0},{9,1},... | collective-permute-start | bytes 405512 | tf_op jit(solution)/shard_map/ppermute | solution.py:287
  10.3 10.8 %collective-permute-start.1 = (bf16[48,1408]{1,0:T(8,128)(2,1)}, bf16[48,1408]{1,0:T(8,128)(2,1)S(1)}, u32[]{:S(2)}, u32[]{:S(2)}) collective-permute-start(bf16[48,1408]{1,0:T(8,128)(2,1)} %get-tuple-element.34), channel_id=1, source_target_pairs={{0,12},{1,13},{2,14},{3,15},{4,8},{5,9},{6,10},{7,11},{8,4},{9,5},... | collective-permute-start | bytes 405512 | tf_op jit(solution)/shard_map/ppermute | solution.py:287
  14.5 8.4 %collective-permute-start.4 = (bf16[96,1408]{1,0:T(8,128)(2,1)S(1)}, bf16[96,1408]{1,0:T(8,128)(2,1)S(1)}, u32[]{:S(2)}, u32[]{:S(2)}) collective-permute-start(bf16[96,1408]{1,0:T(8,128)(2,1)S(1)} %constant_dynamic-update-slice_fusion.2.refs_0_.near_x), channel_id=1, source_target_pairs={{0,2},{1,3},{2,0},{3,1},{4,6},{5,7},{6,4},{7,5},{8,10},{9,11},{10,... | collective-permute-start | bytes 811016 | tf_op jit(solution)/shard_map/ppermute | solution.py:287
  21.2 7.3 %collective-permute-start.2 = (bf16[96,1408]{1,0:T(8,128)(2,1)S(1)}, bf16[96,1408]{1,0:T(8,128)(2,1)S(1)}, u32[]{:S(2)}, u32[]{:S(2)}) collective-permute-start(bf16[96,1408]{1,0:T(8,128)(2,1)S(1)} %constant_dynamic-update-slice_fusion.refs_0_), channel_id=1, source_target_pairs={{0,2},{1,3},{2,0},{3,1},{4,6},{5,7},{6,4},{7,5},{8,10},{9,11},{10,... | collective-permute-start | bytes 811016 | tf_op jit(solution)/shard_map/ppermute | solution.py:287
  22.8 1.5 %collective-permute-start.5 = (bf16[96,1152]{1,0:T(8,128)(2,1)S(1)}, bf16[96,1152]{1,0:T(8,128)(2,1)S(1)}, u32[]{:S(2)}, u32[]{:S(2)}) collective-permute-start(bf16[96,1152]{1,0:T(8,128)(2,1)S(1)} %slice.16), channel_id=1, source_target_pairs={{0,1},{1,0},{2,3},{3,2},{4,5},{5,4},{6,7},{7,6},{8,9},{9,8},{10,11... | collective-permute-start | bytes 663560 | tf_op jit(solution)/shard_map/ppermute | solution.py:287
  22.9 1.7 %collective-permute-start.6 = (bf16[96,1152]{1,0:T(8,128)(2,1)S(1)}, bf16[96,1152]{1,0:T(8,128)(2,1)S(1)}, u32[]{:S(2)}, u32[]{:S(2)}) collective-permute-start(bf16[96,1152]{1,0:T(8,128)(2,1)S(1)} %slice.17), channel_id=1, source_target_pairs={{0,1},{1,0},{2,3},{3,2},{4,5},{5,4},{6,7},{7,6},{8,9},{9,8},{10,11... | collective-permute-start | bytes 663560 | tf_op jit(solution)/shard_map/ppermute | solution.py:287
  28.5 1.5 %collective-permute-start.7 = (bf16[96,1152]{1,0:T(8,128)(2,1)S(1)}, bf16[96,1152]{1,0:T(8,128)(2,1)S(1)}, u32[]{:S(2)}, u32[]{:S(2)}) collective-permute-start(bf16[96,1152]{1,0:T(8,128)(2,1)S(1)} %slice.14), channel_id=1, source_target_pairs={{0,1},{1,0},{2,3},{3,2},{4,5},{5,4},{6,7},{7,6},{8,9},{9,8},{10,11... | collective-permute-start | bytes 663560 | tf_op jit(solution)/shard_map/ppermute | solution.py:287
  28.6 1.8 %collective-permute-start.8 = (bf16[96,1152]{1,0:T(8,128)(2,1)S(1)}, bf16[96,1152]{1,0:T(8,128)(2,1)S(1)}, u32[]{:S(2)}, u32[]{:S(2)}) collective-permute-start(bf16[96,1152]{1,0:T(8,128)(2,1)S(1)} %slice.15), channel_id=1, source_target_pairs={{0,1},{1,0},{2,3},{3,2},{4,5},{5,4},{6,7},{7,6},{8,9},{9,8},{10,11... | collective-permute-start | bytes 663560 | tf_op jit(solution)/shard_map/ppermute | solution.py:287
  31.3 7.8 %collective-permute-start.10 = (bf16[96,256]{1,0:T(8,128)(2,1)S(1)}, bf16[96,256]{1,0:T(8,128)(2,1)S(1)}, u32[]{:S(2)}, u32[]{:S(2)}) collective-permute-start(bf16[96,256]{1,0:T(8,128)(2,1)S(1)} %get-tuple-element.42), channel_id=1, source_target_pairs={{0,8},{1,9},{2,10},{3,11},{4,12},{5,13},{6,14},{7,15},{8,0},{9,1},... | collective-permute-start | bytes 147464 | tf_op jit(solution)/shard_map/ppermute | solution.py:287
  35.5 6.0 %collective-permute-start.11 = (bf16[96,256]{1,0:T(8,128)(2,1)S(1)}, bf16[96,256]{1,0:T(8,128)(2,1)S(1)}, u32[]{:S(2)}, u32[]{:S(2)}) collective-permute-start(bf16[96,256]{1,0:T(8,128)(2,1)S(1)} %get-tuple-element.43), channel_id=1, source_target_pairs={{0,12},{1,13},{2,14},{3,15},{4,8},{5,9},{6,10},{7,11},{8,4},{9,5},... | collective-permute-start | bytes 147464 | tf_op jit(solution)/shard_map/ppermute | solution.py:287
  36.9 4.6 %collective-permute-start.9 = (bf16[96,256]{1,0:T(8,128)(2,1)S(1)}, bf16[96,256]{1,0:T(8,128)(2,1)S(1)}, u32[]{:S(2)}, u32[]{:S(2)}) collective-permute-start(bf16[96,256]{1,0:T(8,128)(2,1)S(1)} %get-tuple-element.41), channel_id=1, source_target_pairs={{0,4},{1,5},{2,6},{3,7},{4,0},{5,1},{6,2},{7,3},{8,12},{9,13},{10,... | collective-permute-start | bytes 147464 | tf_op jit(solution)/shard_map/ppermute | solution.py:287
  43.3 10.7 %collective-permute-start.15 = (bf16[4,32,1280]{2,1,0:T(8,128)(2,1)S(1)}, bf16[4,32,1280]{2,1,0:T(8,128)(2,1)S(1)}, u32[]{:S(2)}, u32[]{:S(2)}) collective-permute-start(bf16[4,32,1280]{2,1,0:T(8,128)(2,1)S(1)} %bitcast.34), channel_id=1, source_target_pairs={{0,2},{1,3},{2,0},{3,1},{4,6},{5,7},{6,4},{7,5},{8,10},{9,11},{10,... | collective-permute-start | bytes 983048 | tf_op jit(solution)/shard_map/ppermute | solution.py:287
  44.8 14.8 %collective-permute-start.14 = (bf16[4,32,1280]{2,1,0:T(8,128)(2,1)S(1)}, bf16[4,32,1280]{2,1,0:T(8,128)(2,1)S(1)}, u32[]{:S(2)}, u32[]{:S(2)}) collective-permute-start(bf16[4,32,1280]{2,1,0:T(8,128)(2,1)S(1)} %bitcast.33), channel_id=1, source_target_pairs={{0,2},{1,3},{2,0},{3,1},{4,6},{5,7},{6,4},{7,5},{8,10},{9,11},{10,... | collective-permute-start | bytes 983048 | tf_op jit(solution)/shard_map/ppermute | solution.py:287
  54.1 6.8 %collective-permute-start.16 = (bf16[32,1280]{1,0:T(8,128)(2,1)S(1)}, bf16[32,1280]{1,0:T(8,128)(2,1)S(1)}, u32[]{:S(2)}, u32[]{:S(2)}) collective-permute-start(bf16[32,1280]{1,0:T(8,128)(2,1)S(1)} %get-tuple-element.71), channel_id=1, source_target_pairs={{0,8},{1,9},{2,10},{3,11},{4,12},{5,13},{6,14},{7,15},{8,0},{9,1},... | collective-permute-start | bytes 245768 | tf_op jit(solution)/shard_map/ppermute | solution.py:287
  55.3 7.9 %collective-permute-start.18 = (bf16[32,896]{1,0:T(8,128)(2,1)S(1)}, bf16[32,896]{1,0:T(8,128)(2,1)S(1)}, u32[]{:S(2)}, u32[]{:S(2)}) collective-permute-start(bf16[32,896]{1,0:T(8,128)(2,1)S(1)} %get-tuple-element.53), channel_id=1, source_target_pairs={{0,4},{1,5},{2,6},{3,7},{4,0},{5,1},{6,2},{7,3},{8,12},{9,13},{10,... | collective-permute-start | bytes 172040 | tf_op jit(solution)/shard_map/ppermute | solution.py:287
  56.8 8.0 %collective-permute-start.19 = (bf16[32,896]{1,0:T(8,128)(2,1)S(1)}, bf16[32,896]{1,0:T(8,128)(2,1)S(1)}, u32[]{:S(2)}, u32[]{:S(2)}) collective-permute-start(bf16[32,896]{1,0:T(8,128)(2,1)S(1)} %get-tuple-element.54), channel_id=1, source_target_pairs={{0,8},{1,9},{2,10},{3,11},{4,12},{5,13},{6,14},{7,15},{8,0},{9,1},... | collective-permute-start | bytes 172040 | tf_op jit(solution)/shard_map/ppermute | solution.py:287
  57.3 7.4 %collective-permute-start.20 = (bf16[32,896]{1,0:T(8,128)(2,1)S(1)}, bf16[32,896]{1,0:T(8,128)(2,1)S(1)}, u32[]{:S(2)}, u32[]{:S(2)}) collective-permute-start(bf16[32,896]{1,0:T(8,128)(2,1)S(1)} %get-tuple-element.55), channel_id=1, source_target_pairs={{0,12},{1,13},{2,14},{3,15},{4,8},{5,9},{6,10},{7,11},{8,4},{9,5},... | collective-permute-start | bytes 172040 | tf_op jit(solution)/shard_map/ppermute | solution.py:287
  61.0 6.0 %collective-permute-start.17 = (bf16[32,1280]{1,0:T(8,128)(2,1)S(1)}, bf16[32,1280]{1,0:T(8,128)(2,1)S(1)}, u32[]{:S(2)}, u32[]{:S(2)}) collective-permute-start(bf16[32,1280]{1,0:T(8,128)(2,1)S(1)} %get-tuple-element.67), channel_id=1, source_target_pairs={{0,4},{1,5},{2,6},{3,7},{4,0},{5,1},{6,2},{7,3},{8,12},{9,13},{10,... | collective-permute-start | bytes 245768 | tf_op jit(solution)/shard_map/ppermute | solution.py:287
  61.1 8.6 %collective-permute-start.21 = (bf16[32,1280]{1,0:T(8,128)(2,1)S(1)}, bf16[32,1280]{1,0:T(8,128)(2,1)S(1)}, u32[]{:S(2)}, u32[]{:S(2)}) collective-permute-start(bf16[32,1280]{1,0:T(8,128)(2,1)S(1)} %get-tuple-element.69), channel_id=1, source_target_pairs={{0,4},{1,5},{2,6},{3,7},{4,0},{5,1},{6,2},{7,3},{8,12},{9,13},{10,... | collective-permute-start | bytes 245768 | tf_op jit(solution)/shard_map/ppermute | solution.py:287
  63.1 6.6 %collective-permute-start.22 = (bf16[32,1280]{1,0:T(8,128)(2,1)S(1)}, bf16[32,1280]{1,0:T(8,128)(2,1)S(1)}, u32[]{:S(2)}, u32[]{:S(2)}) collective-permute-start(bf16[32,1280]{1,0:T(8,128)(2,1)S(1)} %get-tuple-element.68), channel_id=1, source_target_pairs={{0,12},{1,13},{2,14},{3,15},{4,8},{5,9},{6,10},{7,11},{8,4},{9,5},... | collective-permute-start | bytes 245768 | tf_op jit(solution)/shard_map/ppermute | solution.py:287
  64.7 8.6 %collective-permute-start.23 = (bf16[32,1280]{1,0:T(8,128)(2,1)S(1)}, bf16[32,1280]{1,0:T(8,128)(2,1)S(1)}, u32[]{:S(2)}, u32[]{:S(2)}) collective-permute-start(bf16[32,1280]{1,0:T(8,128)(2,1)S(1)} %get-tuple-element.65), channel_id=1, source_target_pairs={{0,8},{1,9},{2,10},{3,11},{4,12},{5,13},{6,14},{7,15},{8,0},{9,1},... | collective-permute-start | bytes 245768 | tf_op jit(solution)/shard_map/ppermute | solution.py:287
  64.8 8.6 %collective-permute-start.24 = (bf16[32,1280]{1,0:T(8,128)(2,1)S(1)}, bf16[32,1280]{1,0:T(8,128)(2,1)S(1)}, u32[]{:S(2)}, u32[]{:S(2)}) collective-permute-start(bf16[32,1280]{1,0:T(8,128)(2,1)S(1)} %get-tuple-element.64), channel_id=1, source_target_pairs={{0,12},{1,13},{2,14},{3,15},{4,8},{5,9},{6,10},{7,11},{8,4},{9,5},... | collective-permute-start | bytes 245768 | tf_op jit(solution)/shard_map/ppermute | solution.py:287
  (3 other events, 16.7 us)

commit v15 on v14

--- a/solution.py
+++ b/solution.py
@@ -395,8 +395,11 @@
         step = 2
         while len(parts) > 1:
             got = [exchange(send, step) for send in parts[1::2]]
-            if i and step == 2:
-                got[0], blocks[2] = lax.optimization_barrier((got[0], blocks[2]))
+            if step == 2:
+                if i:
+                    got[0], blocks[2] = lax.optimization_barrier((got[0], blocks[2]))
+                else:
+                    got[0], *columns = lax.optimization_barrier((got[0], *columns))
             parts = [
                 (keep.astype(F32) + other.astype(F32)).astype(BF16)
                 for keep, other in zip(parts[::2], got)

time: 74.6 us -> 74.1 us (level)
  transfers between devices with their start and end apart: 25 -> 25, of which waited for: 13 -> 16; matrix products, arithmetic and copies ran while one was open for 2% -> 2% of each run, Pallas kernels for 6% -> 6%
where the time goes in v15:
time: 74.1 us; the launch traced here: 73.9 us
  waiting for transfers between devices  31 us (42%)
  starting transfers between devices  29.6 us (40%)
  Pallas kernels  11.2 us (15%)
  local copies, waits for them, and re-layouts  1.11 us (1%)
  between operations  0.82 us (1%)
    ppermute x25, waiting for transfers between devices, exchange(): return lax.ppermute(block, AXES, [(i, i ^ step) for i in range(count)])  31 us
    ppermute x25, starting transfers between devices, exchange(): return lax.ppermute(block, AXES, [(i, i ^ step) for i in range(count)])  29.6 us
    pallas_call x7, Pallas kernels, call(): pl.pallas_call(body, out_shape=shapes, in_specs=spaces, out_specs=[VMEM]...  11.2 us
  transfers between devices with their start and end apart: 25, of which 16 were waited for; matrix products, arithmetic and copies ran while one was open for 2% of the time, Pallas kernels for 6%

profile of v15, /device:TPU:0, one launch (start us, length us, event | category | flops | bytes accessed | tf_op | source)
XLA Modules:
  0.0 73.9 jit_solution(15347841297472031726)
XLA Ops:
  0.6 3.9 %shard_map.68 = (bf16[48,1408]{1,0:T(8,128)(2,1)}, bf16[48,1408]{1,0:T(8,128)(2,1)}, bf16[48,1408]{1,0:T(8,128)(2,1)}, bf16[48,1408]{1,0:T(8,128)(2,1)}, f32[16,48]{1,0:T(8,128)}) custom-call(bf16[48,3584]{1,0:T(8,128)(2,1)} %tokens.1, bf16[384,2560]{1,0:T(8,128)(2,1)} %bitcast.28, f32[32,2560]{1,0:T(8,128)} %bitcast.35, s32[8,48]{1,0:T(8,128)} %bitcast.37, ...), custom_call_target="tpu_custom_call" | custom-call | flops 1 | bytes 1 | tf_op jit(solution)/shard_map/pallas_call | solution.py:39
  5.1 2.7 %collective-permute-start.3 = (bf16[48,1408]{1,0:T(8,128)(2,1)}, bf16[48,1408]{1,0:T(8,128)(2,1)S(1)}, u32[]{:S(2)}, u32[]{:S(2)}) collective-permute-start(bf16[48,1408]{1,0:T(8,128)(2,1)} %get-tuple-element.41), channel_id=1, source_target_pairs={{0,4},{1,5},{2,6},{3,7},{4,0},{5,1},{6,2},{7,3},{8,12},{9,13},{10,... | collective-permute-start | bytes 405512 | tf_op jit(solution)/shard_map/ppermute | solution.py:287
  7.8 2.6 %collective-permute-start = (bf16[48,1408]{1,0:T(8,128)(2,1)}, bf16[48,1408]{1,0:T(8,128)(2,1)S(1)}, u32[]{:S(2)}, u32[]{:S(2)}) collective-permute-start(bf16[48,1408]{1,0:T(8,128)(2,1)} %get-tuple-element.38), channel_id=1, source_target_pairs={{0,8},{1,9},{2,10},{3,11},{4,12},{5,13},{6,14},{7,15},{8,0},{9,1},... | collective-permute-start | bytes 405512 | tf_op jit(solution)/shard_map/ppermute | solution.py:287
  11.3 3.2 %collective-permute-done.3 = bf16[48,1408]{1,0:T(8,128)(2,1)S(1)} collective-permute-done((bf16[48,1408]{1,0:T(8,128)(2,1)}, bf16[48,1408]{1,0:T(8,128)(2,1)S(1)}, u32[]{:S(2)}, u32[]{:S(2)}) %collective-permute-start.3) | collective-permute-done | bytes 135200 | tf_op jit(solution)/shard_map/ppermute | solution.py:287
  14.5 1.8 %collective-permute-start.4 = (bf16[96,1408]{1,0:T(8,128)(2,1)S(1)}, bf16[96,1408]{1,0:T(8,128)(2,1)S(1)}, u32[]{:S(2)}, u32[]{:S(2)}) collective-permute-start(bf16[96,1408]{1,0:T(8,128)(2,1)S(1)} %constant_dynamic-update-slice_fusion.2.refs_0_.near_x), channel_id=1, source_target_pairs={{0,2},{1,3},{2,0},{3,1},{4,6},{5,7},{6,4},{7,5},{8,10},{9,11},{10,... | collective-permute-start | bytes 811016 | tf_op jit(solution)/shard_map/ppermute | solution.py:287
  16.3 4.9 %collective-permute-done = bf16[48,1408]{1,0:T(8,128)(2,1)S(1)} collective-permute-done((bf16[48,1408]{1,0:T(8,128)(2,1)}, bf16[48,1408]{1,0:T(8,128)(2,1)S(1)}, u32[]{:S(2)}, u32[]{:S(2)}) %collective-permute-start) | collective-permute-done | bytes 135200 | tf_op jit(solution)/shard_map/ppermute | solution.py:287
  21.2 1.6 %collective-permute-start.2 = (bf16[96,1408]{1,0:T(8,128)(2,1)S(1)}, bf16[96,1408]{1,0:T(8,128)(2,1)S(1)}, u32[]{:S(2)}, u32[]{:S(2)}) collective-permute-start(bf16[96,1408]{1,0:T(8,128)(2,1)S(1)} %constant_dynamic-update-slice_fusion.refs_0_), channel_id=1, source_target_pairs={{0,2},{1,3},{2,0},{3,1},{4,6},{5,7},{6,4},{7,5},{8,10},{9,11},{10,... | collective-permute-start | bytes 811016 | tf_op jit(solution)/shard_map/ppermute | solution.py:287
  25.3 3.2 %collective-permute-done.2.refs_1_ = bf16[96,1408]{1,0:T(8,128)(2,1)S(1)} collective-permute-done((bf16[96,1408]{1,0:T(8,128)(2,1)S(1)}, bf16[96,1408]{1,0:T(8,128)(2,1)S(1)}, u32[]{:S(2)}, u32[]{:S(2)}) %collective-permute-start.2) | collective-permute-done | bytes 270368 | tf_op jit(solution)/shard_map/ppermute | solution.py:287
  31.3 4.2 %collective-permute-start.10 = (bf16[96,256]{1,0:T(8,128)(2,1)S(1)}, bf16[96,256]{1,0:T(8,128)(2,1)S(1)}, u32[]{:S(2)}, u32[]{:S(2)}) collective-permute-start(bf16[96,256]{1,0:T(8,128)(2,1)S(1)} %get-tuple-element.47), channel_id=1, source_target_pairs={{0,8},{1,9},{2,10},{3,11},{4,12},{5,13},{6,14},{7,15},{8,0},{9,1},... | collective-permute-start | bytes 147464 | tf_op jit(solution)/shard_map/ppermute | solution.py:287
  35.5 1.4 %collective-permute-start.11 = (bf16[96,256]{1,0:T(8,128)(2,1)S(1)}, bf16[96,256]{1,0:T(8,128)(2,1)S(1)}, u32[]{:S(2)}, u32[]{:S(2)}) collective-permute-start(bf16[96,256]{1,0:T(8,128)(2,1)S(1)} %get-tuple-element.48), channel_id=1, source_target_pairs={{0,12},{1,13},{2,14},{3,15},{4,8},{5,9},{6,10},{7,11},{8,4},{9,5},... | collective-permute-start | bytes 147464 | tf_op jit(solution)/shard_map/ppermute | solution.py:287
  39.1 2.4 %collective-permute-done.11.z3 = bf16[96,256]{1,0:T(8,128)(2,1)S(1)} collective-permute-done((bf16[96,256]{1,0:T(8,128)(2,1)S(1)}, bf16[96,256]{1,0:T(8,128)(2,1)S(1)}, u32[]{:S(2)}, u32[]{:S(2)}) %collective-permute-start.11) | collective-permute-done | bytes 49184 | tf_op jit(solution)/shard_map/ppermute | solution.py:287
  41.5 1.8 %shard_map.72 = (bf16[128,1280]{1,0:T(8,128)(2,1)S(1)}, bf16[128,1280]{1,0:T(8,128)(2,1)S(1)}, bf16[128,1280]{1,0:T(8,128)(2,1)S(1)}, bf16[128,1280]{1,0:T(8,128)(2,1)S(1)}) custom-call(bf16[96,256]{1,0:T(8,128)(2,1)S(1)} %get-tuple-element.45.z0, bf16[96,256]{1,0:T(8,128)(2,1)S(1)} %collective-permute-done.9.z1, ...), custom_call_target="tpu_custom_call" | custom-call | flops 1 | bytes 1 | tf_op jit(solution)/shard_map/pallas_call | solution.py:39
  43.3 1.6 %collective-permute-start.15 = (bf16[4,32,1280]{2,1,0:T(8,128)(2,1)S(1)}, bf16[4,32,1280]{2,1,0:T(8,128)(2,1)S(1)}, u32[]{:S(2)}, u32[]{:S(2)}) collective-permute-start(bf16[4,32,1280]{2,1,0:T(8,128)(2,1)S(1)} %bitcast.34), channel_id=1, source_target_pairs={{0,2},{1,3},{2,0},{3,1},{4,6},{5,7},{6,4},{7,5},{8,10},{9,11},{10,... | collective-permute-start | bytes 983048 | tf_op jit(solution)/shard_map/ppermute | solution.py:287
  45.1 2.4 %collective-permute-start.17 = (bf16[32,896]{1,0:T(8,128)(2,1)S(1)}, bf16[32,896]{1,0:T(8,128)(2,1)S(1)}, u32[]{:S(2)}, u32[]{:S(2)}) collective-permute-start(bf16[32,896]{1,0:T(8,128)(2,1)S(1)} %get-tuple-element.58), channel_id=1, source_target_pairs={{0,8},{1,9},{2,10},{3,11},{4,12},{5,13},{6,14},{7,15},{8,0},{9,1},... | collective-permute-start | bytes 172040 | tf_op jit(solution)/shard_map/ppermute | solution.py:287
  47.4 1.8 %collective-permute-start.18 = (bf16[32,896]{1,0:T(8,128)(2,1)S(1)}, bf16[32,896]{1,0:T(8,128)(2,1)S(1)}, u32[]{:S(2)}, u32[]{:S(2)}) collective-permute-start(bf16[32,896]{1,0:T(8,128)(2,1)S(1)} %get-tuple-element.59), channel_id=1, source_target_pairs={{0,12},{1,13},{2,14},{3,15},{4,8},{5,9},{6,10},{7,11},{8,4},{9,5},... | collective-permute-start | bytes 172040 | tf_op jit(solution)/shard_map/ppermute | solution.py:287
  50.1 3.3 %collective-permute-done.18.c3 = bf16[32,896]{1,0:T(8,128)(2,1)S(1)} collective-permute-done((bf16[32,896]{1,0:T(8,128)(2,1)S(1)}, bf16[32,896]{1,0:T(8,128)(2,1)S(1)}, u32[]{:S(2)}, u32[]{:S(2)}) %collective-permute-start.18) | collective-permute-done | bytes 57376 | tf_op jit(solution)/shard_map/ppermute | solution.py:287
  54.0 1.2 %collective-permute-start.19 = (bf16[32,1280]{1,0:T(8,128)(2,1)S(1)}, bf16[32,1280]{1,0:T(8,128)(2,1)S(1)}, u32[]{:S(2)}, u32[]{:S(2)}) collective-permute-start(bf16[32,1280]{1,0:T(8,128)(2,1)S(1)} %get-tuple-element.81), channel_id=1, source_target_pairs={{0,8},{1,9},{2,10},{3,11},{4,12},{5,13},{6,14},{7,15},{8,0},{9,1},... | collective-permute-start | bytes 245768 | tf_op jit(solution)/shard_map/ppermute | solution.py:287
  55.3 3.5 %collective-permute-done.14 = bf16[4,32,1280]{2,1,0:T(8,128)(2,1)S(1)} collective-permute-done((bf16[4,32,1280]{2,1,0:T(8,128)(2,1)S(1)}, bf16[4,32,1280]{2,1,0:T(8,128)(2,1)S(1)}, u32[]{:S(2)}, u32[]{:S(2)}) %collective-permute-start.14) | collective-permute-done | bytes 327712 | tf_op jit(solution)/shard_map/ppermute | solution.py:287
  58.7 1.4 %collective-permute-done.19.refs_2_ = bf16[32,1280]{1,0:T(8,128)(2,1)S(1)} collective-permute-done((bf16[32,1280]{1,0:T(8,128)(2,1)S(1)}, bf16[32,1280]{1,0:T(8,128)(2,1)S(1)}, u32[]{:S(2)}, u32[]{:S(2)}) %collective-permute-start.19) | collective-permute-done | bytes 81952 | tf_op jit(solution)/shard_map/ppermute | solution.py:287
  60.3 2.0 %collective-permute-start.21 = (bf16[32,1280]{1,0:T(8,128)(2,1)S(1)}, bf16[32,1280]{1,0:T(8,128)(2,1)S(1)}, u32[]{:S(2)}, u32[]{:S(2)}) collective-permute-start(bf16[32,1280]{1,0:T(8,128)(2,1)S(1)} %get-tuple-element.79), channel_id=1, source_target_pairs={{0,4},{1,5},{2,6},{3,7},{4,0},{5,1},{6,2},{7,3},{8,12},{9,13},{10,... | collective-permute-start | bytes 245768 | tf_op jit(solution)/shard_map/ppermute | solution.py:287
  62.3 2.3 %collective-permute-start.22 = (bf16[32,1280]{1,0:T(8,128)(2,1)S(1)}, bf16[32,1280]{1,0:T(8,128)(2,1)S(1)}, u32[]{:S(2)}, u32[]{:S(2)}) collective-permute-start(bf16[32,1280]{1,0:T(8,128)(2,1)S(1)} %get-tuple-element.78), channel_id=1, source_target_pairs={{0,12},{1,13},{2,14},{3,15},{4,8},{5,9},{6,10},{7,11},{8,4},{9,5},... | collective-permute-start | bytes 245768 | tf_op jit(solution)/shard_map/ppermute | solution.py:287
  64.6 1.6 %collective-permute-start.24 = (bf16[32,1280]{1,0:T(8,128)(2,1)S(1)}, bf16[32,1280]{1,0:T(8,128)(2,1)S(1)}, u32[]{:S(2)}, u32[]{:S(2)}) collective-permute-start(bf16[32,1280]{1,0:T(8,128)(2,1)S(1)} %get-tuple-element.74), channel_id=1, source_target_pairs={{0,12},{1,13},{2,14},{3,15},{4,8},{5,9},{6,10},{7,11},{8,4},{9,5},... | collective-permute-start | bytes 245768 | tf_op jit(solution)/shard_map/ppermute | solution.py:287
  66.2 2.7 %shard_map.73 = (f32[32,32]{1,0:T(8,128)S(1)}, f32[32,3584]{1,0:T(8,128)}) custom-call(bf16[32,896]{1,0:T(8,128)(2,1)S(1)} %get-tuple-element.66.c0, bf16[32,896]{1,0:T(8,128)(2,1)S(1)} %collective-permute-done.16.c1, bf16[32,896]{1,0:T(8,128)(2,1)S(1)} %collective-permute-done.17.c2, bf16[32,896]{1,0:T(8,128)(2,1)S(1)} %collective-permute-done.18.c3), custom_call_target="tpu_custom_call" | custom-call | flops 1 | bytes 1 | tf_op jit(solution)/shard_map/pallas_call | solution.py:39
  68.9 4.0 %collective-permute-done.23.refs_6_ = bf16[32,1280]{1,0:T(8,128)(2,1)S(1)} collective-permute-done((bf16[32,1280]{1,0:T(8,128)(2,1)S(1)}, bf16[32,1280]{1,0:T(8,128)(2,1)S(1)}, u32[]{:S(2)}, u32[]{:S(2)}) %collective-permute-start.23) | collective-permute-done | bytes 81952 | tf_op jit(solution)/shard_map/ppermute | solution.py:287
  (49 shorter events, 11.9 us)
Async XLA Ops:
  4.6 36.9 %collective-permute-start.13 = (bf16[384,2560]{1,0:T(8,128)(2,1)S(1)}, bf16[384,2560]{1,0:T(8,128)(2,1)S(1)}, u32[]{:S(2)}, u32[]{:S(2)}) collective-permute-start(bf16[384,2560]{1,0:T(8,128)(2,1)S(1)} %bitcast.29), channel_id=1, source_target_pairs={{0,1},{1,0},{2,3},{3,2},{4,5},{5,4},{6,7},{7,6},{8,9},{9,8},{10,11... | collective-permute-start | bytes 5898248 | tf_op jit(solution)/shard_map/ppermute | solution.py:287
  5.1 9.4 %collective-permute-start.3 = (bf16[48,1408]{1,0:T(8,128)(2,1)}, bf16[48,1408]{1,0:T(8,128)(2,1)S(1)}, u32[]{:S(2)}, u32[]{:S(2)}) collective-permute-start(bf16[48,1408]{1,0:T(8,128)(2,1)} %get-tuple-element.41), channel_id=1, source_target_pairs={{0,4},{1,5},{2,6},{3,7},{4,0},{5,1},{6,2},{7,3},{8,12},{9,13},{10,... | collective-permute-start | bytes 405512 | tf_op jit(solution)/shard_map/ppermute | solution.py:287
  7.8 13.4 %collective-permute-start = (bf16[48,1408]{1,0:T(8,128)(2,1)}, bf16[48,1408]{1,0:T(8,128)(2,1)S(1)}, u32[]{:S(2)}, u32[]{:S(2)}) collective-permute-start(bf16[48,1408]{1,0:T(8,128)(2,1)} %get-tuple-element.38), channel_id=1, source_target_pairs={{0,8},{1,9},{2,10},{3,11},{4,12},{5,13},{6,14},{7,15},{8,0},{9,1},... | collective-permute-start | bytes 405512 | tf_op jit(solution)/shard_map/ppermute | solution.py:287
  10.3 10.8 %collective-permute-start.1 = (bf16[48,1408]{1,0:T(8,128)(2,1)}, bf16[48,1408]{1,0:T(8,128)(2,1)S(1)}, u32[]{:S(2)}, u32[]{:S(2)}) collective-permute-start(bf16[48,1408]{1,0:T(8,128)(2,1)} %get-tuple-element.39), channel_id=1, source_target_pairs={{0,12},{1,13},{2,14},{3,15},{4,8},{5,9},{6,10},{7,11},{8,4},{9,5},... | collective-permute-start | bytes 405512 | tf_op jit(solution)/shard_map/ppermute | solution.py:287
  14.5 8.4 %collective-permute-start.4 = (bf16[96,1408]{1,0:T(8,128)(2,1)S(1)}, bf16[96,1408]{1,0:T(8,128)(2,1)S(1)}, u32[]{:S(2)}, u32[]{:S(2)}) collective-permute-start(bf16[96,1408]{1,0:T(8,128)(2,1)S(1)} %constant_dynamic-update-slice_fusion.2.refs_0_.near_x), channel_id=1, source_target_pairs={{0,2},{1,3},{2,0},{3,1},{4,6},{5,7},{6,4},{7,5},{8,10},{9,11},{10,... | collective-permute-start | bytes 811016 | tf_op jit(solution)/shard_map/ppermute | solution.py:287
  21.2 7.3 %collective-permute-start.2 = (bf16[96,1408]{1,0:T(8,128)(2,1)S(1)}, bf16[96,1408]{1,0:T(8,128)(2,1)S(1)}, u32[]{:S(2)}, u32[]{:S(2)}) collective-permute-start(bf16[96,1408]{1,0:T(8,128)(2,1)S(1)} %constant_dynamic-update-slice_fusion.refs_0_), channel_id=1, source_target_pairs={{0,2},{1,3},{2,0},{3,1},{4,6},{5,7},{6,4},{7,5},{8,10},{9,11},{10,... | collective-permute-start | bytes 811016 | tf_op jit(solution)/shard_map/ppermute | solution.py:287
  22.8 1.5 %collective-permute-start.5 = (bf16[96,1152]{1,0:T(8,128)(2,1)S(1)}, bf16[96,1152]{1,0:T(8,128)(2,1)S(1)}, u32[]{:S(2)}, u32[]{:S(2)}) collective-permute-start(bf16[96,1152]{1,0:T(8,128)(2,1)S(1)} %slice.16), channel_id=1, source_target_pairs={{0,1},{1,0},{2,3},{3,2},{4,5},{5,4},{6,7},{7,6},{8,9},{9,8},{10,11... | collective-permute-start | bytes 663560 | tf_op jit(solution)/shard_map/ppermute | solution.py:287
  22.9 1.7 %collective-permute-start.6 = (bf16[96,1152]{1,0:T(8,128)(2,1)S(1)}, bf16[96,1152]{1,0:T(8,128)(2,1)S(1)}, u32[]{:S(2)}, u32[]{:S(2)}) collective-permute-start(bf16[96,1152]{1,0:T(8,128)(2,1)S(1)} %slice.17), channel_id=1, source_target_pairs={{0,1},{1,0},{2,3},{3,2},{4,5},{5,4},{6,7},{7,6},{8,9},{9,8},{10,11... | collective-permute-start | bytes 663560 | tf_op jit(solution)/shard_map/ppermute | solution.py:287
  28.5 1.5 %collective-permute-start.7 = (bf16[96,1152]{1,0:T(8,128)(2,1)S(1)}, bf16[96,1152]{1,0:T(8,128)(2,1)S(1)}, u32[]{:S(2)}, u32[]{:S(2)}) collective-permute-start(bf16[96,1152]{1,0:T(8,128)(2,1)S(1)} %slice.14), channel_id=1, source_target_pairs={{0,1},{1,0},{2,3},{3,2},{4,5},{5,4},{6,7},{7,6},{8,9},{9,8},{10,11... | collective-permute-start | bytes 663560 | tf_op jit(solution)/shard_map/ppermute | solution.py:287
  28.6 1.8 %collective-permute-start.8 = (bf16[96,1152]{1,0:T(8,128)(2,1)S(1)}, bf16[96,1152]{1,0:T(8,128)(2,1)S(1)}, u32[]{:S(2)}, u32[]{:S(2)}) collective-permute-start(bf16[96,1152]{1,0:T(8,128)(2,1)S(1)} %slice.15), channel_id=1, source_target_pairs={{0,1},{1,0},{2,3},{3,2},{4,5},{5,4},{6,7},{7,6},{8,9},{9,8},{10,11... | collective-permute-start | bytes 663560 | tf_op jit(solution)/shard_map/ppermute | solution.py:287
  31.3 7.8 %collective-permute-start.10 = (bf16[96,256]{1,0:T(8,128)(2,1)S(1)}, bf16[96,256]{1,0:T(8,128)(2,1)S(1)}, u32[]{:S(2)}, u32[]{:S(2)}) collective-permute-start(bf16[96,256]{1,0:T(8,128)(2,1)S(1)} %get-tuple-element.47), channel_id=1, source_target_pairs={{0,8},{1,9},{2,10},{3,11},{4,12},{5,13},{6,14},{7,15},{8,0},{9,1},... | collective-permute-start | bytes 147464 | tf_op jit(solution)/shard_map/ppermute | solution.py:287
  35.5 6.0 %collective-permute-start.11 = (bf16[96,256]{1,0:T(8,128)(2,1)S(1)}, bf16[96,256]{1,0:T(8,128)(2,1)S(1)}, u32[]{:S(2)}, u32[]{:S(2)}) collective-permute-start(bf16[96,256]{1,0:T(8,128)(2,1)S(1)} %get-tuple-element.48), channel_id=1, source_target_pairs={{0,12},{1,13},{2,14},{3,15},{4,8},{5,9},{6,10},{7,11},{8,4},{9,5},... | collective-permute-start | bytes 147464 | tf_op jit(solution)/shard_map/ppermute | solution.py:287
  36.9 4.6 %collective-permute-start.9 = (bf16[96,256]{1,0:T(8,128)(2,1)S(1)}, bf16[96,256]{1,0:T(8,128)(2,1)S(1)}, u32[]{:S(2)}, u32[]{:S(2)}) collective-permute-start(bf16[96,256]{1,0:T(8,128)(2,1)S(1)} %get-tuple-element.46), channel_id=1, source_target_pairs={{0,4},{1,5},{2,6},{3,7},{4,0},{5,1},{6,2},{7,3},{8,12},{9,13},{10,... | collective-permute-start | bytes 147464 | tf_op jit(solution)/shard_map/ppermute | solution.py:287
  43.3 10.6 %collective-permute-start.15 = (bf16[4,32,1280]{2,1,0:T(8,128)(2,1)S(1)}, bf16[4,32,1280]{2,1,0:T(8,128)(2,1)S(1)}, u32[]{:S(2)}, u32[]{:S(2)}) collective-permute-start(bf16[4,32,1280]{2,1,0:T(8,128)(2,1)S(1)} %bitcast.34), channel_id=1, source_target_pairs={{0,2},{1,3},{2,0},{3,1},{4,6},{5,7},{6,4},{7,5},{8,10},{9,11},{10,... | collective-permute-start | bytes 983048 | tf_op jit(solution)/shard_map/ppermute | solution.py:287
  44.8 4.9 %collective-permute-start.16 = (bf16[32,896]{1,0:T(8,128)(2,1)S(1)}, bf16[32,896]{1,0:T(8,128)(2,1)S(1)}, u32[]{:S(2)}, u32[]{:S(2)}) collective-permute-start(bf16[32,896]{1,0:T(8,128)(2,1)S(1)} %get-tuple-element.57), channel_id=1, source_target_pairs={{0,4},{1,5},{2,6},{3,7},{4,0},{5,1},{6,2},{7,3},{8,12},{9,13},{10,... | collective-permute-start | bytes 172040 | tf_op jit(solution)/shard_map/ppermute | solution.py:287
  45.1 5.1 %collective-permute-start.17 = (bf16[32,896]{1,0:T(8,128)(2,1)S(1)}, bf16[32,896]{1,0:T(8,128)(2,1)S(1)}, u32[]{:S(2)}, u32[]{:S(2)}) collective-permute-start(bf16[32,896]{1,0:T(8,128)(2,1)S(1)} %get-tuple-element.58), channel_id=1, source_target_pairs={{0,8},{1,9},{2,10},{3,11},{4,12},{5,13},{6,14},{7,15},{8,0},{9,1},... | collective-permute-start | bytes 172040 | tf_op jit(solution)/shard_map/ppermute | solution.py:287
  47.4 6.0 %collective-permute-start.18 = (bf16[32,896]{1,0:T(8,128)(2,1)S(1)}, bf16[32,896]{1,0:T(8,128)(2,1)S(1)}, u32[]{:S(2)}, u32[]{:S(2)}) collective-permute-start(bf16[32,896]{1,0:T(8,128)(2,1)S(1)} %get-tuple-element.59), channel_id=1, source_target_pairs={{0,12},{1,13},{2,14},{3,15},{4,8},{5,9},{6,10},{7,11},{8,4},{9,5},... | collective-permute-start | bytes 172040 | tf_op jit(solution)/shard_map/ppermute | solution.py:287
  49.2 9.5 %collective-permute-start.14 = (bf16[4,32,1280]{2,1,0:T(8,128)(2,1)S(1)}, bf16[4,32,1280]{2,1,0:T(8,128)(2,1)S(1)}, u32[]{:S(2)}, u32[]{:S(2)}) collective-permute-start(bf16[4,32,1280]{2,1,0:T(8,128)(2,1)S(1)} %bitcast.33), channel_id=1, source_target_pairs={{0,2},{1,3},{2,0},{3,1},{4,6},{5,7},{6,4},{7,5},{8,10},{9,11},{10,... | collective-permute-start | bytes 983048 | tf_op jit(solution)/shard_map/ppermute | solution.py:287
  54.0 6.1 %collective-permute-start.19 = (bf16[32,1280]{1,0:T(8,128)(2,1)S(1)}, bf16[32,1280]{1,0:T(8,128)(2,1)S(1)}, u32[]{:S(2)}, u32[]{:S(2)}) collective-permute-start(bf16[32,1280]{1,0:T(8,128)(2,1)S(1)} %get-tuple-element.81), channel_id=1, source_target_pairs={{0,8},{1,9},{2,10},{3,11},{4,12},{5,13},{6,14},{7,15},{8,0},{9,1},... | collective-permute-start | bytes 245768 | tf_op jit(solution)/shard_map/ppermute | solution.py:287
  60.2 5.9 %collective-permute-start.20 = (bf16[32,1280]{1,0:T(8,128)(2,1)S(1)}, bf16[32,1280]{1,0:T(8,128)(2,1)S(1)}, u32[]{:S(2)}, u32[]{:S(2)}) collective-permute-start(bf16[32,1280]{1,0:T(8,128)(2,1)S(1)} %get-tuple-element.77), channel_id=1, source_target_pairs={{0,4},{1,5},{2,6},{3,7},{4,0},{5,1},{6,2},{7,3},{8,12},{9,13},{10,... | collective-permute-start | bytes 245768 | tf_op jit(solution)/shard_map/ppermute | solution.py:287
  60.3 8.6 %collective-permute-start.21 = (bf16[32,1280]{1,0:T(8,128)(2,1)S(1)}, bf16[32,1280]{1,0:T(8,128)(2,1)S(1)}, u32[]{:S(2)}, u32[]{:S(2)}) collective-permute-start(bf16[32,1280]{1,0:T(8,128)(2,1)S(1)} %get-tuple-element.79), channel_id=1, source_target_pairs={{0,4},{1,5},{2,6},{3,7},{4,0},{5,1},{6,2},{7,3},{8,12},{9,13},{10,... | collective-permute-start | bytes 245768 | tf_op jit(solution)/shard_map/ppermute | solution.py:287
  62.3 6.6 %collective-permute-start.22 = (bf16[32,1280]{1,0:T(8,128)(2,1)S(1)}, bf16[32,1280]{1,0:T(8,128)(2,1)S(1)}, u32[]{:S(2)}, u32[]{:S(2)}) collective-permute-start(bf16[32,1280]{1,0:T(8,128)(2,1)S(1)} %get-tuple-element.78), channel_id=1, source_target_pairs={{0,12},{1,13},{2,14},{3,15},{4,8},{5,9},{6,10},{7,11},{8,4},{9,5},... | collective-permute-start | bytes 245768 | tf_op jit(solution)/shard_map/ppermute | solution.py:287
  64.6 8.2 %collective-permute-start.23 = (bf16[32,1280]{1,0:T(8,128)(2,1)S(1)}, bf16[32,1280]{1,0:T(8,128)(2,1)S(1)}, u32[]{:S(2)}, u32[]{:S(2)}) collective-permute-start(bf16[32,1280]{1,0:T(8,128)(2,1)S(1)} %get-tuple-element.75), channel_id=1, source_target_pairs={{0,8},{1,9},{2,10},{3,11},{4,12},{5,13},{6,14},{7,15},{8,0},{9,1},... | collective-permute-start | bytes 245768 | tf_op jit(solution)/shard_map/ppermute | solution.py:287
  64.6 8.2 %collective-permute-start.24 = (bf16[32,1280]{1,0:T(8,128)(2,1)S(1)}, bf16[32,1280]{1,0:T(8,128)(2,1)S(1)}, u32[]{:S(2)}, u32[]{:S(2)}) collective-permute-start(bf16[32,1280]{1,0:T(8,128)(2,1)S(1)} %get-tuple-element.74), channel_id=1, source_target_pairs={{0,12},{1,13},{2,14},{3,15},{4,8},{5,9},{6,10},{7,11},{8,4},{9,5},... | collective-permute-start | bytes 245768 | tf_op jit(solution)/shard_map/ppermute | solution.py:287
  (3 other events, 16.7 us)

commit v16 on v14

--- a/solution.py
+++ b/solution.py
@@ -395,8 +395,8 @@
         step = 2
         while len(parts) > 1:
             got = [exchange(send, step) for send in parts[1::2]]
-            if i and step == 2:
-                got[0], blocks[2] = lax.optimization_barrier((got[0], blocks[2]))
+            if i == 0 and step == 2:
+                got[0], *columns = lax.optimization_barrier((got[0], *columns))
             parts = [
                 (keep.astype(F32) + other.astype(F32)).astype(BF16)
                 for keep, other in zip(parts[::2], got)

time: 74.6 us -> 77.9 us (1.044)
  waiting for transfers between devices: 31.5 us -> 34 us
  starting transfers between devices: 29.5 us -> 30.4 us
    ppermute x25, waiting for transfers between devices: 31.5 us -> 34 us  [exchange(): return lax.ppermute(block, AXES, [(i, i ^ step) for i in range(count)])]
    ppermute x25, starting transfers between devices: 29.5 us -> 30.4 us  [exchange(): return lax.ppermute(block, AXES, [(i, i ^ step) for i in range(count)])]
  transfers between devices with their start and end apart: 25 -> 25, of which waited for: 13 -> 15; matrix products, arithmetic and copies ran while one was open for 2% -> 1% of each run, Pallas kernels for 6% -> 6%
where the time goes in v16:
time: 77.9 us; the launch traced here: 77.7 us
  waiting for transfers between devices  34 us (44%)
  starting transfers between devices  30.4 us (39%)
  Pallas kernels  11.2 us (14%)
  local copies, waits for them, and re-layouts  1.11 us (1%)
  between operations  0.81 us (1%)
    ppermute x25, waiting for transfers between devices, exchange(): return lax.ppermute(block, AXES, [(i, i ^ step) for i in range(count)])  34 us
    ppermute x25, starting transfers between devices, exchange(): return lax.ppermute(block, AXES, [(i, i ^ step) for i in range(count)])  30.4 us
    pallas_call x7, Pallas kernels, call(): pl.pallas_call(body, out_shape=shapes, in_specs=spaces, out_specs=[VMEM]...  11.2 us
  transfers between devices with their start and end apart: 25, of which 15 were waited for; matrix products, arithmetic and copies ran while one was open for 1% of the time, Pallas kernels for 6%

profile of v16, /device:TPU:0, one launch (start us, length us, event | category | flops | bytes accessed | tf_op | source)
XLA Modules:
  0.0 77.7 jit_solution(14056240512361758739)
XLA Ops:
  0.6 3.9 %shard_map.68 = (bf16[48,1408]{1,0:T(8,128)(2,1)}, bf16[48,1408]{1,0:T(8,128)(2,1)}, bf16[48,1408]{1,0:T(8,128)(2,1)}, bf16[48,1408]{1,0:T(8,128)(2,1)}, f32[16,48]{1,0:T(8,128)}) custom-call(bf16[48,3584]{1,0:T(8,128)(2,1)} %tokens.1, bf16[384,2560]{1,0:T(8,128)(2,1)} %bitcast.28, f32[32,2560]{1,0:T(8,128)} %bitcast.35, s32[8,48]{1,0:T(8,128)} %bitcast.37, ...), custom_call_target="tpu_custom_call" | custom-call | flops 1 | bytes 1 | tf_op jit(solution)/shard_map/pallas_call | solution.py:39
  5.1 2.7 %collective-permute-start.3 = (bf16[48,1408]{1,0:T(8,128)(2,1)}, bf16[48,1408]{1,0:T(8,128)(2,1)S(1)}, u32[]{:S(2)}, u32[]{:S(2)}) collective-permute-start(bf16[48,1408]{1,0:T(8,128)(2,1)} %get-tuple-element.39), channel_id=1, source_target_pairs={{0,4},{1,5},{2,6},{3,7},{4,0},{5,1},{6,2},{7,3},{8,12},{9,13},{10,... | collective-permute-start | bytes 405512 | tf_op jit(solution)/shard_map/ppermute | solution.py:287
  7.8 2.6 %collective-permute-start = (bf16[48,1408]{1,0:T(8,128)(2,1)}, bf16[48,1408]{1,0:T(8,128)(2,1)S(1)}, u32[]{:S(2)}, u32[]{:S(2)}) collective-permute-start(bf16[48,1408]{1,0:T(8,128)(2,1)} %get-tuple-element.36), channel_id=1, source_target_pairs={{0,8},{1,9},{2,10},{3,11},{4,12},{5,13},{6,14},{7,15},{8,0},{9,1},... | collective-permute-start | bytes 405512 | tf_op jit(solution)/shard_map/ppermute | solution.py:287
  11.3 3.2 %collective-permute-done.3 = bf16[48,1408]{1,0:T(8,128)(2,1)S(1)} collective-permute-done((bf16[48,1408]{1,0:T(8,128)(2,1)}, bf16[48,1408]{1,0:T(8,128)(2,1)S(1)}, u32[]{:S(2)}, u32[]{:S(2)}) %collective-permute-start.3) | collective-permute-done | bytes 135200 | tf_op jit(solution)/shard_map/ppermute | solution.py:287
  14.5 1.8 %collective-permute-start.4 = (bf16[96,1408]{1,0:T(8,128)(2,1)S(1)}, bf16[96,1408]{1,0:T(8,128)(2,1)S(1)}, u32[]{:S(2)}, u32[]{:S(2)}) collective-permute-start(bf16[96,1408]{1,0:T(8,128)(2,1)S(1)} %constant_dynamic-update-slice_fusion.2.refs_0_.near_x), channel_id=1, source_target_pairs={{0,2},{1,3},{2,0},{3,1},{4,6},{5,7},{6,4},{7,5},{8,10},{9,11},{10,... | collective-permute-start | bytes 811016 | tf_op jit(solution)/shard_map/ppermute | solution.py:287
  16.3 4.9 %collective-permute-done = bf16[48,1408]{1,0:T(8,128)(2,1)S(1)} collective-permute-done((bf16[48,1408]{1,0:T(8,128)(2,1)}, bf16[48,1408]{1,0:T(8,128)(2,1)S(1)}, u32[]{:S(2)}, u32[]{:S(2)}) %collective-permute-start) | collective-permute-done | bytes 135200 | tf_op jit(solution)/shard_map/ppermute | solution.py:287
  21.2 1.6 %collective-permute-start.2 = (bf16[96,1408]{1,0:T(8,128)(2,1)S(1)}, bf16[96,1408]{1,0:T(8,128)(2,1)S(1)}, u32[]{:S(2)}, u32[]{:S(2)}) collective-permute-start(bf16[96,1408]{1,0:T(8,128)(2,1)S(1)} %constant_dynamic-update-slice_fusion.refs_0_), channel_id=1, source_target_pairs={{0,2},{1,3},{2,0},{3,1},{4,6},{5,7},{6,4},{7,5},{8,10},{9,11},{10,... | collective-permute-start | bytes 811016 | tf_op jit(solution)/shard_map/ppermute | solution.py:287
  25.3 3.2 %collective-permute-done.2.refs_1_ = bf16[96,1408]{1,0:T(8,128)(2,1)S(1)} collective-permute-done((bf16[96,1408]{1,0:T(8,128)(2,1)S(1)}, bf16[96,1408]{1,0:T(8,128)(2,1)S(1)}, u32[]{:S(2)}, u32[]{:S(2)}) %collective-permute-start.2) | collective-permute-done | bytes 270368 | tf_op jit(solution)/shard_map/ppermute | solution.py:287
  31.3 4.2 %collective-permute-start.10 = (bf16[96,256]{1,0:T(8,128)(2,1)S(1)}, bf16[96,256]{1,0:T(8,128)(2,1)S(1)}, u32[]{:S(2)}, u32[]{:S(2)}) collective-permute-start(bf16[96,256]{1,0:T(8,128)(2,1)S(1)} %get-tuple-element.45), channel_id=1, source_target_pairs={{0,8},{1,9},{2,10},{3,11},{4,12},{5,13},{6,14},{7,15},{8,0},{9,1},... | collective-permute-start | bytes 147464 | tf_op jit(solution)/shard_map/ppermute | solution.py:287
  35.5 1.4 %collective-permute-start.11 = (bf16[96,256]{1,0:T(8,128)(2,1)S(1)}, bf16[96,256]{1,0:T(8,128)(2,1)S(1)}, u32[]{:S(2)}, u32[]{:S(2)}) collective-permute-start(bf16[96,256]{1,0:T(8,128)(2,1)S(1)} %get-tuple-element.46), channel_id=1, source_target_pairs={{0,12},{1,13},{2,14},{3,15},{4,8},{5,9},{6,10},{7,11},{8,4},{9,5},... | collective-permute-start | bytes 147464 | tf_op jit(solution)/shard_map/ppermute | solution.py:287
  39.1 2.4 %collective-permute-done.11.z3 = bf16[96,256]{1,0:T(8,128)(2,1)S(1)} collective-permute-done((bf16[96,256]{1,0:T(8,128)(2,1)S(1)}, bf16[96,256]{1,0:T(8,128)(2,1)S(1)}, u32[]{:S(2)}, u32[]{:S(2)}) %collective-permute-start.11) | collective-permute-done | bytes 49184 | tf_op jit(solution)/shard_map/ppermute | solution.py:287
  41.5 1.8 %shard_map.72 = (bf16[128,1280]{1,0:T(8,128)(2,1)S(1)}, bf16[128,1280]{1,0:T(8,128)(2,1)S(1)}, bf16[128,1280]{1,0:T(8,128)(2,1)S(1)}, bf16[128,1280]{1,0:T(8,128)(2,1)S(1)}) custom-call(bf16[96,256]{1,0:T(8,128)(2,1)S(1)} %get-tuple-element.43.z0, bf16[96,256]{1,0:T(8,128)(2,1)S(1)} %collective-permute-done.9.z1, ...), custom_call_target="tpu_custom_call" | custom-call | flops 1 | bytes 1 | tf_op jit(solution)/shard_map/pallas_call | solution.py:39
  43.3 1.6 %collective-permute-start.16 = (bf16[4,32,1280]{2,1,0:T(8,128)(2,1)S(1)}, bf16[4,32,1280]{2,1,0:T(8,128)(2,1)S(1)}, u32[]{:S(2)}, u32[]{:S(2)}) collective-permute-start(bf16[4,32,1280]{2,1,0:T(8,128)(2,1)S(1)} %bitcast.34), channel_id=1, source_target_pairs={{0,2},{1,3},{2,0},{3,1},{4,6},{5,7},{6,4},{7,5},{8,10},{9,11},{10,... | collective-permute-start | bytes 983048 | tf_op jit(solution)/shard_map/ppermute | solution.py:287
  45.6 2.4 %collective-permute-start.18 = (bf16[32,896]{1,0:T(8,128)(2,1)S(1)}, bf16[32,896]{1,0:T(8,128)(2,1)S(1)}, u32[]{:S(2)}, u32[]{:S(2)}) collective-permute-start(bf16[32,896]{1,0:T(8,128)(2,1)S(1)} %get-tuple-element.55), channel_id=1, source_target_pairs={{0,8},{1,9},{2,10},{3,11},{4,12},{5,13},{6,14},{7,15},{8,0},{9,1},... | collective-permute-start | bytes 172040 | tf_op jit(solution)/shard_map/ppermute | solution.py:287
  48.0 1.8 %collective-permute-start.19 = (bf16[32,896]{1,0:T(8,128)(2,1)S(1)}, bf16[32,896]{1,0:T(8,128)(2,1)S(1)}, u32[]{:S(2)}, u32[]{:S(2)}) collective-permute-start(bf16[32,896]{1,0:T(8,128)(2,1)S(1)} %get-tuple-element.56), channel_id=1, source_target_pairs={{0,12},{1,13},{2,14},{3,15},{4,8},{5,9},{6,10},{7,11},{8,4},{9,5},... | collective-permute-start | bytes 172040 | tf_op jit(solution)/shard_map/ppermute | solution.py:287
  50.7 3.3 %collective-permute-done.19.c3 = bf16[32,896]{1,0:T(8,128)(2,1)S(1)} collective-permute-done((bf16[32,896]{1,0:T(8,128)(2,1)S(1)}, bf16[32,896]{1,0:T(8,128)(2,1)S(1)}, u32[]{:S(2)}, u32[]{:S(2)}) %collective-permute-start.19) | collective-permute-done | bytes 57376 | tf_op jit(solution)/shard_map/ppermute | solution.py:287
  54.0 4.8 %collective-permute-done.14 = bf16[4,32,1280]{2,1,0:T(8,128)(2,1)S(1)} collective-permute-done((bf16[4,32,1280]{2,1,0:T(8,128)(2,1)S(1)}, bf16[4,32,1280]{2,1,0:T(8,128)(2,1)S(1)}, u32[]{:S(2)}, u32[]{:S(2)}) %collective-permute-start.14) | collective-permute-done | bytes 327712 | tf_op jit(solution)/shard_map/ppermute | solution.py:287
  59.5 1.6 %collective-permute-start.20 = (bf16[32,1280]{1,0:T(8,128)(2,1)S(1)}, bf16[32,1280]{1,0:T(8,128)(2,1)S(1)}, u32[]{:S(2)}, u32[]{:S(2)}) collective-permute-start(bf16[32,1280]{1,0:T(8,128)(2,1)S(1)} %get-tuple-element.76), channel_id=1, source_target_pairs={{0,4},{1,5},{2,6},{3,7},{4,0},{5,1},{6,2},{7,3},{8,12},{9,13},{10,... | collective-permute-start | bytes 245768 | tf_op jit(solution)/shard_map/ppermute | solution.py:287
  61.1 1.5 %collective-permute-start.21 = (bf16[32,1280]{1,0:T(8,128)(2,1)S(1)}, bf16[32,1280]{1,0:T(8,128)(2,1)S(1)}, u32[]{:S(2)}, u32[]{:S(2)}) collective-permute-start(bf16[32,1280]{1,0:T(8,128)(2,1)S(1)} %get-tuple-element.75), channel_id=1, source_target_pairs={{0,8},{1,9},{2,10},{3,11},{4,12},{5,13},{6,14},{7,15},{8,0},{9,1},... | collective-permute-start | bytes 245768 | tf_op jit(solution)/shard_map/ppermute | solution.py:287
  62.6 1.4 %collective-permute-start.22 = (bf16[32,1280]{1,0:T(8,128)(2,1)S(1)}, bf16[32,1280]{1,0:T(8,128)(2,1)S(1)}, u32[]{:S(2)}, u32[]{:S(2)}) collective-permute-start(bf16[32,1280]{1,0:T(8,128)(2,1)S(1)} %get-tuple-element.74), channel_id=1, source_target_pairs={{0,12},{1,13},{2,14},{3,15},{4,8},{5,9},{6,10},{7,11},{8,4},{9,5},... | collective-permute-start | bytes 245768 | tf_op jit(solution)/shard_map/ppermute | solution.py:287
  64.0 2.0 %collective-permute-start.23 = (bf16[32,1280]{1,0:T(8,128)(2,1)S(1)}, bf16[32,1280]{1,0:T(8,128)(2,1)S(1)}, u32[]{:S(2)}, u32[]{:S(2)}) collective-permute-start(bf16[32,1280]{1,0:T(8,128)(2,1)S(1)} %get-tuple-element.71), channel_id=1, source_target_pairs={{0,8},{1,9},{2,10},{3,11},{4,12},{5,13},{6,14},{7,15},{8,0},{9,1},... | collective-permute-start | bytes 245768 | tf_op jit(solution)/shard_map/ppermute | solution.py:287
  67.0 2.7 %shard_map.73 = (f32[32,32]{1,0:T(8,128)S(1)}, f32[32,3584]{1,0:T(8,128)}) custom-call(bf16[32,896]{1,0:T(8,128)(2,1)S(1)} %get-tuple-element.61.c0, bf16[32,896]{1,0:T(8,128)(2,1)S(1)} %collective-permute-done.17.c1, bf16[32,896]{1,0:T(8,128)(2,1)S(1)} %collective-permute-done.18.c2, bf16[32,896]{1,0:T(8,128)(2,1)S(1)} %collective-permute-done.19.c3), custom_call_target="tpu_custom_call" | custom-call | flops 1 | bytes 1 | tf_op jit(solution)/shard_map/pallas_call | solution.py:39
  69.7 3.8 %collective-permute-done.21.refs_2_ = bf16[32,1280]{1,0:T(8,128)(2,1)S(1)} collective-permute-done((bf16[32,1280]{1,0:T(8,128)(2,1)S(1)}, bf16[32,1280]{1,0:T(8,128)(2,1)S(1)}, u32[]{:S(2)}, u32[]{:S(2)}) %collective-permute-start.21) | collective-permute-done | bytes 81952 | tf_op jit(solution)/shard_map/ppermute | solution.py:287
  73.6 3.1 %collective-permute-done.23.refs_6_ = bf16[32,1280]{1,0:T(8,128)(2,1)S(1)} collective-permute-done((bf16[32,1280]{1,0:T(8,128)(2,1)S(1)}, bf16[32,1280]{1,0:T(8,128)(2,1)S(1)}, u32[]{:S(2)}, u32[]{:S(2)}) %collective-permute-start.23) | collective-permute-done | bytes 81952 | tf_op jit(solution)/shard_map/ppermute | solution.py:287
  (49 shorter events, 13.5 us)
Async XLA Ops:
  4.6 36.9 %collective-permute-start.13 = (bf16[384,2560]{1,0:T(8,128)(2,1)S(1)}, bf16[384,2560]{1,0:T(8,128)(2,1)S(1)}, u32[]{:S(2)}, u32[]{:S(2)}) collective-permute-start(bf16[384,2560]{1,0:T(8,128)(2,1)S(1)} %bitcast.29), channel_id=1, source_target_pairs={{0,1},{1,0},{2,3},{3,2},{4,5},{5,4},{6,7},{7,6},{8,9},{9,8},{10,11... | collective-permute-start | bytes 5898248 | tf_op jit(solution)/shard_map/ppermute | solution.py:287
  5.1 9.4 %collective-permute-start.3 = (bf16[48,1408]{1,0:T(8,128)(2,1)}, bf16[48,1408]{1,0:T(8,128)(2,1)S(1)}, u32[]{:S(2)}, u32[]{:S(2)}) collective-permute-start(bf16[48,1408]{1,0:T(8,128)(2,1)} %get-tuple-element.39), channel_id=1, source_target_pairs={{0,4},{1,5},{2,6},{3,7},{4,0},{5,1},{6,2},{7,3},{8,12},{9,13},{10,... | collective-permute-start | bytes 405512 | tf_op jit(solution)/shard_map/ppermute | solution.py:287
  7.8 13.4 %collective-permute-start = (bf16[48,1408]{1,0:T(8,128)(2,1)}, bf16[48,1408]{1,0:T(8,128)(2,1)S(1)}, u32[]{:S(2)}, u32[]{:S(2)}) collective-permute-start(bf16[48,1408]{1,0:T(8,128)(2,1)} %get-tuple-element.36), channel_id=1, source_target_pairs={{0,8},{1,9},{2,10},{3,11},{4,12},{5,13},{6,14},{7,15},{8,0},{9,1},... | collective-permute-start | bytes 405512 | tf_op jit(solution)/shard_map/ppermute | solution.py:287
  10.3 10.8 %collective-permute-start.1 = (bf16[48,1408]{1,0:T(8,128)(2,1)}, bf16[48,1408]{1,0:T(8,128)(2,1)S(1)}, u32[]{:S(2)}, u32[]{:S(2)}) collective-permute-start(bf16[48,1408]{1,0:T(8,128)(2,1)} %get-tuple-element.37), channel_id=1, source_target_pairs={{0,12},{1,13},{2,14},{3,15},{4,8},{5,9},{6,10},{7,11},{8,4},{9,5},... | collective-permute-start | bytes 405512 | tf_op jit(solution)/shard_map/ppermute | solution.py:287
  14.5 8.4 %collective-permute-start.4 = (bf16[96,1408]{1,0:T(8,128)(2,1)S(1)}, bf16[96,1408]{1,0:T(8,128)(2,1)S(1)}, u32[]{:S(2)}, u32[]{:S(2)}) collective-permute-start(bf16[96,1408]{1,0:T(8,128)(2,1)S(1)} %constant_dynamic-update-slice_fusion.2.refs_0_.near_x), channel_id=1, source_target_pairs={{0,2},{1,3},{2,0},{3,1},{4,6},{5,7},{6,4},{7,5},{8,10},{9,11},{10,... | collective-permute-start | bytes 811016 | tf_op jit(solution)/shard_map/ppermute | solution.py:287
  21.2 7.3 %collective-permute-start.2 = (bf16[96,1408]{1,0:T(8,128)(2,1)S(1)}, bf16[96,1408]{1,0:T(8,128)(2,1)S(1)}, u32[]{:S(2)}, u32[]{:S(2)}) collective-permute-start(bf16[96,1408]{1,0:T(8,128)(2,1)S(1)} %constant_dynamic-update-slice_fusion.refs_0_), channel_id=1, source_target_pairs={{0,2},{1,3},{2,0},{3,1},{4,6},{5,7},{6,4},{7,5},{8,10},{9,11},{10,... | collective-permute-start | bytes 811016 | tf_op jit(solution)/shard_map/ppermute | solution.py:287
  22.8 1.5 %collective-permute-start.5 = (bf16[96,1152]{1,0:T(8,128)(2,1)S(1)}, bf16[96,1152]{1,0:T(8,128)(2,1)S(1)}, u32[]{:S(2)}, u32[]{:S(2)}) collective-permute-start(bf16[96,1152]{1,0:T(8,128)(2,1)S(1)} %slice.16), channel_id=1, source_target_pairs={{0,1},{1,0},{2,3},{3,2},{4,5},{5,4},{6,7},{7,6},{8,9},{9,8},{10,11... | collective-permute-start | bytes 663560 | tf_op jit(solution)/shard_map/ppermute | solution.py:287
  22.9 1.7 %collective-permute-start.6 = (bf16[96,1152]{1,0:T(8,128)(2,1)S(1)}, bf16[96,1152]{1,0:T(8,128)(2,1)S(1)}, u32[]{:S(2)}, u32[]{:S(2)}) collective-permute-start(bf16[96,1152]{1,0:T(8,128)(2,1)S(1)} %slice.17), channel_id=1, source_target_pairs={{0,1},{1,0},{2,3},{3,2},{4,5},{5,4},{6,7},{7,6},{8,9},{9,8},{10,11... | collective-permute-start | bytes 663560 | tf_op jit(solution)/shard_map/ppermute | solution.py:287
  28.5 1.5 %collective-permute-start.7 = (bf16[96,1152]{1,0:T(8,128)(2,1)S(1)}, bf16[96,1152]{1,0:T(8,128)(2,1)S(1)}, u32[]{:S(2)}, u32[]{:S(2)}) collective-permute-start(bf16[96,1152]{1,0:T(8,128)(2,1)S(1)} %slice.14), channel_id=1, source_target_pairs={{0,1},{1,0},{2,3},{3,2},{4,5},{5,4},{6,7},{7,6},{8,9},{9,8},{10,11... | collective-permute-start | bytes 663560 | tf_op jit(solution)/shard_map/ppermute | solution.py:287
  28.6 1.8 %collective-permute-start.8 = (bf16[96,1152]{1,0:T(8,128)(2,1)S(1)}, bf16[96,1152]{1,0:T(8,128)(2,1)S(1)}, u32[]{:S(2)}, u32[]{:S(2)}) collective-permute-start(bf16[96,1152]{1,0:T(8,128)(2,1)S(1)} %slice.15), channel_id=1, source_target_pairs={{0,1},{1,0},{2,3},{3,2},{4,5},{5,4},{6,7},{7,6},{8,9},{9,8},{10,11... | collective-permute-start | bytes 663560 | tf_op jit(solution)/shard_map/ppermute | solution.py:287
  31.3 7.8 %collective-permute-start.10 = (bf16[96,256]{1,0:T(8,128)(2,1)S(1)}, bf16[96,256]{1,0:T(8,128)(2,1)S(1)}, u32[]{:S(2)}, u32[]{:S(2)}) collective-permute-start(bf16[96,256]{1,0:T(8,128)(2,1)S(1)} %get-tuple-element.45), channel_id=1, source_target_pairs={{0,8},{1,9},{2,10},{3,11},{4,12},{5,13},{6,14},{7,15},{8,0},{9,1},... | collective-permute-start | bytes 147464 | tf_op jit(solution)/shard_map/ppermute | solution.py:287
  35.5 6.0 %collective-permute-start.11 = (bf16[96,256]{1,0:T(8,128)(2,1)S(1)}, bf16[96,256]{1,0:T(8,128)(2,1)S(1)}, u32[]{:S(2)}, u32[]{:S(2)}) collective-permute-start(bf16[96,256]{1,0:T(8,128)(2,1)S(1)} %get-tuple-element.46), channel_id=1, source_target_pairs={{0,12},{1,13},{2,14},{3,15},{4,8},{5,9},{6,10},{7,11},{8,4},{9,5},... | collective-permute-start | bytes 147464 | tf_op jit(solution)/shard_map/ppermute | solution.py:287
  36.9 4.6 %collective-permute-start.9 = (bf16[96,256]{1,0:T(8,128)(2,1)S(1)}, bf16[96,256]{1,0:T(8,128)(2,1)S(1)}, u32[]{:S(2)}, u32[]{:S(2)}) collective-permute-start(bf16[96,256]{1,0:T(8,128)(2,1)S(1)} %get-tuple-element.44), channel_id=1, source_target_pairs={{0,4},{1,5},{2,6},{3,7},{4,0},{5,1},{6,2},{7,3},{8,12},{9,13},{10,... | collective-permute-start | bytes 147464 | tf_op jit(solution)/shard_map/ppermute | solution.py:287
  43.3 10.7 %collective-permute-start.16 = (bf16[4,32,1280]{2,1,0:T(8,128)(2,1)S(1)}, bf16[4,32,1280]{2,1,0:T(8,128)(2,1)S(1)}, u32[]{:S(2)}, u32[]{:S(2)}) collective-permute-start(bf16[4,32,1280]{2,1,0:T(8,128)(2,1)S(1)} %bitcast.34), channel_id=1, source_target_pairs={{0,2},{1,3},{2,0},{3,1},{4,6},{5,7},{6,4},{7,5},{8,10},{9,11},{10,... | collective-permute-start | bytes 983048 | tf_op jit(solution)/shard_map/ppermute | solution.py:287
  44.8 13.9 %collective-permute-start.14 = (bf16[4,32,1280]{2,1,0:T(8,128)(2,1)S(1)}, bf16[4,32,1280]{2,1,0:T(8,128)(2,1)S(1)}, u32[]{:S(2)}, u32[]{:S(2)}) collective-permute-start(bf16[4,32,1280]{2,1,0:T(8,128)(2,1)S(1)} %bitcast.33), channel_id=1, source_target_pairs={{0,2},{1,3},{2,0},{3,1},{4,6},{5,7},{6,4},{7,5},{8,10},{9,11},{10,... | collective-permute-start | bytes 983048 | tf_op jit(solution)/shard_map/ppermute | solution.py:287
  45.4 4.4 %collective-permute-start.17 = (bf16[32,896]{1,0:T(8,128)(2,1)S(1)}, bf16[32,896]{1,0:T(8,128)(2,1)S(1)}, u32[]{:S(2)}, u32[]{:S(2)}) collective-permute-start(bf16[32,896]{1,0:T(8,128)(2,1)S(1)} %get-tuple-element.54), channel_id=1, source_target_pairs={{0,4},{1,5},{2,6},{3,7},{4,0},{5,1},{6,2},{7,3},{8,12},{9,13},{10,... | collective-permute-start | bytes 172040 | tf_op jit(solution)/shard_map/ppermute | solution.py:287
  45.6 5.1 %collective-permute-start.18 = (bf16[32,896]{1,0:T(8,128)(2,1)S(1)}, bf16[32,896]{1,0:T(8,128)(2,1)S(1)}, u32[]{:S(2)}, u32[]{:S(2)}) collective-permute-start(bf16[32,896]{1,0:T(8,128)(2,1)S(1)} %get-tuple-element.55), channel_id=1, source_target_pairs={{0,8},{1,9},{2,10},{3,11},{4,12},{5,13},{6,14},{7,15},{8,0},{9,1},... | collective-permute-start | bytes 172040 | tf_op jit(solution)/shard_map/ppermute | solution.py:287
  48.0 6.0 %collective-permute-start.19 = (bf16[32,896]{1,0:T(8,128)(2,1)S(1)}, bf16[32,896]{1,0:T(8,128)(2,1)S(1)}, u32[]{:S(2)}, u32[]{:S(2)}) collective-permute-start(bf16[32,896]{1,0:T(8,128)(2,1)S(1)} %get-tuple-element.56), channel_id=1, source_target_pairs={{0,12},{1,13},{2,14},{3,15},{4,8},{5,9},{6,10},{7,11},{8,4},{9,5},... | collective-permute-start | bytes 172040 | tf_op jit(solution)/shard_map/ppermute | solution.py:287
  58.9 7.1 %collective-permute-start.15 = (bf16[32,1280]{1,0:T(8,128)(2,1)S(1)}, bf16[32,1280]{1,0:T(8,128)(2,1)S(1)}, u32[]{:S(2)}, u32[]{:S(2)}) collective-permute-start(bf16[32,1280]{1,0:T(8,128)(2,1)S(1)} %get-tuple-element.73), channel_id=1, source_target_pairs={{0,4},{1,5},{2,6},{3,7},{4,0},{5,1},{6,2},{7,3},{8,12},{9,13},{10,... | collective-permute-start | bytes 245768 | tf_op jit(solution)/shard_map/ppermute | solution.py:287
  59.5 10.2 %collective-permute-start.20 = (bf16[32,1280]{1,0:T(8,128)(2,1)S(1)}, bf16[32,1280]{1,0:T(8,128)(2,1)S(1)}, u32[]{:S(2)}, u32[]{:S(2)}) collective-permute-start(bf16[32,1280]{1,0:T(8,128)(2,1)S(1)} %get-tuple-element.76), channel_id=1, source_target_pairs={{0,4},{1,5},{2,6},{3,7},{4,0},{5,1},{6,2},{7,3},{8,12},{9,13},{10,... | collective-permute-start | bytes 245768 | tf_op jit(solution)/shard_map/ppermute | solution.py:287
  61.1 12.4 %collective-permute-start.21 = (bf16[32,1280]{1,0:T(8,128)(2,1)S(1)}, bf16[32,1280]{1,0:T(8,128)(2,1)S(1)}, u32[]{:S(2)}, u32[]{:S(2)}) collective-permute-start(bf16[32,1280]{1,0:T(8,128)(2,1)S(1)} %get-tuple-element.75), channel_id=1, source_target_pairs={{0,8},{1,9},{2,10},{3,11},{4,12},{5,13},{6,14},{7,15},{8,0},{9,1},... | collective-permute-start | bytes 245768 | tf_op jit(solution)/shard_map/ppermute | solution.py:287
  62.6 11.0 %collective-permute-start.22 = (bf16[32,1280]{1,0:T(8,128)(2,1)S(1)}, bf16[32,1280]{1,0:T(8,128)(2,1)S(1)}, u32[]{:S(2)}, u32[]{:S(2)}) collective-permute-start(bf16[32,1280]{1,0:T(8,128)(2,1)S(1)} %get-tuple-element.74), channel_id=1, source_target_pairs={{0,12},{1,13},{2,14},{3,15},{4,8},{5,9},{6,10},{7,11},{8,4},{9,5},... | collective-permute-start | bytes 245768 | tf_op jit(solution)/shard_map/ppermute | solution.py:287
  64.0 12.7 %collective-permute-start.23 = (bf16[32,1280]{1,0:T(8,128)(2,1)S(1)}, bf16[32,1280]{1,0:T(8,128)(2,1)S(1)}, u32[]{:S(2)}, u32[]{:S(2)}) collective-permute-start(bf16[32,1280]{1,0:T(8,128)(2,1)S(1)} %get-tuple-element.71), channel_id=1, source_target_pairs={{0,8},{1,9},{2,10},{3,11},{4,12},{5,13},{6,14},{7,15},{8,0},{9,1},... | collective-permute-start | bytes 245768 | tf_op jit(solution)/shard_map/ppermute | solution.py:287
  66.0 10.6 %collective-permute-start.24 = (bf16[32,1280]{1,0:T(8,128)(2,1)S(1)}, bf16[32,1280]{1,0:T(8,128)(2,1)S(1)}, u32[]{:S(2)}, u32[]{:S(2)}) collective-permute-start(bf16[32,1280]{1,0:T(8,128)(2,1)S(1)} %get-tuple-element.70), channel_id=1, source_target_pairs={{0,12},{1,13},{2,14},{3,15},{4,8},{5,9},{6,10},{7,11},{8,4},{9,5},... | collective-permute-start | bytes 245768 | tf_op jit(solution)/shard_map/ppermute | solution.py:287
  (3 other events, 16.7 us)

commit v17 on v16

--- a/solution.py
+++ b/solution.py
@@ -22,6 +22,10 @@
 def dot(left, right, left_dim, right_dim):
     dims = (((left_dim,), (right_dim,)), ((), ()))
     return lax.dot_general(left, right, dims, preferred_element_type=F32)
+
+
+def add(left, right):
+    return (left.astype(F32) + right.astype(F32)).astype(BF16)
 
 
 def iota(shape, dim):
@@ -212,9 +216,9 @@
     blocks, out = refs[:-1], refs[-1]
     rank, size = blocks[0].shape
     left = jnp.concatenate(pieces(inverse[...] * scale, 3), axis=0)
-    left = jnp.concatenate([left] * SLICES, axis=1)
-    for i in range(len(blocks) // SLICES):
-        right = jnp.concatenate([b[...] for b in blocks[i * SLICES : (i + 1) * SLICES]], axis=0)
+    left = jnp.concatenate([left] * 2, axis=1)
+    for i in range(len(blocks) // 2):
+        right = jnp.concatenate([b[...] for b in blocks[2 * i : 2 * i + 2]], axis=0)
         part = dot(left, right, 1, 0)
         out[:, i * size : (i + 1) * size] = part[:rank] + part[rank : 2 * rank] + part[2 * rank :]
 
@@ -388,30 +392,33 @@
         limit=limit,
     )
     columns = list(columns[:1]) + [exchange(columns[j], j * line) for j in range(1, SLICES)]
-    blocks = []
+    kept, gone = [], []
     for i in range(CHUNKS):
         parts = terms[i * low : (i + 1) * low]
         parts = [term.reshape(SLICES, rank, piece) for term in parts]
         step = 2
         while len(parts) > 1:
             got = [exchange(send, step) for send in parts[1::2]]
-            if i == 0 and step == 2:
+            if step == 2 and i == 0:
                 got[0], *columns = lax.optimization_barrier((got[0], *columns))
-            parts = [
-                (keep.astype(F32) + other.astype(F32)).astype(BF16)
-                for keep, other in zip(parts[::2], got)
-            ]
+                inverse, basis = call(
+                    inverse_kernel,
+                    [shape((rank, rank), F32), shape((rank, width // n_dp), F32)],
+                    [VMEM] * SLICES,
+                    [pltpu.VMEM((SLICES, rank, share), BF16)],
+                    *columns,
+                )
+            if step == 2 and i == 1:
+                got[0], gone[0], inverse = lax.optimization_barrier((got[0], gone[0], inverse))
+            parts = [add(keep, other) for keep, other in zip(parts[::2], got)]
             step *= 2
         own = [lax.dynamic_index_in_dim(parts[0], place ^ j, 0, False) for j in range(SLICES)]
-        blocks += own[:1] + [exchange(own[j], j * line) for j in range(1, SLICES)]
-    blocks[-3], *columns = lax.optimization_barrier((blocks[-3], *columns))
-    inverse, basis = call(
-        inverse_kernel,
-        [shape((rank, rank), F32), shape((rank, width // n_dp), F32)],
-        [VMEM] * SLICES,
-        [pltpu.VMEM((SLICES, rank, share), BF16)],
-        *columns,
-    )
+        kept.append(jnp.stack(own[::2]))
+        gone.append(exchange(jnp.stack(own[1::2]), line))
+    blocks = []
+    for keep, other in zip(kept, gone):
+        both = add(keep, other)
+        blocks += [both[0], exchange(both[1], 2 * line)]
     [coeffs] = call(
         functools.partial(coeffs_kernel, scale),
         [shape((rank, part), F32)],

time: 77.9 us -> 73.1 us (0.938)
  starting transfers between devices: 30.4 us -> 25.9 us
    ppermute x25 -> x23, starting transfers between devices: 30.4 us -> 25.9 us  [exchange(): return lax.ppermute(block, AXES, [(i, i ^ step) for i in range(count)])]
    ppermute x25 -> x23, waiting for transfers between devices: 34 us -> 33.5 us  [exchange(): return lax.ppermute(block, AXES, [(i, i ^ step) for i in range(count)])]
  transfers between devices with their start and end apart: 25 -> 23, of which waited for: 15 -> 18; matrix products, arithmetic and copies ran while one was open for 1% -> 2% of each run, Pallas kernels for 6% -> 6%
where the time goes in v17:
time: 73.1 us; the launch traced here: 72.9 us
  waiting for transfers between devices  33.5 us (46%)
  starting transfers between devices  25.9 us (35%)
  Pallas kernels  11.2 us (15%)
  local copies, waits for them, and re-layouts  1.14 us (2%)
  between operations  0.85 us (1%)
    ppermute x23, waiting for transfers between devices, exchange(): return lax.ppermute(block, AXES, [(i, i ^ step) for i in range(count)])  33.5 us
    ppermute x23, starting transfers between devices, exchange(): return lax.ppermute(block, AXES, [(i, i ^ step) for i in range(count)])  25.9 us
    pallas_call x7, Pallas kernels, call(): pl.pallas_call(body, out_shape=shapes, in_specs=spaces, out_specs=[VMEM]...  11.2 us
  transfers between devices with their start and end apart: 23, of which 18 were waited for; matrix products, arithmetic and copies ran while one was open for 2% of the time, Pallas kernels for 6%

profile of v17, /device:TPU:0, one launch (start us, length us, event | category | flops | bytes accessed | tf_op | source)
XLA Modules:
  0.0 72.9 jit_solution(13041846915501931427)
XLA Ops:
  0.6 3.9 %shard_map.68 = (bf16[48,1408]{1,0:T(8,128)(2,1)}, bf16[48,1408]{1,0:T(8,128)(2,1)}, bf16[48,1408]{1,0:T(8,128)(2,1)}, bf16[48,1408]{1,0:T(8,128)(2,1)}, f32[16,48]{1,0:T(8,128)}) custom-call(bf16[48,3584]{1,0:T(8,128)(2,1)} %tokens.1, bf16[384,2560]{1,0:T(8,128)(2,1)} %bitcast.20, f32[32,2560]{1,0:T(8,128)} %bitcast.27, s32[8,48]{1,0:T(8,128)} %bitcast.29, ...), custom_call_target="tpu_custom_call" | custom-call | flops 1 | bytes 1 | tf_op jit(solution)/shard_map/pallas_call | solution.py:43
  5.1 2.7 %collective-permute-start.3 = (bf16[48,1408]{1,0:T(8,128)(2,1)}, bf16[48,1408]{1,0:T(8,128)(2,1)S(1)}, u32[]{:S(2)}, u32[]{:S(2)}) collective-permute-start(bf16[48,1408]{1,0:T(8,128)(2,1)} %get-tuple-element.37), channel_id=1, source_target_pairs={{0,4},{1,5},{2,6},{3,7},{4,0},{5,1},{6,2},{7,3},{8,12},{9,13},{10,... | collective-permute-start | bytes 405512 | tf_op jit(solution)/shard_map/ppermute | solution.py:291
  7.8 2.6 %collective-permute-start = (bf16[48,1408]{1,0:T(8,128)(2,1)}, bf16[48,1408]{1,0:T(8,128)(2,1)S(1)}, u32[]{:S(2)}, u32[]{:S(2)}) collective-permute-start(bf16[48,1408]{1,0:T(8,128)(2,1)} %get-tuple-element.34), channel_id=1, source_target_pairs={{0,8},{1,9},{2,10},{3,11},{4,12},{5,13},{6,14},{7,15},{8,0},{9,1},... | collective-permute-start | bytes 405512 | tf_op jit(solution)/shard_map/ppermute | solution.py:291
  10.3 0.9 %constant_dynamic-update-slice_fusion.3 = bf16[96,1408]{1,0:T(8,128)(2,1)S(1)} fusion(bf16[48,1408]{1,0:T(8,128)(2,1)} %get-tuple-element.36), kind=kLoop, calls=%fused_computation.15 | loop fusion | bytes 270336
  11.3 3.2 %collective-permute-done.3 = bf16[48,1408]{1,0:T(8,128)(2,1)S(1)} collective-permute-done((bf16[48,1408]{1,0:T(8,128)(2,1)}, bf16[48,1408]{1,0:T(8,128)(2,1)S(1)}, u32[]{:S(2)}, u32[]{:S(2)}) %collective-permute-start.3) | collective-permute-done | bytes 135200 | tf_op jit(solution)/shard_map/ppermute | solution.py:291
  14.5 1.8 %collective-permute-start.4 = (bf16[96,1408]{1,0:T(8,128)(2,1)S(1)}, bf16[96,1408]{1,0:T(8,128)(2,1)S(1)}, u32[]{:S(2)}, u32[]{:S(2)}) collective-permute-start(bf16[96,1408]{1,0:T(8,128)(2,1)S(1)} %constant_dynamic-update-slice_fusion.2.refs_0_.near_x), channel_id=1, source_target_pairs={{0,2},{1,3},{2,0},{3,1},{4,6},{5,7},{6,4},{7,5},{8,10},{9,11},{10,... | collective-permute-start | bytes 811016 | tf_op jit(solution)/shard_map/ppermute | solution.py:291
  16.3 4.9 %collective-permute-done = bf16[48,1408]{1,0:T(8,128)(2,1)S(1)} collective-permute-done((bf16[48,1408]{1,0:T(8,128)(2,1)}, bf16[48,1408]{1,0:T(8,128)(2,1)S(1)}, u32[]{:S(2)}, u32[]{:S(2)}) %collective-permute-start) | collective-permute-done | bytes 135200 | tf_op jit(solution)/shard_map/ppermute | solution.py:291
  21.2 1.6 %collective-permute-start.2 = (bf16[96,1408]{1,0:T(8,128)(2,1)S(1)}, bf16[96,1408]{1,0:T(8,128)(2,1)S(1)}, u32[]{:S(2)}, u32[]{:S(2)}) collective-permute-start(bf16[96,1408]{1,0:T(8,128)(2,1)S(1)} %constant_dynamic-update-slice_fusion.refs_0_), channel_id=1, source_target_pairs={{0,2},{1,3},{2,0},{3,1},{4,6},{5,7},{6,4},{7,5},{8,10},{9,11},{10,... | collective-permute-start | bytes 811016 | tf_op jit(solution)/shard_map/ppermute | solution.py:291
  25.3 3.2 %collective-permute-done.2.refs_1_ = bf16[96,1408]{1,0:T(8,128)(2,1)S(1)} collective-permute-done((bf16[96,1408]{1,0:T(8,128)(2,1)S(1)}, bf16[96,1408]{1,0:T(8,128)(2,1)S(1)}, u32[]{:S(2)}, u32[]{:S(2)}) %collective-permute-start.2) | collective-permute-done | bytes 270368 | tf_op jit(solution)/shard_map/ppermute | solution.py:291
  31.3 4.2 %collective-permute-start.10 = (bf16[96,256]{1,0:T(8,128)(2,1)S(1)}, bf16[96,256]{1,0:T(8,128)(2,1)S(1)}, u32[]{:S(2)}, u32[]{:S(2)}) collective-permute-start(bf16[96,256]{1,0:T(8,128)(2,1)S(1)} %get-tuple-element.43), channel_id=1, source_target_pairs={{0,8},{1,9},{2,10},{3,11},{4,12},{5,13},{6,14},{7,15},{8,0},{9,1},... | collective-permute-start | bytes 147464 | tf_op jit(solution)/shard_map/ppermute | solution.py:291
  35.5 1.4 %collective-permute-start.11 = (bf16[96,256]{1,0:T(8,128)(2,1)S(1)}, bf16[96,256]{1,0:T(8,128)(2,1)S(1)}, u32[]{:S(2)}, u32[]{:S(2)}) collective-permute-start(bf16[96,256]{1,0:T(8,128)(2,1)S(1)} %get-tuple-element.44), channel_id=1, source_target_pairs={{0,12},{1,13},{2,14},{3,15},{4,8},{5,9},{6,10},{7,11},{8,4},{9,5},... | collective-permute-start | bytes 147464 | tf_op jit(solution)/shard_map/ppermute | solution.py:291
  36.9 1.2 %collective-permute-done.12.pair = f32[16,48]{1,0:T(8,128)S(1)} collective-permute-done((f32[16,48]{1,0:T(8,128)S(1)}, f32[16,48]{1,0:T(8,128)S(1)}, u32[]{:S(2)}, u32[]{:S(2)}) %collective-permute-start.12) | collective-permute-done | bytes 3104 | tf_op jit(solution)/shard_map/ppermute | solution.py:291
  39.1 2.4 %collective-permute-done.11.z3 = bf16[96,256]{1,0:T(8,128)(2,1)S(1)} collective-permute-done((bf16[96,256]{1,0:T(8,128)(2,1)S(1)}, bf16[96,256]{1,0:T(8,128)(2,1)S(1)}, u32[]{:S(2)}, u32[]{:S(2)}) %collective-permute-start.11) | collective-permute-done | bytes 49184 | tf_op jit(solution)/shard_map/ppermute | solution.py:291
  41.5 1.8 %shard_map.72 = (bf16[128,1280]{1,0:T(8,128)(2,1)S(1)}, bf16[128,1280]{1,0:T(8,128)(2,1)S(1)}, bf16[128,1280]{1,0:T(8,128)(2,1)S(1)}, bf16[128,1280]{1,0:T(8,128)(2,1)S(1)}) custom-call(bf16[96,256]{1,0:T(8,128)(2,1)S(1)} %get-tuple-element.41.z0, bf16[96,256]{1,0:T(8,128)(2,1)S(1)} %collective-permute-done.9.z1, ...), custom_call_target="tpu_custom_call" | custom-call | flops 1 | bytes 1 | tf_op jit(solution)/shard_map/pallas_call | solution.py:43
  43.3 1.6 %collective-permute-start.14 = (bf16[4,32,1280]{2,1,0:T(8,128)(2,1)S(1)}, bf16[4,32,1280]{2,1,0:T(8,128)(2,1)S(1)}, u32[]{:S(2)}, u32[]{:S(2)}) collective-permute-start(bf16[4,32,1280]{2,1,0:T(8,128)(2,1)S(1)} %bitcast.26), channel_id=1, source_target_pairs={{0,2},{1,3},{2,0},{3,1},{4,6},{5,7},{6,4},{7,5},{8,10},{9,11},{10,... | collective-permute-start | bytes 983048 | tf_op jit(solution)/shard_map/ppermute | solution.py:291
  45.1 2.4 %collective-permute-start.16 = (bf16[32,896]{1,0:T(8,128)(2,1)S(1)}, bf16[32,896]{1,0:T(8,128)(2,1)S(1)}, u32[]{:S(2)}, u32[]{:S(2)}) collective-permute-start(bf16[32,896]{1,0:T(8,128)(2,1)S(1)} %get-tuple-element.51), channel_id=1, source_target_pairs={{0,8},{1,9},{2,10},{3,11},{4,12},{5,13},{6,14},{7,15},{8,0},{9,1},... | collective-permute-start | bytes 172040 | tf_op jit(solution)/shard_map/ppermute | solution.py:291
  47.4 1.8 %collective-permute-start.17 = (bf16[32,896]{1,0:T(8,128)(2,1)S(1)}, bf16[32,896]{1,0:T(8,128)(2,1)S(1)}, u32[]{:S(2)}, u32[]{:S(2)}) collective-permute-start(bf16[32,896]{1,0:T(8,128)(2,1)S(1)} %get-tuple-element.52), channel_id=1, source_target_pairs={{0,12},{1,13},{2,14},{3,15},{4,8},{5,9},{6,10},{7,11},{8,4},{9,5},... | collective-permute-start | bytes 172040 | tf_op jit(solution)/shard_map/ppermute | solution.py:291
  50.1 3.3 %collective-permute-done.17.c3 = bf16[32,896]{1,0:T(8,128)(2,1)S(1)} collective-permute-done((bf16[32,896]{1,0:T(8,128)(2,1)S(1)}, bf16[32,896]{1,0:T(8,128)(2,1)S(1)}, u32[]{:S(2)}, u32[]{:S(2)}) %collective-permute-start.17) | collective-permute-done | bytes 57376 | tf_op jit(solution)/shard_map/ppermute | solution.py:291
  54.4 2.7 %shard_map.73 = (f32[32,32]{1,0:T(8,128)S(1)}, f32[32,3584]{1,0:T(8,128)}) custom-call(bf16[32,896]{1,0:T(8,128)(2,1)S(1)} %get-tuple-element.53.c0, bf16[32,896]{1,0:T(8,128)(2,1)S(1)} %collective-permute-done.15.c1, bf16[32,896]{1,0:T(8,128)(2,1)S(1)} %collective-permute-done.16.c2, bf16[32,896]{1,0:T(8,128)(2,1)S(1)} %collective-permute-done.17.c3), custom_call_target="tpu_custom_call" | custom-call | flops 1 | bytes 1 | tf_op jit(solution)/shard_map/pallas_call | solution.py:43
  57.1 1.6 %collective-permute-done.18 = bf16[4,32,1280]{2,1,0:T(8,128)(2,1)S(1)} collective-permute-done((bf16[4,32,1280]{2,1,0:T(8,128)(2,1)S(1)}, bf16[4,32,1280]{2,1,0:T(8,128)(2,1)S(1)}, u32[]{:S(2)}, u32[]{:S(2)}) %collective-permute-start.18) | collective-permute-done | bytes 327712 | tf_op jit(solution)/shard_map/ppermute | solution.py:291
  60.0 2.5 %collective-permute-start.20 = (bf16[32,1280]{1,0:T(8,128)(2,1)S(1)}, bf16[32,1280]{1,0:T(8,128)(2,1)S(1)}, u32[]{:S(2)}, u32[]{:S(2)}) collective-permute-start(bf16[32,1280]{1,0:T(8,128)(2,1)S(1)} %get-tuple-element.76), channel_id=1, source_target_pairs={{0,8},{1,9},{2,10},{3,11},{4,12},{5,13},{6,14},{7,15},{8,0},{9,1},... | collective-permute-start | bytes 245768 | tf_op jit(solution)/shard_map/ppermute | solution.py:291
  62.5 3.7 %collective-permute-done.21 = bf16[2,32,1280]{2,1,0:T(8,128)(2,1)S(1)} collective-permute-done((bf16[2,32,1280]{2,1,0:T(8,128)(2,1)S(1)}, bf16[2,32,1280]{2,1,0:T(8,128)(2,1)S(1)}, u32[]{:S(2)}, u32[]{:S(2)}) %collective-permute-start.21) | collective-permute-done | bytes 163872 | tf_op jit(solution)/shard_map/ppermute | solution.py:291
  66.8 5.1 %collective-permute-done.22.refs_3_ = bf16[32,1280]{1,0:T(8,128)(2,1)S(1)} collective-permute-done((bf16[32,1280]{1,0:T(8,128)(2,1)S(1)}, bf16[32,1280]{1,0:T(8,128)(2,1)S(1)}, u32[]{:S(2)}, u32[]{:S(2)}) %collective-permute-start.22) | collective-permute-done | bytes 81952 | tf_op jit(solution)/shard_map/ppermute | solution.py:291
  71.9 1.1 %shard_map.74 = f32[32,2560]{1,0:T(8,128)} custom-call(f32[32,32]{1,0:T(8,128)S(1)} %get-tuple-element.62.inverse, bf16[32,1280]{1,0:T(8,128)(2,1)S(1)} %get-tuple-element.77.refs_0_, bf16[32,1280]{1,0:T(8,128)(2,1)S(1)} %collective-permute-done.20.refs_1_, bf16[32,1280]{1,0:T(8,128)(2,1)S(1)} %get-tuple-element.75.refs_2_, ...), custom_call_target="tpu_custom_call" | custom-call | flops 1 | bytes 1 | tf_op jit(solution)/shard_map/pallas_call | solution.py:43
  (51 shorter events, 10.8 us)
Async XLA Ops:
  4.6 36.9 %collective-permute-start.13 = (bf16[384,2560]{1,0:T(8,128)(2,1)S(1)}, bf16[384,2560]{1,0:T(8,128)(2,1)S(1)}, u32[]{:S(2)}, u32[]{:S(2)}) collective-permute-start(bf16[384,2560]{1,0:T(8,128)(2,1)S(1)} %bitcast.21), channel_id=1, source_target_pairs={{0,1},{1,0},{2,3},{3,2},{4,5},{5,4},{6,7},{7,6},{8,9},{9,8},{10,11... | collective-permute-start | bytes 5898248 | tf_op jit(solution)/shard_map/ppermute | solution.py:291
  5.1 9.4 %collective-permute-start.3 = (bf16[48,1408]{1,0:T(8,128)(2,1)}, bf16[48,1408]{1,0:T(8,128)(2,1)S(1)}, u32[]{:S(2)}, u32[]{:S(2)}) collective-permute-start(bf16[48,1408]{1,0:T(8,128)(2,1)} %get-tuple-element.37), channel_id=1, source_target_pairs={{0,4},{1,5},{2,6},{3,7},{4,0},{5,1},{6,2},{7,3},{8,12},{9,13},{10,... | collective-permute-start | bytes 405512 | tf_op jit(solution)/shard_map/ppermute | solution.py:291
  7.8 13.4 %collective-permute-start = (bf16[48,1408]{1,0:T(8,128)(2,1)}, bf16[48,1408]{1,0:T(8,128)(2,1)S(1)}, u32[]{:S(2)}, u32[]{:S(2)}) collective-permute-start(bf16[48,1408]{1,0:T(8,128)(2,1)} %get-tuple-element.34), channel_id=1, source_target_pairs={{0,8},{1,9},{2,10},{3,11},{4,12},{5,13},{6,14},{7,15},{8,0},{9,1},... | collective-permute-start | bytes 405512 | tf_op jit(solution)/shard_map/ppermute | solution.py:291
  10.3 10.8 %collective-permute-start.1 = (bf16[48,1408]{1,0:T(8,128)(2,1)}, bf16[48,1408]{1,0:T(8,128)(2,1)S(1)}, u32[]{:S(2)}, u32[]{:S(2)}) collective-permute-start(bf16[48,1408]{1,0:T(8,128)(2,1)} %get-tuple-element.35), channel_id=1, source_target_pairs={{0,12},{1,13},{2,14},{3,15},{4,8},{5,9},{6,10},{7,11},{8,4},{9,5},... | collective-permute-start | bytes 405512 | tf_op jit(solution)/shard_map/ppermute | solution.py:291
  14.5 8.4 %collective-permute-start.4 = (bf16[96,1408]{1,0:T(8,128)(2,1)S(1)}, bf16[96,1408]{1,0:T(8,128)(2,1)S(1)}, u32[]{:S(2)}, u32[]{:S(2)}) collective-permute-start(bf16[96,1408]{1,0:T(8,128)(2,1)S(1)} %constant_dynamic-update-slice_fusion.2.refs_0_.near_x), channel_id=1, source_target_pairs={{0,2},{1,3},{2,0},{3,1},{4,6},{5,7},{6,4},{7,5},{8,10},{9,11},{10,... | collective-permute-start | bytes 811016 | tf_op jit(solution)/shard_map/ppermute | solution.py:291
  21.2 7.3 %collective-permute-start.2 = (bf16[96,1408]{1,0:T(8,128)(2,1)S(1)}, bf16[96,1408]{1,0:T(8,128)(2,1)S(1)}, u32[]{:S(2)}, u32[]{:S(2)}) collective-permute-start(bf16[96,1408]{1,0:T(8,128)(2,1)S(1)} %constant_dynamic-update-slice_fusion.refs_0_), channel_id=1, source_target_pairs={{0,2},{1,3},{2,0},{3,1},{4,6},{5,7},{6,4},{7,5},{8,10},{9,11},{10,... | collective-permute-start | bytes 811016 | tf_op jit(solution)/shard_map/ppermute | solution.py:291
  22.8 1.5 %collective-permute-start.5 = (bf16[96,1152]{1,0:T(8,128)(2,1)S(1)}, bf16[96,1152]{1,0:T(8,128)(2,1)S(1)}, u32[]{:S(2)}, u32[]{:S(2)}) collective-permute-start(bf16[96,1152]{1,0:T(8,128)(2,1)S(1)} %slice.32), channel_id=1, source_target_pairs={{0,1},{1,0},{2,3},{3,2},{4,5},{5,4},{6,7},{7,6},{8,9},{9,8},{10,11... | collective-permute-start | bytes 663560 | tf_op jit(solution)/shard_map/ppermute | solution.py:291
  22.9 1.7 %collective-permute-start.6 = (bf16[96,1152]{1,0:T(8,128)(2,1)S(1)}, bf16[96,1152]{1,0:T(8,128)(2,1)S(1)}, u32[]{:S(2)}, u32[]{:S(2)}) collective-permute-start(bf16[96,1152]{1,0:T(8,128)(2,1)S(1)} %slice.33), channel_id=1, source_target_pairs={{0,1},{1,0},{2,3},{3,2},{4,5},{5,4},{6,7},{7,6},{8,9},{9,8},{10,11... | collective-permute-start | bytes 663560 | tf_op jit(solution)/shard_map/ppermute | solution.py:291
  25.2 11.6 %copy-start.1 = (f32[16,48]{1,0:T(8,128)S(1)}, f32[16,48]{1,0:T(8,128)}, u32[]{:S(2)}) copy-start(f32[16,48]{1,0:T(8,128)} %get-tuple-element.46.own) | copy-start | bytes 9220
  28.5 1.5 %collective-permute-start.7 = (bf16[96,1152]{1,0:T(8,128)(2,1)S(1)}, bf16[96,1152]{1,0:T(8,128)(2,1)S(1)}, u32[]{:S(2)}, u32[]{:S(2)}) collective-permute-start(bf16[96,1152]{1,0:T(8,128)(2,1)S(1)} %slice.26), channel_id=1, source_target_pairs={{0,1},{1,0},{2,3},{3,2},{4,5},{5,4},{6,7},{7,6},{8,9},{9,8},{10,11... | collective-permute-start | bytes 663560 | tf_op jit(solution)/shard_map/ppermute | solution.py:291
  28.6 1.8 %collective-permute-start.8 = (bf16[96,1152]{1,0:T(8,128)(2,1)S(1)}, bf16[96,1152]{1,0:T(8,128)(2,1)S(1)}, u32[]{:S(2)}, u32[]{:S(2)}) collective-permute-start(bf16[96,1152]{1,0:T(8,128)(2,1)S(1)} %slice.27), channel_id=1, source_target_pairs={{0,1},{1,0},{2,3},{3,2},{4,5},{5,4},{6,7},{7,6},{8,9},{9,8},{10,11... | collective-permute-start | bytes 663560 | tf_op jit(solution)/shard_map/ppermute | solution.py:291
  31.3 7.8 %collective-permute-start.10 = (bf16[96,256]{1,0:T(8,128)(2,1)S(1)}, bf16[96,256]{1,0:T(8,128)(2,1)S(1)}, u32[]{:S(2)}, u32[]{:S(2)}) collective-permute-start(bf16[96,256]{1,0:T(8,128)(2,1)S(1)} %get-tuple-element.43), channel_id=1, source_target_pairs={{0,8},{1,9},{2,10},{3,11},{4,12},{5,13},{6,14},{7,15},{8,0},{9,1},... | collective-permute-start | bytes 147464 | tf_op jit(solution)/shard_map/ppermute | solution.py:291
  35.5 6.0 %collective-permute-start.11 = (bf16[96,256]{1,0:T(8,128)(2,1)S(1)}, bf16[96,256]{1,0:T(8,128)(2,1)S(1)}, u32[]{:S(2)}, u32[]{:S(2)}) collective-permute-start(bf16[96,256]{1,0:T(8,128)(2,1)S(1)} %get-tuple-element.44), channel_id=1, source_target_pairs={{0,12},{1,13},{2,14},{3,15},{4,8},{5,9},{6,10},{7,11},{8,4},{9,5},... | collective-permute-start | bytes 147464 | tf_op jit(solution)/shard_map/ppermute | solution.py:291
  36.9 4.6 %collective-permute-start.9 = (bf16[96,256]{1,0:T(8,128)(2,1)S(1)}, bf16[96,256]{1,0:T(8,128)(2,1)S(1)}, u32[]{:S(2)}, u32[]{:S(2)}) collective-permute-start(bf16[96,256]{1,0:T(8,128)(2,1)S(1)} %get-tuple-element.42), channel_id=1, source_target_pairs={{0,4},{1,5},{2,6},{3,7},{4,0},{5,1},{6,2},{7,3},{8,12},{9,13},{10,... | collective-permute-start | bytes 147464 | tf_op jit(solution)/shard_map/ppermute | solution.py:291
  36.9 1.2 %collective-permute-start.12 = (f32[16,48]{1,0:T(8,128)S(1)}, f32[16,48]{1,0:T(8,128)S(1)}, u32[]{:S(2)}, u32[]{:S(2)}) collective-permute-start(f32[16,48]{1,0:T(8,128)S(1)} %copy-done.1), channel_id=1, source_target_pairs={{0,1},{1,0},{2,3},{3,2},{4,5},{5,4},{6,7},{7,6},{8,9},{9,8},{10,11... | collective-permute-start | bytes 9224 | tf_op jit(solution)/shard_map/ppermute | solution.py:291
  43.3 10.6 %collective-permute-start.14 = (bf16[4,32,1280]{2,1,0:T(8,128)(2,1)S(1)}, bf16[4,32,1280]{2,1,0:T(8,128)(2,1)S(1)}, u32[]{:S(2)}, u32[]{:S(2)}) collective-permute-start(bf16[4,32,1280]{2,1,0:T(8,128)(2,1)S(1)} %bitcast.26), channel_id=1, source_target_pairs={{0,2},{1,3},{2,0},{3,1},{4,6},{5,7},{6,4},{7,5},{8,10},{9,11},{10,... | collective-permute-start | bytes 983048 | tf_op jit(solution)/shard_map/ppermute | solution.py:291
  44.8 4.9 %collective-permute-start.15 = (bf16[32,896]{1,0:T(8,128)(2,1)S(1)}, bf16[32,896]{1,0:T(8,128)(2,1)S(1)}, u32[]{:S(2)}, u32[]{:S(2)}) collective-permute-start(bf16[32,896]{1,0:T(8,128)(2,1)S(1)} %get-tuple-element.50), channel_id=1, source_target_pairs={{0,4},{1,5},{2,6},{3,7},{4,0},{5,1},{6,2},{7,3},{8,12},{9,13},{10,... | collective-permute-start | bytes 172040 | tf_op jit(solution)/shard_map/ppermute | solution.py:291
  45.1 5.1 %collective-permute-start.16 = (bf16[32,896]{1,0:T(8,128)(2,1)S(1)}, bf16[32,896]{1,0:T(8,128)(2,1)S(1)}, u32[]{:S(2)}, u32[]{:S(2)}) collective-permute-start(bf16[32,896]{1,0:T(8,128)(2,1)S(1)} %get-tuple-element.51), channel_id=1, source_target_pairs={{0,8},{1,9},{2,10},{3,11},{4,12},{5,13},{6,14},{7,15},{8,0},{9,1},... | collective-permute-start | bytes 172040 | tf_op jit(solution)/shard_map/ppermute | solution.py:291
  47.4 6.0 %collective-permute-start.17 = (bf16[32,896]{1,0:T(8,128)(2,1)S(1)}, bf16[32,896]{1,0:T(8,128)(2,1)S(1)}, u32[]{:S(2)}, u32[]{:S(2)}) collective-permute-start(bf16[32,896]{1,0:T(8,128)(2,1)S(1)} %get-tuple-element.52), channel_id=1, source_target_pairs={{0,12},{1,13},{2,14},{3,15},{4,8},{5,9},{6,10},{7,11},{8,4},{9,5},... | collective-permute-start | bytes 172040 | tf_op jit(solution)/shard_map/ppermute | solution.py:291
  49.2 9.5 %collective-permute-start.18 = (bf16[4,32,1280]{2,1,0:T(8,128)(2,1)S(1)}, bf16[4,32,1280]{2,1,0:T(8,128)(2,1)S(1)}, u32[]{:S(2)}, u32[]{:S(2)}) collective-permute-start(bf16[4,32,1280]{2,1,0:T(8,128)(2,1)S(1)} %bitcast.25), channel_id=1, source_target_pairs={{0,2},{1,3},{2,0},{3,1},{4,6},{5,7},{6,4},{7,5},{8,10},{9,11},{10,... | collective-permute-start | bytes 983048 | tf_op jit(solution)/shard_map/ppermute | solution.py:291
  54.1 5.4 %collective-permute-start.19 = (bf16[2,32,1280]{2,1,0:T(8,128)(2,1)S(1)}, bf16[2,32,1280]{2,1,0:T(8,128)(2,1)S(1)}, u32[]{:S(2)}, u32[]{:S(2)}) collective-permute-start(bf16[2,32,1280]{2,1,0:T(8,128)(2,1)S(1)} %pad_maximum_fusion), channel_id=1, source_target_pairs={{0,4},{1,5},{2,6},{3,7},{4,0},{5,1},{6,2},{7,3},{8,12},{9,13},{10,... | collective-permute-start | bytes 491528 | tf_op jit(solution)/shard_map/ppermute | solution.py:291
  59.6 6.6 %collective-permute-start.21 = (bf16[2,32,1280]{2,1,0:T(8,128)(2,1)S(1)}, bf16[2,32,1280]{2,1,0:T(8,128)(2,1)S(1)}, u32[]{:S(2)}, u32[]{:S(2)}) collective-permute-start(bf16[2,32,1280]{2,1,0:T(8,128)(2,1)S(1)} %pad_maximum_fusion.1), channel_id=1, source_target_pairs={{0,4},{1,5},{2,6},{3,7},{4,0},{5,1},{6,2},{7,3},{8,12},{9,13},{10,... | collective-permute-start | bytes 491528 | tf_op jit(solution)/shard_map/ppermute | solution.py:291
  60.0 6.7 %collective-permute-start.20 = (bf16[32,1280]{1,0:T(8,128)(2,1)S(1)}, bf16[32,1280]{1,0:T(8,128)(2,1)S(1)}, u32[]{:S(2)}, u32[]{:S(2)}) collective-permute-start(bf16[32,1280]{1,0:T(8,128)(2,1)S(1)} %get-tuple-element.76), channel_id=1, source_target_pairs={{0,8},{1,9},{2,10},{3,11},{4,12},{5,13},{6,14},{7,15},{8,0},{9,1},... | collective-permute-start | bytes 245768 | tf_op jit(solution)/shard_map/ppermute | solution.py:291
  66.2 5.6 %collective-permute-start.22 = (bf16[32,1280]{1,0:T(8,128)(2,1)S(1)}, bf16[32,1280]{1,0:T(8,128)(2,1)S(1)}, u32[]{:S(2)}, u32[]{:S(2)}) collective-permute-start(bf16[32,1280]{1,0:T(8,128)(2,1)S(1)} %get-tuple-element.74), channel_id=1, source_target_pairs={{0,8},{1,9},{2,10},{3,11},{4,12},{5,13},{6,14},{7,15},{8,0},{9,1},... | collective-permute-start | bytes 245768 | tf_op jit(solution)/shard_map/ppermute | solution.py:291
  (1 other events, 3.9 us)

commit v18 on v17

--- a/solution.py
+++ b/solution.py
@@ -82,15 +82,14 @@
     return copies
 
 
-def first_kernel(groups, tokens, cot_at, sketch_at, ids_at, probs_at, *refs):
-    outs, pairs, (cot, sketch, ids, probs, sems, x_sems) = refs[:SLICES], refs[SLICES], refs[5:]
-    core, _, place, _ = position()
+def first_kernel(groups, cot_at, sketch_at, ids_at, probs_at, *refs):
+    out, pairs, (cot, sketch, ids, probs, sems) = refs[0], refs[1], refs[2:]
+    core = position()[0]
     rows, hidden = cot.shape
     tok = pairs.shape[1]
     top = rows // tok
     rank = sketch.shape[0]
-    share = tokens.shape[1] // SLICES
-    lanes = (outs[0].shape[1] - share) // groups
+    lanes = out.shape[1] // groups
     parts = 5
     piece = hidden // parts
     sources = [(ids_at, ids), (probs_at, probs), (sketch_at, sketch)]
@@ -98,11 +97,6 @@
         cut = pl.ds(i * piece, piece)
         sources.append((cot_at.at[:, cut], cot.at[:, cut]))
     copies = load(sources, sems)
-    sources = []
-    for j, out in enumerate(outs):
-        cut = pl.ds(pl.multiple_of((place ^ j) * share, share), share)
-        sources.append((tokens.at[:, cut], out.at[:, pl.ds(lanes, share)]))
-    x_copies = load(sources, x_sems)
     copies[0].wait()
     copies[1].wait()
     pairs[:top] = ids[...].astype(F32)
@@ -123,52 +117,40 @@
     for i in range(groups):
         name = block + (core ^ i) if groups == 2 else block
         y = jnp.where(names == name.astype(F32), tiled, 0.0).astype(BF16)
-        y = dot(pick, y, 0, 0).astype(BF16)
-        for out in outs:
-            out[:, i * (lanes + share) : i * (lanes + share) + lanes] = y
-    for copy in x_copies:
-        copy.wait()
-
-
-def gather(near, far, x, y, sems):
-    share, lanes = x.shape[1], y.shape[1]
-    rows = near[0].shape[0]
+        out[:, i * lanes : (i + 1) * lanes] = dot(pick, y, 0, 0).astype(BF16)
+
+
+def product(refs, x, y, sems):
+    lanes = y.shape[1]
     sources = []
-    for i, (a, b) in enumerate(zip(near, far)):
-        cut = pl.ds(2 * i * rows, rows)
-        sources.append((a.at[:, pl.ds(0, lanes)], y.at[cut]))
-        sources.append((a.at[:, pl.ds(lanes, share)], x.at[cut]))
-        cut = pl.ds((2 * i + 1) * rows, rows)
-        sources.append((b.at[:, pl.ds(0, share)], x.at[cut]))
-        sources.append((b.at[:, pl.ds(share, lanes)], y.at[cut]))
+    for i in range(4):
+        rows = x.shape[0] // 4
+        sources.append((refs[i], x.at[pl.ds(i * rows, rows)]))
+    for i in range(2):
+        rows = y.shape[0] // 2
+        sources.append((refs[4 + i].at[:, pl.ds(0, lanes)], y.at[pl.ds(i * rows, rows)]))
     for copy in load(sources, sems):
         copy.wait()
-
-
-def columns_kernel(n, *refs):
-    out, x, y, sems = refs[2 * n :]
-    gather(refs[:n], refs[n : 2 * n], x, y, sems)
-    out[...] = dot(y[...], x[...], 0, 0)
-
-
-def z_kernel(n, low, part, near_x, far_x, *refs):
-    outs, (x, y, columns, sems) = refs[2 * n : -4], refs[-4:]
+    return dot(y[...], x[...], 0, 0)
+
+
+def columns_kernel(*refs):
+    refs[6][...] = product(refs[:6], *refs[7:])
+
+
+def z_kernel(low, *refs):
+    part, own, outs, columns = refs[0], refs[1:5], refs[11:-4], refs[-4]
     _, lower, place, _ = position()
-    gather(refs[:n], refs[n : 2 * n], x, y, sems)
+    total = (part[...] + product(refs[5:11], *refs[-3:])).astype(BF16)
+    columns[...] = total
     rank = columns.shape[0] // (SLICES * low)
-    share = x.shape[1]
-    lanes = y.shape[1]
-    rows = near_x.shape[0]
+    rows = own[0].shape[0]
     tok = rows // 2
-    total = (part[...] + dot(y[...], x[...], 0, 0)).astype(BF16)
-    columns[...] = total
-    own = jnp.concatenate([near_x[:, lanes : lanes + share], far_x[:, :share]], axis=0)
-    halves = [dot(own, total, 1, 1), dot(x[: 2 * rows], total, 1, 1)]
+    z = dot(jnp.concatenate([x[...] for x in own], axis=0), total, 1, 1).astype(BF16)
     for j in range(SLICES):
-        half = halves[j // 2].astype(BF16)
-        start = j % 2 * tok
-        outs[j][:tok] = half[start : start + tok]
-        outs[j][tok:] = half[rows + start : rows + start + tok]
+        for core in range(2):
+            start = 2 * core * rows + j * tok
+            outs[j][core * tok : (core + 1) * tok] = z[start : start + tok]
         expert = (place ^ j) * low + lower
         outs[SLICES + j][...] = columns[pl.ds(pl.multiple_of(expert * rank, rank), rank)]
 
@@ -292,26 +274,28 @@
 
     cot = cotangents.reshape(rows, hidden)
 
-    *blocks, pairs = call(
+    cuts = [
+        lax.dynamic_slice_in_dim(tokens, (place ^ j) * share, share, axis=1) for j in range(SLICES)
+    ]
+    cuts = cuts[:1] + [exchange(cuts[j], j * line) for j in range(1, SLICES)]
+
+    y, pairs = call(
         functools.partial(first_kernel, groups),
-        [shape((tok, groups * lanes + share), BF16)] * SLICES + [shape((2 * top, tok), F32)],
-        [HBM] * 5,
+        [shape((tok, groups * lanes), BF16), shape((2 * top, tok), F32)],
+        [HBM] * 4,
         [
             pltpu.VMEM((rows, hidden), BF16),
             pltpu.VMEM((rank, hidden), F32),
             pltpu.VMEM((top, tok), jnp.int32),
             pltpu.VMEM((top, tok), F32),
             pltpu.SemaphoreType.DMA((8,)),
-            pltpu.SemaphoreType.DMA((SLICES,)),
         ],
-        tokens,
         cot,
         sketch.T,
         expert_ids.T,
         route_probs.T,
         limit=LARGE,
     )
-    blocks = blocks[:1] + [exchange(blocks[j], j * line) for j in range(1, SLICES)]
 
     pairs, send = lax.optimization_barrier((pairs, cot))
     pairs = [pairs, exchange(pairs, 1)]
@@ -321,52 +305,49 @@
         send = lax.dynamic_slice_in_dim(send, (1 - half) * part, part, axis=1)
     other = exchange(send, 1)
 
-    near = [[jnp.concatenate(blocks[i : i + 2], axis=0)] for i in range(0, SLICES, 2)]
+    y, cuts[2], cuts[3] = lax.optimization_barrier((y, cuts[2], cuts[3]))
+    ys = [jnp.concatenate([y] + [exchange(y, j * line) for j in range(1, SLICES)], axis=0)]
+    xs = [[jnp.concatenate(cuts[:2], axis=0)], [jnp.concatenate(cuts[2:], axis=0)]]
     step = 2
     while step < line:
-        near = [side + [exchange(b, step) for b in side] for side in near]
+        xs = [side + [exchange(b, step) for b in side] for side in xs]
+        ys = ys + [exchange(b, step) for b in ys]
         step *= 2
-    n = len(near[0])
     skip = lanes if groups == 2 else 0
-
-    far = [exchange(b[:, skip:], 1) for b in near[0]]
+    lines = [
+        (*near, *[exchange(b, 1) for b in near], y, exchange(y[:, skip:], 1))
+        for *near, y in zip(*xs, ys)
+    ]
+
     if n_dp == 1:
         work = [
-            pltpu.VMEM((4 * n * tok, share), BF16),
-            pltpu.VMEM((4 * n * tok, lanes), BF16),
-            pltpu.SemaphoreType.DMA((4 * n,)),
+            pltpu.VMEM((2 * SLICES * tok, share), BF16),
+            pltpu.VMEM((2 * SLICES * tok, lanes), BF16),
+            pltpu.SemaphoreType.DMA((6,)),
         ]
         [columns] = call(
-            functools.partial(columns_kernel, n),
-            [shape((lanes, share), F32)],
-            [HBM] * (2 * n),
-            work,
-            *near[0],
-            *far,
+            columns_kernel, [shape((lanes, share), F32)], [HBM] * 6, work, *lines[0]
         )
-        near[1], columns = lax.optimization_barrier((near[1], columns))
         zs = call(
-            functools.partial(z_kernel, n, low),
+            functools.partial(z_kernel, low),
             [shape((2 * tok, lanes), BF16)] * SLICES + [shape((rank, share), BF16)] * SLICES,
-            [VMEM] * 3 + [HBM] * (2 * n),
-            work[:2] + [pltpu.VMEM((lanes, share), BF16)] + work[2:],
+            [VMEM] * 5 + [HBM] * 6,
+            [pltpu.VMEM((lanes, share), BF16)] + work,
             columns,
-            near[0][0],
-            far[0],
-            *near[1],
-            *[exchange(b[:, skip:], 1) for b in near[1]],
+            *lines[0][:4],
+            *lines[1],
         )
     else:
-        far = [far, [exchange(b[:, skip:], 1) for b in near[1]]]
-        rows_all = jnp.concatenate(near[0] + far[0] + near[1] + far[1], axis=0)
-        columns = dot(rows_all[:, :lanes], rows_all[:, lanes:], 0, 0).astype(BF16)
+        left = jnp.concatenate([y for *_, a, b in lines for y in (a, b)], axis=0)
+        right = jnp.concatenate([x for row in lines for x in row[:4]], axis=0)
+        columns = dot(left, right, 0, 0).astype(BF16)
         zs, own = [], []
         for j in range(SLICES):
             here = slice(j % 2 * tok, (j % 2 + 1) * tok)
-            x = jnp.concatenate([near[j // 2][0][here], far[j // 2][0][here]], axis=0)
+            x = jnp.concatenate([lines[0][j // 2][here], lines[0][2 + j // 2][here]], axis=0)
             start = ((place ^ j) * low + lower) * rank
             own.append(lax.dynamic_slice_in_dim(columns, start, rank, axis=0))
-            zs.append(dot(x[:, lanes:], columns, 1, 1).astype(BF16))
+            zs.append(dot(x, columns, 1, 1).astype(BF16))
         zs = zs + own
     columns = zs[SLICES:]
     zs = list(zs[:1]) + [exchange(zs[j], j * line) for j in range(1, SLICES)]

time: 73.1 us -> 82.7 us (1.13)
  starting transfers between devices: 25.9 us -> 31.6 us
  Pallas kernels: 11.2 us -> 14.5 us
    ppermute x23 -> x29, starting transfers between devices: 25.9 us -> 31.6 us  [exchange(): return lax.ppermute(block, AXES, [(i, i ^ step) for i in range(count)])]
    pallas_call x7, Pallas kernels: 11.2 us -> 14.5 us  [call(): pl.pallas_call(body, out_shape=shapes, in_specs=spaces, out_specs=[VMEM]...]
    ppermute x23 -> x29, waiting for transfers between devices: 33.5 us -> 34.2 us  [exchange(): return lax.ppermute(block, AXES, [(i, i ^ step) for i in range(count)])]
  transfers between devices with their start and end apart: 23 -> 29, of which waited for: 18 -> 16; matrix products, arithmetic and copies ran while one was open for 2% -> 1% of each run, Pallas kernels for 6% -> 8%
where the time goes in v18:
time: 82.7 us; the launch traced here: 82.5 us
  waiting for transfers between devices  34.2 us (41%)
  starting transfers between devices  31.6 us (38%)
  Pallas kernels  14.5 us (18%)
  local copies, waits for them, and re-layouts  0.99 us (1%)
  between operations  0.89 us (1%)
    ppermute x29, waiting for transfers between devices, exchange(): return lax.ppermute(block, AXES, [(i, i ^ step) for i in range(count)])  34.2 us
    ppermute x29, starting transfers between devices, exchange(): return lax.ppermute(block, AXES, [(i, i ^ step) for i in range(count)])  31.6 us
    pallas_call x7, Pallas kernels, call(): pl.pallas_call(body, out_shape=shapes, in_specs=spaces, out_specs=[VMEM]...  14.5 us
  transfers between devices with their start and end apart: 29, of which 16 were waited for; matrix products, arithmetic and copies ran while one was open for 1% of the time, Pallas kernels for 8%

profile of v18, /device:TPU:0, one launch (start us, length us, event | category | flops | bytes accessed | tf_op | source)
XLA Modules:
  0.0 82.5 jit_solution(11869003643824395902)
XLA Ops:
  0.7 3.7 %shard_map.68 = (bf16[48,512]{1,0:T(8,128)(2,1)}, f32[16,48]{1,0:T(8,128)}) custom-call(bf16[384,2560]{1,0:T(8,128)(2,1)} %bitcast.20, f32[32,2560]{1,0:T(8,128)} %bitcast.27, s32[8,48]{1,0:T(8,128)} %bitcast.29, f32[8,48]{1,0:T(8,128)} %bitcast.30), custom_call_target="tpu_custom_call" | custom-call | flops 1 | bytes 1 | tf_op jit(solution)/shard_map/pallas_call | solution.py:43
  4.9 4.7 %collective-permute-start.2 = (bf16[48,896]{1,0:T(8,128)(2,1)S(1)}, bf16[48,896]{1,0:T(8,128)(2,1)S(1)}, u32[]{:S(2)}, u32[]{:S(2)}) collective-permute-start(bf16[48,896]{1,0:T(8,128)(2,1)S(1)} %get-tuple-element.60), channel_id=1, source_target_pairs={{0,12},{1,13},{2,14},{3,15},{4,8},{5,9},{6,10},{7,11},{8,4},{9,5},... | collective-permute-start | bytes 258056 | tf_op jit(solution)/shard_map/ppermute | solution.py:273
  10.3 2.8 %collective-permute-done.2 = bf16[48,896]{1,0:T(8,128)(2,1)S(1)} collective-permute-done((bf16[48,896]{1,0:T(8,128)(2,1)S(1)}, bf16[48,896]{1,0:T(8,128)(2,1)S(1)}, u32[]{:S(2)}, u32[]{:S(2)}) %collective-permute-start.2) | collective-permute-done | bytes 86048 | tf_op jit(solution)/shard_map/ppermute | solution.py:273
  13.2 4.3 %collective-permute-done.1 = bf16[48,896]{1,0:T(8,128)(2,1)S(1)} collective-permute-done((bf16[48,896]{1,0:T(8,128)(2,1)S(1)}, bf16[48,896]{1,0:T(8,128)(2,1)S(1)}, u32[]{:S(2)}, u32[]{:S(2)}) %collective-permute-start.1) | collective-permute-done | bytes 86048 | tf_op jit(solution)/shard_map/ppermute | solution.py:273
  17.5 2.5 %collective-permute-start.7 = (bf16[48,512]{1,0:T(8,128)(2,1)}, bf16[48,512]{1,0:T(8,128)(2,1)S(1)}, u32[]{:S(2)}, u32[]{:S(2)}) collective-permute-start(bf16[48,512]{1,0:T(8,128)(2,1)} %get-tuple-element.34), channel_id=1, source_target_pairs={{0,12},{1,13},{2,14},{3,15},{4,8},{5,9},{6,10},{7,11},{8,4},{9,5},... | collective-permute-start | bytes 147464 | tf_op jit(solution)/shard_map/ppermute | solution.py:273
  20.0 1.9 %collective-permute-start.5 = (bf16[48,512]{1,0:T(8,128)(2,1)}, bf16[48,512]{1,0:T(8,128)(2,1)S(1)}, u32[]{:S(2)}, u32[]{:S(2)}) collective-permute-start(bf16[48,512]{1,0:T(8,128)(2,1)} %get-tuple-element.34), channel_id=1, source_target_pairs={{0,4},{1,5},{2,6},{3,7},{4,0},{5,1},{6,2},{7,3},{8,12},{9,13},{10,... | collective-permute-start | bytes 147464 | tf_op jit(solution)/shard_map/ppermute | solution.py:273
  22.7 1.6 %collective-permute-done.5 = bf16[48,512]{1,0:T(8,128)(2,1)S(1)} collective-permute-done((bf16[48,512]{1,0:T(8,128)(2,1)}, bf16[48,512]{1,0:T(8,128)(2,1)S(1)}, u32[]{:S(2)}, u32[]{:S(2)}) %collective-permute-start.5) | collective-permute-done | bytes 49184 | tf_op jit(solution)/shard_map/ppermute | solution.py:273
  28.3 3.3 %collective-permute-done.10.refs_6_ = bf16[96,896]{1,0:T(8,128)(2,1)S(1)} collective-permute-done((bf16[96,896]{1,0:T(8,128)(2,1)S(1)}, bf16[96,896]{1,0:T(8,128)(2,1)S(1)}, u32[]{:S(2)}, u32[]{:S(2)}) %collective-permute-start.10) | collective-permute-done | bytes 172064 | tf_op jit(solution)/shard_map/ppermute | solution.py:273
  31.6 5.5 %collective-permute-done.9.refs_5_ = bf16[96,896]{1,0:T(8,128)(2,1)S(1)} collective-permute-done((bf16[96,896]{1,0:T(8,128)(2,1)S(1)}, bf16[96,896]{1,0:T(8,128)(2,1)S(1)}, u32[]{:S(2)}, u32[]{:S(2)}) %collective-permute-start.9) | collective-permute-done | bytes 172064 | tf_op jit(solution)/shard_map/ppermute | solution.py:273
  37.8 1.5 %shard_map.69.refs_0_ = f32[256,896]{1,0:T(8,128)S(1)} custom-call(bf16[96,896]{1,0:T(8,128)(2,1)S(1)} %pad_maximum_fusion.refs_0_.refs_1_, bf16[96,896]{1,0:T(8,128)(2,1)S(1)} %constant_dynamic-update-slice_fusion.refs_1_.refs_2_, bf16[96,896]{1,0:T(8,128)(2,1)S(1)} %collective-permute-done.3.refs_2_.refs_3_, ...), custom_call_target="tpu_custom_call" | custom-call | flops 1 | bytes 1 | tf_op jit(solution)/shard_map/pallas_call | solution.py:43
  39.3 1.9 %shard_map.70 = (bf16[96,256]{1,0:T(8,128)(2,1)S(1)}, bf16[96,256]{1,0:T(8,128)(2,1)S(1)}, bf16[96,256]{1,0:T(8,128)(2,1)S(1)}, bf16[96,256]{1,0:T(8,128)(2,1)S(...) custom-call(f32[256,896]{1,0:T(8,128)S(1)} %shard_map.69.refs_0_, ...), custom_call_target="tpu_custom_call" | custom-call | flops 1 | bytes 1 | tf_op jit(solution)/shard_map/pallas_call | solution.py:43
  41.3 2.0 %collective-permute-start.15 = (bf16[96,256]{1,0:T(8,128)(2,1)S(1)}, bf16[96,256]{1,0:T(8,128)(2,1)S(1)}, u32[]{:S(2)}, u32[]{:S(2)}) collective-permute-start(bf16[96,256]{1,0:T(8,128)(2,1)S(1)} %get-tuple-element.36), channel_id=1, source_target_pairs={{0,4},{1,5},{2,6},{3,7},{4,0},{5,1},{6,2},{7,3},{8,12},{9,13},{10,... | collective-permute-start | bytes 147464 | tf_op jit(solution)/shard_map/ppermute | solution.py:273
  44.2 1.6 %collective-permute-start.17 = (bf16[96,256]{1,0:T(8,128)(2,1)S(1)}, bf16[96,256]{1,0:T(8,128)(2,1)S(1)}, u32[]{:S(2)}, u32[]{:S(2)}) collective-permute-start(bf16[96,256]{1,0:T(8,128)(2,1)S(1)} %get-tuple-element.38), channel_id=1, source_target_pairs={{0,12},{1,13},{2,14},{3,15},{4,8},{5,9},{6,10},{7,11},{8,4},{9,5},... | collective-permute-start | bytes 147464 | tf_op jit(solution)/shard_map/ppermute | solution.py:273
  47.1 3.2 %collective-permute-done.16.z2 = bf16[96,256]{1,0:T(8,128)(2,1)S(1)} collective-permute-done((bf16[96,256]{1,0:T(8,128)(2,1)S(1)}, bf16[96,256]{1,0:T(8,128)(2,1)S(1)}, u32[]{:S(2)}, u32[]{:S(2)}) %collective-permute-start.16) | collective-permute-done | bytes 49184 | tf_op jit(solution)/shard_map/ppermute | solution.py:273
  50.3 3.3 %shard_map.72 = (bf16[128,1280]{1,0:T(8,128)(2,1)S(1)}, bf16[128,1280]{1,0:T(8,128)(2,1)S(1)}, bf16[128,1280]{1,0:T(8,128)(2,1)S(1)}, bf16[128,1280]{1,0:T(8,128)(2,1)S(1)}) custom-call(bf16[96,256]{1,0:T(8,128)(2,1)S(1)} %get-tuple-element.35.z0, bf16[96,256]{1,0:T(8,128)(2,1)S(1)} %collective-permute-done.15.z1, ...), custom_call_target="tpu_custom_call" | custom-call | flops 1 | bytes 1 | tf_op jit(solution)/shard_map/pallas_call | solution.py:43
  53.7 1.6 %collective-permute-start.20 = (bf16[4,32,1280]{2,1,0:T(8,128)(2,1)S(1)}, bf16[4,32,1280]{2,1,0:T(8,128)(2,1)S(1)}, u32[]{:S(2)}, u32[]{:S(2)}) collective-permute-start(bf16[4,32,1280]{2,1,0:T(8,128)(2,1)S(1)} %bitcast.26), channel_id=1, source_target_pairs={{0,2},{1,3},{2,0},{3,1},{4,6},{5,7},{6,4},{7,5},{8,10},{9,11},{10,... | collective-permute-start | bytes 983048 | tf_op jit(solution)/shard_map/ppermute | solution.py:273
  57.7 1.9 %collective-permute-start.23 = (bf16[32,896]{1,0:T(8,128)(2,1)S(1)}, bf16[32,896]{1,0:T(8,128)(2,1)S(1)}, u32[]{:S(2)}, u32[]{:S(2)}) collective-permute-start(bf16[32,896]{1,0:T(8,128)(2,1)S(1)} %get-tuple-element.46), channel_id=1, source_target_pairs={{0,12},{1,13},{2,14},{3,15},{4,8},{5,9},{6,10},{7,11},{8,4},{9,5},... | collective-permute-start | bytes 172040 | tf_op jit(solution)/shard_map/ppermute | solution.py:273
  60.2 2.5 %collective-permute-done.22.c2 = bf16[32,896]{1,0:T(8,128)(2,1)S(1)} collective-permute-done((bf16[32,896]{1,0:T(8,128)(2,1)S(1)}, bf16[32,896]{1,0:T(8,128)(2,1)S(1)}, u32[]{:S(2)}, u32[]{:S(2)}) %collective-permute-start.22) | collective-permute-done | bytes 57376 | tf_op jit(solution)/shard_map/ppermute | solution.py:273
  64.2 1.6 %collective-permute-start.25 = (bf16[2,32,1280]{2,1,0:T(8,128)(2,1)S(1)}, bf16[2,32,1280]{2,1,0:T(8,128)(2,1)S(1)}, u32[]{:S(2)}, u32[]{:S(2)}) collective-permute-start(bf16[2,32,1280]{2,1,0:T(8,128)(2,1)S(1)} %pad_maximum_fusion.1), channel_id=1, source_target_pairs={{0,4},{1,5},{2,6},{3,7},{4,0},{5,1},{6,2},{7,3},{8,12},{9,13},{10,... | collective-permute-start | bytes 491528 | tf_op jit(solution)/shard_map/ppermute | solution.py:273
  65.8 2.7 %shard_map.73 = (f32[32,32]{1,0:T(8,128)S(1)}, f32[32,3584]{1,0:T(8,128)}) custom-call(bf16[32,896]{1,0:T(8,128)(2,1)S(1)} %get-tuple-element.47.c0, bf16[32,896]{1,0:T(8,128)(2,1)S(1)} %collective-permute-done.21.c1, bf16[32,896]{1,0:T(8,128)(2,1)S(1)} %collective-permute-done.22.c2, bf16[32,896]{1,0:T(8,128)(2,1)S(1)} %collective-permute-done.23.c3), custom_call_target="tpu_custom_call" | custom-call | flops 1 | bytes 1 | tf_op jit(solution)/shard_map/pallas_call | solution.py:43
  69.7 1.9 %collective-permute-start.27 = (bf16[2,32,1280]{2,1,0:T(8,128)(2,1)S(1)}, bf16[2,32,1280]{2,1,0:T(8,128)(2,1)S(1)}, u32[]{:S(2)}, u32[]{:S(2)}) collective-permute-start(bf16[2,32,1280]{2,1,0:T(8,128)(2,1)S(1)} %pad_maximum_fusion.2), channel_id=1, source_target_pairs={{0,4},{1,5},{2,6},{3,7},{4,0},{5,1},{6,2},{7,3},{8,12},{9,13},{10,... | collective-permute-start | bytes 491528 | tf_op jit(solution)/shard_map/ppermute | solution.py:273
  72.3 3.7 %collective-permute-done.27 = bf16[2,32,1280]{2,1,0:T(8,128)(2,1)S(1)} collective-permute-done((bf16[2,32,1280]{2,1,0:T(8,128)(2,1)S(1)}, bf16[2,32,1280]{2,1,0:T(8,128)(2,1)S(1)}, u32[]{:S(2)}, u32[]{:S(2)}) %collective-permute-start.27) | collective-permute-done | bytes 163872 | tf_op jit(solution)/shard_map/ppermute | solution.py:273
  76.1 1.9 %collective-permute-start.28 = (bf16[32,1280]{1,0:T(8,128)(2,1)S(1)}, bf16[32,1280]{1,0:T(8,128)(2,1)S(1)}, u32[]{:S(2)}, u32[]{:S(2)}) collective-permute-start(bf16[32,1280]{1,0:T(8,128)(2,1)S(1)} %get-tuple-element.72), channel_id=1, source_target_pairs={{0,8},{1,9},{2,10},{3,11},{4,12},{5,13},{6,14},{7,15},{8,0},{9,1},... | collective-permute-start | bytes 245768 | tf_op jit(solution)/shard_map/ppermute | solution.py:273
  79.5 2.0 %collective-permute-done.28.refs_3_ = bf16[32,1280]{1,0:T(8,128)(2,1)S(1)} collective-permute-done((bf16[32,1280]{1,0:T(8,128)(2,1)S(1)}, bf16[32,1280]{1,0:T(8,128)(2,1)S(1)}, u32[]{:S(2)}, u32[]{:S(2)}) %collective-permute-start.28) | collective-permute-done | bytes 81952 | tf_op jit(solution)/shard_map/ppermute | solution.py:273
  (67 shorter events, 17.9 us)
Async XLA Ops:
  4.4 45.9 %collective-permute-start.19 = (bf16[384,2560]{1,0:T(8,128)(2,1)S(1)}, bf16[384,2560]{1,0:T(8,128)(2,1)}, u32[]{:S(2)}, u32[]{:S(2)}) collective-permute-start(bf16[384,2560]{1,0:T(8,128)(2,1)S(1)} %bitcast.21), channel_id=1, source_target_pairs={{0,1},{1,0},{2,3},{3,2},{4,5},{5,4},{6,7},{7,6},{8,9},{9,8},{10,11... | collective-permute-start | bytes 5898248 | tf_op jit(solution)/shard_map/ppermute | solution.py:273
  4.9 8.2 %collective-permute-start.2 = (bf16[48,896]{1,0:T(8,128)(2,1)S(1)}, bf16[48,896]{1,0:T(8,128)(2,1)S(1)}, u32[]{:S(2)}, u32[]{:S(2)}) collective-permute-start(bf16[48,896]{1,0:T(8,128)(2,1)S(1)} %get-tuple-element.60), channel_id=1, source_target_pairs={{0,12},{1,13},{2,14},{3,15},{4,8},{5,9},{6,10},{7,11},{8,4},{9,5},... | collective-permute-start | bytes 258056 | tf_op jit(solution)/shard_map/ppermute | solution.py:273
  9.7 7.8 %collective-permute-start.1 = (bf16[48,896]{1,0:T(8,128)(2,1)S(1)}, bf16[48,896]{1,0:T(8,128)(2,1)S(1)}, u32[]{:S(2)}, u32[]{:S(2)}) collective-permute-start(bf16[48,896]{1,0:T(8,128)(2,1)S(1)} %get-tuple-element.63), channel_id=1, source_target_pairs={{0,8},{1,9},{2,10},{3,11},{4,12},{5,13},{6,14},{7,15},{8,0},{9,1},... | collective-permute-start | bytes 258056 | tf_op jit(solution)/shard_map/ppermute | solution.py:273
  9.7 17.1 %collective-permute-start = (bf16[48,896]{1,0:T(8,128)(2,1)S(1)}, bf16[48,896]{1,0:T(8,128)(2,1)S(1)}, u32[]{:S(2)}, u32[]{:S(2)}) collective-permute-start(bf16[48,896]{1,0:T(8,128)(2,1)S(1)} %get-tuple-element.61), channel_id=1, source_target_pairs={{0,4},{1,5},{2,6},{3,7},{4,0},{5,1},{6,2},{7,3},{8,12},{9,13},{10,... | collective-permute-start | bytes 258056 | tf_op jit(solution)/shard_map/ppermute | solution.py:273
  17.5 8.3 %collective-permute-start.7 = (bf16[48,512]{1,0:T(8,128)(2,1)}, bf16[48,512]{1,0:T(8,128)(2,1)S(1)}, u32[]{:S(2)}, u32[]{:S(2)}) collective-permute-start(bf16[48,512]{1,0:T(8,128)(2,1)} %get-tuple-element.34), channel_id=1, source_target_pairs={{0,12},{1,13},{2,14},{3,15},{4,8},{5,9},{6,10},{7,11},{8,4},{9,5},... | collective-permute-start | bytes 147464 | tf_op jit(solution)/shard_map/ppermute | solution.py:273
  20.0 5.8 %collective-permute-start.6 = (bf16[48,512]{1,0:T(8,128)(2,1)}, bf16[48,512]{1,0:T(8,128)(2,1)S(1)}, u32[]{:S(2)}, u32[]{:S(2)}) collective-permute-start(bf16[48,512]{1,0:T(8,128)(2,1)} %get-tuple-element.34), channel_id=1, source_target_pairs={{0,8},{1,9},{2,10},{3,11},{4,12},{5,13},{6,14},{7,15},{8,0},{9,1},... | collective-permute-start | bytes 147464 | tf_op jit(solution)/shard_map/ppermute | solution.py:273
  20.0 4.3 %collective-permute-start.5 = (bf16[48,512]{1,0:T(8,128)(2,1)}, bf16[48,512]{1,0:T(8,128)(2,1)S(1)}, u32[]{:S(2)}, u32[]{:S(2)}) collective-permute-start(bf16[48,512]{1,0:T(8,128)(2,1)} %get-tuple-element.34), channel_id=1, source_target_pairs={{0,4},{1,5},{2,6},{3,7},{4,0},{5,1},{6,2},{7,3},{8,12},{9,13},{10,... | collective-permute-start | bytes 147464 | tf_op jit(solution)/shard_map/ppermute | solution.py:273
  24.3 7.3 %collective-permute-start.10 = (bf16[96,896]{1,0:T(8,128)(2,1)S(1)}, bf16[96,896]{1,0:T(8,128)(2,1)S(1)}, u32[]{:S(2)}, u32[]{:S(2)}) collective-permute-start(bf16[96,896]{1,0:T(8,128)(2,1)S(1)} %constant_dynamic-update-slice_fusion.refs_1_.refs_2_), channel_id=1, source_target_pairs={{0,2},{1,3},{2,0},{3,1},{4,6},{5,7},{6,4},{7,5},{8,10},{9,11},{10,... | collective-permute-start | bytes 516104 | tf_op jit(solution)/shard_map/ppermute | solution.py:273
  25.9 11.3 %collective-permute-start.13 = (bf16[192,512]{1,0:T(8,128)(2,1)S(1)}, bf16[192,512]{1,0:T(8,128)(2,1)S(1)}, u32[]{:S(2)}, u32[]{:S(2)}) collective-permute-start(bf16[192,512]{1,0:T(8,128)(2,1)S(1)} %constant_dynamic-update-slice_fusion.2.refs_4_), channel_id=1, source_target_pairs={{0,2},{1,3},{2,0},{3,1},{4,6},{5,7},{6,4},{7,5},{8,10},{9,11},{10,... | collective-permute-start | bytes 589832 | tf_op jit(solution)/shard_map/ppermute | solution.py:273
  26.9 10.3 %collective-permute-start.9 = (bf16[96,896]{1,0:T(8,128)(2,1)S(1)}, bf16[96,896]{1,0:T(8,128)(2,1)S(1)}, u32[]{:S(2)}, u32[]{:S(2)}) collective-permute-start(bf16[96,896]{1,0:T(8,128)(2,1)S(1)} %pad_maximum_fusion.refs_0_.refs_1_), channel_id=1, source_target_pairs={{0,2},{1,3},{2,0},{3,1},{4,6},{5,7},{6,4},{7,5},{8,10},{9,11},{10,... | collective-permute-start | bytes 516104 | tf_op jit(solution)/shard_map/ppermute | solution.py:273
  28.1 9.5 %collective-permute-start.4 = (bf16[96,896]{1,0:T(8,128)(2,1)S(1)}, bf16[96,896]{1,0:T(8,128)(2,1)S(1)}, u32[]{:S(2)}, u32[]{:S(2)}) collective-permute-start(bf16[96,896]{1,0:T(8,128)(2,1)S(1)} %constant_dynamic-update-slice_fusion.refs_1_.refs_2_), channel_id=1, source_target_pairs={{0,1},{1,0},{2,3},{3,2},{4,5},{5,4},{6,7},{7,6},{8,9},{9,8},{10,11... | collective-permute-start | bytes 516104 | tf_op jit(solution)/shard_map/ppermute | solution.py:273
  31.6 6.1 %collective-permute-start.3 = (bf16[96,896]{1,0:T(8,128)(2,1)S(1)}, bf16[96,896]{1,0:T(8,128)(2,1)S(1)}, u32[]{:S(2)}, u32[]{:S(2)}) collective-permute-start(bf16[96,896]{1,0:T(8,128)(2,1)S(1)} %pad_maximum_fusion.refs_0_.refs_1_), channel_id=1, source_target_pairs={{0,1},{1,0},{2,3},{3,2},{4,5},{5,4},{6,7},{7,6},{8,9},{9,8},{10,11... | collective-permute-start | bytes 516104 | tf_op jit(solution)/shard_map/ppermute | solution.py:273
  41.3 5.9 %collective-permute-start.15 = (bf16[96,256]{1,0:T(8,128)(2,1)S(1)}, bf16[96,256]{1,0:T(8,128)(2,1)S(1)}, u32[]{:S(2)}, u32[]{:S(2)}) collective-permute-start(bf16[96,256]{1,0:T(8,128)(2,1)S(1)} %get-tuple-element.36), channel_id=1, source_target_pairs={{0,4},{1,5},{2,6},{3,7},{4,0},{5,1},{6,2},{7,3},{8,12},{9,13},{10,... | collective-permute-start | bytes 147464 | tf_op jit(solution)/shard_map/ppermute | solution.py:273
  43.3 7.1 %collective-permute-start.16 = (bf16[96,256]{1,0:T(8,128)(2,1)S(1)}, bf16[96,256]{1,0:T(8,128)(2,1)S(1)}, u32[]{:S(2)}, u32[]{:S(2)}) collective-permute-start(bf16[96,256]{1,0:T(8,128)(2,1)S(1)} %get-tuple-element.37), channel_id=1, source_target_pairs={{0,8},{1,9},{2,10},{3,11},{4,12},{5,13},{6,14},{7,15},{8,0},{9,1},... | collective-permute-start | bytes 147464 | tf_op jit(solution)/shard_map/ppermute | solution.py:273
  44.2 6.2 %collective-permute-start.17 = (bf16[96,256]{1,0:T(8,128)(2,1)S(1)}, bf16[96,256]{1,0:T(8,128)(2,1)S(1)}, u32[]{:S(2)}, u32[]{:S(2)}) collective-permute-start(bf16[96,256]{1,0:T(8,128)(2,1)S(1)} %get-tuple-element.38), channel_id=1, source_target_pairs={{0,12},{1,13},{2,14},{3,15},{4,8},{5,9},{6,10},{7,11},{8,4},{9,5},... | collective-permute-start | bytes 147464 | tf_op jit(solution)/shard_map/ppermute | solution.py:273
  53.7 10.4 %collective-permute-start.20 = (bf16[4,32,1280]{2,1,0:T(8,128)(2,1)S(1)}, bf16[4,32,1280]{2,1,0:T(8,128)(2,1)S(1)}, u32[]{:S(2)}, u32[]{:S(2)}) collective-permute-start(bf16[4,32,1280]{2,1,0:T(8,128)(2,1)S(1)} %bitcast.26), channel_id=1, source_target_pairs={{0,2},{1,3},{2,0},{3,1},{4,6},{5,7},{6,4},{7,5},{8,10},{9,11},{10,... | collective-permute-start | bytes 983048 | tf_op jit(solution)/shard_map/ppermute | solution.py:273
  55.2 4.9 %collective-permute-start.21 = (bf16[32,896]{1,0:T(8,128)(2,1)S(1)}, bf16[32,896]{1,0:T(8,128)(2,1)S(1)}, u32[]{:S(2)}, u32[]{:S(2)}) collective-permute-start(bf16[32,896]{1,0:T(8,128)(2,1)S(1)} %get-tuple-element.44), channel_id=1, source_target_pairs={{0,4},{1,5},{2,6},{3,7},{4,0},{5,1},{6,2},{7,3},{8,12},{9,13},{10,... | collective-permute-start | bytes 172040 | tf_op jit(solution)/shard_map/ppermute | solution.py:273
  56.5 6.2 %collective-permute-start.22 = (bf16[32,896]{1,0:T(8,128)(2,1)S(1)}, bf16[32,896]{1,0:T(8,128)(2,1)S(1)}, u32[]{:S(2)}, u32[]{:S(2)}) collective-permute-start(bf16[32,896]{1,0:T(8,128)(2,1)S(1)} %get-tuple-element.45), channel_id=1, source_target_pairs={{0,8},{1,9},{2,10},{3,11},{4,12},{5,13},{6,14},{7,15},{8,0},{9,1},... | collective-permute-start | bytes 172040 | tf_op jit(solution)/shard_map/ppermute | solution.py:273
  57.7 6.1 %collective-permute-start.23 = (bf16[32,896]{1,0:T(8,128)(2,1)S(1)}, bf16[32,896]{1,0:T(8,128)(2,1)S(1)}, u32[]{:S(2)}, u32[]{:S(2)}) collective-permute-start(bf16[32,896]{1,0:T(8,128)(2,1)S(1)} %get-tuple-element.46), channel_id=1, source_target_pairs={{0,12},{1,13},{2,14},{3,15},{4,8},{5,9},{6,10},{7,11},{8,4},{9,5},... | collective-permute-start | bytes 172040 | tf_op jit(solution)/shard_map/ppermute | solution.py:273
  59.6 9.7 %collective-permute-start.24 = (bf16[4,32,1280]{2,1,0:T(8,128)(2,1)S(1)}, bf16[4,32,1280]{2,1,0:T(8,128)(2,1)S(1)}, u32[]{:S(2)}, u32[]{:S(2)}) collective-permute-start(bf16[4,32,1280]{2,1,0:T(8,128)(2,1)S(1)} %bitcast.25), channel_id=1, source_target_pairs={{0,2},{1,3},{2,0},{3,1},{4,6},{5,7},{6,4},{7,5},{8,10},{9,11},{10,... | collective-permute-start | bytes 983048 | tf_op jit(solution)/shard_map/ppermute | solution.py:273
  64.2 5.4 %collective-permute-start.25 = (bf16[2,32,1280]{2,1,0:T(8,128)(2,1)S(1)}, bf16[2,32,1280]{2,1,0:T(8,128)(2,1)S(1)}, u32[]{:S(2)}, u32[]{:S(2)}) collective-permute-start(bf16[2,32,1280]{2,1,0:T(8,128)(2,1)S(1)} %pad_maximum_fusion.1), channel_id=1, source_target_pairs={{0,4},{1,5},{2,6},{3,7},{4,0},{5,1},{6,2},{7,3},{8,12},{9,13},{10,... | collective-permute-start | bytes 491528 | tf_op jit(solution)/shard_map/ppermute | solution.py:273
  69.7 6.3 %collective-permute-start.27 = (bf16[2,32,1280]{2,1,0:T(8,128)(2,1)S(1)}, bf16[2,32,1280]{2,1,0:T(8,128)(2,1)S(1)}, u32[]{:S(2)}, u32[]{:S(2)}) collective-permute-start(bf16[2,32,1280]{2,1,0:T(8,128)(2,1)S(1)} %pad_maximum_fusion.2), channel_id=1, source_target_pairs={{0,4},{1,5},{2,6},{3,7},{4,0},{5,1},{6,2},{7,3},{8,12},{9,13},{10,... | collective-permute-start | bytes 491528 | tf_op jit(solution)/shard_map/ppermute | solution.py:273
  71.7 7.8 %collective-permute-start.26 = (bf16[32,1280]{1,0:T(8,128)(2,1)S(1)}, bf16[32,1280]{1,0:T(8,128)(2,1)S(1)}, u32[]{:S(2)}, u32[]{:S(2)}) collective-permute-start(bf16[32,1280]{1,0:T(8,128)(2,1)S(1)} %get-tuple-element.74), channel_id=1, source_target_pairs={{0,8},{1,9},{2,10},{3,11},{4,12},{5,13},{6,14},{7,15},{8,0},{9,1},... | collective-permute-start | bytes 245768 | tf_op jit(solution)/shard_map/ppermute | solution.py:273
  76.1 5.4 %collective-permute-start.28 = (bf16[32,1280]{1,0:T(8,128)(2,1)S(1)}, bf16[32,1280]{1,0:T(8,128)(2,1)S(1)}, u32[]{:S(2)}, u32[]{:S(2)}) collective-permute-start(bf16[32,1280]{1,0:T(8,128)(2,1)S(1)} %get-tuple-element.72), channel_id=1, source_target_pairs={{0,8},{1,9},{2,10},{3,11},{4,12},{5,13},{6,14},{7,15},{8,0},{9,1},... | collective-permute-start | bytes 245768 | tf_op jit(solution)/shard_map/ppermute | solution.py:273
  (8 other events, 24.6 us)

commit v19 on v17

--- a/solution.py
+++ b/solution.py
@@ -85,18 +85,18 @@
 def first_kernel(groups, tokens, cot_at, sketch_at, ids_at, probs_at, *refs):
     outs, pairs, (cot, sketch, ids, probs, sems, x_sems) = refs[:SLICES], refs[SLICES], refs[5:]
     core, _, place, _ = position()
-    rows, hidden = cot.shape
+    rows = cot.shape[0]
     tok = pairs.shape[1]
     top = rows // tok
     rank = sketch.shape[0]
     share = tokens.shape[1] // SLICES
     lanes = (outs[0].shape[1] - share) // groups
-    parts = 5
-    piece = hidden // parts
+    parts = 4
+    piece = rows // parts
     sources = [(ids_at, ids), (probs_at, probs), (sketch_at, sketch)]
     for i in range(parts):
         cut = pl.ds(i * piece, piece)
-        sources.append((cot_at.at[:, cut], cot.at[:, cut]))
+        sources.append((cot_at.at[cut], cot.at[cut]))
     copies = load(sources, sems)
     sources = []
     for j, out in enumerate(outs):
@@ -110,11 +110,12 @@
     names, weights = pair_columns(pairs[:top], pairs[top:])
     copies[2].wait()
     both = jnp.concatenate(pieces(sketch[...], 2), axis=0)
-    pair = 0.0
-    for i in range(parts):
+    pair = []
+    for i in range(0, parts, 2):
         copies[3 + i].wait()
-        here = slice(i * piece, (i + 1) * piece)
-        pair = pair + dot(cot[:, here], both[:, here], 1, 1)
+        copies[4 + i].wait()
+        pair.append(dot(cot[i * piece : (i + 2) * piece], both, 1, 1))
+    pair = jnp.concatenate(pair, axis=0)
     pair = (pair[:, :rank] + pair[:, rank:]) * weights
     lane = iota((rank, lanes), 1)
     tiled = dot(pair.astype(BF16), (iota((rank, lanes), 0) == lane % rank).astype(BF16), 1, 0)
@@ -151,24 +152,24 @@
     out[...] = dot(y[...], x[...], 0, 0)
 
 
-def z_kernel(n, low, part, near_x, far_x, *refs):
+def z_kernel(n, low, part, near_a, near_b, far_a, far_b, *refs):
     outs, (x, y, columns, sems) = refs[2 * n : -4], refs[-4:]
     _, lower, place, _ = position()
     gather(refs[:n], refs[n : 2 * n], x, y, sems)
     rank = columns.shape[0] // (SLICES * low)
     share = x.shape[1]
     lanes = y.shape[1]
-    rows = near_x.shape[0]
+    rows = near_a.shape[0]
     tok = rows // 2
     total = (part[...] + dot(y[...], x[...], 0, 0)).astype(BF16)
     columns[...] = total
-    own = jnp.concatenate([near_x[:, lanes : lanes + share], far_x[:, :share]], axis=0)
-    halves = [dot(own, total, 1, 1), dot(x[: 2 * rows], total, 1, 1)]
+    own = [near_a[:, lanes : lanes + share], near_b[:, lanes : lanes + share]]
+    own = jnp.concatenate(own + [far_a[:, :share], far_b[:, :share]], axis=0)
+    z = dot(own, total, 1, 1).astype(BF16)
     for j in range(SLICES):
-        half = halves[j // 2].astype(BF16)
-        start = j % 2 * tok
-        outs[j][:tok] = half[start : start + tok]
-        outs[j][tok:] = half[rows + start : rows + start + tok]
+        for core in range(2):
+            start = 2 * core * rows + j * tok
+            outs[j][core * tok : (core + 1) * tok] = z[start : start + tok]
         expert = (place ^ j) * low + lower
         outs[SLICES + j][...] = columns[pl.ds(pl.multiple_of(expert * rank, rank), rank)]
 
@@ -326,44 +327,50 @@
     while step < line:
         near = [side + [exchange(b, step) for b in side] for side in near]
         step *= 2
-    n = len(near[0])
     skip = lanes if groups == 2 else 0
 
-    far = [exchange(b[:, skip:], 1) for b in near[0]]
+    first = [near[0][0], near[1][0]]
+    late = near[0][1:] + near[1][1:]
+    far = [exchange(b[:, skip:], 1) for b in first]
     if n_dp == 1:
-        work = [
-            pltpu.VMEM((4 * n * tok, share), BF16),
-            pltpu.VMEM((4 * n * tok, lanes), BF16),
-            pltpu.SemaphoreType.DMA((4 * n,)),
-        ]
         [columns] = call(
-            functools.partial(columns_kernel, n),
+            functools.partial(columns_kernel, 2),
             [shape((lanes, share), F32)],
-            [HBM] * (2 * n),
-            work,
-            *near[0],
+            [HBM] * 4,
+            [
+                pltpu.VMEM((8 * tok, share), BF16),
+                pltpu.VMEM((8 * tok, lanes), BF16),
+                pltpu.SemaphoreType.DMA((8,)),
+            ],
+            *first,
             *far,
         )
-        near[1], columns = lax.optimization_barrier((near[1], columns))
+        late[-1], columns = lax.optimization_barrier((late[-1], columns))
+        count_late = len(late)
         zs = call(
-            functools.partial(z_kernel, n, low),
+            functools.partial(z_kernel, count_late, low),
             [shape((2 * tok, lanes), BF16)] * SLICES + [shape((rank, share), BF16)] * SLICES,
-            [VMEM] * 3 + [HBM] * (2 * n),
-            work[:2] + [pltpu.VMEM((lanes, share), BF16)] + work[2:],
+            [VMEM] * 5 + [HBM] * (2 * count_late),
+            [
+                pltpu.VMEM((4 * count_late * tok, share), BF16),
+                pltpu.VMEM((4 * count_late * tok, lanes), BF16),
+                pltpu.VMEM((lanes, share), BF16),
+                pltpu.SemaphoreType.DMA((4 * count_late,)),
+            ],
             columns,
-            near[0][0],
-            far[0],
-            *near[1],
-            *[exchange(b[:, skip:], 1) for b in near[1]],
+            *first,
+            *far,
+            *late,
+            *[exchange(b[:, skip:], 1) for b in late],
         )
     else:
-        far = [far, [exchange(b[:, skip:], 1) for b in near[1]]]
-        rows_all = jnp.concatenate(near[0] + far[0] + near[1] + far[1], axis=0)
+        far += [exchange(b[:, skip:], 1) for b in late]
+        rows_all = jnp.concatenate(first + late + far, axis=0)
         columns = dot(rows_all[:, :lanes], rows_all[:, lanes:], 0, 0).astype(BF16)
         zs, own = [], []
         for j in range(SLICES):
             here = slice(j % 2 * tok, (j % 2 + 1) * tok)
-            x = jnp.concatenate([near[j // 2][0][here], far[j // 2][0][here]], axis=0)
+            x = jnp.concatenate([first[j // 2][here], far[j // 2][here]], axis=0)
             start = ((place ^ j) * low + lower) * rank
             own.append(lax.dynamic_slice_in_dim(columns, start, rank, axis=0))
             zs.append(dot(x[:, lanes:], columns, 1, 1).astype(BF16))

time: 73.1 us -> 78.2 us (1.070)
  waiting for transfers between devices: 33.5 us -> 40 us
  starting transfers between devices: 25.9 us -> 24.5 us
    ppermute x23, waiting for transfers between devices: 33.5 us -> 40 us  [exchange(): return lax.ppermute(block, AXES, [(i, i ^ step) for i in range(count)])]
    ppermute x23, starting transfers between devices: 25.9 us -> 24.5 us  [exchange(): return lax.ppermute(block, AXES, [(i, i ^ step) for i in range(count)])]
  transfers between devices with their start and end apart: 23 -> 23, of which waited for: 18 -> 16; matrix products, arithmetic and copies ran while one was open for 2% -> 2% of each run, Pallas kernels for 6% -> 6%
where the time goes in v19:
time: 78.2 us; the launch traced here: 78 us
  waiting for transfers between devices  40 us (51%)
  starting transfers between devices  24.5 us (31%)
  Pallas kernels  11.3 us (14%)
  local copies, waits for them, and re-layouts  1.14 us (1%)
  between operations  0.85 us (1%)
    ppermute x23, waiting for transfers between devices, exchange(): return lax.ppermute(block, AXES, [(i, i ^ step) for i in range(count)])  40 us
    ppermute x23, starting transfers between devices, exchange(): return lax.ppermute(block, AXES, [(i, i ^ step) for i in range(count)])  24.5 us
    pallas_call x7, Pallas kernels, call(): pl.pallas_call(body, out_shape=shapes, in_specs=spaces, out_specs=[VMEM]...  11.3 us
  transfers between devices with their start and end apart: 23, of which 16 were waited for; matrix products, arithmetic and copies ran while one was open for 2% of the time, Pallas kernels for 6%

profile of v19, /device:TPU:0, one launch (start us, length us, event | category | flops | bytes accessed | tf_op | source)
XLA Modules:
  0.0 78.0 jit_solution(12030999029010566983)
XLA Ops:
  0.6 4.0 %shard_map.68 = (bf16[48,1408]{1,0:T(8,128)(2,1)}, bf16[48,1408]{1,0:T(8,128)(2,1)}, bf16[48,1408]{1,0:T(8,128)(2,1)}, bf16[48,1408]{1,0:T(8,128)(2,1)}, f32[16,48]{1,0:T(8,128)}) custom-call(bf16[48,3584]{1,0:T(8,128)(2,1)} %tokens.1, bf16[384,2560]{1,0:T(8,128)(2,1)} %bitcast.20, f32[32,2560]{1,0:T(8,128)} %bitcast.27, s32[8,48]{1,0:T(8,128)} %bitcast.29, ...), custom_call_target="tpu_custom_call" | custom-call | flops 1 | bytes 1 | tf_op jit(solution)/shard_map/pallas_call | solution.py:43
  5.1 2.6 %collective-permute-start.3 = (bf16[48,1408]{1,0:T(8,128)(2,1)}, bf16[48,1408]{1,0:T(8,128)(2,1)S(1)}, u32[]{:S(2)}, u32[]{:S(2)}) collective-permute-start(bf16[48,1408]{1,0:T(8,128)(2,1)} %get-tuple-element.36), channel_id=1, source_target_pairs={{0,4},{1,5},{2,6},{3,7},{4,0},{5,1},{6,2},{7,3},{8,12},{9,13},{10,... | collective-permute-start | bytes 405512 | tf_op jit(solution)/shard_map/ppermute | solution.py:292
  7.8 2.6 %collective-permute-start = (bf16[48,1408]{1,0:T(8,128)(2,1)}, bf16[48,1408]{1,0:T(8,128)(2,1)S(1)}, u32[]{:S(2)}, u32[]{:S(2)}) collective-permute-start(bf16[48,1408]{1,0:T(8,128)(2,1)} %get-tuple-element.33), channel_id=1, source_target_pairs={{0,8},{1,9},{2,10},{3,11},{4,12},{5,13},{6,14},{7,15},{8,0},{9,1},... | collective-permute-start | bytes 405512 | tf_op jit(solution)/shard_map/ppermute | solution.py:292
  11.3 9.9 %collective-permute-done = bf16[48,1408]{1,0:T(8,128)(2,1)S(1)} collective-permute-done((bf16[48,1408]{1,0:T(8,128)(2,1)}, bf16[48,1408]{1,0:T(8,128)(2,1)S(1)}, u32[]{:S(2)}, u32[]{:S(2)}) %collective-permute-start) | collective-permute-done | bytes 135200 | tf_op jit(solution)/shard_map/ppermute | solution.py:292
  21.2 1.6 %collective-permute-start.2 = (bf16[96,1408]{1,0:T(8,128)(2,1)S(1)}, bf16[96,1408]{1,0:T(8,128)(2,1)S(1)}, u32[]{:S(2)}, u32[]{:S(2)}) collective-permute-start(bf16[96,1408]{1,0:T(8,128)(2,1)S(1)} %constant_dynamic-update-slice_fusion.refs_1_.near_b), channel_id=1, source_target_pairs={{0,2},{1,3},{2,0},{3,1},{4,6},{5,7},{6,4},{7,5},{8,10},{9,11},{10,... | collective-permute-start | bytes 811016 | tf_op jit(solution)/shard_map/ppermute | solution.py:292
  24.0 1.0 %collective-permute-done.4.refs_2_.far_a = bf16[96,1152]{1,0:T(8,128)(2,1)S(1)} collective-permute-done((bf16[96,1152]{1,0:T(8,128)(2,1)S(1)}, bf16[96,1152]{1,0:T(8,128)(2,1)S(1)}, u32[]{:S(2)}, u32[]{:S(2)}) %collective-permute-start.4) | collective-permute-done | bytes 221216 | tf_op jit(solution)/shard_map/ppermute | solution.py:292
  25.9 4.8 %collective-permute-done.2.refs_1_ = bf16[96,1408]{1,0:T(8,128)(2,1)S(1)} collective-permute-done((bf16[96,1408]{1,0:T(8,128)(2,1)S(1)}, bf16[96,1408]{1,0:T(8,128)(2,1)S(1)}, u32[]{:S(2)}, u32[]{:S(2)}) %collective-permute-start.2) | collective-permute-done | bytes 270368 | tf_op jit(solution)/shard_map/ppermute | solution.py:292
  30.8 3.3 %collective-permute-done.6.refs_0_ = bf16[96,1408]{1,0:T(8,128)(2,1)S(1)} collective-permute-done((bf16[96,1408]{1,0:T(8,128)(2,1)S(1)}, bf16[96,1408]{1,0:T(8,128)(2,1)S(1)}, u32[]{:S(2)}, u32[]{:S(2)}) %collective-permute-start.6) | collective-permute-done | bytes 270368 | tf_op jit(solution)/shard_map/ppermute | solution.py:292
  34.2 1.5 %collective-permute-done.7.refs_2_ = bf16[96,1152]{1,0:T(8,128)(2,1)S(1)} collective-permute-done((bf16[96,1152]{1,0:T(8,128)(2,1)S(1)}, bf16[96,1152]{1,0:T(8,128)(2,1)S(1)}, u32[]{:S(2)}, u32[]{:S(2)}) %collective-permute-start.7) | collective-permute-done | bytes 221216 | tf_op jit(solution)/shard_map/ppermute | solution.py:292
  36.7 4.4 %collective-permute-start.10 = (bf16[96,256]{1,0:T(8,128)(2,1)S(1)}, bf16[96,256]{1,0:T(8,128)(2,1)S(1)}, u32[]{:S(2)}, u32[]{:S(2)}) collective-permute-start(bf16[96,256]{1,0:T(8,128)(2,1)S(1)} %get-tuple-element.41), channel_id=1, source_target_pairs={{0,8},{1,9},{2,10},{3,11},{4,12},{5,13},{6,14},{7,15},{8,0},{9,1},... | collective-permute-start | bytes 147464 | tf_op jit(solution)/shard_map/ppermute | solution.py:292
  41.1 1.3 %collective-permute-start.11 = (bf16[96,256]{1,0:T(8,128)(2,1)S(1)}, bf16[96,256]{1,0:T(8,128)(2,1)S(1)}, u32[]{:S(2)}, u32[]{:S(2)}) collective-permute-start(bf16[96,256]{1,0:T(8,128)(2,1)S(1)} %get-tuple-element.42), channel_id=1, source_target_pairs={{0,12},{1,13},{2,14},{3,15},{4,8},{5,9},{6,10},{7,11},{8,4},{9,5},... | collective-permute-start | bytes 147464 | tf_op jit(solution)/shard_map/ppermute | solution.py:292
  42.4 1.2 %collective-permute-done.12.pair = f32[16,48]{1,0:T(8,128)S(1)} collective-permute-done((f32[16,48]{1,0:T(8,128)S(1)}, f32[16,48]{1,0:T(8,128)S(1)}, u32[]{:S(2)}, u32[]{:S(2)}) %collective-permute-start.12) | collective-permute-done | bytes 3104 | tf_op jit(solution)/shard_map/ppermute | solution.py:292
  44.6 2.4 %collective-permute-done.11.z3 = bf16[96,256]{1,0:T(8,128)(2,1)S(1)} collective-permute-done((bf16[96,256]{1,0:T(8,128)(2,1)S(1)}, bf16[96,256]{1,0:T(8,128)(2,1)S(1)}, u32[]{:S(2)}, u32[]{:S(2)}) %collective-permute-start.11) | collective-permute-done | bytes 49184 | tf_op jit(solution)/shard_map/ppermute | solution.py:292
  47.0 1.8 %shard_map.72 = (bf16[128,1280]{1,0:T(8,128)(2,1)S(1)}, bf16[128,1280]{1,0:T(8,128)(2,1)S(1)}, bf16[128,1280]{1,0:T(8,128)(2,1)S(1)}, bf16[128,1280]{1,0:T(8,128)(2,1)S(1)}) custom-call(bf16[96,256]{1,0:T(8,128)(2,1)S(1)} %get-tuple-element.39.z0, bf16[96,256]{1,0:T(8,128)(2,1)S(1)} %collective-permute-done.9.z1, ...), custom_call_target="tpu_custom_call" | custom-call | flops 1 | bytes 1 | tf_op jit(solution)/shard_map/pallas_call | solution.py:43
  48.8 1.6 %collective-permute-start.14 = (bf16[4,32,1280]{2,1,0:T(8,128)(2,1)S(1)}, bf16[4,32,1280]{2,1,0:T(8,128)(2,1)S(1)}, u32[]{:S(2)}, u32[]{:S(2)}) collective-permute-start(bf16[4,32,1280]{2,1,0:T(8,128)(2,1)S(1)} %bitcast.26), channel_id=1, source_target_pairs={{0,2},{1,3},{2,0},{3,1},{4,6},{5,7},{6,4},{7,5},{8,10},{9,11},{10,... | collective-permute-start | bytes 983048 | tf_op jit(solution)/shard_map/ppermute | solution.py:292
  50.6 2.4 %collective-permute-start.16 = (bf16[32,896]{1,0:T(8,128)(2,1)S(1)}, bf16[32,896]{1,0:T(8,128)(2,1)S(1)}, u32[]{:S(2)}, u32[]{:S(2)}) collective-permute-start(bf16[32,896]{1,0:T(8,128)(2,1)S(1)} %get-tuple-element.49), channel_id=1, source_target_pairs={{0,8},{1,9},{2,10},{3,11},{4,12},{5,13},{6,14},{7,15},{8,0},{9,1},... | collective-permute-start | bytes 172040 | tf_op jit(solution)/shard_map/ppermute | solution.py:292
  53.0 1.8 %collective-permute-start.17 = (bf16[32,896]{1,0:T(8,128)(2,1)S(1)}, bf16[32,896]{1,0:T(8,128)(2,1)S(1)}, u32[]{:S(2)}, u32[]{:S(2)}) collective-permute-start(bf16[32,896]{1,0:T(8,128)(2,1)S(1)} %get-tuple-element.50), channel_id=1, source_target_pairs={{0,12},{1,13},{2,14},{3,15},{4,8},{5,9},{6,10},{7,11},{8,4},{9,5},... | collective-permute-start | bytes 172040 | tf_op jit(solution)/shard_map/ppermute | solution.py:292
  55.7 3.3 %collective-permute-done.17.c3 = bf16[32,896]{1,0:T(8,128)(2,1)S(1)} collective-permute-done((bf16[32,896]{1,0:T(8,128)(2,1)S(1)}, bf16[32,896]{1,0:T(8,128)(2,1)S(1)}, u32[]{:S(2)}, u32[]{:S(2)}) %collective-permute-start.17) | collective-permute-done | bytes 57376 | tf_op jit(solution)/shard_map/ppermute | solution.py:292
  60.0 2.7 %shard_map.73 = (f32[32,32]{1,0:T(8,128)S(1)}, f32[32,3584]{1,0:T(8,128)}) custom-call(bf16[32,896]{1,0:T(8,128)(2,1)S(1)} %get-tuple-element.51.c0, bf16[32,896]{1,0:T(8,128)(2,1)S(1)} %collective-permute-done.15.c1, bf16[32,896]{1,0:T(8,128)(2,1)S(1)} %collective-permute-done.16.c2, bf16[32,896]{1,0:T(8,128)(2,1)S(1)} %collective-permute-done.17.c3), custom_call_target="tpu_custom_call" | custom-call | flops 1 | bytes 1 | tf_op jit(solution)/shard_map/pallas_call | solution.py:43
  62.7 1.5 %collective-permute-done.18 = bf16[4,32,1280]{2,1,0:T(8,128)(2,1)S(1)} collective-permute-done((bf16[4,32,1280]{2,1,0:T(8,128)(2,1)S(1)}, bf16[4,32,1280]{2,1,0:T(8,128)(2,1)S(1)}, u32[]{:S(2)}, u32[]{:S(2)}) %collective-permute-start.18) | collective-permute-done | bytes 327712 | tf_op jit(solution)/shard_map/ppermute | solution.py:292
  65.6 2.4 %collective-permute-start.20 = (bf16[32,1280]{1,0:T(8,128)(2,1)S(1)}, bf16[32,1280]{1,0:T(8,128)(2,1)S(1)}, u32[]{:S(2)}, u32[]{:S(2)}) collective-permute-start(bf16[32,1280]{1,0:T(8,128)(2,1)S(1)} %get-tuple-element.74), channel_id=1, source_target_pairs={{0,8},{1,9},{2,10},{3,11},{4,12},{5,13},{6,14},{7,15},{8,0},{9,1},... | collective-permute-start | bytes 245768 | tf_op jit(solution)/shard_map/ppermute | solution.py:292
  68.0 3.5 %collective-permute-done.21 = bf16[2,32,1280]{2,1,0:T(8,128)(2,1)S(1)} collective-permute-done((bf16[2,32,1280]{2,1,0:T(8,128)(2,1)S(1)}, bf16[2,32,1280]{2,1,0:T(8,128)(2,1)S(1)}, u32[]{:S(2)}, u32[]{:S(2)}) %collective-permute-start.21) | collective-permute-done | bytes 163872 | tf_op jit(solution)/shard_map/ppermute | solution.py:292
  71.8 5.2 %collective-permute-done.22.refs_3_ = bf16[32,1280]{1,0:T(8,128)(2,1)S(1)} collective-permute-done((bf16[32,1280]{1,0:T(8,128)(2,1)S(1)}, bf16[32,1280]{1,0:T(8,128)(2,1)S(1)}, u32[]{:S(2)}, u32[]{:S(2)}) %collective-permute-start.22) | collective-permute-done | bytes 81952 | tf_op jit(solution)/shard_map/ppermute | solution.py:292
  77.0 1.1 %shard_map.74 = f32[32,2560]{1,0:T(8,128)} custom-call(f32[32,32]{1,0:T(8,128)S(1)} %get-tuple-element.60.inverse, bf16[32,1280]{1,0:T(8,128)(2,1)S(1)} %get-tuple-element.75.refs_0_, bf16[32,1280]{1,0:T(8,128)(2,1)S(1)} %collective-permute-done.20.refs_1_, bf16[32,1280]{1,0:T(8,128)(2,1)S(1)} %get-tuple-element.73.refs_2_, ...), custom_call_target="tpu_custom_call" | custom-call | flops 1 | bytes 1 | tf_op jit(solution)/shard_map/pallas_call | solution.py:43
  (51 shorter events, 9.7 us)
Async XLA Ops:
  4.6 42.4 %collective-permute-start.13 = (bf16[384,2560]{1,0:T(8,128)(2,1)S(1)}, bf16[384,2560]{1,0:T(8,128)(2,1)S(1)}, u32[]{:S(2)}, u32[]{:S(2)}) collective-permute-start(bf16[384,2560]{1,0:T(8,128)(2,1)S(1)} %bitcast.21), channel_id=1, source_target_pairs={{0,1},{1,0},{2,3},{3,2},{4,5},{5,4},{6,7},{7,6},{8,9},{9,8},{10,11... | collective-permute-start | bytes 5898248 | tf_op jit(solution)/shard_map/ppermute | solution.py:292
  5.1 17.6 %collective-permute-start.3 = (bf16[48,1408]{1,0:T(8,128)(2,1)}, bf16[48,1408]{1,0:T(8,128)(2,1)S(1)}, u32[]{:S(2)}, u32[]{:S(2)}) collective-permute-start(bf16[48,1408]{1,0:T(8,128)(2,1)} %get-tuple-element.36), channel_id=1, source_target_pairs={{0,4},{1,5},{2,6},{3,7},{4,0},{5,1},{6,2},{7,3},{8,12},{9,13},{10,... | collective-permute-start | bytes 405512 | tf_op jit(solution)/shard_map/ppermute | solution.py:292
  7.8 13.4 %collective-permute-start = (bf16[48,1408]{1,0:T(8,128)(2,1)}, bf16[48,1408]{1,0:T(8,128)(2,1)S(1)}, u32[]{:S(2)}, u32[]{:S(2)}) collective-permute-start(bf16[48,1408]{1,0:T(8,128)(2,1)} %get-tuple-element.33), channel_id=1, source_target_pairs={{0,8},{1,9},{2,10},{3,11},{4,12},{5,13},{6,14},{7,15},{8,0},{9,1},... | collective-permute-start | bytes 405512 | tf_op jit(solution)/shard_map/ppermute | solution.py:292
  10.4 10.8 %collective-permute-start.1 = (bf16[48,1408]{1,0:T(8,128)(2,1)}, bf16[48,1408]{1,0:T(8,128)(2,1)S(1)}, u32[]{:S(2)}, u32[]{:S(2)}) collective-permute-start(bf16[48,1408]{1,0:T(8,128)(2,1)} %get-tuple-element.34), channel_id=1, source_target_pairs={{0,12},{1,13},{2,14},{3,15},{4,8},{5,9},{6,10},{7,11},{8,4},{9,5},... | collective-permute-start | bytes 405512 | tf_op jit(solution)/shard_map/ppermute | solution.py:292
  21.2 9.5 %collective-permute-start.2 = (bf16[96,1408]{1,0:T(8,128)(2,1)S(1)}, bf16[96,1408]{1,0:T(8,128)(2,1)S(1)}, u32[]{:S(2)}, u32[]{:S(2)}) collective-permute-start(bf16[96,1408]{1,0:T(8,128)(2,1)S(1)} %constant_dynamic-update-slice_fusion.refs_1_.near_b), channel_id=1, source_target_pairs={{0,2},{1,3},{2,0},{3,1},{4,6},{5,7},{6,4},{7,5},{8,10},{9,11},{10,... | collective-permute-start | bytes 811016 | tf_op jit(solution)/shard_map/ppermute | solution.py:292
  22.8 11.3 %collective-permute-start.6 = (bf16[96,1408]{1,0:T(8,128)(2,1)S(1)}, bf16[96,1408]{1,0:T(8,128)(2,1)S(1)}, u32[]{:S(2)}, u32[]{:S(2)}) collective-permute-start(bf16[96,1408]{1,0:T(8,128)(2,1)S(1)} %constant_dynamic-update-slice_fusion.2.refs_0_.near_a), channel_id=1, source_target_pairs={{0,2},{1,3},{2,0},{3,1},{4,6},{5,7},{6,4},{7,5},{8,10},{9,11},{10,... | collective-permute-start | bytes 811016 | tf_op jit(solution)/shard_map/ppermute | solution.py:292
  23.4 1.5 %collective-permute-start.4 = (bf16[96,1152]{1,0:T(8,128)(2,1)S(1)}, bf16[96,1152]{1,0:T(8,128)(2,1)S(1)}, u32[]{:S(2)}, u32[]{:S(2)}) collective-permute-start(bf16[96,1152]{1,0:T(8,128)(2,1)S(1)} %slice.32), channel_id=1, source_target_pairs={{0,1},{1,0},{2,3},{3,2},{4,5},{5,4},{6,7},{7,6},{8,9},{9,8},{10,11... | collective-permute-start | bytes 663560 | tf_op jit(solution)/shard_map/ppermute | solution.py:292
  23.5 1.8 %collective-permute-start.5 = (bf16[96,1152]{1,0:T(8,128)(2,1)S(1)}, bf16[96,1152]{1,0:T(8,128)(2,1)S(1)}, u32[]{:S(2)}, u32[]{:S(2)}) collective-permute-start(bf16[96,1152]{1,0:T(8,128)(2,1)S(1)} %slice.33), channel_id=1, source_target_pairs={{0,1},{1,0},{2,3},{3,2},{4,5},{5,4},{6,7},{7,6},{8,9},{9,8},{10,11... | collective-permute-start | bytes 663560 | tf_op jit(solution)/shard_map/ppermute | solution.py:292
  25.9 16.5 %copy-start.1 = (f32[16,48]{1,0:T(8,128)S(1)}, f32[16,48]{1,0:T(8,128)}, u32[]{:S(2)}) copy-start(f32[16,48]{1,0:T(8,128)} %get-tuple-element.44.own) | copy-start | bytes 9220
  30.7 3.5 %collective-permute-start.8 = (bf16[96,1152]{1,0:T(8,128)(2,1)S(1)}, bf16[96,1152]{1,0:T(8,128)(2,1)S(1)}, u32[]{:S(2)}, u32[]{:S(2)}) collective-permute-start(bf16[96,1152]{1,0:T(8,128)(2,1)S(1)} %slice.27), channel_id=1, source_target_pairs={{0,1},{1,0},{2,3},{3,2},{4,5},{5,4},{6,7},{7,6},{8,9},{9,8},{10,11... | collective-permute-start | bytes 663560 | tf_op jit(solution)/shard_map/ppermute | solution.py:292
  34.2 1.5 %collective-permute-start.7 = (bf16[96,1152]{1,0:T(8,128)(2,1)S(1)}, bf16[96,1152]{1,0:T(8,128)(2,1)S(1)}, u32[]{:S(2)}, u32[]{:S(2)}) collective-permute-start(bf16[96,1152]{1,0:T(8,128)(2,1)S(1)} %slice.34), channel_id=1, source_target_pairs={{0,1},{1,0},{2,3},{3,2},{4,5},{5,4},{6,7},{7,6},{8,9},{9,8},{10,11... | collective-permute-start | bytes 663560 | tf_op jit(solution)/shard_map/ppermute | solution.py:292
  36.7 8.0 %collective-permute-start.10 = (bf16[96,256]{1,0:T(8,128)(2,1)S(1)}, bf16[96,256]{1,0:T(8,128)(2,1)S(1)}, u32[]{:S(2)}, u32[]{:S(2)}) collective-permute-start(bf16[96,256]{1,0:T(8,128)(2,1)S(1)} %get-tuple-element.41), channel_id=1, source_target_pairs={{0,8},{1,9},{2,10},{3,11},{4,12},{5,13},{6,14},{7,15},{8,0},{9,1},... | collective-permute-start | bytes 147464 | tf_op jit(solution)/shard_map/ppermute | solution.py:292
  41.1 6.0 %collective-permute-start.11 = (bf16[96,256]{1,0:T(8,128)(2,1)S(1)}, bf16[96,256]{1,0:T(8,128)(2,1)S(1)}, u32[]{:S(2)}, u32[]{:S(2)}) collective-permute-start(bf16[96,256]{1,0:T(8,128)(2,1)S(1)} %get-tuple-element.42), channel_id=1, source_target_pairs={{0,12},{1,13},{2,14},{3,15},{4,8},{5,9},{6,10},{7,11},{8,4},{9,5},... | collective-permute-start | bytes 147464 | tf_op jit(solution)/shard_map/ppermute | solution.py:292
  42.4 4.6 %collective-permute-start.9 = (bf16[96,256]{1,0:T(8,128)(2,1)S(1)}, bf16[96,256]{1,0:T(8,128)(2,1)S(1)}, u32[]{:S(2)}, u32[]{:S(2)}) collective-permute-start(bf16[96,256]{1,0:T(8,128)(2,1)S(1)} %get-tuple-element.40), channel_id=1, source_target_pairs={{0,4},{1,5},{2,6},{3,7},{4,0},{5,1},{6,2},{7,3},{8,12},{9,13},{10,... | collective-permute-start | bytes 147464 | tf_op jit(solution)/shard_map/ppermute | solution.py:292
  42.4 1.2 %collective-permute-start.12 = (f32[16,48]{1,0:T(8,128)S(1)}, f32[16,48]{1,0:T(8,128)S(1)}, u32[]{:S(2)}, u32[]{:S(2)}) collective-permute-start(f32[16,48]{1,0:T(8,128)S(1)} %copy-done.1), channel_id=1, source_target_pairs={{0,1},{1,0},{2,3},{3,2},{4,5},{5,4},{6,7},{7,6},{8,9},{9,8},{10,11... | collective-permute-start | bytes 9224 | tf_op jit(solution)/shard_map/ppermute | solution.py:292
  48.8 10.5 %collective-permute-start.14 = (bf16[4,32,1280]{2,1,0:T(8,128)(2,1)S(1)}, bf16[4,32,1280]{2,1,0:T(8,128)(2,1)S(1)}, u32[]{:S(2)}, u32[]{:S(2)}) collective-permute-start(bf16[4,32,1280]{2,1,0:T(8,128)(2,1)S(1)} %bitcast.26), channel_id=1, source_target_pairs={{0,2},{1,3},{2,0},{3,1},{4,6},{5,7},{6,4},{7,5},{8,10},{9,11},{10,... | collective-permute-start | bytes 983048 | tf_op jit(solution)/shard_map/ppermute | solution.py:292
  50.4 4.9 %collective-permute-start.15 = (bf16[32,896]{1,0:T(8,128)(2,1)S(1)}, bf16[32,896]{1,0:T(8,128)(2,1)S(1)}, u32[]{:S(2)}, u32[]{:S(2)}) collective-permute-start(bf16[32,896]{1,0:T(8,128)(2,1)S(1)} %get-tuple-element.48), channel_id=1, source_target_pairs={{0,4},{1,5},{2,6},{3,7},{4,0},{5,1},{6,2},{7,3},{8,12},{9,13},{10,... | collective-permute-start | bytes 172040 | tf_op jit(solution)/shard_map/ppermute | solution.py:292
  50.6 5.1 %collective-permute-start.16 = (bf16[32,896]{1,0:T(8,128)(2,1)S(1)}, bf16[32,896]{1,0:T(8,128)(2,1)S(1)}, u32[]{:S(2)}, u32[]{:S(2)}) collective-permute-start(bf16[32,896]{1,0:T(8,128)(2,1)S(1)} %get-tuple-element.49), channel_id=1, source_target_pairs={{0,8},{1,9},{2,10},{3,11},{4,12},{5,13},{6,14},{7,15},{8,0},{9,1},... | collective-permute-start | bytes 172040 | tf_op jit(solution)/shard_map/ppermute | solution.py:292
  53.0 6.0 %collective-permute-start.17 = (bf16[32,896]{1,0:T(8,128)(2,1)S(1)}, bf16[32,896]{1,0:T(8,128)(2,1)S(1)}, u32[]{:S(2)}, u32[]{:S(2)}) collective-permute-start(bf16[32,896]{1,0:T(8,128)(2,1)S(1)} %get-tuple-element.50), channel_id=1, source_target_pairs={{0,12},{1,13},{2,14},{3,15},{4,8},{5,9},{6,10},{7,11},{8,4},{9,5},... | collective-permute-start | bytes 172040 | tf_op jit(solution)/shard_map/ppermute | solution.py:292
  54.8 9.4 %collective-permute-start.18 = (bf16[4,32,1280]{2,1,0:T(8,128)(2,1)S(1)}, bf16[4,32,1280]{2,1,0:T(8,128)(2,1)S(1)}, u32[]{:S(2)}, u32[]{:S(2)}) collective-permute-start(bf16[4,32,1280]{2,1,0:T(8,128)(2,1)S(1)} %bitcast.25), channel_id=1, source_target_pairs={{0,2},{1,3},{2,0},{3,1},{4,6},{5,7},{6,4},{7,5},{8,10},{9,11},{10,... | collective-permute-start | bytes 983048 | tf_op jit(solution)/shard_map/ppermute | solution.py:292
  59.5 5.4 %collective-permute-start.19 = (bf16[2,32,1280]{2,1,0:T(8,128)(2,1)S(1)}, bf16[2,32,1280]{2,1,0:T(8,128)(2,1)S(1)}, u32[]{:S(2)}, u32[]{:S(2)}) collective-permute-start(bf16[2,32,1280]{2,1,0:T(8,128)(2,1)S(1)} %pad_maximum_fusion), channel_id=1, source_target_pairs={{0,4},{1,5},{2,6},{3,7},{4,0},{5,1},{6,2},{7,3},{8,12},{9,13},{10,... | collective-permute-start | bytes 491528 | tf_op jit(solution)/shard_map/ppermute | solution.py:292
  65.0 6.5 %collective-permute-start.21 = (bf16[2,32,1280]{2,1,0:T(8,128)(2,1)S(1)}, bf16[2,32,1280]{2,1,0:T(8,128)(2,1)S(1)}, u32[]{:S(2)}, u32[]{:S(2)}) collective-permute-start(bf16[2,32,1280]{2,1,0:T(8,128)(2,1)S(1)} %pad_maximum_fusion.1), channel_id=1, source_target_pairs={{0,4},{1,5},{2,6},{3,7},{4,0},{5,1},{6,2},{7,3},{8,12},{9,13},{10,... | collective-permute-start | bytes 491528 | tf_op jit(solution)/shard_map/ppermute | solution.py:292
  65.6 6.2 %collective-permute-start.20 = (bf16[32,1280]{1,0:T(8,128)(2,1)S(1)}, bf16[32,1280]{1,0:T(8,128)(2,1)S(1)}, u32[]{:S(2)}, u32[]{:S(2)}) collective-permute-start(bf16[32,1280]{1,0:T(8,128)(2,1)S(1)} %get-tuple-element.74), channel_id=1, source_target_pairs={{0,8},{1,9},{2,10},{3,11},{4,12},{5,13},{6,14},{7,15},{8,0},{9,1},... | collective-permute-start | bytes 245768 | tf_op jit(solution)/shard_map/ppermute | solution.py:292
  71.6 5.4 %collective-permute-start.22 = (bf16[32,1280]{1,0:T(8,128)(2,1)S(1)}, bf16[32,1280]{1,0:T(8,128)(2,1)S(1)}, u32[]{:S(2)}, u32[]{:S(2)}) collective-permute-start(bf16[32,1280]{1,0:T(8,128)(2,1)S(1)} %get-tuple-element.72), channel_id=1, source_target_pairs={{0,8},{1,9},{2,10},{3,11},{4,12},{5,13},{6,14},{7,15},{8,0},{9,1},... | collective-permute-start | bytes 245768 | tf_op jit(solution)/shard_map/ppermute | solution.py:292
  (1 other events, 4.0 us)
